TPU v7x, 32 devices: a whole 2x2x4 slice. The times are simulated.
32 devices in a mesh: gx: 4 (over y, x), gy: 2 (over core), gz: 4 (over z).
Axes of the slice: x: 2, y: 2, z: 4, core: 2. Of those that a mesh axis runs over, the one named last changes fastest.
Arguments:
- right_side: float32 [1, 64, 32, 512], P(None, 'gz', 'gy', 'gx'), may hold values from -6 to 6
- coefficient: float32 [64, 32, 512], P('gz', 'gy', 'gx'), may hold values from 0.25 to 4
Outputs:
- solution: float32 [1, 64, 32, 512], P(None, 'gz', 'gy', 'gx')
- residual: float32 [1, 64, 32, 512], P(None, 'gz', 'gy', 'gx')
All inputs are finite; a program needn't handle non-finite values.
Results may differ from a plain program's by a relative error of at most 0.0005.
Values sent between devices are 32-bit elements; how exact they have to be, the bound alone decides.
No kernel may reach another device: no remote copies, remote signals or barrier semaphores. Data moves between devices by JAX's collectives and lax.ppermute only.
A program may use at most 192 MiB of HBM per device.

v0:
```python
import jax
import jax.numpy as jnp
from jax import lax
from jax.sharding import PartitionSpec as P

LEVELS = 5
DEGREE = 3


eig_low = 0.5
eig_high = 2.0
centre_value = 0.5 * (eig_low + eig_high)
half_width = 0.5 * (eig_high - eig_low)
first_scale = 1.0 / centre_value


def extended(cells, sides, width):
    for axis, dim in sides:
        count = lax.axis_size(axis)
        ends = count - 1
        head = lax.slice_in_dim(cells, 0, width, axis=dim)
        tail = lax.slice_in_dim(cells, cells.shape[dim] - width, cells.shape[dim], axis=dim)
        cells = jnp.concatenate(
            [
                lax.ppermute(tail, axis, [(i, (i + 1) % count) for i in range(ends)]),
                cells,
                lax.ppermute(head, axis, [((i + 1) % count, i) for i in range(ends)]),
            ],
            axis=dim,
        )
    return cells


def from_partner(value, axis, distance):
    mask = 2**distance
    pairs = [(source, source ^ mask) for source in range(lax.axis_size(axis))]
    return lax.ppermute(value, axis, pairs)


def cheb_terms():
    rho_now = half_width / centre_value
    listed = []
    for iteration in range(1, DEGREE):
        rho_next = 1.0 / (2.0 * centre_value / half_width - rho_now)
        listed.append((rho_next * rho_now, 2.0 * rho_next / half_width))
        rho_now = rho_next
    return listed


def face_terms(coef_pad):
    face_z = 0.5 * (coef_pad[:, 1:, 1:-1, 1:-1] + coef_pad[:, :-1, 1:-1, 1:-1])
    face_y = 0.5 * (coef_pad[:, 1:-1, 1:, 1:-1] + coef_pad[:, 1:-1, :-1, 1:-1])
    face_x = 0.5 * (coef_pad[:, 1:-1, 1:-1, 1:] + coef_pad[:, 1:-1, 1:-1, :-1])
    diagonal = (
        face_z[:, 1:]
        + face_z[:, :-1]
        + face_y[:, :, 1:]
        + face_y[:, :, :-1]
        + face_x[..., 1:]
        + face_x[..., :-1]
    )
    return (face_z, face_y, face_x, diagonal)


def apply_padded(field_pad, face_set):
    face_z, face_y, face_x, diagonal = face_set
    result = diagonal * field_pad[:, 1:-1, 1:-1, 1:-1]
    result = (
        result
        - face_z[:, 1:] * field_pad[:, 2:, 1:-1, 1:-1]
        - face_z[:, :-1] * field_pad[:, :-2, 1:-1, 1:-1]
    )
    result = (
        result
        - face_y[:, :, 1:] * field_pad[:, 1:-1, 2:, 1:-1]
        - face_y[:, :, :-1] * field_pad[:, 1:-1, :-2, 1:-1]
    )
    result = (
        result
        - face_x[..., 1:] * field_pad[:, 1:-1, 1:-1, 2:]
        - face_x[..., :-1] * field_pad[:, 1:-1, 1:-1, :-2]
    )
    return result


def restrict(field):
    comp_count, z_cells, y_cells, x_cells = field.shape
    blocks = field.reshape(comp_count, z_cells // 2, 2, y_cells // 2, 2, x_cells // 2, 2)
    return jnp.mean(blocks, axis=(2, 4, 6))


def refine(coarse_pad, axis_dim):
    cell_count = coarse_pad.shape[axis_dim] - 2
    centre_cells = lax.slice_in_dim(coarse_pad, 1, cell_count + 1, axis=axis_dim)
    low_cells = lax.slice_in_dim(coarse_pad, 0, cell_count, axis=axis_dim)
    high_cells = lax.slice_in_dim(coarse_pad, 2, cell_count + 2, axis=axis_dim)
    even_cells = 0.75 * centre_cells + 0.25 * low_cells
    odd_cells = 0.75 * centre_cells + 0.25 * high_cells
    stacked = jnp.stack([even_cells, odd_cells], axis=axis_dim + 1)
    new_shape = list(centre_cells.shape)
    new_shape[axis_dim] = 2 * cell_count
    return stacked.reshape(new_shape)


def prolong(coarse_pad):
    return refine(refine(refine(coarse_pad, 3), 2), 1)


def split_rim(field):
    return extended(field, (("gx", 3), ("gy", 2), ("gz", 1)), 1)


def slab_rim(field):
    padded = extended(field, (("gz", 1),), 1)
    return jnp.pad(padded, ((0, 0), (0, 0), (1, 1), (1, 1)))


def apply_level(field, face_set, joined):
    if joined:
        field_pad = slab_rim(field)
    else:
        field_pad = split_rim(field)
    return apply_padded(field_pad, face_set)


def smooth(estimate, residual, face_set, joined):
    diagonal = face_set[3]
    update = residual / diagonal * first_scale
    estimate = estimate + update
    for keep_scale, push_scale in cheb_terms():
        residual = residual - apply_level(update, face_set, joined)
        update = keep_scale * update + push_scale * (residual / diagonal)
        estimate = estimate + update
    return estimate


def plain_smooth(source, coef_level, joined):
    if joined:
        coef_pad = slab_rim(coef_level)
    else:
        coef_pad = split_rim(coef_level)
    face_set = face_terms(coef_pad)
    return (smooth(jnp.zeros_like(source), source, face_set, joined), face_set)


def join_block(joined_block):
    for bit_index in range(lax.axis_size("gx").bit_length() - 1):
        partner = from_partner(joined_block, "gx", bit_index)
        lower_half = lax.axis_index("gx") // (1 << bit_index) % 2 == 0
        joined_block = jnp.where(
            lower_half,
            jnp.concatenate([joined_block, partner], axis=3),
            jnp.concatenate([partner, joined_block], axis=3),
        )
    for bit_index in range(lax.axis_size("gy").bit_length() - 1):
        partner = from_partner(joined_block, "gy", bit_index)
        lower_half = lax.axis_index("gy") // (1 << bit_index) % 2 == 0
        joined_block = jnp.where(
            lower_half,
            jnp.concatenate([joined_block, partner], axis=2),
            jnp.concatenate([partner, joined_block], axis=2),
        )
    return joined_block


def coarse_rim(correction, coarse_joined, fine_joined):
    if not coarse_joined:
        return extended(correction, (("gx", 3), ("gy", 2), ("gz", 1)), 1)
    padded = slab_rim(correction)
    if fine_joined:
        return padded
    row_count = (padded.shape[2] - 2) // lax.axis_size("gy")
    col_count = (padded.shape[3] - 2) // lax.axis_size("gx")
    padded = lax.dynamic_slice_in_dim(padded, lax.axis_index("gy") * row_count, row_count + 2, 2)
    return lax.dynamic_slice_in_dim(padded, lax.axis_index("gx") * col_count, col_count + 2, 3)


def vcycle(level_index, source, coef_level, join_level):
    joined = level_index >= join_level
    comp_count = source.shape[0]
    estimate, face_set = plain_smooth(source, coef_level, joined)
    if level_index == LEVELS - 1:
        return (estimate, face_set)
    residual = source - apply_level(estimate, face_set, joined)
    coarse_source = 4.0 * restrict(residual)
    coarse_coef = restrict(coef_level)
    if level_index + 1 == join_level:
        stacked = join_block(jnp.concatenate([coarse_source, coarse_coef], axis=0))
        coarse_source = stacked[:comp_count]
        coarse_coef = stacked[comp_count:]
    correction, unused = vcycle(level_index + 1, coarse_source, coarse_coef, join_level)
    estimate = estimate + prolong(coarse_rim(correction, level_index + 1 >= join_level, joined))
    estimate = smooth(estimate, source - apply_level(estimate, face_set, joined), face_set, joined)
    return (estimate, face_set)


def local(right_side, coefficient):
    join_level = 3
    coef_level = coefficient[None]
    solution, face_set = vcycle(0, right_side, coef_level, join_level)
    residual = right_side - apply_level(solution, face_set, False)
    return (solution, residual)


def solution(mesh):
    return jax.shard_map(
        local,
        mesh=mesh,
        in_specs=(P(None, "gz", "gy", "gx"), P("gz", "gy", "gx")),
        out_specs=(P(None, "gz", "gy", "gx"), P(None, "gz", "gy", "gx")),
        check_vma=False,
    )
```

profile of v0, /device:TPU:0, one launch (start us, length us, event | category | flops | bytes accessed | tf_op | source)
XLA Modules:
  0.0 641.2 jit_solution(16422763764174371785)
XLA Ops:
  1.8 4.8 collective-permute-start
  40.9 9.7 %reshape_broadcast_in_dim.3 = f32[8,2,8,2,64,2]{5,4,3,2,1,0:T(8,128)} reshape(f32[16,16,128]{2,1,0:T(8,128)S(1)} %copy-done) | data formatting | bytes 262144 | tf_op jit(solution)/shard_map/reshape;broadcast_in_dim | solution.py:88
  56.0 4.8 collective-permute-start.11
  83.5 4.9 collective-permute-start.17
  97.7 4.9 collective-permute-start.29
  115.9 9.7 %reshape.388 = f32[8,2,8,2,64,2]{5,4,3,2,1,0:T(8,128)} reshape(f32[1,16,16,128]{3,2,1,0:T(8,128)S(1)} %fusion.71) | data formatting | bytes 262144 | tf_op jit(solution)/shard_map/reshape | solution.py:88
  135.1 4.9 collective-permute-done.31
  150.3 4.8 collective-permute-start.35
  173.0 4.8 collective-permute-start.41
  186.5 4.8 collective-permute-start.53
  210.6 4.9 collective-permute-done.55
  221.3 4.8 collective-permute-start.59
  243.8 4.8 collective-permute-start.65
  264.3 4.8 collective-permute-start.71
  280.8 4.8 collective-permute-start.76
  288.5 4.8 collective-permute-start.78
  400.8 4.9 collective-permute-done.106
  411.5 4.8 collective-permute-start.110
  434.0 4.8 collective-permute-start.116
  498.9 4.8 collective-permute-start.134
  519.9 4.8 collective-permute-start.140
  588.7 4.8 collective-permute-start.158
  611.2 4.8 collective-permute-start.164
  633.7 4.8 collective-permute-start.170
  (530 shorter events, 511.7 us)
Async XLA Ops:
  1.8 7.6 %collective-permute-start = (f32[1,16,16,1]{3,2,1,0:T(8,128)S(1)}, f32[1,16,16,1]{3,2,1,0:T(8,128)S(1)}, u32[]{:S(2)}, u32[]{:S(2)}) collective-permute-start(f32[1,16,16,1]{3,2,1,0:T(8,128)S(1)} %get-tuple-element.90), channel_id=1, source_target_pairs={{0,8},{8,16},{16,24},{1,9},{9,17},{17,25},{2,10},{10,18},{18,26},{... | collective-permute-start | bytes 3080 | tf_op jit(solution)/shard_map/ppermute | solution.py:25
  6.7 7.5 %collective-permute-start.1 = (f32[1,16,16,1]{3,2,1,0:T(8,128)S(1)}, f32[1,16,16,1]{3,2,1,0:T(8,128)S(1)}, u32[]{:S(2)}, u32[]{:S(2)}) collective-permute-start(f32[1,16,16,1]{3,2,1,0:T(8,128)S(1)} %get-tuple-element.91), channel_id=1, source_target_pairs={{8,0},{16,8},{24,16},{9,1},{17,9},{25,17},{10,2},{18,10},{26,18},{... | collective-permute-start | bytes 3080 | tf_op jit(solution)/shard_map/ppermute | solution.py:27
  38.3 16.3 %collective-permute-start.8 = (f32[1,16,1,130]{3,2,1,0:T(1,128)S(1)}, f32[1,16,1,130]{3,2,1,0:T(1,128)S(1)}, u32[]{:S(2)}, u32[]{:S(2)}) collective-permute-start(f32[1,16,1,130]{3,2,1,0:T(1,128)S(1)} %get-tuple-element.71), channel_id=1, source_target_pairs={{0,4},{1,5},{2,6},{3,7},{8,12},{9,13},{10,14},{11,15},{16,20},{17,... | collective-permute-start | bytes 24968 | tf_op jit(solution)/shard_map/ppermute | solution.py:25
  39.6 15.0 %collective-permute-start.9 = (f32[1,16,1,130]{3,2,1,0:T(1,128)S(1)}, f32[1,16,1,130]{3,2,1,0:T(1,128)S(1)}, u32[]{:S(2)}, u32[]{:S(2)}) collective-permute-start(f32[1,16,1,130]{3,2,1,0:T(1,128)S(1)} %get-tuple-element.70), channel_id=1, source_target_pairs={{4,0},{5,1},{6,2},{7,3},{12,8},{13,9},{14,10},{15,11},{20,16},{21,... | collective-permute-start | bytes 24968 | tf_op jit(solution)/shard_map/ppermute | solution.py:27
  62.9 11.9 %collective-permute-start.12 = (f32[1,16,16,1]{3,2,1,0:T(8,128)S(1)}, f32[1,16,16,1]{3,2,1,0:T(8,128)S(1)}, u32[]{:S(2)}, u32[]{:S(2)}) collective-permute-start(f32[1,16,16,1]{3,2,1,0:T(8,128)S(1)} %get-tuple-element.87), channel_id=1, source_target_pairs={{0,8},{8,16},{16,24},{1,9},{9,17},{17,25},{2,10},{10,18},{18,26},{... | collective-permute-start | bytes 3080 | tf_op jit(solution)/shard_map/ppermute | solution.py:25
  66.3 8.5 %collective-permute-start.13 = (f32[1,16,16,1]{3,2,1,0:T(8,128)S(1)}, f32[1,16,16,1]{3,2,1,0:T(8,128)S(1)}, u32[]{:S(2)}, u32[]{:S(2)}) collective-permute-start(f32[1,16,16,1]{3,2,1,0:T(8,128)S(1)} %get-tuple-element.86), channel_id=1, source_target_pairs={{8,0},{16,8},{24,16},{9,1},{17,9},{25,17},{10,2},{18,10},{26,18},{... | collective-permute-start | bytes 3080 | tf_op jit(solution)/shard_map/ppermute | solution.py:27
  67.7 9.9 %collective-permute-start.24 = (f32[1,8,8,1]{3,2,1,0:T(8,128)S(1)}, f32[1,8,8,1]{3,2,1,0:T(8,128)S(1)}, u32[]{:S(2)}, u32[]{:S(2)}) collective-permute-start(f32[1,8,8,1]{3,2,1,0:T(8,128)S(1)} %get-tuple-element.148), channel_id=1, source_target_pairs={{0,8},{8,16},{16,24},{1,9},{9,17},{17,25},{2,10},{10,18},{18,26},{... | collective-permute-start | bytes 776 | tf_op jit(solution)/shard_map/ppermute | solution.py:25
  78.1 18.1 %collective-permute-start.26 = (f32[1,8,1,66]{3,2,1,0:T(1,128)S(1)}, f32[1,8,1,66]{3,2,1,0:T(1,128)S(1)}, u32[]{:S(2)}, u32[]{:S(2)}) collective-permute-start(f32[1,8,1,66]{3,2,1,0:T(1,128)S(1)} %get-tuple-element.125), channel_id=1, source_target_pairs={{0,4},{1,5},{2,6},{3,7},{8,12},{9,13},{10,14},{11,15},{16,20},{17,... | collective-permute-start | bytes 6344 | tf_op jit(solution)/shard_map/ppermute | solution.py:25
  80.8 15.5 %collective-permute-start.27 = (f32[1,8,1,66]{3,2,1,0:T(1,128)S(1)}, f32[1,8,1,66]{3,2,1,0:T(1,128)S(1)}, u32[]{:S(2)}, u32[]{:S(2)}) collective-permute-start(f32[1,8,1,66]{3,2,1,0:T(1,128)S(1)} %get-tuple-element.124), channel_id=1, source_target_pairs={{4,0},{5,1},{6,2},{7,3},{12,8},{13,9},{14,10},{15,11},{20,16},{21,... | collective-permute-start | bytes 6344 | tf_op jit(solution)/shard_map/ppermute | solution.py:27
  90.4 12.2 %collective-permute-start.18 = (f32[1,16,16,1]{3,2,1,0:T(8,128)S(1)}, f32[1,16,16,1]{3,2,1,0:T(8,128)S(1)}, u32[]{:S(2)}, u32[]{:S(2)}) collective-permute-start(f32[1,16,16,1]{3,2,1,0:T(8,128)S(1)} %get-tuple-element.85), channel_id=1, source_target_pairs={{0,8},{8,16},{16,24},{1,9},{9,17},{17,25},{2,10},{10,18},{18,26},{... | collective-permute-start | bytes 3080 | tf_op jit(solution)/shard_map/ppermute | solution.py:25
  95.0 8.2 %collective-permute-start.19 = (f32[1,16,16,1]{3,2,1,0:T(8,128)S(1)}, f32[1,16,16,1]{3,2,1,0:T(8,128)S(1)}, u32[]{:S(2)}, u32[]{:S(2)}) collective-permute-start(f32[1,16,16,1]{3,2,1,0:T(8,128)S(1)} %get-tuple-element.84), channel_id=1, source_target_pairs={{8,0},{16,8},{24,16},{9,1},{17,9},{25,17},{10,2},{18,10},{26,18},{... | collective-permute-start | bytes 3080 | tf_op jit(solution)/shard_map/ppermute | solution.py:27
  96.4 17.6 %collective-permute-start.28 = (f32[1,1,10,66]{3,2,1,0:T(8,128)S(1)}, f32[1,1,10,66]{3,2,1,0:T(8,128)S(1)}, u32[]{:S(2)}, u32[]{:S(2)}) collective-permute-start(f32[1,1,10,66]{3,2,1,0:T(8,128)S(1)} %get-tuple-element.106), channel_id=1, source_target_pairs={{1,0},{2,1},{3,2},{5,4},{6,5},{7,6},{9,8},{10,9},{11,10},{13,12},{... | collective-permute-start | bytes 7928 | tf_op jit(solution)/shard_map/ppermute | solution.py:27
  97.7 16.3 %collective-permute-start.29 = (f32[1,1,10,66]{3,2,1,0:T(8,128)S(1)}, f32[1,1,10,66]{3,2,1,0:T(8,128)S(1)}, u32[]{:S(2)}, u32[]{:S(2)}) collective-permute-start(f32[1,1,10,66]{3,2,1,0:T(8,128)S(1)} %get-tuple-element.107), channel_id=1, source_target_pairs={{0,1},{1,2},{2,3},{4,5},{5,6},{6,7},{8,9},{9,10},{10,11},{12,13},{... | collective-permute-start | bytes 7928 | tf_op jit(solution)/shard_map/ppermute | solution.py:25
  140.1 8.8 %collective-permute-start.32 = (f32[1,8,1,66]{3,2,1,0:T(1,128)S(1)}, f32[1,8,1,66]{3,2,1,0:T(1,128)S(1)}, u32[]{:S(2)}, u32[]{:S(2)}) collective-permute-start(f32[1,8,1,66]{3,2,1,0:T(1,128)S(1)} %get-tuple-element.123), channel_id=1, source_target_pairs={{0,4},{1,5},{2,6},{3,7},{8,12},{9,13},{10,14},{11,15},{16,20},{17,... | collective-permute-start | bytes 6344 | tf_op jit(solution)/shard_map/ppermute | solution.py:25
  141.4 7.5 %collective-permute-start.33 = (f32[1,8,1,66]{3,2,1,0:T(1,128)S(1)}, f32[1,8,1,66]{3,2,1,0:T(1,128)S(1)}, u32[]{:S(2)}, u32[]{:S(2)}) collective-permute-start(f32[1,8,1,66]{3,2,1,0:T(1,128)S(1)} %get-tuple-element.122), channel_id=1, source_target_pairs={{4,0},{5,1},{6,2},{7,3},{12,8},{13,9},{14,10},{15,11},{20,16},{21,... | collective-permute-start | bytes 6344 | tf_op jit(solution)/shard_map/ppermute | solution.py:27
  142.8 12.4 %collective-permute-start.48 = (f32[1,4,4,1]{3,2,1,0:T(4,128)S(1)}, f32[1,4,4,1]{3,2,1,0:T(4,128)S(1)}, u32[]{:S(2)}, u32[]{:S(2)}) collective-permute-start(f32[1,4,4,1]{3,2,1,0:T(4,128)S(1)} %get-tuple-element.208), channel_id=1, source_target_pairs={{0,8},{8,16},{16,24},{1,9},{9,17},{17,25},{2,10},{10,18},{18,26},{... | collective-permute-start | bytes 200 | tf_op jit(solution)/shard_map/ppermute | solution.py:25
  147.6 7.6 %collective-permute-start.49 = (f32[1,4,4,1]{3,2,1,0:T(4,128)S(1)}, f32[1,4,4,1]{3,2,1,0:T(4,128)S(1)}, u32[]{:S(2)}, u32[]{:S(2)}) collective-permute-start(f32[1,4,4,1]{3,2,1,0:T(4,128)S(1)} %get-tuple-element.209), channel_id=1, source_target_pairs={{8,0},{16,8},{24,16},{9,1},{17,9},{25,17},{10,2},{18,10},{26,18},{... | collective-permute-start | bytes 200 | tf_op jit(solution)/shard_map/ppermute | solution.py:27
  156.8 8.5 %collective-permute-start.36 = (f32[1,8,8,1]{3,2,1,0:T(8,128)S(1)}, f32[1,8,8,1]{3,2,1,0:T(8,128)S(1)}, u32[]{:S(2)}, u32[]{:S(2)}) collective-permute-start(f32[1,8,8,1]{3,2,1,0:T(8,128)S(1)} %get-tuple-element.145), channel_id=1, source_target_pairs={{0,8},{8,16},{16,24},{1,9},{9,17},{17,25},{2,10},{10,18},{18,26},{... | collective-permute-start | bytes 776 | tf_op jit(solution)/shard_map/ppermute | solution.py:25
  162.6 15.2 %collective-permute-start.50 = (f32[1,4,1,34]{3,2,1,0:T(1,128)S(1)}, f32[1,4,1,34]{3,2,1,0:T(1,128)S(1)}, u32[]{:S(2)}, u32[]{:S(2)}) collective-permute-start(f32[1,4,1,34]{3,2,1,0:T(1,128)S(1)} %get-tuple-element.185), channel_id=1, source_target_pairs={{0,4},{1,5},{2,6},{3,7},{8,12},{9,13},{10,14},{11,15},{16,20},{17,... | collective-permute-start | bytes 1640 | tf_op jit(solution)/shard_map/ppermute | solution.py:25
  164.0 13.8 %collective-permute-start.51 = (f32[1,4,1,34]{3,2,1,0:T(1,128)S(1)}, f32[1,4,1,34]{3,2,1,0:T(1,128)S(1)}, u32[]{:S(2)}, u32[]{:S(2)}) collective-permute-start(f32[1,4,1,34]{3,2,1,0:T(1,128)S(1)} %get-tuple-element.184), channel_id=1, source_target_pairs={{4,0},{5,1},{6,2},{7,3},{12,8},{13,9},{14,10},{15,11},{20,16},{21,... | collective-permute-start | bytes 1640 | tf_op jit(solution)/shard_map/ppermute | solution.py:27
  179.5 11.8 %collective-permute-start.42 = (f32[1,8,8,1]{3,2,1,0:T(8,128)S(1)}, f32[1,8,8,1]{3,2,1,0:T(8,128)S(1)}, u32[]{:S(2)}, u32[]{:S(2)}) collective-permute-start(f32[1,8,8,1]{3,2,1,0:T(8,128)S(1)} %get-tuple-element.143), channel_id=1, source_target_pairs={{0,8},{8,16},{16,24},{1,9},{9,17},{17,25},{2,10},{10,18},{18,26},{... | collective-permute-start | bytes 776 | tf_op jit(solution)/shard_map/ppermute | solution.py:25
  183.9 7.4 %collective-permute-start.43 = (f32[1,8,8,1]{3,2,1,0:T(8,128)S(1)}, f32[1,8,8,1]{3,2,1,0:T(8,128)S(1)}, u32[]{:S(2)}, u32[]{:S(2)}) collective-permute-start(f32[1,8,8,1]{3,2,1,0:T(8,128)S(1)} %get-tuple-element.142), channel_id=1, source_target_pairs={{8,0},{16,8},{24,16},{9,1},{17,9},{25,17},{10,2},{18,10},{26,18},{... | collective-permute-start | bytes 776 | tf_op jit(solution)/shard_map/ppermute | solution.py:27
  185.2 16.7 %collective-permute-start.52 = (f32[1,1,6,34]{3,2,1,0:T(8,128)S(1)}, f32[1,1,6,34]{3,2,1,0:T(8,128)S(1)}, u32[]{:S(2)}, u32[]{:S(2)}) collective-permute-start(f32[1,1,6,34]{3,2,1,0:T(8,128)S(1)} %get-tuple-element.164), channel_id=1, source_target_pairs={{1,0},{2,1},{3,2},{5,4},{6,5},{7,6},{9,8},{10,9},{11,10},{13,12},{... | collective-permute-start | bytes 2456 | tf_op jit(solution)/shard_map/ppermute | solution.py:27
  186.5 15.4 %collective-permute-start.53 = (f32[1,1,6,34]{3,2,1,0:T(8,128)S(1)}, f32[1,1,6,34]{3,2,1,0:T(8,128)S(1)}, u32[]{:S(2)}, u32[]{:S(2)}) collective-permute-start(f32[1,1,6,34]{3,2,1,0:T(8,128)S(1)} %get-tuple-element.165), channel_id=1, source_target_pairs={{0,1},{1,2},{2,3},{4,5},{5,6},{6,7},{8,9},{9,10},{10,11},{12,13},{... | collective-permute-start | bytes 2456 | tf_op jit(solution)/shard_map/ppermute | solution.py:25
  (150 other events, 809.5 us)
where the time goes:
time: 646 us; the launch traced here: 641 us
  starting transfers between devices  401 us (62%)
  waiting for transfers between devices  183 us (28%)
  local copies, waits for them, and re-layouts  26.6 us (4%)
  other arithmetic  26.4 us (4%)
    ppermute x84, starting transfers between devices, extended(): lax.ppermute(tail, axis, [(i, (i + 1) % count) for i in range(ends)])  292 us
    ppermute x84, waiting for transfers between devices, extended(): lax.ppermute(head, axis, [((i + 1) % count, i) for i in range(ends)])  126 us
    ppermute x84, starting transfers between devices, extended(): lax.ppermute(head, axis, [((i + 1) % count, i) for i in range(ends)])  109 us
    ppermute x84, waiting for transfers between devices, extended(): lax.ppermute(tail, axis, [(i, (i + 1) % count) for i in range(ends)])  49.5 us
  transfers between devices with their start and end apart: 171, of which 88 were waited for; matrix products, arithmetic and copies ran while one was open for 3% of the time, Pallas kernels for 0%

commit v1 on v0

--- a/solution.py
+++ b/solution.py
@@ -1,6 +1,10 @@
+import functools
+
 import jax
 import jax.numpy as jnp
 from jax import lax
+from jax.experimental import pallas as pl
+from jax.experimental.pallas import tpu as pltpu
 from jax.sharding import PartitionSpec as P
 
 LEVELS = 5
@@ -202,9 +206,469 @@
     return (solution, residual)
 
 
+HALO_Z = 7
+HALO_Y = 8
+HALO_X = 8
+PAD = 3
+BF16 = jnp.bfloat16
+F32 = jnp.float32
+
+
+def parts_of(value):
+    high = value.astype(BF16)
+    return high, (value - high.astype(F32)).astype(BF16)
+
+
+def times_right(value, matrix):
+    high, low = parts_of(value)
+    return jnp.dot(high, matrix, preferred_element_type=F32) + jnp.dot(
+        low, matrix, preferred_element_type=F32
+    )
+
+
+def times_left(matrix, value):
+    high, low = parts_of(value)
+    return jnp.dot(matrix, high, preferred_element_type=F32) + jnp.dot(
+        matrix, low, preferred_element_type=F32
+    )
+
+
+def turned(value, shift, axis):
+    return pltpu.roll(value, shift % value.shape[axis], axis)
+
+
+def plane_neighbours(field, face_y, face_x):
+    return (
+        face_y * turned(field, -1, 0)
+        + turned(face_y * field, 1, 0)
+        + face_x * turned(field, -1, 1)
+        + turned(face_x * field, 1, 1)
+    )
+
+
+def plane_faces(coef, faces, start, stop, link_y, link_x, source=None, update=None):
+    face_z, face_y, face_x, diagonal, inverse = faces
+    back_y = None if link_y is None else turned(link_y, 1, 0)
+    back_x = None if link_x is None else turned(link_x, 1, 1)
+
+    def masked(value, mask):
+        return value if mask is None else value * mask
+
+    def body(plane, below):
+        own = coef[plane]
+        above = 0.5 * (own + coef[plane + 1])
+        up_y = 0.5 * (own + masked(turned(own, -1, 0), link_y))
+        down_y = 0.5 * (own + masked(turned(own, 1, 0), back_y))
+        up_x = 0.5 * (own + masked(turned(own, -1, 1), link_x))
+        down_x = 0.5 * (own + masked(turned(own, 1, 1), back_x))
+        total = above + below + up_y + down_y + up_x + down_x
+        turned_over = jnp.where(own > 0.0, 1.0 / jnp.where(own > 0.0, total, 1.0), 0.0)
+        face_z[plane] = above
+        face_y[plane] = masked(up_y, link_y)
+        face_x[plane] = masked(up_x, link_x)
+        diagonal[plane] = total
+        inverse[plane] = turned_over
+        if update is not None:
+            update[plane] = source[plane] * turned_over * first_scale
+        return above
+
+    lax.fori_loop(start, stop, body, 0.5 * (coef[start] + coef[start - 1]) if start else 0.5 * coef[0])
+
+
+def plane_sweep(faces, start, stop, field, finish):
+    face_z, face_y, face_x, diagonal, inverse = faces
+
+    def body(plane, below):
+        own = field[plane]
+        face = face_z[plane]
+        value = (
+            diagonal[plane] * own
+            - face * field[plane + 1]
+            - below
+            - plane_neighbours(own, face_y[plane], face_x[plane])
+        )
+        finish(plane, own, value)
+        return face * own
+
+    lax.fori_loop(start, stop, body, face_z[start - 1] * field[start - 1])
+
+
+def plane_steps(faces, ranges, source, residual, update, estimate, from_zero):
+    inverse = faces[4]
+    for step, ((keep, push), (start, stop)) in enumerate(zip(cheb_terms(), ranges)):
+        fresh = from_zero and step == 0
+
+        def finish(plane, own, value, keep=keep, push=push, fresh=fresh):
+            left = (source if fresh else residual)[plane] - value
+            new = keep * own + push * (left * inverse[plane])
+            residual[plane] = left
+            update[plane] = new
+            estimate[plane] = (own if fresh else estimate[plane]) + new
+
+        plane_sweep(faces, start, stop, update, finish)
+
+
+def plane_restart(faces, start, stop, source, residual, update, estimate):
+    inverse = faces[4]
+
+    def finish(plane, own, value):
+        left = source[plane] - value
+        new = left * inverse[plane] * first_scale
+        residual[plane] = left
+        update[plane] = new
+        estimate[plane] = own + new
+
+    plane_sweep(faces, start, stop, estimate, finish)
+
+
+def sheet_faces(coef, shape):
+    z_cells, y_cells, x_cells = shape
+    row = lax.broadcasted_iota(jnp.int32, coef.shape, 0)
+    lane = lax.broadcasted_iota(jnp.int32, coef.shape, 1)
+    links = (
+        (row < (z_cells - 1) * y_cells, y_cells, 0),
+        (row % y_cells < y_cells - 1, 1, 0),
+        (lane < x_cells - 1, 1, 1),
+    )
+    inside = lane < x_cells
+    total = 3.0 * coef
+    faces = []
+    for link, shift, axis in links:
+        above = jnp.where(link, turned(coef, -shift, axis), 0.0)
+        below = turned(jnp.where(link, coef, 0.0), shift, axis)
+        faces.append((jnp.where(link, 0.5 * (coef + above), 0.0), shift, axis))
+        total = total + 0.5 * (above + below)
+    inverse = jnp.where(inside, 1.0 / jnp.where(inside, total, 1.0), 0.0)
+    return faces, total, inverse
+
+
+def sheet_apply(field, face_set):
+    faces, diagonal, _ = face_set
+    value = diagonal * field
+    for face, shift, axis in faces:
+        value = value - (face * turned(field, -shift, axis) + turned(face * field, shift, axis))
+    return value
+
+
+def sheet_smooth(residual, face_set, estimate=None):
+    inverse = face_set[2]
+    update = residual * inverse * first_scale
+    estimate = update if estimate is None else estimate + update
+    for keep, push in cheb_terms():
+        residual = residual - sheet_apply(update, face_set)
+        update = keep * update + push * (residual * inverse)
+        estimate = estimate + update
+    return estimate, residual, update
+
+
+def sheet_cycle(source, coef, shape, depth, matrices):
+    face_set = sheet_faces(coef, shape)
+    estimate, residual, update = sheet_smooth(source, face_set)
+    if depth == LEVELS - 1:
+        return estimate
+    residual = residual - sheet_apply(update, face_set)
+    left_down, right_down, left_up, right_up = (ref[...] for ref in matrices[0])
+    coarse_source = 4.0 * times_right(times_left(left_down, residual), right_down)
+    coarse_coef = times_right(times_left(left_down, coef), right_down)
+    coarse_shape = tuple(count // 2 for count in shape)
+    correction = sheet_cycle(coarse_source, coarse_coef, coarse_shape, depth + 1, matrices[1:])
+    estimate = estimate + times_left(left_up, times_right(correction, right_up))
+    return sheet_smooth(source - sheet_apply(estimate, face_set), face_set, estimate)[0]
+
+
+def weight(fine, coarse):
+    own = fine >> 1
+    other = jnp.where(fine % 2 == 0, own - 1, own + 1)
+    return jnp.where(coarse == own, 0.75, 0.0) + jnp.where(coarse == other, 0.25, 0.0)
+
+
+def table(shape):
+    return jnp.arange(shape[0])[:, None], jnp.arange(shape[1])[None, :]
+
+
+def sheet_matrices(fine_shape, lanes):
+    z_cells, y_cells, x_cells = fine_shape
+    rows, coarse_rows = z_cells * y_cells, z_cells * y_cells // 4
+    half = y_cells // 2
+    coarse, fine = table((coarse_rows, rows))
+    same_z = coarse // half == fine // y_cells // 2
+    left_down = jnp.where(same_z & (coarse % half == fine % y_cells // 2), 0.25, 0.0)
+    fine, coarse = table((lanes, 128))
+    right_down = jnp.where((fine // 2 == coarse) & (fine < x_cells), 0.5, 0.0)
+    fine, coarse = table((rows, coarse_rows))
+    left_up = weight(fine // y_cells, coarse // half) * weight(fine % y_cells, coarse % half)
+    coarse, fine = table((128, lanes))
+    right_up = jnp.where((fine < x_cells) & (coarse < x_cells // 2), weight(fine, coarse), 0.0)
+    return [matrix.astype(BF16) for matrix in (left_down, right_down, left_up, right_up)]
+
+
+def own_down_matrices(z_pairs, y_cells, x_cells):
+    half = y_cells // 2
+    coarse, fine = table((z_pairs * half, z_pairs * y_cells))
+    left = jnp.where((coarse // half == fine // y_cells) & (coarse % half == fine % y_cells // 2), 1.0, 0.0)
+    fine, coarse = table((x_cells, x_cells))
+    right_source = jnp.where(fine // 2 == coarse, 0.5, 0.0)
+    right_coef = jnp.where(fine // 2 + x_cells // 2 == coarse, 0.125, 0.0)
+    return [matrix.astype(BF16) for matrix in (left, right_source, right_coef)]
+
+
+def one_down_matrices(z_pairs, y_cells, x_cells):
+    half = y_cells // 2
+    coarse, fine = table((z_pairs * half, z_pairs * y_cells))
+    left = jnp.where((coarse // half == fine // y_cells) & (coarse % half == fine % y_cells // 2), 1.0, 0.0)
+    fine, coarse = table((x_cells, 128))
+    right = jnp.where(fine // 2 == coarse, 0.125, 0.0)
+    return [matrix.astype(BF16) for matrix in (left, right)]
+
+
+def plane_up_matrices(planes, fine_y, coarse_y, fine_x, coarse_x):
+    rows = fine_y.shape[0]
+    fine, coarse = table((planes * rows, planes * coarse_y))
+    left = jnp.where(
+        fine // rows == coarse // coarse_y,
+        weight(jnp.tile(fine_y, planes)[:, None], coarse % coarse_y),
+        0.0,
+    )
+    coarse = jnp.arange(coarse_x)[:, None]
+    right = weight(fine_x[None, :], coarse)
+    return [left.astype(BF16), right.astype(BF16)]
+
+
+def link_mask(rows, lanes):
+    row = lax.broadcasted_iota(jnp.int32, (rows, lanes), 0)
+    last = jnp.where(lax.axis_index("gy") == 0, rows - 1, rows - HALO_Y - 1)
+    return jnp.where(row == last, 0.0, 1.0)
+
+
+def first_kernel(
+    coef, source, left, right_source, right_coef, message, estimate, face_z, face_y, face_x,
+    diagonal, inverse, residual, update, pair_source, pair_coef,
+):
+    planes, rows, lanes = source.shape
+    own_y = rows - HALO_Y
+    faces = (face_z, face_y, face_x, diagonal, inverse)
+    link_y = link_mask(rows, lanes)
+    plane_faces(coef, faces, 0, planes, link_y, None, source, update)
+    ranges = [(step + 2, planes - step - 2) for step in range(DEGREE - 1)]
+    plane_steps(faces, ranges, source, residual, update, estimate, True)
+
+    def finish(plane, own, value):
+        residual[plane] = residual[plane] - value
+
+    plane_sweep(faces, HALO_Z, planes - HALO_Z, update, finish)
+    for pair in range((planes - 2 * HALO_Z) // 2):
+        low = HALO_Z + 2 * pair
+        target = pl.ds(pair * own_y, own_y)
+        pair_source[target] = residual[low, :own_y, :128] + residual[low + 1, :own_y, :128]
+        pair_coef[target] = coef[low, :own_y, :128] + coef[low + 1, :own_y, :128]
+    message[...] = times_right(times_left(left[...], pair_source[...]), right_source[...]) + times_right(
+        times_left(left[...], pair_coef[...]), right_coef[...]
+    )
+
+
+def second_kernel(counts, depth_matrices, *refs):
+    x_count, y_count, z_count = counts
+    gathered, coef, source, estimate, up_left, up_right = refs[:6]
+    mid_refs = refs[6:10]
+    sheet_refs = refs[10 : 10 + depth_matrices]
+    solution, residual_out = refs[10 + depth_matrices : 12 + depth_matrices]
+    scratch = refs[12 + depth_matrices :]
+    mid_source, mid_coef, mid_residual, mid_update, mid_estimate, mid_correction = scratch[:6]
+    mid_faces = scratch[6:11]
+    pairs, wide = scratch[11:13]
+    faces = scratch[13:18]
+    residual, update, current = scratch[18:21]
+
+    planes, rows, lanes = source.shape
+    own_y = rows - HALO_Y
+    mid_z, mid_y, mid_x = z_count * 8, y_count * 8, x_count * 64
+    z_index = lax.axis_index("gz")
+
+    zero = jnp.zeros((PAD, mid_y, mid_x), F32)
+    for ref in (mid_coef, mid_update, mid_estimate, mid_faces[0]):
+        ref[pl.ds(0, PAD)] = zero
+        ref[pl.ds(PAD + mid_z, PAD)] = zero
+
+    low_half = lax.broadcasted_iota(jnp.int32, (8, 128), 1) < 64
+
+    def unpack(z_block, carry):
+        for y_block in range(y_count):
+            for x_pair in range(x_count // 2):
+                place = (z_block * y_count + y_block) * x_count + 2 * x_pair
+                for plane in range(8):
+                    even = gathered[place, pl.ds(plane * 8, 8)]
+                    odd = gathered[place + 1, pl.ds(plane * 8, 8)]
+                    target = PAD + z_block * 8 + plane
+                    where = (target, pl.ds(y_block * 8, 8), pl.ds(x_pair * 128, 128))
+                    mid_source[where] = jnp.where(low_half, even, turned(odd, 64, 1))
+                    mid_coef[where] = jnp.where(low_half, turned(even, 64, 1), odd)
+        return carry
+
+    lax.fori_loop(0, z_count, unpack, 0)
+
+    row = lax.broadcasted_iota(jnp.int32, (mid_y, mid_x), 0)
+    lane = lax.broadcasted_iota(jnp.int32, (mid_y, mid_x), 1)
+    link_y = jnp.where(row == mid_y - 1, 0.0, 1.0)
+    link_x = jnp.where(lane == mid_x - 1, 0.0, 1.0)
+    start, stop = PAD, PAD + mid_z
+    plane_faces(mid_coef, mid_faces, start, stop, link_y, link_x, mid_source, mid_update)
+    ranges = [(start, stop)] * (DEGREE - 1)
+    plane_steps(mid_faces, ranges, mid_source, mid_residual, mid_update, mid_estimate, True)
+
+    def finish_mid(plane, own, value):
+        mid_residual[plane] = mid_residual[plane] - value
+
+    plane_sweep(mid_faces, start, stop, mid_update, finish_mid)
+
+    left_down, right_down, mid_left_up, mid_right_up = mid_refs
+    sheets = []
+    for ref, scale in ((mid_residual, 4.0), (mid_coef, 1.0)):
+        for pair in range(mid_z // 2):
+            low = PAD + 2 * pair
+            pairs[pl.ds(pair * mid_y, mid_y)] = ref[low] + ref[low + 1]
+        sheets.append(scale * times_right(times_left(left_down[...], pairs[...]), right_down[...]))
+    shape = (mid_z // 2, mid_y // 2, mid_x // 2)
+    matrices = [sheet_refs[4 * index : 4 * index + 4] for index in range(depth_matrices // 4)]
+    correction = sheet_cycle(sheets[0], sheets[1], shape, 2, matrices)
+
+    raised = times_left(mid_left_up[...], times_right(correction, mid_right_up[...]))
+    mid_correction[pl.ds(1, mid_z // 2)] = raised.reshape(mid_z // 2, mid_y, mid_x)
+    mid_correction[pl.ds(0, 1)] = zero[:1]
+    mid_correction[pl.ds(1 + mid_z // 2, 1)] = zero[:1]
+
+    def add_mid(pair, carry):
+        own = 0.75 * mid_correction[pair + 1]
+        low = PAD + 2 * pair
+        mid_estimate[low] = mid_estimate[low] + (own + 0.25 * mid_correction[pair])
+        mid_estimate[low + 1] = mid_estimate[low + 1] + (own + 0.25 * mid_correction[pair + 2])
+        return carry
+
+    def clipped(margin):
+        low = jnp.maximum(z_index * 8 - margin, 0)
+        high = jnp.minimum(z_index * 8 + 8 + margin, mid_z)
+        return PAD + low, PAD + high
+
+    low, high = clipped(6)
+    lax.fori_loop((low - PAD) // 2, (high - PAD) // 2, add_mid, 0)
+    plane_restart(mid_faces, *clipped(5), mid_source, mid_residual, mid_update, mid_estimate)
+    plane_steps(
+        mid_faces, [clipped(4), clipped(3)], mid_source, mid_residual, mid_update, mid_estimate, False
+    )
+
+    link = link_mask(rows, lanes)
+    plane_faces(coef, faces, 0, planes, link, None)
+    coarse_planes = up_left.shape[1] // mid_y
+    near = mid_estimate[pl.ds(z_index * 8, coarse_planes)].reshape(coarse_planes * mid_y, mid_x)
+    raised = times_left(up_left[...], times_right(near, up_right[...]))
+    wide[...] = raised.reshape(coarse_planes, rows, lanes)
+    inverse = faces[4]
+
+    def add_fine(place, carry):
+        own = 0.75 * wide[place]
+        for offset, other in ((0, place - 1), (1, place + 1)):
+            plane = 2 * place + 1 + offset
+            step = own + 0.25 * wide[other]
+            current[plane] = estimate[plane] + jnp.where(inverse[plane] > 0.0, step, 0.0)
+        return carry
+
+    lax.fori_loop(1, coarse_planes - 1, add_fine, 0)
+    plane_restart(faces, HALO_Z - 3, planes - HALO_Z + 3, source, residual, update, current)
+    ranges = [(HALO_Z - 2, planes - HALO_Z + 2), (HALO_Z - 1, planes - HALO_Z + 1)]
+    plane_steps(faces, ranges, source, residual, update, current, False)
+
+    def finish(plane, own, value):
+        residual_out[plane - HALO_Z] = (residual[plane] - value)[:own_y, :128]
+        solution[plane - HALO_Z] = current[plane, :own_y, :128]
+
+    plane_sweep(faces, HALO_Z, planes - HALO_Z, update, finish)
+
+
+def window_of(blocks):
+    x_count, z_count = lax.axis_size("gx"), lax.axis_size("gz")
+    up = lambda count: [(i, i + 1) for i in range(count - 1)]
+    down = lambda count: [(i + 1, i) for i in range(count - 1)]
+    after = lax.ppermute(blocks[..., :HALO_X], "gx", down(x_count))
+    before = lax.ppermute(blocks[..., -HALO_X:], "gx", up(x_count))
+    gap = jnp.zeros(blocks.shape[:3] + (128 - 2 * HALO_X,), F32)
+    blocks = jnp.concatenate([blocks, after, gap, before], axis=3)
+    own_y = blocks.shape[2]
+    side = jnp.where(lax.axis_index("gy") == 0, blocks[:, :, own_y - HALO_Y :], blocks[:, :, :HALO_Y])
+    blocks = jnp.concatenate([blocks, lax.ppermute(side, "gy", [(0, 1), (1, 0)])], axis=2)
+    above = lax.ppermute(blocks[:, :HALO_Z], "gz", down(z_count))
+    below = lax.ppermute(blocks[:, -HALO_Z:], "gz", up(z_count))
+    return jnp.concatenate([below, blocks, above], axis=1)
+
+
+def near_local(right_side, coefficient):
+    counts = tuple(lax.axis_size(axis) for axis in ("gx", "gy", "gz"))
+    x_count, y_count, z_count = counts
+    _, own_z, own_y, own_x = right_side.shape
+    window = window_of(jnp.concatenate([right_side, coefficient[None]], axis=0))
+    planes, rows, lanes = window.shape[1:]
+    source, coef = window[0], jnp.pad(window[1], ((0, 1), (0, 0), (0, 0)))
+    vmem = pl.BlockSpec(memory_space=pltpu.VMEM)
+    params = pltpu.CompilerParams(vmem_limit_bytes=48 * 1024 * 1024)
+    window_scratch = pltpu.VMEM((planes + 1, rows, lanes), F32)
+    down = own_down_matrices(own_z // 2, own_y, own_x)
+    message, estimate = pl.pallas_call(
+        first_kernel,
+        out_shape=(
+            jax.ShapeDtypeStruct((own_z * own_y // 4, own_x), F32),
+            jax.ShapeDtypeStruct((planes, rows, lanes), F32),
+        ),
+        in_specs=[vmem] * 5,
+        out_specs=(vmem, vmem),
+        scratch_shapes=[window_scratch] * 7 + [pltpu.VMEM((own_z * own_y // 2, own_x), F32)] * 2,
+        compiler_params=params,
+        name="first",
+    )(coef, source, *down)
+    gathered = lax.all_gather(message, ("gz", "gy", "gx"))
+
+    mid = (own_z * z_count // 2, own_y * y_count // 2, own_x * x_count // 2)
+    row = jnp.arange(rows)
+    y_index = lax.axis_index("gy")
+    fine_y = jnp.where(row < own_y, y_index * own_y + row, jnp.where(y_index == 0, row, row - HALO_Y))
+    lane = jnp.arange(lanes)
+    fine_x = lax.axis_index("gx") * own_x + jnp.where(lane < lanes - HALO_X, lane, lane - lanes)
+    coarse_planes = own_z // 2 + 2 * PAD
+    up = plane_up_matrices(coarse_planes, fine_y, mid[1], fine_x, mid[2])
+    mid_down = one_down_matrices(mid[0] // 2, mid[1], mid[2])
+    mid_up = plane_up_matrices(
+        mid[0] // 2, jnp.arange(mid[1]), mid[1] // 2, jnp.arange(mid[2]), mid[2] // 2
+    )
+    shape = tuple(count // 2 for count in mid)
+    sheets = []
+    for level in range(2, LEVELS - 1):
+        sheets += sheet_matrices(shape, 128)
+        shape = tuple(count // 2 for count in shape)
+    mid_scratch = pltpu.VMEM((mid[0] + 2 * PAD, mid[1], mid[2]), F32)
+    solution, residual = pl.pallas_call(
+        functools.partial(second_kernel, counts, len(sheets)),
+        out_shape=(jax.ShapeDtypeStruct((own_z, own_y, own_x), F32),) * 2,
+        in_specs=[vmem] * (10 + len(sheets)),
+        out_specs=(vmem, vmem),
+        scratch_shapes=[mid_scratch] * 5
+        + [pltpu.VMEM((mid[0] // 2 + 2, mid[1], mid[2]), F32)]
+        + [mid_scratch] * 5
+        + [
+            pltpu.VMEM((mid[0] // 2 * mid[1], mid[2]), F32),
+            pltpu.VMEM((coarse_planes, rows, lanes), F32),
+        ]
+        + [window_scratch] * 8,
+        compiler_params=params,
+        name="second",
+    )(gathered, coef, source, estimate, *up, *mid_down, *mid_up, *sheets)
+    return solution[None], residual[None]
+
+
+def fits(mesh):
+    shape = dict(mesh.shape)
+    return shape["gy"] == 2 and shape["gx"] == 4 and shape["gz"] <= 4
+
+
 def solution(mesh):
     return jax.shard_map(
-        local,
+        near_local if fits(mesh) else local,
         mesh=mesh,
         in_specs=(P(None, "gz", "gy", "gx"), P("gz", "gy", "gx")),
         out_specs=(P(None, "gz", "gy", "gx"), P(None, "gz", "gy", "gx")),

time: 646 us -> 145 us (0.22)
  starting transfers between devices: 401 us -> 12.1 us
  waiting for transfers between devices: 183 us -> 74 us
  Pallas kernels: 0 us -> 38.4 us
  local copies, waits for them, and re-layouts: 26.6 us -> 1.57 us
  other arithmetic: 26.4 us -> 4.36 us
  between operations: 3.46 us -> 14.4 us
    ppermute x171 -> x5, starting transfers between devices: 401 us -> 12 us  [the longest x1 5.49 us: window_of(): before = lax.ppermute(blocks[..., -HALO_X:], 'gx', up(x_count))]
    ppermute x171 -> x5, waiting for transfers between devices: 183 us -> 16.5 us  [the longest x1 6.02 us: window_of(): below = lax.ppermute(blocks[:, -HALO_Z:], 'gz', up(z_count))]
    all_gather x0 -> x1, waiting for transfers between devices: none -> 57.5 us  [near_local(): gathered = lax.all_gather(message, ('gz', 'gy', 'gx'))]
    pallas_call x0 -> x2, Pallas kernels: none -> 38.4 us  [the longest x1 28.8 us: near_local(): pl.pallas_call(functools.partial(second_kernel, counts, len(sheets)), out...]
    another operation x13 -> x4, local copies, waits for them, and re-layouts: 11.3 us -> 0.17 us  [plane_up_matrices(): jnp.tile(fine_y, planes)[:, None]]
    reshape x3 -> x0, local copies, waits for them, and re-layouts: 10.9 us -> none  [restrict(): field.reshape(comp_count, z_cells // 2, 2, y_cells // 2, 2, x_cells // 2, 2)]
    reduce_sum x9 -> x0, other arithmetic: 8.82 us -> none  [restrict(): return jnp.mean(blocks, axis=(2, 4, 6))]
  transfers between devices with their start and end apart: 171 -> 6, of which waited for: 88 -> 6; matrix products, arithmetic and copies ran while one was open for 3% -> 1% of each run, Pallas kernels for 0% -> 0%
where the time goes in v1:
time: 145 us
  waiting for transfers between devices  74 us (51%)
  Pallas kernels  38.4 us (26%)
  between operations  14.4 us (10%)
  starting transfers between devices  12.1 us (8%)
  other arithmetic  4.36 us (3%)
  local copies, waits for them, and re-layouts  1.57 us (1%)
    all_gather x1, waiting for transfers between devices, near_local(): gathered = lax.all_gather(message, ('gz', 'gy', 'gx'))  57.5 us
    pallas_call x1, Pallas kernels, near_local(): pl.pallas_call(functools.partial(second_kernel, counts, len(sheets)), out...  28.8 us
    pallas_call x1, Pallas kernels, near_local(): pl.pallas_call(first_kernel, out_shape=(jax.ShapeDtypeStruct((own_z * own...  9.63 us
    ppermute x1, waiting for transfers between devices, window_of(): below = lax.ppermute(blocks[:, -HALO_Z:], 'gz', up(z_count))  6.02 us
    ppermute x1, starting transfers between devices, window_of(): before = lax.ppermute(blocks[..., -HALO_X:], 'gx', up(x_count))  5.49 us
    ppermute x1, waiting for transfers between devices, window_of(): after = lax.ppermute(blocks[..., :HALO_X], 'gx', down(x_count))  4.57 us
    ppermute x1, waiting for transfers between devices, window_of(): above = lax.ppermute(blocks[:, :HALO_Z], 'gz', down(z_count))  4.13 us
    ppermute x1, starting transfers between devices, window_of(): below = lax.ppermute(blocks[:, -HALO_Z:], 'gz', up(z_count))  3.74 us
  transfers between devices with their start and end apart: 6, of which 6 were waited for; matrix products, arithmetic and copies ran while one was open for 1% of the time, Pallas kernels for 0%

profile of v1, /device:TPU:0, one launch (start us, length us, event | category | flops | bytes accessed | tf_op | source)
XLA Modules:
  0.0 144.8 jit_solution(14066294213719623413)
XLA Ops:
  7.2 1.2 slice_maximum_fusion
  8.5 1.4 collective-permute-start
  9.9 5.5 %collective-permute-start.1 = (f32[2,16,16,8]{3,2,1,0:T(8,128)S(1)}, f32[2,16,16,8]{3,2,1,0:T(8,128)S(1)}, u32[]{:S(2)}, u32[]{:S(2)}) collective-permute-start(f32[2,16,16,8]{3,2,1,0:T(8,128)S(1)} %get-tuple-element.15), channel_id=1, source_target_pairs={{0,8},{8,16},{16,24},{1,9},{9,17},{17,25},{2,10},{10,18},{18,26},{... | collective-permute-start | bytes 49160 | tf_op jit(solution)/shard_map/ppermute | solution.py:591
  16.0 4.6 %collective-permute-done = f32[2,16,16,8]{3,2,1,0:T(8,128)S(1)} collective-permute-done((f32[2,16,16,8]{3,2,1,0:T(8,128)S(1)}, f32[2,16,16,8]{3,2,1,0:T(8,128)S(1)}, u32[]{:S(2)}, u32[]{:S(2)}) %collective-permute-start) | collective-permute-done | bytes 16416 | tf_op jit(solution)/shard_map/ppermute | solution.py:590
  20.6 0.4 collective-permute-done.1
  20.9 1.2 pad_maximum_fusion.1
  22.3 1.4 collective-permute-done.2
  23.8 0.2 pad_maximum_fusion.7
  24.0 3.7 %collective-permute-start.3 = (f32[2,7,24,256]{3,2,1,0:T(8,128)S(1)}, f32[2,7,24,256]{3,2,1,0:T(8,128)S(1)}, u32[]{:S(2)}, u32[]{:S(2)}) collective-permute-start(f32[2,7,24,256]{3,2,1,0:T(8,128)S(1)} %get-tuple-element.12), channel_id=1, source_target_pairs={{0,1},{1,2},{2,3},{4,5},{5,6},{6,7},{8,9},{9,10},{10,11},{12,13},{... | collective-permute-start | bytes 1032200 | tf_op jit(solution)/shard_map/ppermute | solution.py:598
  27.7 1.3 collective-permute-start.4
  29.1 0.1 select_convert_fusion.4
  29.3 6.0 %collective-permute-done.3 = f32[2,7,24,256]{3,2,1,0:T(8,128)S(1)} collective-permute-done((f32[2,7,24,256]{3,2,1,0:T(8,128)S(1)}, f32[2,7,24,256]{3,2,1,0:T(8,128)S(1)}, u32[]{:S(2)}, u32[]{:S(2)}) %collective-permute-start.3) | collective-permute-done | bytes 344096 | tf_op jit(solution)/shard_map/ppermute | solution.py:598
  35.3 4.1 %collective-permute-done.4 = f32[2,7,24,256]{3,2,1,0:T(8,128)S(1)} collective-permute-done((f32[2,7,24,256]{3,2,1,0:T(8,128)S(1)}, f32[2,7,24,256]{3,2,1,0:T(8,128)S(1)}, u32[]{:S(2)}, u32[]{:S(2)}) %collective-permute-start.4) | collective-permute-done | bytes 344096 | tf_op jit(solution)/shard_map/ppermute | solution.py:597
  39.4 0.2 pad_maximum_fusion
  39.7 0.1 slice_bitcast_fusion
  39.8 9.6 %first.1 = (f32[64,128]{1,0:T(8,128)}, f32[30,24,256]{2,1,0:T(8,128)S(1)}) custom-call(f32[31,24,256]{2,1,0:T(8,128)S(1)} %pad.4.coef.refs_1_, f32[30,24,256]{2,1,0:T(8,128)S(1)} %get-tuple-element.10.source.refs_2_, bf16[64,128]{1,0:T(8,128)(2,1)S(1)} %select_convert_fusion.10.left, bf16[128,128]{1,0:T(8,128)(2,1)S(1)} %get-tuple-element.24.right_source, ...), custom_call_target="tpu_custom_call" | custom-call | tf_op jit(solution)/shard_map/first/pallas_call | solution.py:613
  49.6 0.1 multiply_convert_fusion.refs_12_
  49.7 0.1 select_convert_fusion.2.refs_7_
  49.9 0.1 select_convert_fusion.3.refs_6_
  50.0 0.2 select_convert_fusion.1.refs_8_
  50.2 0.2 select_convert_fusion.refs_4_
  50.5 57.5 %all-gather.3.cloned.1.call-done = f32[2048,128]{1,0:T(8,128)} async-done(((f32[64,128]{1,0:T(8,128)}), f32[2048,128]{1,0:T(8,128)}) %all-gather.3.cloned.1.call-update) | async-done | bytes 1048592 | tf_op jit(solution)/shard_map/all_gather | solution.py:625
  108.0 1.2 copy-done
  109.2 28.8 %second.1 = (f32[16,16,128]{2,1,0:T(8,128)}, f32[16,16,128]{2,1,0:T(8,128)}) custom-call(f32[32,64,128]{2,1,0:T(8,128)S(1)} %bitcast.8, f32[31,24,256]{2,1,0:T(8,128)S(1)} %pad.4.coef.refs_1_, f32[30,24,256]{2,1,0:T(8,128)S(1)} %get-tuple-element.10.source.refs_2_, f32[30,24,256]{2,1,0:T(8,128)S(1)} %get-tuple-element.7.refs_3_, ...), custom_call_target="tpu_custom_call" | custom-call | tf_op jit(solution)/shard_map/second/pallas_call | solution.py:645
  (47 shorter events, 1.1 us)
Async XLA Ops:
  7.2 100.8 %all-gather.3.cloned.1.call-start = ((), (), s32[]{:S(2)}) async-start(), calls=%async_computation | async-start | bytes 1081344 | tf_op jit(solution)/shard_map/all_gather | solution.py:625
  8.4 15.3 %copy-start.1 = (f32[16,16,128]{2,1,0:T(8,128)S(1)}, f32[16,16,128]{2,1,0:T(8,128)}, u32[]{:S(2)}) copy-start(f32[16,16,128]{2,1,0:T(8,128)} %param.3) | copy-start | bytes 393220
  8.4 15.3 %copy-start.2 = (f32[1,16,16,128]{3,2,1,0:T(8,128)S(1)}, f32[1,16,16,128]{3,2,1,0:T(8,128)}, u32[]{:S(2)}) copy-start(f32[1,16,16,128]{3,2,1,0:T(8,128)} %param.2) | copy-start | bytes 393220
  8.5 12.1 %collective-permute-start = (f32[2,16,16,8]{3,2,1,0:T(8,128)S(1)}, f32[2,16,16,8]{3,2,1,0:T(8,128)S(1)}, u32[]{:S(2)}, u32[]{:S(2)}) collective-permute-start(f32[2,16,16,8]{3,2,1,0:T(8,128)S(1)} %get-tuple-element.14), channel_id=1, source_target_pairs={{8,0},{16,8},{24,16},{9,1},{17,9},{25,17},{10,2},{18,10},{26,18},{... | collective-permute-start | bytes 49160 | tf_op jit(solution)/shard_map/ppermute | solution.py:590
  9.9 11.0 %collective-permute-start.1 = (f32[2,16,16,8]{3,2,1,0:T(8,128)S(1)}, f32[2,16,16,8]{3,2,1,0:T(8,128)S(1)}, u32[]{:S(2)}, u32[]{:S(2)}) collective-permute-start(f32[2,16,16,8]{3,2,1,0:T(8,128)S(1)} %get-tuple-element.15), channel_id=1, source_target_pairs={{0,8},{8,16},{16,24},{1,9},{9,17},{17,25},{2,10},{10,18},{18,26},{... | collective-permute-start | bytes 49160 | tf_op jit(solution)/shard_map/ppermute | solution.py:591
  22.2 1.6 %collective-permute-start.2 = (f32[2,16,8,256]{3,2,1,0:T(8,128)S(1)}, f32[2,16,8,256]{3,2,1,0:T(8,128)S(1)}, u32[]{:S(2)}, u32[]{:S(2)}) collective-permute-start(f32[2,16,8,256]{3,2,1,0:T(8,128)S(1)} %slice_select_fusion), channel_id=1, source_target_pairs={{0,4},{4,0},{1,5},{5,1},{2,6},{6,2},{3,7},{7,3},{8,12},{12,8},{9,1... | collective-permute-start | bytes 786440 | tf_op jit(solution)/shard_map/ppermute | solution.py:596
  24.0 11.3 %collective-permute-start.3 = (f32[2,7,24,256]{3,2,1,0:T(8,128)S(1)}, f32[2,7,24,256]{3,2,1,0:T(8,128)S(1)}, u32[]{:S(2)}, u32[]{:S(2)}) collective-permute-start(f32[2,7,24,256]{3,2,1,0:T(8,128)S(1)} %get-tuple-element.12), channel_id=1, source_target_pairs={{0,1},{1,2},{2,3},{4,5},{5,6},{6,7},{8,9},{9,10},{10,11},{12,13},{... | collective-permute-start | bytes 1032200 | tf_op jit(solution)/shard_map/ppermute | solution.py:598
  27.7 11.7 %collective-permute-start.4 = (f32[2,7,24,256]{3,2,1,0:T(8,128)S(1)}, f32[2,7,24,256]{3,2,1,0:T(8,128)S(1)}, u32[]{:S(2)}, u32[]{:S(2)}) collective-permute-start(f32[2,7,24,256]{3,2,1,0:T(8,128)S(1)} %get-tuple-element.13), channel_id=1, source_target_pairs={{1,0},{2,1},{3,2},{5,4},{6,5},{7,6},{9,8},{10,9},{11,10},{13,12},{... | collective-permute-start | bytes 1032200 | tf_op jit(solution)/shard_map/ppermute | solution.py:597
  108.0 1.2 copy-start
Sparse Core Ops, SparseCore 0:
  49.6 58.3 all-gather.2

commit v2 on v1

--- a/solution.py
+++ b/solution.py
@@ -2,6 +2,7 @@
 
 import jax
 import jax.numpy as jnp
+import numpy as np
 from jax import lax
 from jax.experimental import pallas as pl
 from jax.experimental.pallas import tpu as pltpu
@@ -239,58 +240,75 @@
 
 def plane_neighbours(field, face_y, face_x):
     return (
-        face_y * turned(field, -1, 0)
-        + turned(face_y * field, 1, 0)
-        + face_x * turned(field, -1, 1)
-        + turned(face_x * field, 1, 1)
-    )
-
-
-def plane_faces(coef, faces, start, stop, link_y, link_x, source=None, update=None):
+        face_y * turned(field, -1, 1)
+        + turned(face_y * field, 1, 1)
+        + face_x * turned(field, -1, 2)
+        + turned(face_x * field, 1, 2)
+    )
+
+
+def shifted_in(first, block):
+    return jnp.concatenate([first, block[:-1]], axis=0)
+
+
+def in_blocks(start, stop, block, body, carry):
+    def step(index, carry):
+        return body(pl.ds(start + index * block, block), pl.ds(start + index * block + 1, block), carry)
+
+    lax.fori_loop(0, (stop - start) // block, step, carry)
+
+
+def plane_faces(coef, faces, start, stop, link_y, link_x, source, update, block=2):
     face_z, face_y, face_x, diagonal, inverse = faces
-    back_y = None if link_y is None else turned(link_y, 1, 0)
-    back_x = None if link_x is None else turned(link_x, 1, 1)
+    back_y = None if link_y is None else turned(link_y, 1, 1)
+    back_x = None if link_x is None else turned(link_x, 1, 2)
 
     def masked(value, mask):
         return value if mask is None else value * mask
 
-    def body(plane, below):
-        own = coef[plane]
-        above = 0.5 * (own + coef[plane + 1])
-        up_y = 0.5 * (own + masked(turned(own, -1, 0), link_y))
-        down_y = 0.5 * (own + masked(turned(own, 1, 0), back_y))
-        up_x = 0.5 * (own + masked(turned(own, -1, 1), link_x))
-        down_x = 0.5 * (own + masked(turned(own, 1, 1), back_x))
-        total = above + below + up_y + down_y + up_x + down_x
-        turned_over = jnp.where(own > 0.0, 1.0 / jnp.where(own > 0.0, total, 1.0), 0.0)
-        face_z[plane] = above
-        face_y[plane] = masked(up_y, link_y)
-        face_x[plane] = masked(up_x, link_x)
-        diagonal[plane] = total
-        inverse[plane] = turned_over
-        if update is not None:
-            update[plane] = source[plane] * turned_over * first_scale
-        return above
-
-    lax.fori_loop(start, stop, body, 0.5 * (coef[start] + coef[start - 1]) if start else 0.5 * coef[0])
-
-
-def plane_sweep(faces, start, stop, field, finish):
+    def body(here, after, below):
+        own = coef[here]
+        above = 0.5 * (own + coef[after])
+        up_y = 0.5 * (own + masked(turned(own, -1, 1), link_y))
+        down_y = 0.5 * (own + masked(turned(own, 1, 1), back_y))
+        up_x = 0.5 * (own + masked(turned(own, -1, 2), link_x))
+        down_x = 0.5 * (own + masked(turned(own, 1, 2), back_x))
+        total = above + shifted_in(below, above) + up_y + down_y + up_x + down_x
+        over = jnp.where(own > 0.0, 1.0 / jnp.where(own > 0.0, total, 1.0), 0.0)
+        first = source[here] * over * first_scale
+        face_z[here] = above
+        face_y[here] = masked(up_y, link_y)
+        face_x[here] = masked(up_x, link_x)
+        diagonal[here] = total
+        inverse[here] = over
+        update[here] = first
+        return above[-1:]
+
+    below = coef[pl.ds(start, 1)]
+    if start:
+        below = below + coef[pl.ds(start - 1, 1)]
+    in_blocks(start, stop, block, body, 0.5 * below)
+
+
+def plane_sweep(faces, start, stop, field, finish, block=2):
     face_z, face_y, face_x, diagonal, inverse = faces
 
-    def body(plane, below):
-        own = field[plane]
-        face = face_z[plane]
+    def body(here, after, below):
+        own = field[here]
+        face = face_z[here]
+        product = face * own
+        store = finish(here, own)
         value = (
-            diagonal[plane] * own
-            - face * field[plane + 1]
-            - below
-            - plane_neighbours(own, face_y[plane], face_x[plane])
+            diagonal[here] * own
+            - face * field[after]
+            - shifted_in(below, product)
+            - plane_neighbours(own, face_y[here], face_x[here])
         )
-        finish(plane, own, value)
-        return face * own
-
-    lax.fori_loop(start, stop, body, face_z[start - 1] * field[start - 1])
+        store(value)
+        return product[-1:]
+
+    before = pl.ds(start - 1, 1)
+    in_blocks(start, stop, block, body, face_z[before] * field[before])
 
 
 def plane_steps(faces, ranges, source, residual, update, estimate, from_zero):
@@ -298,12 +316,19 @@
     for step, ((keep, push), (start, stop)) in enumerate(zip(cheb_terms(), ranges)):
         fresh = from_zero and step == 0
 
-        def finish(plane, own, value, keep=keep, push=push, fresh=fresh):
-            left = (source if fresh else residual)[plane] - value
-            new = keep * own + push * (left * inverse[plane])
-            residual[plane] = left
-            update[plane] = new
-            estimate[plane] = (own if fresh else estimate[plane]) + new
+        def finish(here, own, keep=keep, push=push, fresh=fresh):
+            before = (source if fresh else residual)[here]
+            over = inverse[here]
+            total = own if fresh else estimate[here]
+
+            def store(value):
+                left = before - value
+                new = keep * own + push * (left * over)
+                residual[here] = left
+                update[here] = new
+                estimate[here] = total + new
+
+            return store
 
         plane_sweep(faces, start, stop, update, finish)
 
@@ -311,14 +336,32 @@
 def plane_restart(faces, start, stop, source, residual, update, estimate):
     inverse = faces[4]
 
-    def finish(plane, own, value):
-        left = source[plane] - value
-        new = left * inverse[plane] * first_scale
-        residual[plane] = left
-        update[plane] = new
-        estimate[plane] = own + new
+    def finish(here, own):
+        before = source[here]
+        over = inverse[here]
+
+        def store(value):
+            left = before - value
+            new = left * over * first_scale
+            residual[here] = left
+            update[here] = new
+            estimate[here] = own + new
+
+        return store
 
     plane_sweep(faces, start, stop, estimate, finish)
+
+
+def plane_residual(faces, start, stop, residual, update):
+    def finish(here, own):
+        before = residual[here]
+
+        def store(value):
+            residual[here] = before - value
+
+        return store
+
+    plane_sweep(faces, start, stop, update, finish)
 
 
 def sheet_faces(coef, shape):
@@ -376,14 +419,14 @@
     return sheet_smooth(source - sheet_apply(estimate, face_set), face_set, estimate)[0]
 
 
-def weight(fine, coarse):
+def weight(fine, coarse, xp=np):
     own = fine >> 1
-    other = jnp.where(fine % 2 == 0, own - 1, own + 1)
-    return jnp.where(coarse == own, 0.75, 0.0) + jnp.where(coarse == other, 0.25, 0.0)
-
-
-def table(shape):
-    return jnp.arange(shape[0])[:, None], jnp.arange(shape[1])[None, :]
+    other = xp.where(fine % 2 == 0, own - 1, own + 1)
+    return xp.where(coarse == own, 0.75, 0.0) + xp.where(coarse == other, 0.25, 0.0)
+
+
+def table(shape, xp=np):
+    return xp.arange(shape[0])[:, None], xp.arange(shape[1])[None, :]
 
 
 def sheet_matrices(fine_shape, lanes):
@@ -392,70 +435,166 @@
     half = y_cells // 2
     coarse, fine = table((coarse_rows, rows))
     same_z = coarse // half == fine // y_cells // 2
-    left_down = jnp.where(same_z & (coarse % half == fine % y_cells // 2), 0.25, 0.0)
+    left_down = np.where(same_z & (coarse % half == fine % y_cells // 2), 0.25, 0.0)
     fine, coarse = table((lanes, 128))
-    right_down = jnp.where((fine // 2 == coarse) & (fine < x_cells), 0.5, 0.0)
+    right_down = np.where((fine // 2 == coarse) & (fine < x_cells), 0.5, 0.0)
     fine, coarse = table((rows, coarse_rows))
     left_up = weight(fine // y_cells, coarse // half) * weight(fine % y_cells, coarse % half)
     coarse, fine = table((128, lanes))
-    right_up = jnp.where((fine < x_cells) & (coarse < x_cells // 2), weight(fine, coarse), 0.0)
+    right_up = np.where((fine < x_cells) & (coarse < x_cells // 2), weight(fine, coarse), 0.0)
     return [matrix.astype(BF16) for matrix in (left_down, right_down, left_up, right_up)]
 
 
-def own_down_matrices(z_pairs, y_cells, x_cells):
+def pair_rows_matrix(z_pairs, y_cells):
     half = y_cells // 2
     coarse, fine = table((z_pairs * half, z_pairs * y_cells))
-    left = jnp.where((coarse // half == fine // y_cells) & (coarse % half == fine % y_cells // 2), 1.0, 0.0)
+    same = (coarse // half == fine // y_cells) & (coarse % half == fine % y_cells // 2)
+    return np.where(same, 1.0, 0.0).astype(BF16)
+
+
+def own_down_matrices(z_pairs, y_cells, x_cells):
     fine, coarse = table((x_cells, x_cells))
-    right_source = jnp.where(fine // 2 == coarse, 0.5, 0.0)
-    right_coef = jnp.where(fine // 2 + x_cells // 2 == coarse, 0.125, 0.0)
-    return [matrix.astype(BF16) for matrix in (left, right_source, right_coef)]
+    right_source = np.where(fine // 2 == coarse, 0.5, 0.0)
+    right_coef = np.where(fine // 2 + x_cells // 2 == coarse, 0.125, 0.0)
+    return [pair_rows_matrix(z_pairs, y_cells), right_source.astype(BF16), right_coef.astype(BF16)]
 
 
 def one_down_matrices(z_pairs, y_cells, x_cells):
-    half = y_cells // 2
-    coarse, fine = table((z_pairs * half, z_pairs * y_cells))
-    left = jnp.where((coarse // half == fine // y_cells) & (coarse % half == fine % y_cells // 2), 1.0, 0.0)
     fine, coarse = table((x_cells, 128))
-    right = jnp.where(fine // 2 == coarse, 0.125, 0.0)
-    return [matrix.astype(BF16) for matrix in (left, right)]
-
-
-def plane_up_matrices(planes, fine_y, coarse_y, fine_x, coarse_x):
+    right = np.where(fine // 2 == coarse, 0.125, 0.0)
+    return [pair_rows_matrix(z_pairs, y_cells), right.astype(BF16)]
+
+
+def plane_up_matrices(planes, fine_y, coarse_y, fine_x, coarse_x, xp=np):
     rows = fine_y.shape[0]
-    fine, coarse = table((planes * rows, planes * coarse_y))
-    left = jnp.where(
+    fine, coarse = table((planes * rows, planes * coarse_y), xp)
+    left = xp.where(
         fine // rows == coarse // coarse_y,
-        weight(jnp.tile(fine_y, planes)[:, None], coarse % coarse_y),
+        weight(xp.tile(fine_y, planes)[:, None], coarse % coarse_y, xp),
         0.0,
     )
-    coarse = jnp.arange(coarse_x)[:, None]
-    right = weight(fine_x[None, :], coarse)
+    coarse = xp.arange(coarse_x)[:, None]
+    right = weight(fine_x[None, :], coarse, xp)
     return [left.astype(BF16), right.astype(BF16)]
 
 
+def swap_pairs(count, odd):
+    pairs = {index: index for index in range(count)}
+    for index in range(1 if odd else 0, count - 1, 2):
+        pairs[index], pairs[index + 1] = index + 1, index
+    return [pairs[index] for index in range(count)]
+
+
+def swapped(value, axes, partners):
+    places = [0]
+    for partner in partners:
+        places = [place * len(partner) + other for place in places for other in partner]
+    return lax.ppermute(value, axes, list(enumerate(places)))
+
+
 def link_mask(rows, lanes):
-    row = lax.broadcasted_iota(jnp.int32, (rows, lanes), 0)
+    row = lax.broadcasted_iota(jnp.int32, (1, rows, lanes), 1)
     last = jnp.where(lax.axis_index("gy") == 0, rows - 1, rows - HALO_Y - 1)
     return jnp.where(row == last, 0.0, 1.0)
 
 
-def first_kernel(
-    coef, source, left, right_source, right_coef, message, estimate, face_z, face_y, face_x,
-    diagonal, inverse, residual, update, pair_source, pair_coef,
-):
+def lanes_of(shape):
+    return lax.broadcasted_iota(jnp.int32, shape, len(shape) - 1)
+
+
+def pack_kernel(source, coef, side, z_a, z_b, x_a, x_b, c_aa, c_ab, c_ba, c_bb):
+    planes, own_y, _ = source.shape
+    z_even = lax.axis_index("gz") % 2 == 0
+    x_even = lax.axis_index("gx") % 2 == 0
+    for which, ref in enumerate((source, coef)):
+        for target, top in ((z_a, z_even), (z_b, jnp.logical_not(z_even))):
+            first = jnp.where(top, planes - HALO_Z, 0)
+            target[which, :, :own_y] = ref[pl.ds(first, HALO_Z)]
+            target[which, :, own_y:] = side[which, pl.ds(first, HALO_Z)]
+    lane = lanes_of((own_y + HALO_Y, 128))
+    rights, lefts = [], []
+    for which, ref in enumerate((source, coef)):
+        right = left = jnp.zeros(lane.shape, F32)
+        for plane in range(planes):
+            value = jnp.concatenate([ref[plane], side[which, plane]], axis=0)
+            slot = (lane >= 8 * plane) & (lane < 8 * plane + 8)
+            right = jnp.where(slot, turned(value, 8 * plane + 8, 1), right)
+            left = jnp.where(slot, turned(value, 8 * plane, 1), left)
+        x_a[which] = jnp.where(x_even, right, left)
+        x_b[which] = jnp.where(x_even, left, right)
+        rights.append(right)
+        lefts.append(left)
+    corners = []
+    for pack in (rights, lefts):
+        bottom = jnp.where(lane < 64, pack[0], turned(pack[1], 64, 1))
+        skip = 8 * (planes - HALO_Z)
+        top = jnp.where(lane < 64, turned(pack[0], -skip, 1), turned(pack[1], 64 - skip, 1))
+        corners.append((top, bottom))
+    for target, right, top in (
+        (c_aa, x_even, z_even),
+        (c_ab, x_even, jnp.logical_not(z_even)),
+        (c_ba, jnp.logical_not(x_even), z_even),
+        (c_bb, jnp.logical_not(x_even), jnp.logical_not(z_even)),
+    ):
+        target[...] = jnp.where(
+            right,
+            jnp.where(top, corners[0][0], corners[0][1]),
+            jnp.where(top, corners[1][0], corners[1][1]),
+        )
+
+
+def fill_window(own, side, got, source, coef, x_count, z_count):
+    z_a, z_b, x_a, x_b, c_aa, c_ab, c_ba, c_bb = got
+    planes, own_y = own[0].shape[:2]
+    rows = own_y + HALO_Y
+    z_index, x_index = lax.axis_index("gz"), lax.axis_index("gx")
+    z_even, x_even = z_index % 2 == 0, x_index % 2 == 0
+    has_above, has_below = z_index < z_count - 1, z_index > 0
+    has_right, has_left = x_index < x_count - 1, x_index > 0
+    above_at, below_at = HALO_Z + planes, 0
+    lane = lanes_of((rows, 128))
+
+    def edges(right, left, shift):
+        value = jnp.where(lane < 8, turned(right, -shift, 1), turned(left, 120 - shift, 1))
+        return jnp.where((lane < 8) | (lane >= 120), value, 0.0)
+
+    def kept(flag, value):
+        return jnp.where(flag, value, 0.0)
+
+    for which, target in enumerate((source, coef)):
+        target[pl.ds(HALO_Z, planes), :own_y, :128] = own[which][...]
+        target[pl.ds(HALO_Z, planes), own_y:, :128] = side[which]
+        above = jnp.where(z_even, z_a[which], z_b[which])
+        target[pl.ds(above_at, HALO_Z), :, :128] = kept(has_above, above)
+        below = jnp.where(z_even, z_b[which], z_a[which])
+        target[pl.ds(below_at, HALO_Z), :, :128] = kept(has_below, below)
+        right = kept(has_right, jnp.where(x_even, x_a[which], x_b[which]))
+        left = kept(has_left, jnp.where(x_even, x_b[which], x_a[which]))
+        for plane in range(planes):
+            target[HALO_Z + plane, :, 128:] = edges(right, left, 8 * plane)
+    for at, flag, is_a in ((above_at, has_above, z_even), (below_at, has_below, jnp.logical_not(z_even))):
+        by_a = jnp.where(is_a, c_aa[...], c_ab[...])
+        by_b = jnp.where(is_a, c_ba[...], c_bb[...])
+        right = kept(flag & has_right, jnp.where(x_even, by_a, by_b))
+        left = kept(flag & has_left, jnp.where(x_even, by_b, by_a))
+        for which, target in enumerate((source, coef)):
+            for plane in range(HALO_Z):
+                target[at + plane, :, 128:] = edges(right, left, 64 * which + 8 * plane)
+    coef[pl.ds(above_at + HALO_Z, 1)] = jnp.zeros((1,) + coef.shape[1:], F32)
+
+
+def first_kernel(counts, *refs):
+    own, side, got = refs[:2], refs[2], refs[3:11]
+    left, right_source, right_coef, message, source, estimate = refs[11:17]
+    faces = refs[17:22]
+    coef, residual, update, pair_source, pair_coef = refs[22:]
+    fill_window(own, side, got, source, coef, *counts)
     planes, rows, lanes = source.shape
     own_y = rows - HALO_Y
-    faces = (face_z, face_y, face_x, diagonal, inverse)
-    link_y = link_mask(rows, lanes)
-    plane_faces(coef, faces, 0, planes, link_y, None, source, update)
+    plane_faces(coef, faces, 0, planes, link_mask(rows, lanes), None, source, update)
     ranges = [(step + 2, planes - step - 2) for step in range(DEGREE - 1)]
     plane_steps(faces, ranges, source, residual, update, estimate, True)
-
-    def finish(plane, own, value):
-        residual[plane] = residual[plane] - value
-
-    plane_sweep(faces, HALO_Z, planes - HALO_Z, update, finish)
+    plane_residual(faces, HALO_Z, planes - HALO_Z, residual, update)
     for pair in range((planes - 2 * HALO_Z) // 2):
         low = HALO_Z + 2 * pair
         target = pl.ds(pair * own_y, own_y)
@@ -468,57 +607,51 @@
 
 def second_kernel(counts, depth_matrices, *refs):
     x_count, y_count, z_count = counts
-    gathered, coef, source, estimate, up_left, up_right = refs[:6]
-    mid_refs = refs[6:10]
-    sheet_refs = refs[10 : 10 + depth_matrices]
-    solution, residual_out = refs[10 + depth_matrices : 12 + depth_matrices]
-    scratch = refs[12 + depth_matrices :]
+    gathered, other, source, estimate = refs[:4]
+    faces = refs[4:9]
+    up_left, up_right = refs[9:11]
+    mid_refs = refs[11:15]
+    sheet_refs = refs[15 : 15 + depth_matrices]
+    solution, residual_out = refs[15 + depth_matrices : 17 + depth_matrices]
+    scratch = refs[17 + depth_matrices :]
     mid_source, mid_coef, mid_residual, mid_update, mid_estimate, mid_correction = scratch[:6]
     mid_faces = scratch[6:11]
-    pairs, wide = scratch[11:13]
-    faces = scratch[13:18]
-    residual, update, current = scratch[18:21]
+    pairs, wide, residual, update, current = scratch[11:]
 
     planes, rows, lanes = source.shape
     own_y = rows - HALO_Y
     mid_z, mid_y, mid_x = z_count * 8, y_count * 8, x_count * 64
-    z_index = lax.axis_index("gz")
+    x_index, y_index, z_index = (lax.axis_index(axis) for axis in ("gx", "gy", "gz"))
 
     zero = jnp.zeros((PAD, mid_y, mid_x), F32)
     for ref in (mid_coef, mid_update, mid_estimate, mid_faces[0]):
         ref[pl.ds(0, PAD)] = zero
         ref[pl.ds(PAD + mid_z, PAD)] = zero
 
-    low_half = lax.broadcasted_iota(jnp.int32, (8, 128), 1) < 64
-
-    def unpack(z_block, carry):
-        for y_block in range(y_count):
-            for x_pair in range(x_count // 2):
-                place = (z_block * y_count + y_block) * x_count + 2 * x_pair
-                for plane in range(8):
-                    even = gathered[place, pl.ds(plane * 8, 8)]
-                    odd = gathered[place + 1, pl.ds(plane * 8, 8)]
-                    target = PAD + z_block * 8 + plane
-                    where = (target, pl.ds(y_block * 8, 8), pl.ds(x_pair * 128, 128))
-                    mid_source[where] = jnp.where(low_half, even, turned(odd, 64, 1))
-                    mid_coef[where] = jnp.where(low_half, turned(even, 64, 1), odd)
-        return carry
-
-    lax.fori_loop(0, z_count, unpack, 0)
-
-    row = lax.broadcasted_iota(jnp.int32, (mid_y, mid_x), 0)
-    lane = lax.broadcasted_iota(jnp.int32, (mid_y, mid_x), 1)
+    low_half = lanes_of((64, 128)) < 64
+    x_even = x_index % 2 == 0
+    for blocks, y_block in ((gathered, y_index), (other, 1 - y_index)):
+        y_rows = pl.ds(pl.multiple_of(y_block * 8, 8), 8)
+        for x_pair in range(x_count // 2):
+            x_lanes = pl.ds(pl.multiple_of(((x_index // 2) ^ x_pair) * 128, 128), 128)
+            for z_block in range(z_count):
+                mine = blocks[2 * x_pair, z_block]
+                partner = blocks[2 * x_pair + 1, z_block]
+                even = jnp.where(x_even, mine, partner)
+                odd = jnp.where(x_even, partner, mine)
+                z_planes = pl.ds(PAD + (z_index ^ z_block) * 8, 8)
+                mid_source[z_planes, y_rows, x_lanes] = jnp.where(low_half, even, turned(odd, 64, 1)).reshape(8, 8, 128)
+                mid_coef[z_planes, y_rows, x_lanes] = jnp.where(low_half, turned(even, 64, 1), odd).reshape(8, 8, 128)
+
+    row = lax.broadcasted_iota(jnp.int32, (1, mid_y, mid_x), 1)
+    lane = lanes_of((1, mid_y, mid_x))
     link_y = jnp.where(row == mid_y - 1, 0.0, 1.0)
     link_x = jnp.where(lane == mid_x - 1, 0.0, 1.0)
     start, stop = PAD, PAD + mid_z
     plane_faces(mid_coef, mid_faces, start, stop, link_y, link_x, mid_source, mid_update)
     ranges = [(start, stop)] * (DEGREE - 1)
     plane_steps(mid_faces, ranges, mid_source, mid_residual, mid_update, mid_estimate, True)
-
-    def finish_mid(plane, own, value):
-        mid_residual[plane] = mid_residual[plane] - value
-
-    plane_sweep(mid_faces, start, stop, mid_update, finish_mid)
+    plane_residual(mid_faces, start, stop, mid_residual, mid_update)
 
     left_down, right_down, mid_left_up, mid_right_up = mid_refs
     sheets = []
@@ -550,13 +683,11 @@
 
     low, high = clipped(6)
     lax.fori_loop((low - PAD) // 2, (high - PAD) // 2, add_mid, 0)
-    plane_restart(mid_faces, *clipped(5), mid_source, mid_residual, mid_update, mid_estimate)
+    plane_restart(mid_faces, *clipped(6), mid_source, mid_residual, mid_update, mid_estimate)
     plane_steps(
-        mid_faces, [clipped(4), clipped(3)], mid_source, mid_residual, mid_update, mid_estimate, False
-    )
-
-    link = link_mask(rows, lanes)
-    plane_faces(coef, faces, 0, planes, link, None)
+        mid_faces, [clipped(4), clipped(4)], mid_source, mid_residual, mid_update, mid_estimate, False
+    )
+
     coarse_planes = up_left.shape[1] // mid_y
     near = mid_estimate[pl.ds(z_index * 8, coarse_planes)].reshape(coarse_planes * mid_y, mid_x)
     raised = times_left(up_left[...], times_right(near, up_right[...]))
@@ -575,89 +706,93 @@
     plane_restart(faces, HALO_Z - 3, planes - HALO_Z + 3, source, residual, update, current)
     ranges = [(HALO_Z - 2, planes - HALO_Z + 2), (HALO_Z - 1, planes - HALO_Z + 1)]
     plane_steps(faces, ranges, source, residual, update, current, False)
-
-    def finish(plane, own, value):
-        residual_out[plane - HALO_Z] = (residual[plane] - value)[:own_y, :128]
-        solution[plane - HALO_Z] = current[plane, :own_y, :128]
-
-    plane_sweep(faces, HALO_Z, planes - HALO_Z, update, finish)
-
-
-def window_of(blocks):
-    x_count, z_count = lax.axis_size("gx"), lax.axis_size("gz")
-    up = lambda count: [(i, i + 1) for i in range(count - 1)]
-    down = lambda count: [(i + 1, i) for i in range(count - 1)]
-    after = lax.ppermute(blocks[..., :HALO_X], "gx", down(x_count))
-    before = lax.ppermute(blocks[..., -HALO_X:], "gx", up(x_count))
-    gap = jnp.zeros(blocks.shape[:3] + (128 - 2 * HALO_X,), F32)
-    blocks = jnp.concatenate([blocks, after, gap, before], axis=3)
-    own_y = blocks.shape[2]
-    side = jnp.where(lax.axis_index("gy") == 0, blocks[:, :, own_y - HALO_Y :], blocks[:, :, :HALO_Y])
-    blocks = jnp.concatenate([blocks, lax.ppermute(side, "gy", [(0, 1), (1, 0)])], axis=2)
-    above = lax.ppermute(blocks[:, :HALO_Z], "gz", down(z_count))
-    below = lax.ppermute(blocks[:, -HALO_Z:], "gz", up(z_count))
-    return jnp.concatenate([below, blocks, above], axis=1)
+    plane_residual(faces, HALO_Z, planes - HALO_Z, residual, update)
+    own_planes = pl.ds(HALO_Z, planes - 2 * HALO_Z)
+    residual_out[...] = residual[own_planes, :own_y, :128]
+    solution[...] = current[own_planes, :own_y, :128]
 
 
 def near_local(right_side, coefficient):
     counts = tuple(lax.axis_size(axis) for axis in ("gx", "gy", "gz"))
     x_count, y_count, z_count = counts
     _, own_z, own_y, own_x = right_side.shape
-    window = window_of(jnp.concatenate([right_side, coefficient[None]], axis=0))
-    planes, rows, lanes = window.shape[1:]
-    source, coef = window[0], jnp.pad(window[1], ((0, 1), (0, 0), (0, 0)))
+    right_side = right_side[0]
+    planes, rows, lanes = own_z + 2 * HALO_Z, own_y + HALO_Y, 2 * own_x
     vmem = pl.BlockSpec(memory_space=pltpu.VMEM)
     params = pltpu.CompilerParams(vmem_limit_bytes=48 * 1024 * 1024)
-    window_scratch = pltpu.VMEM((planes + 1, rows, lanes), F32)
+
+    def call(kernel, name, arguments, shapes, scratch):
+        return pl.pallas_call(
+            kernel,
+            out_shape=tuple(jax.ShapeDtypeStruct(shape, F32) for shape in shapes),
+            in_specs=[vmem] * len(arguments),
+            out_specs=(vmem,) * len(shapes),
+            scratch_shapes=[pltpu.VMEM(shape, F32) for shape in scratch],
+            compiler_params=params,
+            name=name,
+        )(*arguments)
+
+    y_index = lax.axis_index("gy")
+    both = jnp.stack([right_side, coefficient])
+    side = jnp.where(y_index == 0, both[:, :, own_y - HALO_Y :], both[:, :, :HALO_Y])
+    side = swapped(side, "gy", [swap_pairs(y_count, False)])
+    z_shape, x_shape, c_shape = (2, HALO_Z, rows, 128), (2, rows, 128), (rows, 128)
+    sent = call(
+        pack_kernel, "pack", (right_side, coefficient, side), [z_shape] * 2 + [x_shape] * 2 + [c_shape] * 4, []
+    )
+    x_a, x_b = swap_pairs(x_count, False), swap_pairs(x_count, True)
+    z_a, z_b = swap_pairs(z_count, False), swap_pairs(z_count, True)
+    got = [swapped(sent[0], "gz", [z_a]), swapped(sent[1], "gz", [z_b])]
+    got += [swapped(sent[2], "gx", [x_a]), swapped(sent[3], "gx", [x_b])]
+    for message, partners in zip(sent[4:], ((x_a, z_a), (x_a, z_b), (x_b, z_a), (x_b, z_b))):
+        got.append(swapped(message, ("gx", "gz"), partners))
+
+    window, padded = (planes, rows, lanes), (planes + 1, rows, lanes)
     down = own_down_matrices(own_z // 2, own_y, own_x)
-    message, estimate = pl.pallas_call(
-        first_kernel,
-        out_shape=(
-            jax.ShapeDtypeStruct((own_z * own_y // 4, own_x), F32),
-            jax.ShapeDtypeStruct((planes, rows, lanes), F32),
-        ),
-        in_specs=[vmem] * 5,
-        out_specs=(vmem, vmem),
-        scratch_shapes=[window_scratch] * 7 + [pltpu.VMEM((own_z * own_y // 2, own_x), F32)] * 2,
-        compiler_params=params,
-        name="first",
-    )(coef, source, *down)
-    gathered = lax.all_gather(message, ("gz", "gy", "gx"))
+    message, *kept = call(
+        functools.partial(first_kernel, (x_count, z_count)),
+        "first",
+        (right_side, coefficient, side, *got, *down),
+        [(own_z * own_y // 4, own_x)] + [window] * 2 + [window] * 5,
+        [padded, window, padded] + [(own_z * own_y // 2, own_x)] * 2,
+    )
+
+    def with_others(value, axis, count):
+        others = [
+            swapped(value, axis, [[index ^ distance for index in range(count)]]) for distance in range(1, count)
+        ]
+        return jnp.stack([value] + others)
+
+    gathered = with_others(with_others(message, "gz", z_count), "gx", x_count)
+    other = swapped(gathered, "gy", [swap_pairs(y_count, False)])
 
     mid = (own_z * z_count // 2, own_y * y_count // 2, own_x * x_count // 2)
     row = jnp.arange(rows)
-    y_index = lax.axis_index("gy")
     fine_y = jnp.where(row < own_y, y_index * own_y + row, jnp.where(y_index == 0, row, row - HALO_Y))
     lane = jnp.arange(lanes)
     fine_x = lax.axis_index("gx") * own_x + jnp.where(lane < lanes - HALO_X, lane, lane - lanes)
     coarse_planes = own_z // 2 + 2 * PAD
-    up = plane_up_matrices(coarse_planes, fine_y, mid[1], fine_x, mid[2])
+    up = plane_up_matrices(coarse_planes, fine_y, mid[1], fine_x, mid[2], jnp)
     mid_down = one_down_matrices(mid[0] // 2, mid[1], mid[2])
     mid_up = plane_up_matrices(
-        mid[0] // 2, jnp.arange(mid[1]), mid[1] // 2, jnp.arange(mid[2]), mid[2] // 2
+        mid[0] // 2, np.arange(mid[1]), mid[1] // 2, np.arange(mid[2]), mid[2] // 2
     )
     shape = tuple(count // 2 for count in mid)
     sheets = []
     for level in range(2, LEVELS - 1):
         sheets += sheet_matrices(shape, 128)
         shape = tuple(count // 2 for count in shape)
-    mid_scratch = pltpu.VMEM((mid[0] + 2 * PAD, mid[1], mid[2]), F32)
-    solution, residual = pl.pallas_call(
+    mid_padded = (mid[0] + 2 * PAD, mid[1], mid[2])
+    solution, residual = call(
         functools.partial(second_kernel, counts, len(sheets)),
-        out_shape=(jax.ShapeDtypeStruct((own_z, own_y, own_x), F32),) * 2,
-        in_specs=[vmem] * (10 + len(sheets)),
-        out_specs=(vmem, vmem),
-        scratch_shapes=[mid_scratch] * 5
-        + [pltpu.VMEM((mid[0] // 2 + 2, mid[1], mid[2]), F32)]
-        + [mid_scratch] * 5
-        + [
-            pltpu.VMEM((mid[0] // 2 * mid[1], mid[2]), F32),
-            pltpu.VMEM((coarse_planes, rows, lanes), F32),
-        ]
-        + [window_scratch] * 8,
-        compiler_params=params,
-        name="second",
-    )(gathered, coef, source, estimate, *up, *mid_down, *mid_up, *sheets)
+        "second",
+        (gathered, other, *kept, *up, *mid_down, *mid_up, *sheets),
+        [(own_z, own_y, own_x)] * 2,
+        [mid_padded] * 5
+        + [(mid[0] // 2 + 2, mid[1], mid[2])]
+        + [mid_padded] * 5
+        + [(mid[0] // 2 * mid[1], mid[2]), (coarse_planes, rows, lanes), window, padded, padded],
+    )
     return solution[None], residual[None]
 
 

time: 145 us -> 81.4 us (0.56)
  waiting for transfers between devices: 74 us -> 11.5 us
  Pallas kernels: 38.4 us -> 24.4 us
  local copies, waits for them, and re-layouts: 1.57 us -> 15.5 us
  starting transfers between devices: 12.1 us -> 25.9 us
  between operations: 14.4 us -> 0.93 us
  other arithmetic: 4.36 us -> 2.27 us
    all_gather x1 -> x0, waiting for transfers between devices: 57.5 us -> none  [near_local(): gathered = lax.all_gather(message, ('gz', 'gy', 'gx'))]
    unnamed x6 -> x70, local copies, waits for them, and re-layouts: 1.24 us -> 15.4 us
    pallas_call x2 -> x3, Pallas kernels: 38.4 us -> 24.4 us  [call(): pl.pallas_call(kernel, out_shape=tuple((jax.ShapeDtypeStruct(shape, F32)...]
    ppermute x5 -> x16, starting transfers between devices: 12 us -> 25.9 us  [swapped(): return lax.ppermute(value, axes, list(enumerate(places)))]
    ppermute x5 -> x16, waiting for transfers between devices: 16.5 us -> 11.5 us  [swapped(): return lax.ppermute(value, axes, list(enumerate(places)))]
    concatenate x3 -> x0, other arithmetic: 2.63 us -> none  [the longest x1 1.22 us: near_local(): window = window_of(jnp.concatenate([right_side, coefficient[None]], axis=0))]
  transfers between devices with their start and end apart: 6 -> 16, of which waited for: 6 -> 10; matrix products, arithmetic and copies ran while one was open for 1% -> 0% of each run, Pallas kernels for 0% -> 0%
where the time goes in v2:
time: 81.4 us; the launch traced here: 80.6 us
  starting transfers between devices  25.9 us (32%)
  Pallas kernels  24.4 us (30%)
  local copies, waits for them, and re-layouts  15.5 us (19%)
  waiting for transfers between devices  11.5 us (14%)
  other arithmetic  2.27 us (3%)
  between operations  0.93 us (1%)
    ppermute x16, starting transfers between devices, swapped(): return lax.ppermute(value, axes, list(enumerate(places)))  25.9 us
    pallas_call x3, Pallas kernels, call(): pl.pallas_call(kernel, out_shape=tuple((jax.ShapeDtypeStruct(shape, F32)...  24.4 us
    unnamed x70, local copies, waits for them, and re-layouts  15.4 us
    ppermute x16, waiting for transfers between devices, swapped(): return lax.ppermute(value, axes, list(enumerate(places)))  11.5 us
  transfers between devices with their start and end apart: 16, of which 10 were waited for; matrix products, arithmetic and copies ran while one was open for 0% of the time, Pallas kernels for 0%

profile of v2, /device:TPU:0, one launch (start us, length us, event | category | flops | bytes accessed | tf_op | source)
XLA Modules:
  0.0 80.6 jit_solution(10523488221161554921)
XLA Ops:
  0.7 1.0 %fusion.1 = f32[2,16,8,128]{3,2,1,0:T(8,128)S(1)} fusion(f32[1,16,16,128]{3,2,1,0:T(8,128)} %param.17, f32[1,16,16,128]{3,2,1,0:T(8,128)} %bitcast.15, pred[]{:T(512)S(6)} %eq.93), kind=kLoop, calls=%fused_computation.8 | loop fusion | flops 98304 | bytes 393217 | tf_op jit(solution)/shard_map/jit(_where)/select_n | solution.py:737
  2.2 1.0 %collective-permute-done.side.refs_2_ = f32[2,16,8,128]{3,2,1,0:T(8,128)S(1)} collective-permute-done((f32[2,16,8,128]{3,2,1,0:T(8,128)S(1)}, f32[2,16,8,128]{3,2,1,0:T(8,128)S(1)}, u32[]{:S(2)}, u32[]{:S(2)}) %collective-permute-start) | collective-permute-done | bytes 131104 | tf_op jit(solution)/shard_map/ppermute | solution.py:492
  3.5 3.0 %collective-permute-start.1 = (f32[2,7,24,128]{3,2,1,0:T(8,128)S(1)}, f32[2,7,24,128]{3,2,1,0:T(8,128)S(1)}, u32[]{:S(2)}, u32[]{:S(2)}) collective-permute-start(f32[2,7,24,128]{3,2,1,0:T(8,128)S(1)} %get-tuple-element.20), channel_id=1, source_target_pairs={{0,1},{1,0},{2,3},{3,2},{4,5},{5,4},{6,7},{7,6},{8,9},{9,8},{10,11... | collective-permute-start | bytes 516104 | tf_op jit(solution)/shard_map/ppermute | solution.py:492
  7.2 5.4 %collective-permute-start.5 = (f32[24,128]{1,0:T(8,128)S(1)}, f32[24,128]{1,0:T(8,128)S(1)}, u32[]{:S(2)}, u32[]{:S(2)}) collective-permute-start(f32[24,128]{1,0:T(8,128)S(1)} %get-tuple-element.24), channel_id=1, source_target_pairs={{0,9},{1,8},{2,11},{3,10},{8,1},{9,0},{10,3},{11,2},{16,25},{17,24... | collective-permute-start | bytes 36872 | tf_op jit(solution)/shard_map/ppermute | solution.py:492
  13.1 1.1 %collective-permute-done.5.refs_7_ = f32[24,128]{1,0:T(8,128)S(1)} collective-permute-done((f32[24,128]{1,0:T(8,128)S(1)}, f32[24,128]{1,0:T(8,128)S(1)}, u32[]{:S(2)}, u32[]{:S(2)}) %collective-permute-start.5) | collective-permute-done | bytes 12320 | tf_op jit(solution)/shard_map/ppermute | solution.py:492
  16.9 3.5 %collective-permute-start.3 = (f32[2,24,128]{2,1,0:T(8,128)S(1)}, f32[2,24,128]{2,1,0:T(8,128)S(1)}, u32[]{:S(2)}, u32[]{:S(2)}) collective-permute-start(f32[2,24,128]{2,1,0:T(8,128)S(1)} %get-tuple-element.22), channel_id=1, source_target_pairs={{0,8},{8,0},{16,24},{24,16},{1,9},{9,1},{17,25},{25,17},{2,10},{10... | collective-permute-start | bytes 73736 | tf_op jit(solution)/shard_map/ppermute | solution.py:492
  24.2 0.9 %copy-done.8 = f32[2,7,24,128]{3,2,1,0:T(8,128)S(1)} copy-done((f32[2,7,24,128]{3,2,1,0:T(8,128)S(1)}, f32[2,7,24,128]{3,2,1,0:T(8,128)}, u32[]{:S(2)}) %copy-start.8) | copy-done | bytes 172056
  30.9 5.9 %first.1 = (f32[64,128]{1,0:T(8,128)S(1)}, f32[30,24,256]{2,1,0:T(8,128)S(1)}, f32[30,24,256]{2,1,0:T(8,128)S(1)}, f32[30,24,256]{2,1,0:T(8,128)S(1)}, f32[30,24...) custom-call(f32[16,16,128]{2,1,0:T(8,128)S(1)} %bitcast.14, ...), custom_call_target="tpu_custom_call" | custom-call | tf_op jit(solution)/shard_map/first/pallas_call | solution.py:725
  36.8 0.9 %copy-done.2 = f32[30,24,256]{2,1,0:T(8,128)} copy-done((f32[30,24,256]{2,1,0:T(8,128)}, f32[30,24,256]{2,1,0:T(8,128)S(1)}, u32[]{:S(2)}) %copy-start.2) | copy-done | bytes 737304
  37.7 0.9 %copy-done.4 = f32[30,24,256]{2,1,0:T(8,128)} copy-done((f32[30,24,256]{2,1,0:T(8,128)}, f32[30,24,256]{2,1,0:T(8,128)S(1)}, u32[]{:S(2)}) %copy-start.4) | copy-done | bytes 737304
  39.5 1.9 %collective-permute-start.11 = (f32[64,128]{1,0:T(8,128)S(1)}, f32[64,128]{1,0:T(8,128)S(1)}, u32[]{:S(2)}, u32[]{:S(2)}) collective-permute-start(f32[64,128]{1,0:T(8,128)S(1)} %get-tuple-element.28), channel_id=1, source_target_pairs={{0,3},{1,2},{2,1},{3,0},{4,7},{5,6},{6,5},{7,4},{8,11},{9,10},{10,... | collective-permute-start | bytes 98312 | tf_op jit(solution)/shard_map/ppermute | solution.py:492
  41.4 1.0 %collective-permute-start.10 = (f32[64,128]{1,0:T(8,128)S(1)}, f32[64,128]{1,0:T(8,128)S(1)}, u32[]{:S(2)}, u32[]{:S(2)}) collective-permute-start(f32[64,128]{1,0:T(8,128)S(1)} %get-tuple-element.28), channel_id=1, source_target_pairs={{0,2},{1,3},{2,0},{3,1},{4,6},{5,7},{6,4},{7,5},{8,10},{9,11},{10,... | collective-permute-start | bytes 98312 | tf_op jit(solution)/shard_map/ppermute | solution.py:492
  42.4 1.4 %collective-permute-start.9 = (f32[64,128]{1,0:T(8,128)S(1)}, f32[64,128]{1,0:T(8,128)S(1)}, u32[]{:S(2)}, u32[]{:S(2)}) collective-permute-start(f32[64,128]{1,0:T(8,128)S(1)} %get-tuple-element.28), channel_id=1, source_target_pairs={{0,1},{1,0},{2,3},{3,2},{4,5},{5,4},{6,7},{7,6},{8,9},{9,8},{10,11... | collective-permute-start | bytes 98312 | tf_op jit(solution)/shard_map/ppermute | solution.py:492
  43.9 1.3 %collective-permute-done.11 = f32[64,128]{1,0:T(8,128)S(1)} collective-permute-done((f32[64,128]{1,0:T(8,128)S(1)}, f32[64,128]{1,0:T(8,128)S(1)}, u32[]{:S(2)}, u32[]{:S(2)}) %collective-permute-start.11) | collective-permute-done | bytes 32800 | tf_op jit(solution)/shard_map/ppermute | solution.py:492
  45.2 1.0 %collective-permute-done.10 = f32[64,128]{1,0:T(8,128)S(1)} collective-permute-done((f32[64,128]{1,0:T(8,128)S(1)}, f32[64,128]{1,0:T(8,128)S(1)}, u32[]{:S(2)}, u32[]{:S(2)}) %collective-permute-start.10) | collective-permute-done | bytes 32800 | tf_op jit(solution)/shard_map/ppermute | solution.py:492
  46.6 5.1 %collective-permute-start.13 = (f32[4,64,128]{2,1,0:T(8,128)S(1)}, f32[4,64,128]{2,1,0:T(8,128)S(1)}, u32[]{:S(2)}, u32[]{:S(2)}) collective-permute-start(f32[4,64,128]{2,1,0:T(8,128)S(1)} %get-tuple-element.39), channel_id=1, source_target_pairs={{0,16},{8,24},{16,0},{24,8},{1,17},{9,25},{17,1},{25,9},{2,18},{10... | collective-permute-start | bytes 393224 | tf_op jit(solution)/shard_map/ppermute | solution.py:492
  51.6 1.5 %collective-permute-start.14 = (f32[4,64,128]{2,1,0:T(8,128)S(1)}, f32[4,64,128]{2,1,0:T(8,128)}, u32[]{:S(2)}, u32[]{:S(2)}) collective-permute-start(f32[4,64,128]{2,1,0:T(8,128)S(1)} %get-tuple-element.39), channel_id=1, source_target_pairs={{0,24},{8,16},{16,8},{24,0},{1,25},{9,17},{17,9},{25,1},{2,26},{10... | collective-permute-start | bytes 393224 | tf_op jit(solution)/shard_map/ppermute | solution.py:492
  53.2 1.4 %collective-permute-done.13 = f32[4,64,128]{2,1,0:T(8,128)S(1)} collective-permute-done((f32[4,64,128]{2,1,0:T(8,128)S(1)}, f32[4,64,128]{2,1,0:T(8,128)S(1)}, u32[]{:S(2)}, u32[]{:S(2)}) %collective-permute-start.13) | collective-permute-done | bytes 131104 | tf_op jit(solution)/shard_map/ppermute | solution.py:492
  54.6 2.0 %collective-permute-done.12 = f32[4,64,128]{2,1,0:T(8,128)S(1)} collective-permute-done((f32[4,64,128]{2,1,0:T(8,128)S(1)}, f32[4,64,128]{2,1,0:T(8,128)S(1)}, u32[]{:S(2)}, u32[]{:S(2)}) %collective-permute-start.12) | collective-permute-done | bytes 131104 | tf_op jit(solution)/shard_map/ppermute | solution.py:492
  56.6 1.0 %collective-permute-done.14 = f32[4,64,128]{2,1,0:T(8,128)} collective-permute-done((f32[4,64,128]{2,1,0:T(8,128)S(1)}, f32[4,64,128]{2,1,0:T(8,128)}, u32[]{:S(2)}, u32[]{:S(2)}) %collective-permute-start.14) | collective-permute-done | bytes 131104 | tf_op jit(solution)/shard_map/ppermute | solution.py:492
  57.7 1.0 %pad_maximum_fusion.refs_0_ = f32[4,4,64,128]{3,2,1,0:T(8,128)S(1)} fusion(f32[1,4,64,128]{3,2,1,0:T(8,128)} %bitcast.9, f32[1,4,64,128]{3,2,1,0:T(8,128)S(1)} %bitcast.17, f32[1,4,64,128]{3,2,1,0:T(8,128)S(1)} %bitcast.18, f32[1,4,64,128]{3,2,1,0:T(8,128)S(1)} %get-tuple-element.38), kind=kLoop, calls=%fused_computation | loop fusion | flops 393216 | bytes 1048576 | tf_op jit(solution)/shard_map/stack | solution.py:764
  59.1 1.5 %collective-permute-done.15.refs_1_ = f32[4,4,64,128]{3,2,1,0:T(8,128)S(1)} collective-permute-done((f32[4,4,64,128]{3,2,1,0:T(8,128)S(1)}, f32[4,4,64,128]{3,2,1,0:T(8,128)S(1)}, u32[]{:S(2)}, u32[]{:S(2)}) %collective-permute-start.15) | collective-permute-done | bytes 524320 | tf_op jit(solution)/shard_map/ppermute | solution.py:492
  61.3 1.1 %copy-done.5 = f32[30,24,256]{2,1,0:T(8,128)S(1)} copy-done((f32[30,24,256]{2,1,0:T(8,128)S(1)}, f32[30,24,256]{2,1,0:T(8,128)}, u32[]{:S(2)}) %copy-start.5) | copy-done | bytes 737304
  62.4 18.2 %second.1 = (f32[16,16,128]{2,1,0:T(8,128)}, f32[16,16,128]{2,1,0:T(8,128)}) custom-call(f32[4,4,64,128]{3,2,1,0:T(8,128)S(1)} %pad_maximum_fusion.refs_0_, f32[4,4,64,128]{3,2,1,0:T(8,128)S(1)} %collective-permute-done.15.refs_1_, f32[30,24,256]{2,1,0:T(8,128)S(1)} %get-tuple-element.29.refs_2_, f32[30,24,256]{2,1,0:T(8,128)S(1)} %get-tuple-element.30.refs_3_, ...), custom_call_target="tpu_custom_call" | custom-call | tf_op jit(solution)/shard_map/second/pallas_call | solution.py:725
  (93 shorter events, 16.5 us)
Async XLA Ops:
  0.6 2.5 %copy-start = (f32[1,16,16,128]{3,2,1,0:T(8,128)S(1)}, f32[1,16,16,128]{3,2,1,0:T(8,128)}, u32[]{:S(2)}) copy-start(f32[1,16,16,128]{3,2,1,0:T(8,128)} %param.17) | copy-start | bytes 393220
  0.6 2.5 %copy-start.1 = (f32[16,16,128]{2,1,0:T(8,128)S(1)}, f32[16,16,128]{2,1,0:T(8,128)}, u32[]{:S(2)}) copy-start(f32[16,16,128]{2,1,0:T(8,128)} %refs_1_.1) | copy-start | bytes 393220
  1.7 1.5 %collective-permute-start = (f32[2,16,8,128]{3,2,1,0:T(8,128)S(1)}, f32[2,16,8,128]{3,2,1,0:T(8,128)S(1)}, u32[]{:S(2)}, u32[]{:S(2)}) collective-permute-start(f32[2,16,8,128]{3,2,1,0:T(8,128)S(1)} %fusion.1), channel_id=1, source_target_pairs={{0,4},{4,0},{1,5},{5,1},{2,6},{6,2},{3,7},{7,3},{8,12},{12,8},{9,1... | collective-permute-start | bytes 393224 | tf_op jit(solution)/shard_map/ppermute | solution.py:492
  3.5 20.7 %copy-start.9 = (bf16[128,128]{1,0:T(8,128)(2,1)S(1)}, bf16[128,128]{1,0:T(8,128)(2,1)}, u32[]{:S(2)}) copy-start(bf16[128,128]{1,0:T(8,128)(2,1)} %constant.123.clone.refs_12_.refs_16_) | copy-start | bytes 98308
  3.5 20.0 %collective-permute-start.1 = (f32[2,7,24,128]{3,2,1,0:T(8,128)S(1)}, f32[2,7,24,128]{3,2,1,0:T(8,128)S(1)}, u32[]{:S(2)}, u32[]{:S(2)}) collective-permute-start(f32[2,7,24,128]{3,2,1,0:T(8,128)S(1)} %get-tuple-element.20), channel_id=1, source_target_pairs={{0,1},{1,0},{2,3},{3,2},{4,5},{5,4},{6,7},{7,6},{8,9},{9,8},{10,11... | collective-permute-start | bytes 516104 | tf_op jit(solution)/shard_map/ppermute | solution.py:492
  6.5 17.0 %collective-permute-start.2 = (f32[2,7,24,128]{3,2,1,0:T(8,128)S(1)}, f32[2,7,24,128]{3,2,1,0:T(8,128)S(1)}, u32[]{:S(2)}, u32[]{:S(2)}) collective-permute-start(f32[2,7,24,128]{3,2,1,0:T(8,128)S(1)} %get-tuple-element.21), channel_id=1, source_target_pairs={{0,0},{1,2},{2,1},{3,3},{4,4},{5,6},{6,5},{7,7},{8,8},{9,10},{10,9... | collective-permute-start | bytes 516104 | tf_op jit(solution)/shard_map/ppermute | solution.py:492
  7.2 7.1 %collective-permute-start.5 = (f32[24,128]{1,0:T(8,128)S(1)}, f32[24,128]{1,0:T(8,128)S(1)}, u32[]{:S(2)}, u32[]{:S(2)}) collective-permute-start(f32[24,128]{1,0:T(8,128)S(1)} %get-tuple-element.24), channel_id=1, source_target_pairs={{0,9},{1,8},{2,11},{3,10},{8,1},{9,0},{10,3},{11,2},{16,25},{17,24... | collective-permute-start | bytes 36872 | tf_op jit(solution)/shard_map/ppermute | solution.py:492
  12.6 3.7 %collective-permute-start.6 = (f32[24,128]{1,0:T(8,128)S(1)}, f32[24,128]{1,0:T(8,128)S(1)}, u32[]{:S(2)}, u32[]{:S(2)}) collective-permute-start(f32[24,128]{1,0:T(8,128)S(1)} %get-tuple-element.25), channel_id=1, source_target_pairs={{0,8},{1,10},{2,9},{3,11},{8,0},{9,2},{10,1},{11,3},{16,24},{17,26... | collective-permute-start | bytes 36872 | tf_op jit(solution)/shard_map/ppermute | solution.py:492
  13.1 7.2 %collective-permute-start.7 = (f32[24,128]{1,0:T(8,128)S(1)}, f32[24,128]{1,0:T(8,128)S(1)}, u32[]{:S(2)}, u32[]{:S(2)}) collective-permute-start(f32[24,128]{1,0:T(8,128)S(1)} %get-tuple-element.26), channel_id=1, source_target_pairs={{0,1},{1,0},{2,3},{3,2},{8,17},{9,16},{10,19},{11,18},{16,9},{17,8... | collective-permute-start | bytes 36872 | tf_op jit(solution)/shard_map/ppermute | solution.py:492
  14.8 6.9 %collective-permute-start.8 = (f32[24,128]{1,0:T(8,128)S(1)}, f32[24,128]{1,0:T(8,128)S(1)}, u32[]{:S(2)}, u32[]{:S(2)}) collective-permute-start(f32[24,128]{1,0:T(8,128)S(1)} %get-tuple-element.27), channel_id=1, source_target_pairs={{0,0},{1,2},{2,1},{3,3},{8,16},{9,18},{10,17},{11,19},{16,8},{17,1... | collective-permute-start | bytes 36872 | tf_op jit(solution)/shard_map/ppermute | solution.py:492
  16.9 5.5 %collective-permute-start.3 = (f32[2,24,128]{2,1,0:T(8,128)S(1)}, f32[2,24,128]{2,1,0:T(8,128)S(1)}, u32[]{:S(2)}, u32[]{:S(2)}) collective-permute-start(f32[2,24,128]{2,1,0:T(8,128)S(1)} %get-tuple-element.22), channel_id=1, source_target_pairs={{0,8},{8,0},{16,24},{24,16},{1,9},{9,1},{17,25},{25,17},{2,10},{10... | collective-permute-start | bytes 73736 | tf_op jit(solution)/shard_map/ppermute | solution.py:492
  20.9 2.0 %collective-permute-start.4 = (f32[2,24,128]{2,1,0:T(8,128)S(1)}, f32[2,24,128]{2,1,0:T(8,128)S(1)}, u32[]{:S(2)}, u32[]{:S(2)}) collective-permute-start(f32[2,24,128]{2,1,0:T(8,128)S(1)} %get-tuple-element.23), channel_id=1, source_target_pairs={{0,0},{8,16},{16,8},{24,24},{1,1},{9,17},{17,9},{25,25},{2,2},{10,... | collective-permute-start | bytes 73736 | tf_op jit(solution)/shard_map/ppermute | solution.py:492
  39.5 5.7 %collective-permute-start.11 = (f32[64,128]{1,0:T(8,128)S(1)}, f32[64,128]{1,0:T(8,128)S(1)}, u32[]{:S(2)}, u32[]{:S(2)}) collective-permute-start(f32[64,128]{1,0:T(8,128)S(1)} %get-tuple-element.28), channel_id=1, source_target_pairs={{0,3},{1,2},{2,1},{3,0},{4,7},{5,6},{6,5},{7,4},{8,11},{9,10},{10,... | collective-permute-start | bytes 98312 | tf_op jit(solution)/shard_map/ppermute | solution.py:492
  41.4 4.8 %collective-permute-start.10 = (f32[64,128]{1,0:T(8,128)S(1)}, f32[64,128]{1,0:T(8,128)S(1)}, u32[]{:S(2)}, u32[]{:S(2)}) collective-permute-start(f32[64,128]{1,0:T(8,128)S(1)} %get-tuple-element.28), channel_id=1, source_target_pairs={{0,2},{1,3},{2,0},{3,1},{4,6},{5,7},{6,4},{7,5},{8,10},{9,11},{10,... | collective-permute-start | bytes 98312 | tf_op jit(solution)/shard_map/ppermute | solution.py:492
  42.4 4.1 %collective-permute-start.9 = (f32[64,128]{1,0:T(8,128)S(1)}, f32[64,128]{1,0:T(8,128)S(1)}, u32[]{:S(2)}, u32[]{:S(2)}) collective-permute-start(f32[64,128]{1,0:T(8,128)S(1)} %get-tuple-element.28), channel_id=1, source_target_pairs={{0,1},{1,0},{2,3},{3,2},{4,5},{5,4},{6,7},{7,6},{8,9},{9,8},{10,11... | collective-permute-start | bytes 98312 | tf_op jit(solution)/shard_map/ppermute | solution.py:492
  46.6 8.0 %collective-permute-start.13 = (f32[4,64,128]{2,1,0:T(8,128)S(1)}, f32[4,64,128]{2,1,0:T(8,128)S(1)}, u32[]{:S(2)}, u32[]{:S(2)}) collective-permute-start(f32[4,64,128]{2,1,0:T(8,128)S(1)} %get-tuple-element.39), channel_id=1, source_target_pairs={{0,16},{8,24},{16,0},{24,8},{1,17},{9,25},{17,1},{25,9},{2,18},{10... | collective-permute-start | bytes 393224 | tf_op jit(solution)/shard_map/ppermute | solution.py:492
  51.6 5.0 %collective-permute-start.12 = (f32[4,64,128]{2,1,0:T(8,128)S(1)}, f32[4,64,128]{2,1,0:T(8,128)S(1)}, u32[]{:S(2)}, u32[]{:S(2)}) collective-permute-start(f32[4,64,128]{2,1,0:T(8,128)S(1)} %get-tuple-element.39), channel_id=1, source_target_pairs={{0,8},{8,0},{16,24},{24,16},{1,9},{9,1},{17,25},{25,17},{2,10},{10... | collective-permute-start | bytes 393224 | tf_op jit(solution)/shard_map/ppermute | solution.py:492
  51.6 6.0 %collective-permute-start.14 = (f32[4,64,128]{2,1,0:T(8,128)S(1)}, f32[4,64,128]{2,1,0:T(8,128)}, u32[]{:S(2)}, u32[]{:S(2)}) collective-permute-start(f32[4,64,128]{2,1,0:T(8,128)S(1)} %get-tuple-element.39), channel_id=1, source_target_pairs={{0,24},{8,16},{16,8},{24,0},{1,25},{9,17},{17,9},{25,1},{2,26},{10... | collective-permute-start | bytes 393224 | tf_op jit(solution)/shard_map/ppermute | solution.py:492
  53.2 7.4 %copy-start.3 = (f32[30,24,256]{2,1,0:T(8,128)S(1)}, f32[30,24,256]{2,1,0:T(8,128)}, u32[]{:S(2)}) copy-start(f32[30,24,256]{2,1,0:T(8,128)} %copy-done.2) | copy-start | bytes 2211844
  57.6 3.0 %copy-start.16 = (bf16[128,128]{1,0:T(8,128)(2,1)S(1)}, bf16[128,128]{1,0:T(8,128)(2,1)}, u32[]{:S(2)}) copy-start(bf16[128,128]{1,0:T(8,128)(2,1)} %constant.131.clone.refs_18_) | copy-start | bytes 98308
  57.6 3.0 %copy-start.17 = (bf16[128,32]{1,0:T(8,128)(2,1)S(1)}, bf16[128,32]{1,0:T(8,128)(2,1)}, u32[]{:S(2)}) copy-start(bf16[128,32]{1,0:T(8,128)(2,1)} %constant.130.clone.refs_17_) | copy-start | bytes 24580
  57.6 3.0 %copy-start.32 = (bf16[32,8]{1,0:T(8,128)(2,1)S(1)}, bf16[32,8]{1,0:T(8,128)(2,1)}, u32[]{:S(2)}) copy-start(bf16[32,8]{1,0:T(8,128)(2,1)} %constant.134.clone.refs_21_) | copy-start | bytes 1540
  57.6 3.0 %copy-start.33 = (bf16[32,128]{1,0:T(8,128)(2,1)S(1)}, bf16[32,128]{1,0:T(8,128)(2,1)}, u32[]{:S(2)}) copy-start(bf16[32,128]{1,0:T(8,128)(2,1)} %constant.129.clone.refs_15_) | copy-start | bytes 24580
  58.6 2.0 %collective-permute-start.15 = (f32[4,4,64,128]{3,2,1,0:T(8,128)S(1)}, f32[4,4,64,128]{3,2,1,0:T(8,128)S(1)}, u32[]{:S(2)}, u32[]{:S(2)}) collective-permute-start(f32[4,4,64,128]{3,2,1,0:T(8,128)S(1)} %pad_maximum_fusion.refs_0_), channel_id=1, source_target_pairs={{0,4},{4,0},{1,5},{5,1},{2,6},{6,2},{3,7},{7,3},{8,12},{12,8},{9,1... | collective-permute-start | bytes 1572872 | tf_op jit(solution)/shard_map/ppermute | solution.py:492
  (27 other events, 26.7 us)

commit v3 on v2

--- a/solution.py
+++ b/solution.py
@@ -502,17 +502,10 @@
     return lax.broadcasted_iota(jnp.int32, shape, len(shape) - 1)
 
 
-def pack_kernel(source, coef, side, z_a, z_b, x_a, x_b, c_aa, c_ab, c_ba, c_bb):
+def pack_x_kernel(source, coef, side, x_a, x_b):
     planes, own_y, _ = source.shape
-    z_even = lax.axis_index("gz") % 2 == 0
     x_even = lax.axis_index("gx") % 2 == 0
-    for which, ref in enumerate((source, coef)):
-        for target, top in ((z_a, z_even), (z_b, jnp.logical_not(z_even))):
-            first = jnp.where(top, planes - HALO_Z, 0)
-            target[which, :, :own_y] = ref[pl.ds(first, HALO_Z)]
-            target[which, :, own_y:] = side[which, pl.ds(first, HALO_Z)]
     lane = lanes_of((own_y + HALO_Y, 128))
-    rights, lefts = [], []
     for which, ref in enumerate((source, coef)):
         right = left = jnp.zeros(lane.shape, F32)
         for plane in range(planes):
@@ -522,72 +515,72 @@
             left = jnp.where(slot, turned(value, 8 * plane, 1), left)
         x_a[which] = jnp.where(x_even, right, left)
         x_b[which] = jnp.where(x_even, left, right)
-        rights.append(right)
-        lefts.append(left)
-    corners = []
-    for pack in (rights, lefts):
-        bottom = jnp.where(lane < 64, pack[0], turned(pack[1], 64, 1))
-        skip = 8 * (planes - HALO_Z)
-        top = jnp.where(lane < 64, turned(pack[0], -skip, 1), turned(pack[1], 64 - skip, 1))
-        corners.append((top, bottom))
-    for target, right, top in (
-        (c_aa, x_even, z_even),
-        (c_ab, x_even, jnp.logical_not(z_even)),
-        (c_ba, jnp.logical_not(x_even), z_even),
-        (c_bb, jnp.logical_not(x_even), jnp.logical_not(z_even)),
-    ):
-        target[...] = jnp.where(
-            right,
-            jnp.where(top, corners[0][0], corners[0][1]),
-            jnp.where(top, corners[1][0], corners[1][1]),
-        )
+
+
+def kept(flag, value):
+    return jnp.where(flag, value, 0.0)
+
+
+def x_halos(x_a, x_b, which, x_count):
+    x_index = lax.axis_index("gx")
+    x_even = x_index % 2 == 0
+    right = kept(x_index < x_count - 1, jnp.where(x_even, x_a[which], x_b[which]))
+    left = kept(x_index > 0, jnp.where(x_even, x_b[which], x_a[which]))
+    return right, left
+
+
+def pack_z_kernel(x_count, source, coef, side, x_a, x_b, z_a, z_b):
+    planes, own_y, _ = source.shape
+    z_even = lax.axis_index("gz") % 2 == 0
+    lane = lanes_of((own_y + HALO_Y, 128))
+    skip = 8 * (planes - HALO_Z)
+    for which, ref in enumerate((source, coef)):
+        right, left = x_halos(x_a, x_b, which, x_count)
+        bottom = jnp.where(lane < 64, right, turned(left, 64, 1))
+        top = jnp.where(lane < 64, turned(right, -skip, 1), turned(left, 64 - skip, 1))
+        for target, is_top in ((z_a, z_even), (z_b, jnp.logical_not(z_even))):
+            first = jnp.where(is_top, planes - HALO_Z, 0)
+            target[which, :HALO_Z, :own_y] = ref[pl.ds(first, HALO_Z)]
+            target[which, :HALO_Z, own_y:] = side[which, pl.ds(first, HALO_Z)]
+            target[which, HALO_Z] = jnp.where(is_top, top, bottom)
 
 
 def fill_window(own, side, got, source, coef, x_count, z_count):
-    z_a, z_b, x_a, x_b, c_aa, c_ab, c_ba, c_bb = got
+    x_a, x_b, z_a, z_b = got
     planes, own_y = own[0].shape[:2]
     rows = own_y + HALO_Y
-    z_index, x_index = lax.axis_index("gz"), lax.axis_index("gx")
-    z_even, x_even = z_index % 2 == 0, x_index % 2 == 0
-    has_above, has_below = z_index < z_count - 1, z_index > 0
-    has_right, has_left = x_index < x_count - 1, x_index > 0
+    z_index = lax.axis_index("gz")
+    z_even = z_index % 2 == 0
     above_at, below_at = HALO_Z + planes, 0
     lane = lanes_of((rows, 128))
 
-    def edges(right, left, shift):
-        value = jnp.where(lane < 8, turned(right, -shift, 1), turned(left, 120 - shift, 1))
+    def edges(right, left, right_shift, left_shift):
+        value = jnp.where(lane < 8, turned(right, -right_shift, 1), turned(left, 120 - left_shift, 1))
         return jnp.where((lane < 8) | (lane >= 120), value, 0.0)
-
-    def kept(flag, value):
-        return jnp.where(flag, value, 0.0)
 
     for which, target in enumerate((source, coef)):
         target[pl.ds(HALO_Z, planes), :own_y, :128] = own[which][...]
         target[pl.ds(HALO_Z, planes), own_y:, :128] = side[which]
-        above = jnp.where(z_even, z_a[which], z_b[which])
-        target[pl.ds(above_at, HALO_Z), :, :128] = kept(has_above, above)
-        below = jnp.where(z_even, z_b[which], z_a[which])
-        target[pl.ds(below_at, HALO_Z), :, :128] = kept(has_below, below)
-        right = kept(has_right, jnp.where(x_even, x_a[which], x_b[which]))
-        left = kept(has_left, jnp.where(x_even, x_b[which], x_a[which]))
+        right, left = x_halos(x_a, x_b, which, x_count)
         for plane in range(planes):
-            target[HALO_Z + plane, :, 128:] = edges(right, left, 8 * plane)
-    for at, flag, is_a in ((above_at, has_above, z_even), (below_at, has_below, jnp.logical_not(z_even))):
-        by_a = jnp.where(is_a, c_aa[...], c_ab[...])
-        by_b = jnp.where(is_a, c_ba[...], c_bb[...])
-        right = kept(flag & has_right, jnp.where(x_even, by_a, by_b))
-        left = kept(flag & has_left, jnp.where(x_even, by_b, by_a))
-        for which, target in enumerate((source, coef)):
+            target[HALO_Z + plane, :, 128:] = edges(right, left, 8 * plane, 8 * plane)
+        for at, flag, is_a in (
+            (above_at, z_index < z_count - 1, z_even),
+            (below_at, z_index > 0, jnp.logical_not(z_even)),
+        ):
             for plane in range(HALO_Z):
-                target[at + plane, :, 128:] = edges(right, left, 64 * which + 8 * plane)
+                target[at + plane, :, :128] = kept(flag, jnp.where(is_a, z_a[which, plane], z_b[which, plane]))
+            packed = kept(flag, jnp.where(is_a, z_a[which, HALO_Z], z_b[which, HALO_Z]))
+            for plane in range(HALO_Z):
+                target[at + plane, :, 128:] = edges(packed, packed, 8 * plane, 64 + 8 * plane)
     coef[pl.ds(above_at + HALO_Z, 1)] = jnp.zeros((1,) + coef.shape[1:], F32)
 
 
 def first_kernel(counts, *refs):
-    own, side, got = refs[:2], refs[2], refs[3:11]
-    left, right_source, right_coef, message, source, estimate = refs[11:17]
-    faces = refs[17:22]
-    coef, residual, update, pair_source, pair_coef = refs[22:]
+    own, side, got = refs[:2], refs[2], refs[3:7]
+    left, right_source, right_coef, message, source, estimate = refs[7:13]
+    faces = refs[13:18]
+    coef, residual, update, pair_source, pair_coef = refs[18:]
     fill_window(own, side, got, source, coef, *counts)
     planes, rows, lanes = source.shape
     own_y = rows - HALO_Y
@@ -621,7 +614,7 @@
     planes, rows, lanes = source.shape
     own_y = rows - HALO_Y
     mid_z, mid_y, mid_x = z_count * 8, y_count * 8, x_count * 64
-    x_index, y_index, z_index = (lax.axis_index(axis) for axis in ("gx", "gy", "gz"))
+    y_index, z_index = lax.axis_index("gy"), lax.axis_index("gz")
 
     zero = jnp.zeros((PAD, mid_y, mid_x), F32)
     for ref in (mid_coef, mid_update, mid_estimate, mid_faces[0]):
@@ -629,19 +622,15 @@
         ref[pl.ds(PAD + mid_z, PAD)] = zero
 
     low_half = lanes_of((64, 128)) < 64
-    x_even = x_index % 2 == 0
     for blocks, y_block in ((gathered, y_index), (other, 1 - y_index)):
         y_rows = pl.ds(pl.multiple_of(y_block * 8, 8), 8)
         for x_pair in range(x_count // 2):
-            x_lanes = pl.ds(pl.multiple_of(((x_index // 2) ^ x_pair) * 128, 128), 128)
             for z_block in range(z_count):
-                mine = blocks[2 * x_pair, z_block]
-                partner = blocks[2 * x_pair + 1, z_block]
-                even = jnp.where(x_even, mine, partner)
-                odd = jnp.where(x_even, partner, mine)
-                z_planes = pl.ds(PAD + (z_index ^ z_block) * 8, 8)
-                mid_source[z_planes, y_rows, x_lanes] = jnp.where(low_half, even, turned(odd, 64, 1)).reshape(8, 8, 128)
-                mid_coef[z_planes, y_rows, x_lanes] = jnp.where(low_half, turned(even, 64, 1), odd).reshape(8, 8, 128)
+                even = blocks[2 * x_pair, z_block]
+                odd = blocks[2 * x_pair + 1, z_block]
+                where = (pl.ds(PAD + z_block * 8, 8), y_rows, pl.ds(x_pair * 128, 128))
+                mid_source[where] = jnp.where(low_half, even, turned(odd, 64, 1)).reshape(8, 8, 128)
+                mid_coef[where] = jnp.where(low_half, turned(even, 64, 1), odd).reshape(8, 8, 128)
 
     row = lax.broadcasted_iota(jnp.int32, (1, mid_y, mid_x), 1)
     lane = lanes_of((1, mid_y, mid_x))
@@ -719,16 +708,15 @@
     right_side = right_side[0]
     planes, rows, lanes = own_z + 2 * HALO_Z, own_y + HALO_Y, 2 * own_x
     vmem = pl.BlockSpec(memory_space=pltpu.VMEM)
-    params = pltpu.CompilerParams(vmem_limit_bytes=48 * 1024 * 1024)
-
-    def call(kernel, name, arguments, shapes, scratch):
+
+    def call(kernel, name, room, arguments, shapes, scratch):
         return pl.pallas_call(
             kernel,
             out_shape=tuple(jax.ShapeDtypeStruct(shape, F32) for shape in shapes),
             in_specs=[vmem] * len(arguments),
             out_specs=(vmem,) * len(shapes),
             scratch_shapes=[pltpu.VMEM(shape, F32) for shape in scratch],
-            compiler_params=params,
+            compiler_params=pltpu.CompilerParams(vmem_limit_bytes=room * 1024 * 1024),
             name=name,
         )(*arguments)
 
@@ -736,34 +724,30 @@
     both = jnp.stack([right_side, coefficient])
     side = jnp.where(y_index == 0, both[:, :, own_y - HALO_Y :], both[:, :, :HALO_Y])
     side = swapped(side, "gy", [swap_pairs(y_count, False)])
-    z_shape, x_shape, c_shape = (2, HALO_Z, rows, 128), (2, rows, 128), (rows, 128)
+    swaps = [[swap_pairs(count, odd) for odd in (False, True)] for count in (x_count, z_count)]
+    blocks = (right_side, coefficient, side)
+    sent = call(pack_x_kernel, "pack_x", 4, blocks, [(2, rows, 128)] * 2, [])
+    got = [swapped(value, "gx", [pairs]) for value, pairs in zip(sent, swaps[0])]
     sent = call(
-        pack_kernel, "pack", (right_side, coefficient, side), [z_shape] * 2 + [x_shape] * 2 + [c_shape] * 4, []
-    )
-    x_a, x_b = swap_pairs(x_count, False), swap_pairs(x_count, True)
-    z_a, z_b = swap_pairs(z_count, False), swap_pairs(z_count, True)
-    got = [swapped(sent[0], "gz", [z_a]), swapped(sent[1], "gz", [z_b])]
-    got += [swapped(sent[2], "gx", [x_a]), swapped(sent[3], "gx", [x_b])]
-    for message, partners in zip(sent[4:], ((x_a, z_a), (x_a, z_b), (x_b, z_a), (x_b, z_b))):
-        got.append(swapped(message, ("gx", "gz"), partners))
+        functools.partial(pack_z_kernel, x_count), "pack_z", 4, blocks + tuple(got), [(2, HALO_Z + 1, rows, 128)] * 2, []
+    )
+    got += [swapped(value, "gz", [pairs]) for value, pairs in zip(sent, swaps[1])]
 
     window, padded = (planes, rows, lanes), (planes + 1, rows, lanes)
     down = own_down_matrices(own_z // 2, own_y, own_x)
     message, *kept = call(
         functools.partial(first_kernel, (x_count, z_count)),
         "first",
-        (right_side, coefficient, side, *got, *down),
+        8,
+        (*blocks, *got, *down),
         [(own_z * own_y // 4, own_x)] + [window] * 2 + [window] * 5,
         [padded, window, padded] + [(own_z * own_y // 2, own_x)] * 2,
     )
 
-    def with_others(value, axis, count):
-        others = [
-            swapped(value, axis, [[index ^ distance for index in range(count)]]) for distance in range(1, count)
-        ]
-        return jnp.stack([value] + others)
-
-    gathered = with_others(with_others(message, "gz", z_count), "gx", x_count)
+    def to_all(value, axis, count):
+        return lax.all_to_all(jnp.broadcast_to(value, (count,) + value.shape), axis, 0, 0)
+
+    gathered = to_all(to_all(message, "gz", z_count), "gx", x_count)
     other = swapped(gathered, "gy", [swap_pairs(y_count, False)])
 
     mid = (own_z * z_count // 2, own_y * y_count // 2, own_x * x_count // 2)
@@ -786,6 +770,7 @@
     solution, residual = call(
         functools.partial(second_kernel, counts, len(sheets)),
         "second",
+        20,
         (gathered, other, *kept, *up, *mid_down, *mid_up, *sheets),
         [(own_z, own_y, own_x)] * 2,
         [mid_padded] * 5

time: 81.4 us -> 76 us (0.934)
  local copies, waits for them, and re-layouts: 15.5 us -> 9.7 us
  waiting for transfers between devices: 11.5 us -> 16.4 us
  starting transfers between devices: 25.9 us -> 21.7 us
  Pallas kernels: 24.4 us -> 23.5 us
    ppermute x16 -> x6, starting transfers between devices: 25.9 us -> 7.05 us  [swapped(): return lax.ppermute(value, axes, list(enumerate(places)))]
    all_to_all x0 -> x2, starting transfers between devices: none -> 14.7 us  [to_all(): lax.all_to_all(jnp.broadcast_to(value, (count,) + value.shape), axis, 0, 0)]
    all_to_all x0 -> x2, waiting for transfers between devices: none -> 10.2 us  [to_all(): lax.all_to_all(jnp.broadcast_to(value, (count,) + value.shape), axis, 0, 0)]
    unnamed x70 -> x56, local copies, waits for them, and re-layouts: 15.4 us -> 7.51 us
    ppermute x16 -> x6, waiting for transfers between devices: 11.5 us -> 6.23 us  [swapped(): return lax.ppermute(value, axes, list(enumerate(places)))]
    broadcast_in_dim x0 -> x2, local copies, waits for them, and re-layouts: none -> 1.51 us  [to_all(): jnp.broadcast_to(value, (count,) + value.shape)]
    another operation x2 -> x0, other arithmetic: 0.98 us -> none  [with_others(): return jnp.stack([value] + others)]
    pallas_call x3 -> x4, Pallas kernels: 24.4 us -> 23.5 us  [call(): pl.pallas_call(kernel, out_shape=tuple((jax.ShapeDtypeStruct(shape, F32)...]
  transfers between devices with their start and end apart: 16 -> 8, of which waited for: 10 -> 6; matrix products, arithmetic and copies ran while one was open for 0% -> 4% of each run, Pallas kernels for 0% -> 0%
where the time goes in v3:
time: 76 us; the launch traced here: 75.3 us
  Pallas kernels  23.5 us (31%)
  starting transfers between devices  21.7 us (29%)
  waiting for transfers between devices  16.4 us (22%)
  local copies, waits for them, and re-layouts  9.7 us (13%)
  other arithmetic  3.04 us (4%)
  between operations  0.88 us (1%)
    pallas_call x4, Pallas kernels, call(): pl.pallas_call(kernel, out_shape=tuple((jax.ShapeDtypeStruct(shape, F32)...  23.5 us
    all_to_all x2, starting transfers between devices, to_all(): lax.all_to_all(jnp.broadcast_to(value, (count,) + value.shape), axis, 0, 0)  14.7 us
    all_to_all x2, waiting for transfers between devices, to_all(): lax.all_to_all(jnp.broadcast_to(value, (count,) + value.shape), axis, 0, 0)  10.2 us
    unnamed x56, local copies, waits for them, and re-layouts  7.51 us
    ppermute x6, starting transfers between devices, swapped(): return lax.ppermute(value, axes, list(enumerate(places)))  7.05 us
    ppermute x6, waiting for transfers between devices, swapped(): return lax.ppermute(value, axes, list(enumerate(places)))  6.23 us
  transfers between devices with their start and end apart: 8, of which 6 were waited for; matrix products, arithmetic and copies ran while one was open for 4% of the time, Pallas kernels for 0%

profile of v3, /device:TPU:0, one launch (start us, length us, event | category | flops | bytes accessed | tf_op | source)
XLA Modules:
  0.0 75.3 jit_solution(6145525872164778088)
XLA Ops:
  0.7 1.0 %fusion.1 = f32[2,16,8,128]{3,2,1,0:T(8,128)S(1)} fusion(f32[1,16,16,128]{3,2,1,0:T(8,128)} %param.17, f32[1,16,16,128]{3,2,1,0:T(8,128)} %bitcast.7, pred[]{:T(512)S(6)} %eq.93), kind=kLoop, calls=%fused_computation.7 | loop fusion | flops 98304 | bytes 393217 | tf_op jit(solution)/shard_map/jit(_where)/select_n | solution.py:725
  2.2 1.0 %collective-permute-done.side.refs_2_ = f32[2,16,8,128]{3,2,1,0:T(8,128)S(1)} collective-permute-done((f32[2,16,8,128]{3,2,1,0:T(8,128)S(1)}, f32[2,16,8,128]{3,2,1,0:T(8,128)S(1)}, u32[]{:S(2)}, u32[]{:S(2)}) %collective-permute-start) | collective-permute-done | bytes 131104 | tf_op jit(solution)/shard_map/ppermute | solution.py:492
  3.4 2.9 %collective-permute-start.1 = (f32[2,24,128]{2,1,0:T(8,128)S(1)}, f32[2,24,128]{2,1,0:T(8,128)S(1)}, u32[]{:S(2)}, u32[]{:S(2)}) collective-permute-start(f32[2,24,128]{2,1,0:T(8,128)S(1)} %get-tuple-element.16), channel_id=1, source_target_pairs={{0,8},{8,0},{16,24},{24,16},{1,9},{9,1},{17,25},{25,17},{2,10},{10... | collective-permute-start | bytes 73736 | tf_op jit(solution)/shard_map/ppermute | solution.py:492
  6.4 0.8 %collective-permute-start.2 = (f32[2,24,128]{2,1,0:T(8,128)S(1)}, f32[2,24,128]{2,1,0:T(8,128)S(1)}, u32[]{:S(2)}, u32[]{:S(2)}) collective-permute-start(f32[2,24,128]{2,1,0:T(8,128)S(1)} %get-tuple-element.17), channel_id=1, source_target_pairs={{0,0},{8,16},{16,8},{24,24},{1,1},{9,17},{17,9},{25,25},{2,2},{10,... | collective-permute-start | bytes 73736 | tf_op jit(solution)/shard_map/ppermute | solution.py:492
  7.1 1.0 %collective-permute-done.1.x_a.refs_3_ = f32[2,24,128]{2,1,0:T(8,128)S(1)} collective-permute-done((f32[2,24,128]{2,1,0:T(8,128)S(1)}, f32[2,24,128]{2,1,0:T(8,128)S(1)}, u32[]{:S(2)}, u32[]{:S(2)}) %collective-permute-start.1) | collective-permute-done | bytes 24608 | tf_op jit(solution)/shard_map/ppermute | solution.py:492
  8.3 2.2 %collective-permute-start.3 = (f32[2,8,24,128]{3,2,1,0:T(8,128)S(1)}, f32[2,8,24,128]{3,2,1,0:T(8,128)S(1)}, u32[]{:S(2)}, u32[]{:S(2)}) collective-permute-start(f32[2,8,24,128]{3,2,1,0:T(8,128)S(1)} %get-tuple-element.18), channel_id=1, source_target_pairs={{0,1},{1,0},{2,3},{3,2},{4,5},{5,4},{6,7},{7,6},{8,9},{9,8},{10,11... | collective-permute-start | bytes 589832 | tf_op jit(solution)/shard_map/ppermute | solution.py:492
  11.1 3.4 %collective-permute-done.3.refs_5_ = f32[2,8,24,128]{3,2,1,0:T(8,128)S(1)} collective-permute-done((f32[2,8,24,128]{3,2,1,0:T(8,128)S(1)}, f32[2,8,24,128]{3,2,1,0:T(8,128)S(1)}, u32[]{:S(2)}, u32[]{:S(2)}) %collective-permute-start.3) | collective-permute-done | bytes 196640 | tf_op jit(solution)/shard_map/ppermute | solution.py:492
  14.5 6.0 %first.1 = (f32[64,128]{1,0:T(8,128)S(1)}, f32[30,24,256]{2,1,0:T(8,128)S(1)}, f32[30,24,256]{2,1,0:T(8,128)S(1)}, f32[30,24,256]{2,1,0:T(8,128)S(1)}, f32[30,24...) custom-call(f32[16,16,128]{2,1,0:T(8,128)S(1)} %bitcast.6, ...), custom_call_target="tpu_custom_call" | custom-call | tf_op jit(solution)/shard_map/first/pallas_call | solution.py:713
  20.5 0.9 %copy-done.2 = f32[30,24,256]{2,1,0:T(8,128)} copy-done((f32[30,24,256]{2,1,0:T(8,128)}, f32[30,24,256]{2,1,0:T(8,128)S(1)}, u32[]{:S(2)}) %copy-start.2) | copy-done | bytes 737304
  21.4 0.9 %copy-done.4 = f32[30,24,256]{2,1,0:T(8,128)} copy-done((f32[30,24,256]{2,1,0:T(8,128)}, f32[30,24,256]{2,1,0:T(8,128)S(1)}, u32[]{:S(2)}) %copy-start.4) | copy-done | bytes 737304
  22.3 0.9 %copy-done.6 = f32[30,24,256]{2,1,0:T(8,128)} copy-done((f32[30,24,256]{2,1,0:T(8,128)}, f32[30,24,256]{2,1,0:T(8,128)S(1)}, u32[]{:S(2)}) %copy-start.6) | copy-done | bytes 737304
  23.2 0.7 broadcast_in_dim.42
  23.8 7.3 %all-to-all-start = ((f32[4,64,128]{2,1,0:T(8,128)}), f32[4,64,128]{2,1,0:T(8,128)S(1)}, u32[]{:S(2)}, u32[]{:S(2)}) async-start(f32[4,64,128]{2,1,0:T(8,128)} %broadcast_in_dim.42), calls=%async_computation | async-start | bytes 262144 | tf_op jit(solution)/shard_map/all_to_all | solution.py:748
  31.2 0.7 broadcast_in_dim_tile.3
  31.9 5.2 %all-to-all-done = f32[4,64,128]{2,1,0:T(8,128)S(1)} async-done(((f32[4,64,128]{2,1,0:T(8,128)}), f32[4,64,128]{2,1,0:T(8,128)S(1)}, u32[]{:S(2)}, u32[]{:S(2)}) %all-to-all-start) | async-done | bytes 131104 | tf_op jit(solution)/shard_map/all_to_all | solution.py:748
  37.1 0.8 %broadcast_in_dim.43 = f32[4,4,64,128]{3,2,1,0:T(8,128)} broadcast(f32[4,64,128]{2,1,0:T(8,128)S(1)} %all-to-all-done), dimensions={1,2,3} | broadcast | bytes 655360 | tf_op jit(solution)/shard_map/broadcast_in_dim | solution.py:748
  38.0 7.3 %all-to-all-start.1 = ((f32[4,4,64,128]{3,2,1,0:T(8,128)}), f32[4,4,64,128]{3,2,1,0:T(8,128)S(1)}, u32[]{:S(2)}, u32[]{:S(2)}) async-start(f32[4,4,64,128]{3,2,1,0:T(8,128)} %broadcast_in_dim.43), calls=%async_computation.1 | async-start | bytes 1048576 | tf_op jit(solution)/shard_map/all_to_all | solution.py:748
  47.1 5.0 %all-to-all-done.1.refs_0_ = f32[4,4,64,128]{3,2,1,0:T(8,128)S(1)} async-done(((f32[4,4,64,128]{3,2,1,0:T(8,128)}), f32[4,4,64,128]{3,2,1,0:T(8,128)S(1)}, u32[]{:S(2)}, u32[]{:S(2)}) %all-to-all-start.1) | async-done | bytes 524320 | tf_op jit(solution)/shard_map/all_to_all | solution.py:748
  53.1 0.8 %collective-permute-done.5.refs_1_ = f32[4,4,64,128]{3,2,1,0:T(8,128)S(1)} collective-permute-done((f32[4,4,64,128]{3,2,1,0:T(8,128)S(1)}, f32[4,4,64,128]{3,2,1,0:T(8,128)S(1)}, u32[]{:S(2)}, u32[]{:S(2)}) %collective-permute-start.5) | collective-permute-done | bytes 524320 | tf_op jit(solution)/shard_map/ppermute | solution.py:492
  54.0 1.1 %copy-done.3 = f32[30,24,256]{2,1,0:T(8,128)S(1)} copy-done((f32[30,24,256]{2,1,0:T(8,128)S(1)}, f32[30,24,256]{2,1,0:T(8,128)}, u32[]{:S(2)}) %copy-start.3) | copy-done | bytes 737304
  55.1 1.1 %copy-done.5 = f32[30,24,256]{2,1,0:T(8,128)S(1)} copy-done((f32[30,24,256]{2,1,0:T(8,128)S(1)}, f32[30,24,256]{2,1,0:T(8,128)}, u32[]{:S(2)}) %copy-start.5) | copy-done | bytes 737304
  56.3 1.1 %copy-done.7 = f32[30,24,256]{2,1,0:T(8,128)S(1)} copy-done((f32[30,24,256]{2,1,0:T(8,128)S(1)}, f32[30,24,256]{2,1,0:T(8,128)}, u32[]{:S(2)}) %copy-start.7) | copy-done | bytes 737304
  57.4 0.8 %copy-done.16 = bf16[128,32]{1,0:T(8,128)(2,1)S(1)} copy-done((bf16[128,32]{1,0:T(8,128)(2,1)S(1)}, bf16[128,32]{1,0:T(8,128)(2,1)}, u32[]{:S(2)}) %copy-start.16) | copy-done | bytes 8216
  58.1 17.2 %second.1 = (f32[16,16,128]{2,1,0:T(8,128)}, f32[16,16,128]{2,1,0:T(8,128)}) custom-call(f32[4,4,64,128]{3,2,1,0:T(8,128)S(1)} %all-to-all-done.1.refs_0_, f32[4,4,64,128]{3,2,1,0:T(8,128)S(1)} %collective-permute-done.5.refs_1_, f32[30,24,256]{2,1,0:T(8,128)S(1)} %get-tuple-element.21.refs_2_, f32[30,24,256]{2,1,0:T(8,128)S(1)} %get-tuple-element.22.refs_3_, ...), custom_call_target="tpu_custom_call" | custom-call | tf_op jit(solution)/shard_map/second/pallas_call | solution.py:713
  (64 shorter events, 4.4 us)
Async XLA Ops:
  0.6 2.5 %copy-start = (f32[1,16,16,128]{3,2,1,0:T(8,128)S(1)}, f32[1,16,16,128]{3,2,1,0:T(8,128)}, u32[]{:S(2)}) copy-start(f32[1,16,16,128]{3,2,1,0:T(8,128)} %param.17) | copy-start | bytes 393220
  0.6 2.5 %copy-start.1 = (f32[16,16,128]{2,1,0:T(8,128)S(1)}, f32[16,16,128]{2,1,0:T(8,128)}, u32[]{:S(2)}) copy-start(f32[16,16,128]{2,1,0:T(8,128)} %refs_1_.1) | copy-start | bytes 393220
  1.7 1.5 %collective-permute-start = (f32[2,16,8,128]{3,2,1,0:T(8,128)S(1)}, f32[2,16,8,128]{3,2,1,0:T(8,128)S(1)}, u32[]{:S(2)}, u32[]{:S(2)}) collective-permute-start(f32[2,16,8,128]{3,2,1,0:T(8,128)S(1)} %fusion.1), channel_id=1, source_target_pairs={{0,4},{4,0},{1,5},{5,1},{2,6},{6,2},{3,7},{7,3},{8,12},{12,8},{9,1... | collective-permute-start | bytes 393224 | tf_op jit(solution)/shard_map/ppermute | solution.py:492
  3.4 4.7 %collective-permute-start.1 = (f32[2,24,128]{2,1,0:T(8,128)S(1)}, f32[2,24,128]{2,1,0:T(8,128)S(1)}, u32[]{:S(2)}, u32[]{:S(2)}) collective-permute-start(f32[2,24,128]{2,1,0:T(8,128)S(1)} %get-tuple-element.16), channel_id=1, source_target_pairs={{0,8},{8,0},{16,24},{24,16},{1,9},{9,1},{17,25},{25,17},{2,10},{10... | collective-permute-start | bytes 73736 | tf_op jit(solution)/shard_map/ppermute | solution.py:492
  6.3 8.1 %copy-start.8 = (bf16[128,128]{1,0:T(8,128)(2,1)S(1)}, bf16[128,128]{1,0:T(8,128)(2,1)}, u32[]{:S(2)}) copy-start(bf16[128,128]{1,0:T(8,128)(2,1)} %constant.123.clone.refs_8_.refs_16_) | copy-start | bytes 98308
  6.3 8.1 %copy-start.17 = (bf16[128,128]{1,0:T(8,128)(2,1)S(1)}, bf16[128,128]{1,0:T(8,128)(2,1)}, u32[]{:S(2)}) copy-start(bf16[128,128]{1,0:T(8,128)(2,1)} %constant.124.clone.refs_9_) | copy-start | bytes 98308
  6.3 8.2 %copy-start.18 = (bf16[64,128]{1,0:T(8,128)(2,1)S(1)}, bf16[64,128]{1,0:T(8,128)(2,1)}, u32[]{:S(2)}) copy-start(bf16[64,128]{1,0:T(8,128)(2,1)} %constant.122.clone.refs_7_) | copy-start | bytes 49156
  6.4 1.8 %collective-permute-start.2 = (f32[2,24,128]{2,1,0:T(8,128)S(1)}, f32[2,24,128]{2,1,0:T(8,128)S(1)}, u32[]{:S(2)}, u32[]{:S(2)}) collective-permute-start(f32[2,24,128]{2,1,0:T(8,128)S(1)} %get-tuple-element.17), channel_id=1, source_target_pairs={{0,0},{8,16},{16,8},{24,24},{1,1},{9,17},{17,9},{25,25},{2,2},{10,... | collective-permute-start | bytes 73736 | tf_op jit(solution)/shard_map/ppermute | solution.py:492
  8.3 6.2 %collective-permute-start.3 = (f32[2,8,24,128]{3,2,1,0:T(8,128)S(1)}, f32[2,8,24,128]{3,2,1,0:T(8,128)S(1)}, u32[]{:S(2)}, u32[]{:S(2)}) collective-permute-start(f32[2,8,24,128]{3,2,1,0:T(8,128)S(1)} %get-tuple-element.18), channel_id=1, source_target_pairs={{0,1},{1,0},{2,3},{3,2},{4,5},{5,4},{6,7},{7,6},{8,9},{9,8},{10,11... | collective-permute-start | bytes 589832 | tf_op jit(solution)/shard_map/ppermute | solution.py:492
  10.4 4.1 %collective-permute-start.4 = (f32[2,8,24,128]{3,2,1,0:T(8,128)S(1)}, f32[2,8,24,128]{3,2,1,0:T(8,128)S(1)}, u32[]{:S(2)}, u32[]{:S(2)}) collective-permute-start(f32[2,8,24,128]{3,2,1,0:T(8,128)S(1)} %get-tuple-element.19), channel_id=1, source_target_pairs={{0,0},{1,2},{2,1},{3,3},{4,4},{5,6},{6,5},{7,7},{8,8},{9,10},{10,9... | collective-permute-start | bytes 589832 | tf_op jit(solution)/shard_map/ppermute | solution.py:492
  23.8 13.3 %all-to-all-start = ((f32[4,64,128]{2,1,0:T(8,128)}), f32[4,64,128]{2,1,0:T(8,128)S(1)}, u32[]{:S(2)}, u32[]{:S(2)}) async-start(f32[4,64,128]{2,1,0:T(8,128)} %broadcast_in_dim.42), calls=%async_computation | async-start | bytes 262144 | tf_op jit(solution)/shard_map/all_to_all | solution.py:748
  38.0 16.0 %copy-start.15 = (bf16[128,128]{1,0:T(8,128)(2,1)S(1)}, bf16[128,128]{1,0:T(8,128)(2,1)}, u32[]{:S(2)}) copy-start(bf16[128,128]{1,0:T(8,128)(2,1)} %constant.131.clone.refs_18_) | copy-start | bytes 98308
  38.0 16.0 %copy-start.19 = (bf16[32,8]{1,0:T(8,128)(2,1)S(1)}, bf16[32,8]{1,0:T(8,128)(2,1)}, u32[]{:S(2)}) copy-start(bf16[32,8]{1,0:T(8,128)(2,1)} %constant.134.clone.refs_21_) | copy-start | bytes 1540
  38.0 16.0 %copy-start.20 = (bf16[32,128]{1,0:T(8,128)(2,1)S(1)}, bf16[32,128]{1,0:T(8,128)(2,1)}, u32[]{:S(2)}) copy-start(bf16[32,128]{1,0:T(8,128)(2,1)} %constant.129.clone.refs_15_) | copy-start | bytes 24580
  38.0 14.1 %all-to-all-start.1 = ((f32[4,4,64,128]{3,2,1,0:T(8,128)}), f32[4,4,64,128]{3,2,1,0:T(8,128)S(1)}, u32[]{:S(2)}, u32[]{:S(2)}) async-start(f32[4,4,64,128]{3,2,1,0:T(8,128)} %broadcast_in_dim.43), calls=%async_computation.1 | async-start | bytes 1048576 | tf_op jit(solution)/shard_map/all_to_all | solution.py:748
  45.3 1.2 %copy-start.25 = (s32[336]{0:T(512)S(1)}, s32[336]{0:T(512)}, u32[]{:S(2)}) copy-start(s32[336]{0:T(512)} %broadcast_in_dim_tile.3) | copy-start | bytes 4036
  52.0 1.9 %collective-permute-start.5 = (f32[4,4,64,128]{3,2,1,0:T(8,128)S(1)}, f32[4,4,64,128]{3,2,1,0:T(8,128)S(1)}, u32[]{:S(2)}, u32[]{:S(2)}) collective-permute-start(f32[4,4,64,128]{3,2,1,0:T(8,128)S(1)} %all-to-all-done.1.refs_0_), channel_id=1, source_target_pairs={{0,4},{4,0},{1,5},{5,1},{2,6},{6,2},{3,7},{7,3},{8,12},{12,8},{9,1... | collective-permute-start | bytes 1572872 | tf_op jit(solution)/shard_map/ppermute | solution.py:492
  52.1 1.9 %copy-start.12 = (bf16[128,256]{1,0:T(8,128)(2,1)S(1)}, bf16[128,256]{1,0:T(8,128)(2,1)}, u32[]{:S(2)}) copy-start(bf16[128,256]{1,0:T(8,128)(2,1)} %constant.125.clone.refs_11_) | copy-start | bytes 196612
  52.1 1.9 %copy-start.13 = (bf16[128,128]{1,0:T(8,128)(2,1)S(1)}, bf16[128,128]{1,0:T(8,128)(2,1)}, u32[]{:S(2)}) copy-start(bf16[128,128]{1,0:T(8,128)(2,1)} %constant.135.clone.refs_22_) | copy-start | bytes 98308
  52.1 1.9 %copy-start.14 = (bf16[128,128]{1,0:T(8,128)(2,1)S(1)}, bf16[128,128]{1,0:T(8,128)(2,1)}, u32[]{:S(2)}) copy-start(bf16[128,128]{1,0:T(8,128)(2,1)} %constant.133.clone.refs_20_) | copy-start | bytes 98308
  52.2 1.8 %copy-start.21 = (bf16[8,32]{1,0:T(8,128)(2,1)S(1)}, bf16[8,32]{1,0:T(8,128)(2,1)}, u32[]{:S(2)}) copy-start(bf16[8,32]{1,0:T(8,128)(2,1)} %constant.132.clone.refs_19_) | copy-start | bytes 1540
  52.2 1.8 %copy-start.11 = (bf16[256,128]{1,0:T(8,128)(2,1)S(1)}, bf16[256,128]{1,0:T(8,128)(2,1)}, u32[]{:S(2)}) copy-start(bf16[256,128]{1,0:T(8,128)(2,1)} %constant.126.clone.refs_12_) | copy-start | bytes 196612
  52.9 1.1 %copy-start.10 = (bf16[256,128]{1,0:T(8,128)(2,1)S(1)}, bf16[256,128]{1,0:T(8,128)(2,1)}, u32[]{:S(2)}) copy-start(bf16[256,128]{1,0:T(8,128)(2,1)} %constant.127.clone.refs_13_) | copy-start | bytes 196612
  54.0 1.1 %copy-start.3 = (f32[30,24,256]{2,1,0:T(8,128)S(1)}, f32[30,24,256]{2,1,0:T(8,128)}, u32[]{:S(2)}) copy-start(f32[30,24,256]{2,1,0:T(8,128)} %copy-done.2) | copy-start | bytes 2211844
  (12 other events, 10.2 us)

commit v4 on v3

--- a/solution.py
+++ b/solution.py
@@ -419,14 +419,14 @@
     return sheet_smooth(source - sheet_apply(estimate, face_set), face_set, estimate)[0]
 
 
-def weight(fine, coarse, xp=np):
+def weight(fine, coarse):
     own = fine >> 1
-    other = xp.where(fine % 2 == 0, own - 1, own + 1)
-    return xp.where(coarse == own, 0.75, 0.0) + xp.where(coarse == other, 0.25, 0.0)
-
-
-def table(shape, xp=np):
-    return xp.arange(shape[0])[:, None], xp.arange(shape[1])[None, :]
+    other = np.where(fine % 2 == 0, own - 1, own + 1)
+    return np.where(coarse == own, 0.75, 0.0) + np.where(coarse == other, 0.25, 0.0)
+
+
+def table(shape):
+    return np.arange(shape[0])[:, None], np.arange(shape[1])[None, :]
 
 
 def sheet_matrices(fine_shape, lanes):
@@ -465,16 +465,12 @@
     return [pair_rows_matrix(z_pairs, y_cells), right.astype(BF16)]
 
 
-def plane_up_matrices(planes, fine_y, coarse_y, fine_x, coarse_x, xp=np):
+def plane_up_matrices(planes, fine_y, coarse_y, fine_x, coarse_x):
     rows = fine_y.shape[0]
-    fine, coarse = table((planes * rows, planes * coarse_y), xp)
-    left = xp.where(
-        fine // rows == coarse // coarse_y,
-        weight(xp.tile(fine_y, planes)[:, None], coarse % coarse_y, xp),
-        0.0,
-    )
-    coarse = xp.arange(coarse_x)[:, None]
-    right = weight(fine_x[None, :], coarse, xp)
+    fine, coarse = table((planes * rows, planes * coarse_y))
+    near = weight(np.tile(fine_y, planes)[:, None], coarse % coarse_y)
+    left = np.where(fine // rows == coarse // coarse_y, near, 0.0)
+    right = weight(fine_x[None, :], np.arange(coarse_x)[:, None])
     return [left.astype(BF16), right.astype(BF16)]
 
 
@@ -502,14 +498,18 @@
     return lax.broadcasted_iota(jnp.int32, shape, len(shape) - 1)
 
 
-def pack_x_kernel(source, coef, side, x_a, x_b):
+def side_rows():
+    return pl.ds(pl.multiple_of(jnp.where(lax.axis_index("gy") == 0, 0, HALO_Y), HALO_Y), HALO_Y)
+
+
+def pack_x_kernel(source, coef, side_source, side_coef, x_a, x_b):
     planes, own_y, _ = source.shape
     x_even = lax.axis_index("gx") % 2 == 0
     lane = lanes_of((own_y + HALO_Y, 128))
-    for which, ref in enumerate((source, coef)):
+    for which, (ref, side) in enumerate(((source, side_source), (coef, side_coef))):
         right = left = jnp.zeros(lane.shape, F32)
         for plane in range(planes):
-            value = jnp.concatenate([ref[plane], side[which, plane]], axis=0)
+            value = jnp.concatenate([ref[plane], side[plane, side_rows()]], axis=0)
             slot = (lane >= 8 * plane) & (lane < 8 * plane + 8)
             right = jnp.where(slot, turned(value, 8 * plane + 8, 1), right)
             left = jnp.where(slot, turned(value, 8 * plane, 1), left)
@@ -529,19 +529,19 @@
     return right, left
 
 
-def pack_z_kernel(x_count, source, coef, side, x_a, x_b, z_a, z_b):
+def pack_z_kernel(x_count, source, coef, side_source, side_coef, x_a, x_b, z_a, z_b):
     planes, own_y, _ = source.shape
     z_even = lax.axis_index("gz") % 2 == 0
     lane = lanes_of((own_y + HALO_Y, 128))
     skip = 8 * (planes - HALO_Z)
-    for which, ref in enumerate((source, coef)):
+    for which, (ref, side) in enumerate(((source, side_source), (coef, side_coef))):
         right, left = x_halos(x_a, x_b, which, x_count)
         bottom = jnp.where(lane < 64, right, turned(left, 64, 1))
         top = jnp.where(lane < 64, turned(right, -skip, 1), turned(left, 64 - skip, 1))
         for target, is_top in ((z_a, z_even), (z_b, jnp.logical_not(z_even))):
             first = jnp.where(is_top, planes - HALO_Z, 0)
             target[which, :HALO_Z, :own_y] = ref[pl.ds(first, HALO_Z)]
-            target[which, :HALO_Z, own_y:] = side[which, pl.ds(first, HALO_Z)]
+            target[which, :HALO_Z, own_y:] = side[pl.ds(first, HALO_Z), side_rows()]
             target[which, HALO_Z] = jnp.where(is_top, top, bottom)
 
 
@@ -560,7 +560,7 @@
 
     for which, target in enumerate((source, coef)):
         target[pl.ds(HALO_Z, planes), :own_y, :128] = own[which][...]
-        target[pl.ds(HALO_Z, planes), own_y:, :128] = side[which]
+        target[pl.ds(HALO_Z, planes), own_y:, :128] = side[which][:, side_rows()]
         right, left = x_halos(x_a, x_b, which, x_count)
         for plane in range(planes):
             target[HALO_Z + plane, :, 128:] = edges(right, left, 8 * plane, 8 * plane)
@@ -577,16 +577,23 @@
 
 
 def first_kernel(counts, *refs):
-    own, side, got = refs[:2], refs[2], refs[3:7]
-    left, right_source, right_coef, message, source, estimate = refs[7:13]
-    faces = refs[13:18]
-    coef, residual, update, pair_source, pair_coef = refs[18:]
+    own, side, got = refs[:2], refs[2:4], refs[4:8]
+    left, right_source, right_coef, message = refs[8:12]
+    kept_out = refs[12:19]
+    source, estimate, *faces, coef, residual, update, pair_source, pair_coef, done = refs[19:]
     fill_window(own, side, got, source, coef, *counts)
     planes, rows, lanes = source.shape
     own_y = rows - HALO_Y
+    copies = [
+        pltpu.make_async_copy(value, target, done.at[index])
+        for index, (value, target) in enumerate(zip((source, estimate, *faces), kept_out))
+    ]
     plane_faces(coef, faces, 0, planes, link_mask(rows, lanes), None, source, update)
+    for copy in copies[:1] + copies[2:]:
+        copy.start()
     ranges = [(step + 2, planes - step - 2) for step in range(DEGREE - 1)]
     plane_steps(faces, ranges, source, residual, update, estimate, True)
+    copies[1].start()
     plane_residual(faces, HALO_Z, planes - HALO_Z, residual, update)
     for pair in range((planes - 2 * HALO_Z) // 2):
         low = HALO_Z + 2 * pair
@@ -596,17 +603,31 @@
     message[...] = times_right(times_left(left[...], pair_source[...]), right_source[...]) + times_right(
         times_left(left[...], pair_coef[...]), right_coef[...]
     )
-
-
-def second_kernel(counts, depth_matrices, *refs):
+    for copy in copies:
+        copy.wait()
+
+
+def second_kernel(counts, matrix_count, *refs):
     x_count, y_count, z_count = counts
-    gathered, other, source, estimate = refs[:4]
-    faces = refs[4:9]
-    up_left, up_right = refs[9:11]
-    mid_refs = refs[11:15]
-    sheet_refs = refs[15 : 15 + depth_matrices]
-    solution, residual_out = refs[15 + depth_matrices : 17 + depth_matrices]
-    scratch = refs[17 + depth_matrices :]
+    x_index, y_index, z_index = (lax.axis_index(axis) for axis in ("gx", "gy", "gz"))
+    halves, refs = (refs[:x_count], refs[x_count : 2 * x_count]), refs[2 * x_count :]
+    brought, refs = refs[: 7 + matrix_count], refs[7 + matrix_count :]
+    (solution, residual_out), scratch = refs[:2], refs[2:]
+    held, scratch, done = scratch[: 7 + matrix_count], scratch[7 + matrix_count : -1], scratch[-1]
+    copies = []
+    for index, (value, target) in enumerate(zip(brought, held)):
+        if index == 7:
+            value = value.at[y_index]
+        if index == 8:
+            value = value.at[x_index]
+        copies.append(pltpu.make_async_copy(value, target, done.at[index]))
+    for copy in copies[7:] + copies[:7]:
+        copy.start()
+    source, estimate = held[:2]
+    faces = held[2:7]
+    up_left, up_right = held[7:9]
+    mid_refs = held[9:13]
+    sheet_refs = held[13:]
     mid_source, mid_coef, mid_residual, mid_update, mid_estimate, mid_correction = scratch[:6]
     mid_faces = scratch[6:11]
     pairs, wide, residual, update, current = scratch[11:]
@@ -614,7 +635,6 @@
     planes, rows, lanes = source.shape
     own_y = rows - HALO_Y
     mid_z, mid_y, mid_x = z_count * 8, y_count * 8, x_count * 64
-    y_index, z_index = lax.axis_index("gy"), lax.axis_index("gz")
 
     zero = jnp.zeros((PAD, mid_y, mid_x), F32)
     for ref in (mid_coef, mid_update, mid_estimate, mid_faces[0]):
@@ -622,13 +642,17 @@
         ref[pl.ds(PAD + mid_z, PAD)] = zero
 
     low_half = lanes_of((64, 128)) < 64
-    for blocks, y_block in ((gathered, y_index), (other, 1 - y_index)):
+    x_even = x_index % 2 == 0
+    for blocks, y_block in zip(halves, (y_index, 1 - y_index)):
         y_rows = pl.ds(pl.multiple_of(y_block * 8, 8), 8)
         for x_pair in range(x_count // 2):
+            x_lanes = pl.ds(pl.multiple_of(((x_index // 2) ^ x_pair) * 128, 128), 128)
             for z_block in range(z_count):
-                even = blocks[2 * x_pair, z_block]
-                odd = blocks[2 * x_pair + 1, z_block]
-                where = (pl.ds(PAD + z_block * 8, 8), y_rows, pl.ds(x_pair * 128, 128))
+                mine = blocks[2 * x_pair][z_block]
+                partner = blocks[2 * x_pair + 1][z_block]
+                even = jnp.where(x_even, mine, partner)
+                odd = jnp.where(x_even, partner, mine)
+                where = (pl.ds(PAD + (z_index ^ z_block) * 8, 8), y_rows, x_lanes)
                 mid_source[where] = jnp.where(low_half, even, turned(odd, 64, 1)).reshape(8, 8, 128)
                 mid_coef[where] = jnp.where(low_half, turned(even, 64, 1), odd).reshape(8, 8, 128)
 
@@ -642,6 +666,8 @@
     plane_steps(mid_faces, ranges, mid_source, mid_residual, mid_update, mid_estimate, True)
     plane_residual(mid_faces, start, stop, mid_residual, mid_update)
 
+    for copy in copies[7:]:
+        copy.wait()
     left_down, right_down, mid_left_up, mid_right_up = mid_refs
     sheets = []
     for ref, scale in ((mid_residual, 4.0), (mid_coef, 1.0)):
@@ -650,7 +676,7 @@
             pairs[pl.ds(pair * mid_y, mid_y)] = ref[low] + ref[low + 1]
         sheets.append(scale * times_right(times_left(left_down[...], pairs[...]), right_down[...]))
     shape = (mid_z // 2, mid_y // 2, mid_x // 2)
-    matrices = [sheet_refs[4 * index : 4 * index + 4] for index in range(depth_matrices // 4)]
+    matrices = [sheet_refs[index : index + 4] for index in range(0, len(sheet_refs), 4)]
     correction = sheet_cycle(sheets[0], sheets[1], shape, 2, matrices)
 
     raised = times_left(mid_left_up[...], times_right(correction, mid_right_up[...]))
@@ -677,6 +703,8 @@
         mid_faces, [clipped(4), clipped(4)], mid_source, mid_residual, mid_update, mid_estimate, False
     )
 
+    for copy in copies[:7]:
+        copy.wait()
     coarse_planes = up_left.shape[1] // mid_y
     near = mid_estimate[pl.ds(z_index * 8, coarse_planes)].reshape(coarse_planes * mid_y, mid_x)
     raised = times_left(up_left[...], times_right(near, up_right[...]))
@@ -709,23 +737,23 @@
     planes, rows, lanes = own_z + 2 * HALO_Z, own_y + HALO_Y, 2 * own_x
     vmem = pl.BlockSpec(memory_space=pltpu.VMEM)
 
-    def call(kernel, name, room, arguments, shapes, scratch):
+    def call(kernel, name, room, arguments, shapes, scratch, far_arguments=(), far_shapes=(), copies=0):
+        far = pl.BlockSpec(memory_space=pltpu.HBM)
         return pl.pallas_call(
             kernel,
-            out_shape=tuple(jax.ShapeDtypeStruct(shape, F32) for shape in shapes),
-            in_specs=[vmem] * len(arguments),
-            out_specs=(vmem,) * len(shapes),
-            scratch_shapes=[pltpu.VMEM(shape, F32) for shape in scratch],
+            out_shape=tuple(jax.ShapeDtypeStruct(shape, F32) for shape in (*shapes, *far_shapes)),
+            in_specs=[vmem] * len(arguments) + [far] * len(far_arguments),
+            out_specs=(vmem,) * len(shapes) + (far,) * len(far_shapes),
+            scratch_shapes=[pltpu.VMEM(item, F32) if isinstance(item, tuple) else item for item in scratch]
+            + ([pltpu.SemaphoreType.DMA((copies,))] if copies else []),
             compiler_params=pltpu.CompilerParams(vmem_limit_bytes=room * 1024 * 1024),
             name=name,
-        )(*arguments)
-
-    y_index = lax.axis_index("gy")
-    both = jnp.stack([right_side, coefficient])
-    side = jnp.where(y_index == 0, both[:, :, own_y - HALO_Y :], both[:, :, :HALO_Y])
-    side = swapped(side, "gy", [swap_pairs(y_count, False)])
+        )(*arguments, *far_arguments)
+
+    core_pairs = swap_pairs(y_count, False)
+    blocks = (right_side, coefficient)
+    blocks += tuple(swapped(value, "gy", [core_pairs]) for value in blocks)
     swaps = [[swap_pairs(count, odd) for odd in (False, True)] for count in (x_count, z_count)]
-    blocks = (right_side, coefficient, side)
     sent = call(pack_x_kernel, "pack_x", 4, blocks, [(2, rows, 128)] * 2, [])
     got = [swapped(value, "gx", [pairs]) for value, pairs in zip(sent, swaps[0])]
     sent = call(
@@ -735,28 +763,34 @@
 
     window, padded = (planes, rows, lanes), (planes + 1, rows, lanes)
     down = own_down_matrices(own_z // 2, own_y, own_x)
-    message, *kept = call(
+    message, *windows = call(
         functools.partial(first_kernel, (x_count, z_count)),
         "first",
-        8,
+        12,
         (*blocks, *got, *down),
-        [(own_z * own_y // 4, own_x)] + [window] * 2 + [window] * 5,
-        [padded, window, padded] + [(own_z * own_y // 2, own_x)] * 2,
-    )
-
-    def to_all(value, axis, count):
-        return lax.all_to_all(jnp.broadcast_to(value, (count,) + value.shape), axis, 0, 0)
-
-    gathered = to_all(to_all(message, "gz", z_count), "gx", x_count)
-    other = swapped(gathered, "gy", [swap_pairs(y_count, False)])
+        [(own_z * own_y // 4, own_x)],
+        [window] * 7 + [padded, window, padded] + [(own_z * own_y // 2, own_x)] * 2,
+        far_shapes=[window] * 7,
+        copies=7,
+    )
+
+    def from_others(value, axis, count):
+        return [
+            swapped(value, axis, [[index ^ distance for index in range(count)]]) for distance in range(1, count)
+        ]
+
+    mine = jnp.stack([message] + from_others(message, "gz", z_count))
+    parts = [mine] + from_others(mine, "gx", x_count)
+    parts += [swapped(part, "gy", [core_pairs]) for part in parts]
 
     mid = (own_z * z_count // 2, own_y * y_count // 2, own_x * x_count // 2)
-    row = jnp.arange(rows)
-    fine_y = jnp.where(row < own_y, y_index * own_y + row, jnp.where(y_index == 0, row, row - HALO_Y))
-    lane = jnp.arange(lanes)
-    fine_x = lax.axis_index("gx") * own_x + jnp.where(lane < lanes - HALO_X, lane, lane - lanes)
+    row, lane = np.arange(rows), np.arange(lanes)
+    fine_x = np.where(lane < lanes - HALO_X, lane, lane - lanes)
     coarse_planes = own_z // 2 + 2 * PAD
-    up = plane_up_matrices(coarse_planes, fine_y, mid[1], fine_x, mid[2], jnp)
+    fine_y = [row, np.where(row < own_y, own_y + row, row - HALO_Y)]
+    ups = [plane_up_matrices(coarse_planes, cells, mid[1], fine_x, mid[2])[0] for cells in fine_y]
+    rights = [plane_up_matrices(1, row, mid[1], index * own_x + fine_x, mid[2])[1] for index in range(x_count)]
+    up = [np.stack(ups), np.stack(rights)]
     mid_down = one_down_matrices(mid[0] // 2, mid[1], mid[2])
     mid_up = plane_up_matrices(
         mid[0] // 2, np.arange(mid[1]), mid[1] // 2, np.arange(mid[2]), mid[2] // 2
@@ -767,16 +801,22 @@
         sheets += sheet_matrices(shape, 128)
         shape = tuple(count // 2 for count in shape)
     mid_padded = (mid[0] + 2 * PAD, mid[1], mid[2])
+    matrices = [*up, *mid_down, *mid_up, *sheets]
+    held = [pltpu.VMEM(item.shape[1 if item.ndim == 3 else 0 :], BF16) for item in matrices]
     solution, residual = call(
-        functools.partial(second_kernel, counts, len(sheets)),
+        functools.partial(second_kernel, counts, len(matrices)),
         "second",
-        20,
-        (gathered, other, *kept, *up, *mid_down, *mid_up, *sheets),
+        28,
+        parts,
         [(own_z, own_y, own_x)] * 2,
-        [mid_padded] * 5
+        [window] * 7
+        + held
+        + [mid_padded] * 5
         + [(mid[0] // 2 + 2, mid[1], mid[2])]
         + [mid_padded] * 5
         + [(mid[0] // 2 * mid[1], mid[2]), (coarse_planes, rows, lanes), window, padded, padded],
+        far_arguments=(*windows, *(jnp.asarray(item) for item in matrices)),
+        copies=7 + len(matrices),
     )
     return solution[None], residual[None]
 

time: 76 us -> 68.8 us (0.905)
  local copies, waits for them, and re-layouts: 9.7 us -> 1.9 us
  Pallas kernels: 23.5 us -> 29.5 us
  other arithmetic: 3.04 us -> 0.01 us
  waiting for transfers between devices: 16.4 us -> 14.7 us
    all_to_all x2 -> x0, starting transfers between devices: 14.7 us -> none  [to_all(): lax.all_to_all(jnp.broadcast_to(value, (count,) + value.shape), axis, 0, 0)]
    ppermute x6 -> x16, starting transfers between devices: 7.05 us -> 21.5 us  [swapped(): return lax.ppermute(value, axes, list(enumerate(places)))]
    all_to_all x2 -> x0, waiting for transfers between devices: 10.2 us -> none  [to_all(): lax.all_to_all(jnp.broadcast_to(value, (count,) + value.shape), axis, 0, 0)]
    ppermute x6 -> x16, waiting for transfers between devices: 6.23 us -> 14.7 us  [swapped(): return lax.ppermute(value, axes, list(enumerate(places)))]
    pallas_call x4, Pallas kernels: 23.5 us -> 29.5 us  [call(): pl.pallas_call(kernel, out_shape=tuple((jax.ShapeDtypeStruct(shape, F32)...]
    unnamed x56 -> x40, local copies, waits for them, and re-layouts: 7.51 us -> 1.9 us
    select_n x5 -> x0, other arithmetic: 2.2 us -> none  [the longest x1 0.99 us: near_local(): jnp.where(y_index == 0, both[:, :, own_y - HALO_Y:], both[:, :, :HALO_Y])]
    broadcast_in_dim x2 -> x0, local copies, waits for them, and re-layouts: 1.51 us -> none  [to_all(): jnp.broadcast_to(value, (count,) + value.shape)]
  transfers between devices with their start and end apart: 8 -> 16, of which waited for: 6 -> 9; matrix products, arithmetic and copies ran while one was open for 4% -> 0% of each run, Pallas kernels for 0% -> 0%
where the time goes in v4:
time: 68.8 us; the launch traced here: 68.6 us
  Pallas kernels  29.5 us (43%)
  starting transfers between devices  21.5 us (31%)
  waiting for transfers between devices  14.7 us (21%)
  local copies, waits for them, and re-layouts  1.9 us (3%)
  between operations  0.89 us (1%)
    pallas_call x4, Pallas kernels, call(): pl.pallas_call(kernel, out_shape=tuple((jax.ShapeDtypeStruct(shape, F32)...  29.5 us
    ppermute x16, starting transfers between devices, swapped(): return lax.ppermute(value, axes, list(enumerate(places)))  21.5 us
    ppermute x16, waiting for transfers between devices, swapped(): return lax.ppermute(value, axes, list(enumerate(places)))  14.7 us
    unnamed x40, local copies, waits for them, and re-layouts  1.9 us
  transfers between devices with their start and end apart: 16, of which 9 were waited for; matrix products, arithmetic and copies ran while one was open for 0% of the time, Pallas kernels for 0%

profile of v4, /device:TPU:0, one launch (start us, length us, event | category | flops | bytes accessed | tf_op | source)
XLA Modules:
  0.0 68.6 jit_solution(2629745155588516508)
XLA Ops:
  0.6 0.5 collective-permute-start
  1.2 1.1 %collective-permute-done.side_source.refs_2_ = f32[16,16,128]{2,1,0:T(8,128)S(1)} collective-permute-done((f32[16,16,128]{2,1,0:T(8,128)}, f32[16,16,128]{2,1,0:T(8,128)S(1)}, u32[]{:S(2)}, u32[]{:S(2)}) %collective-permute-start) | collective-permute-done | bytes 131104 | tf_op jit(solution)/shard_map/ppermute | solution.py:488
  2.3 0.4 collective-permute-done.1.side_coef.refs_3_
  2.7 0.9 %copy-done = f32[1,16,16,128]{3,2,1,0:T(8,128)S(1)} copy-done((f32[1,16,16,128]{3,2,1,0:T(8,128)S(1)}, f32[1,16,16,128]{3,2,1,0:T(8,128)}, u32[]{:S(2)}) %copy-start) | copy-done | bytes 131096
  3.6 0.9 %copy-done.2 = f32[16,16,128]{2,1,0:T(8,128)S(1)} copy-done((f32[16,16,128]{2,1,0:T(8,128)S(1)}, f32[16,16,128]{2,1,0:T(8,128)}, u32[]{:S(2)}) %copy-start.2) | copy-done | bytes 131096
  4.8 2.7 %collective-permute-start.2 = (f32[2,24,128]{2,1,0:T(8,128)S(1)}, f32[2,24,128]{2,1,0:T(8,128)S(1)}, u32[]{:S(2)}, u32[]{:S(2)}) collective-permute-start(f32[2,24,128]{2,1,0:T(8,128)S(1)} %get-tuple-element.16), channel_id=1, source_target_pairs={{0,8},{8,0},{16,24},{24,16},{1,9},{9,1},{17,25},{25,17},{2,10},{10... | collective-permute-start | bytes 73736 | tf_op jit(solution)/shard_map/ppermute | solution.py:488
  7.5 0.8 %collective-permute-start.3 = (f32[2,24,128]{2,1,0:T(8,128)S(1)}, f32[2,24,128]{2,1,0:T(8,128)S(1)}, u32[]{:S(2)}, u32[]{:S(2)}) collective-permute-start(f32[2,24,128]{2,1,0:T(8,128)S(1)} %get-tuple-element.17), channel_id=1, source_target_pairs={{0,0},{8,16},{16,8},{24,24},{1,1},{9,17},{17,9},{25,25},{2,2},{10,... | collective-permute-start | bytes 73736 | tf_op jit(solution)/shard_map/ppermute | solution.py:488
  8.3 1.0 %collective-permute-done.2.x_a.refs_4_ = f32[2,24,128]{2,1,0:T(8,128)S(1)} collective-permute-done((f32[2,24,128]{2,1,0:T(8,128)S(1)}, f32[2,24,128]{2,1,0:T(8,128)S(1)}, u32[]{:S(2)}, u32[]{:S(2)}) %collective-permute-start.2) | collective-permute-done | bytes 24608 | tf_op jit(solution)/shard_map/ppermute | solution.py:488
  9.4 2.2 %collective-permute-start.4 = (f32[2,8,24,128]{3,2,1,0:T(8,128)S(1)}, f32[2,8,24,128]{3,2,1,0:T(8,128)S(1)}, u32[]{:S(2)}, u32[]{:S(2)}) collective-permute-start(f32[2,8,24,128]{3,2,1,0:T(8,128)S(1)} %get-tuple-element.18), channel_id=1, source_target_pairs={{0,1},{1,0},{2,3},{3,2},{4,5},{5,4},{6,7},{7,6},{8,9},{9,8},{10,11... | collective-permute-start | bytes 589832 | tf_op jit(solution)/shard_map/ppermute | solution.py:488
  11.6 0.8 %collective-permute-start.5 = (f32[2,8,24,128]{3,2,1,0:T(8,128)S(1)}, f32[2,8,24,128]{3,2,1,0:T(8,128)S(1)}, u32[]{:S(2)}, u32[]{:S(2)}) collective-permute-start(f32[2,8,24,128]{3,2,1,0:T(8,128)S(1)} %get-tuple-element.19), channel_id=1, source_target_pairs={{0,0},{1,2},{2,1},{3,3},{4,4},{5,6},{6,5},{7,7},{8,8},{9,10},{10,9... | collective-permute-start | bytes 589832 | tf_op jit(solution)/shard_map/ppermute | solution.py:488
  12.4 3.4 %collective-permute-done.4.refs_6_ = f32[2,8,24,128]{3,2,1,0:T(8,128)S(1)} collective-permute-done((f32[2,8,24,128]{3,2,1,0:T(8,128)S(1)}, f32[2,8,24,128]{3,2,1,0:T(8,128)S(1)}, u32[]{:S(2)}, u32[]{:S(2)}) %collective-permute-start.4) | collective-permute-done | bytes 196640 | tf_op jit(solution)/shard_map/ppermute | solution.py:488
  16.0 8.2 %first.1 = (f32[64,128]{1,0:T(8,128)S(1)}, f32[30,24,256]{2,1,0:T(8,128)S(1)}, f32[30,24,256]{2,1,0:T(8,128)S(1)}, f32[30,24,256]{2,1,0:T(8,128)S(1)}, f32[30,24...) custom-call(f32[16,16,128]{2,1,0:T(8,128)S(1)} %bitcast.10, ...), custom_call_target="tpu_custom_call" | custom-call | tf_op jit(solution)/shard_map/first/pallas_call | solution.py:742
  24.1 3.8 %collective-permute-start.8 = (f32[64,128]{1,0:T(8,128)S(1)}, f32[64,128]{1,0:T(8,128)S(1)}, u32[]{:S(2)}, u32[]{:S(2)}) collective-permute-start(f32[64,128]{1,0:T(8,128)S(1)} %get-tuple-element.20), channel_id=1, source_target_pairs={{0,3},{1,2},{2,1},{3,0},{4,7},{5,6},{6,5},{7,4},{8,11},{9,10},{10,... | collective-permute-start | bytes 98312 | tf_op jit(solution)/shard_map/ppermute | solution.py:488
  28.0 2.6 %collective-permute-start.7 = (f32[64,128]{1,0:T(8,128)S(1)}, f32[64,128]{1,0:T(8,128)S(1)}, u32[]{:S(2)}, u32[]{:S(2)}) collective-permute-start(f32[64,128]{1,0:T(8,128)S(1)} %get-tuple-element.20), channel_id=1, source_target_pairs={{0,2},{1,3},{2,0},{3,1},{4,6},{5,7},{6,4},{7,5},{8,10},{9,11},{10,... | collective-permute-start | bytes 98312 | tf_op jit(solution)/shard_map/ppermute | solution.py:488
  30.8 2.0 %collective-permute-done.7 = f32[64,128]{1,0:T(8,128)S(1)} collective-permute-done((f32[64,128]{1,0:T(8,128)S(1)}, f32[64,128]{1,0:T(8,128)S(1)}, u32[]{:S(2)}, u32[]{:S(2)}) %collective-permute-start.7) | collective-permute-done | bytes 32800 | tf_op jit(solution)/shard_map/ppermute | solution.py:488
  32.8 1.7 %collective-permute-done.6 = f32[64,128]{1,0:T(8,128)S(1)} collective-permute-done((f32[64,128]{1,0:T(8,128)S(1)}, f32[64,128]{1,0:T(8,128)S(1)}, u32[]{:S(2)}, u32[]{:S(2)}) %collective-permute-start.6) | collective-permute-done | bytes 32800 | tf_op jit(solution)/shard_map/ppermute | solution.py:488
  34.5 2.5 %collective-permute-start.11 = (f32[4,64,128]{2,1,0:T(8,128)S(1)}, f32[4,64,128]{2,1,0:T(8,128)S(1)}, u32[]{:S(2)}, u32[]{:S(2)}) collective-permute-start(f32[4,64,128]{2,1,0:T(8,128)S(1)} %pad_maximum_fusion.refs_0_), channel_id=1, source_target_pairs={{0,24},{8,16},{16,8},{24,0},{1,25},{9,17},{17,9},{25,1},{2,26},{10... | collective-permute-start | bytes 393224 | tf_op jit(solution)/shard_map/ppermute | solution.py:488
  37.0 3.7 %collective-permute-start.10 = (f32[4,64,128]{2,1,0:T(8,128)S(1)}, f32[4,64,128]{2,1,0:T(8,128)S(1)}, u32[]{:S(2)}, u32[]{:S(2)}) collective-permute-start(f32[4,64,128]{2,1,0:T(8,128)S(1)} %pad_maximum_fusion.refs_0_), channel_id=1, source_target_pairs={{0,16},{8,24},{16,0},{24,8},{1,17},{9,25},{17,1},{25,9},{2,18},{10... | collective-permute-start | bytes 393224 | tf_op jit(solution)/shard_map/ppermute | solution.py:488
  40.8 1.0 %collective-permute-start.9 = (f32[4,64,128]{2,1,0:T(8,128)S(1)}, f32[4,64,128]{2,1,0:T(8,128)S(1)}, u32[]{:S(2)}, u32[]{:S(2)}) collective-permute-start(f32[4,64,128]{2,1,0:T(8,128)S(1)} %pad_maximum_fusion.refs_0_), channel_id=1, source_target_pairs={{0,8},{8,0},{16,24},{24,16},{1,9},{9,1},{17,25},{25,17},{2,10},{10... | collective-permute-start | bytes 393224 | tf_op jit(solution)/shard_map/ppermute | solution.py:488
  41.8 0.5 collective-permute-start.15
  42.3 2.4 %collective-permute-done.10.refs_2_ = f32[4,64,128]{2,1,0:T(8,128)S(1)} collective-permute-done((f32[4,64,128]{2,1,0:T(8,128)S(1)}, f32[4,64,128]{2,1,0:T(8,128)S(1)}, u32[]{:S(2)}, u32[]{:S(2)}) %collective-permute-start.10) | collective-permute-done | bytes 131104 | tf_op jit(solution)/shard_map/ppermute | solution.py:488
  44.7 1.5 %collective-permute-done.9.refs_1_ = f32[4,64,128]{2,1,0:T(8,128)S(1)} collective-permute-done((f32[4,64,128]{2,1,0:T(8,128)S(1)}, f32[4,64,128]{2,1,0:T(8,128)S(1)}, u32[]{:S(2)}, u32[]{:S(2)}) %collective-permute-start.9) | collective-permute-done | bytes 131104 | tf_op jit(solution)/shard_map/ppermute | solution.py:488
  46.2 1.3 %collective-permute-done.13.refs_5_ = f32[4,64,128]{2,1,0:T(8,128)S(1)} collective-permute-done((f32[4,64,128]{2,1,0:T(8,128)S(1)}, f32[4,64,128]{2,1,0:T(8,128)S(1)}, u32[]{:S(2)}, u32[]{:S(2)}) %collective-permute-start.13) | collective-permute-done | bytes 131104 | tf_op jit(solution)/shard_map/ppermute | solution.py:488
  47.6 21.0 %second.1 = (f32[16,16,128]{2,1,0:T(8,128)}, f32[16,16,128]{2,1,0:T(8,128)}) custom-call(f32[4,64,128]{2,1,0:T(8,128)S(1)} %pad_maximum_fusion.refs_0_, f32[4,64,128]{2,1,0:T(8,128)S(1)} %collective-permute-done.9.refs_1_, f32[4,64,128]{2,1,0:T(8,128)S(1)} %collective-permute-done.10.refs_2_, f32[4,64,128]{2,1,0:T(8,128)S(1)} %collective-permute-done.11.refs_3_, ...), custom_call_target="tpu_custom_call" | custom-call | tf_op jit(solution)/shard_map/second/pallas_call | solution.py:742
  (53 shorter events, 0.8 us)
Async XLA Ops:
  0.6 1.7 %collective-permute-start = (f32[16,16,128]{2,1,0:T(8,128)}, f32[16,16,128]{2,1,0:T(8,128)S(1)}, u32[]{:S(2)}, u32[]{:S(2)}) collective-permute-start(f32[16,16,128]{2,1,0:T(8,128)} %bitcast.7), channel_id=1, source_target_pairs={{0,4},{4,0},{1,5},{5,1},{2,6},{6,2},{3,7},{7,3},{8,12},{12,8},{9,1... | collective-permute-start | bytes 393224 | tf_op jit(solution)/shard_map/ppermute | solution.py:488
  1.1 1.6 %collective-permute-start.1 = (f32[16,16,128]{2,1,0:T(8,128)}, f32[16,16,128]{2,1,0:T(8,128)S(1)}, u32[]{:S(2)}, u32[]{:S(2)}) collective-permute-start(f32[16,16,128]{2,1,0:T(8,128)} %refs_1_.1), channel_id=1, source_target_pairs={{0,4},{4,0},{1,5},{5,1},{2,6},{6,2},{3,7},{7,3},{8,12},{12,8},{9,1... | collective-permute-start | bytes 393224 | tf_op jit(solution)/shard_map/ppermute | solution.py:488
  4.8 4.5 %collective-permute-start.2 = (f32[2,24,128]{2,1,0:T(8,128)S(1)}, f32[2,24,128]{2,1,0:T(8,128)S(1)}, u32[]{:S(2)}, u32[]{:S(2)}) collective-permute-start(f32[2,24,128]{2,1,0:T(8,128)S(1)} %get-tuple-element.16), channel_id=1, source_target_pairs={{0,8},{8,0},{16,24},{24,16},{1,9},{9,1},{17,25},{25,17},{2,10},{10... | collective-permute-start | bytes 73736 | tf_op jit(solution)/shard_map/ppermute | solution.py:488
  7.5 1.8 %collective-permute-start.3 = (f32[2,24,128]{2,1,0:T(8,128)S(1)}, f32[2,24,128]{2,1,0:T(8,128)S(1)}, u32[]{:S(2)}, u32[]{:S(2)}) collective-permute-start(f32[2,24,128]{2,1,0:T(8,128)S(1)} %get-tuple-element.17), channel_id=1, source_target_pairs={{0,0},{8,16},{16,8},{24,24},{1,1},{9,17},{17,9},{25,25},{2,2},{10,... | collective-permute-start | bytes 73736 | tf_op jit(solution)/shard_map/ppermute | solution.py:488
  9.4 6.4 %collective-permute-start.4 = (f32[2,8,24,128]{3,2,1,0:T(8,128)S(1)}, f32[2,8,24,128]{3,2,1,0:T(8,128)S(1)}, u32[]{:S(2)}, u32[]{:S(2)}) collective-permute-start(f32[2,8,24,128]{3,2,1,0:T(8,128)S(1)} %get-tuple-element.18), channel_id=1, source_target_pairs={{0,1},{1,0},{2,3},{3,2},{4,5},{5,4},{6,7},{7,6},{8,9},{9,8},{10,11... | collective-permute-start | bytes 589832 | tf_op jit(solution)/shard_map/ppermute | solution.py:488
  11.6 35.9 %copy-start.4 = (bf16[4,256,256]{2,1,0:T(8,128)(2,1)S(1)}, bf16[4,256,256]{2,1,0:T(8,128)(2,1)}, u32[]{:S(2)}) copy-start(bf16[4,256,256]{2,1,0:T(8,128)(2,1)} %constant.36.clone.refs_16_) | copy-start | bytes 1572868
  11.6 4.2 %collective-permute-start.5 = (f32[2,8,24,128]{3,2,1,0:T(8,128)S(1)}, f32[2,8,24,128]{3,2,1,0:T(8,128)S(1)}, u32[]{:S(2)}, u32[]{:S(2)}) collective-permute-start(f32[2,8,24,128]{3,2,1,0:T(8,128)S(1)} %get-tuple-element.19), channel_id=1, source_target_pairs={{0,0},{1,2},{2,1},{3,3},{4,4},{5,6},{6,5},{7,7},{8,8},{9,10},{10,9... | collective-permute-start | bytes 589832 | tf_op jit(solution)/shard_map/ppermute | solution.py:488
  15.9 31.6 %copy-start.5 = (bf16[2,336,224]{2,1,0:T(8,128)(2,1)S(1)}, bf16[2,336,224]{2,1,0:T(8,128)(2,1)}, u32[]{:S(2)}) copy-start(bf16[2,336,224]{2,1,0:T(8,128)(2,1)} %constant.35.clone.refs_15_) | copy-start | bytes 903172
  15.9 31.6 %copy-start.11 = (bf16[128,128]{1,0:T(8,128)(2,1)S(1)}, bf16[128,128]{1,0:T(8,128)(2,1)}, u32[]{:S(2)}) copy-start(bf16[128,128]{1,0:T(8,128)(2,1)} %constant.47.clone.refs_28_) | copy-start | bytes 98308
  15.9 31.6 %copy-start.12 = (bf16[128,128]{1,0:T(8,128)(2,1)S(1)}, bf16[128,128]{1,0:T(8,128)(2,1)}, u32[]{:S(2)}) copy-start(bf16[128,128]{1,0:T(8,128)(2,1)} %constant.45.clone.refs_26_) | copy-start | bytes 98308
  15.9 31.6 %copy-start.13 = (bf16[128,128]{1,0:T(8,128)(2,1)S(1)}, bf16[128,128]{1,0:T(8,128)(2,1)}, u32[]{:S(2)}) copy-start(bf16[128,128]{1,0:T(8,128)(2,1)} %constant.43.clone.refs_24_) | copy-start | bytes 98308
  15.9 31.6 %copy-start.14 = (bf16[128,32]{1,0:T(8,128)(2,1)S(1)}, bf16[128,32]{1,0:T(8,128)(2,1)}, u32[]{:S(2)}) copy-start(bf16[128,32]{1,0:T(8,128)(2,1)} %constant.42.clone.refs_23_) | copy-start | bytes 24580
  15.9 31.6 %copy-start.19 = (bf16[8,32]{1,0:T(8,128)(2,1)S(1)}, bf16[8,32]{1,0:T(8,128)(2,1)}, u32[]{:S(2)}) copy-start(bf16[8,32]{1,0:T(8,128)(2,1)} %constant.44.clone.refs_25_) | copy-start | bytes 1540
  24.1 6.7 %collective-permute-start.8 = (f32[64,128]{1,0:T(8,128)S(1)}, f32[64,128]{1,0:T(8,128)S(1)}, u32[]{:S(2)}, u32[]{:S(2)}) collective-permute-start(f32[64,128]{1,0:T(8,128)S(1)} %get-tuple-element.20), channel_id=1, source_target_pairs={{0,3},{1,2},{2,1},{3,0},{4,7},{5,6},{6,5},{7,4},{8,11},{9,10},{10,... | collective-permute-start | bytes 98312 | tf_op jit(solution)/shard_map/ppermute | solution.py:488
  28.0 4.8 %collective-permute-start.7 = (f32[64,128]{1,0:T(8,128)S(1)}, f32[64,128]{1,0:T(8,128)S(1)}, u32[]{:S(2)}, u32[]{:S(2)}) collective-permute-start(f32[64,128]{1,0:T(8,128)S(1)} %get-tuple-element.20), channel_id=1, source_target_pairs={{0,2},{1,3},{2,0},{3,1},{4,6},{5,7},{6,4},{7,5},{8,10},{9,11},{10,... | collective-permute-start | bytes 98312 | tf_op jit(solution)/shard_map/ppermute | solution.py:488
  30.5 3.9 %collective-permute-start.6 = (f32[64,128]{1,0:T(8,128)S(1)}, f32[64,128]{1,0:T(8,128)S(1)}, u32[]{:S(2)}, u32[]{:S(2)}) collective-permute-start(f32[64,128]{1,0:T(8,128)S(1)} %get-tuple-element.20), channel_id=1, source_target_pairs={{0,1},{1,0},{2,3},{3,2},{4,5},{5,4},{6,7},{7,6},{8,9},{9,8},{10,11... | collective-permute-start | bytes 98312 | tf_op jit(solution)/shard_map/ppermute | solution.py:488
  34.5 13.1 %copy-start.10 = (bf16[128,256]{1,0:T(8,128)(2,1)S(1)}, bf16[128,256]{1,0:T(8,128)(2,1)}, u32[]{:S(2)}) copy-start(bf16[128,256]{1,0:T(8,128)(2,1)} %constant.37.clone.refs_17_) | copy-start | bytes 196612
  34.5 7.2 %collective-permute-start.11 = (f32[4,64,128]{2,1,0:T(8,128)S(1)}, f32[4,64,128]{2,1,0:T(8,128)S(1)}, u32[]{:S(2)}, u32[]{:S(2)}) collective-permute-start(f32[4,64,128]{2,1,0:T(8,128)S(1)} %pad_maximum_fusion.refs_0_), channel_id=1, source_target_pairs={{0,24},{8,16},{16,8},{24,0},{1,25},{9,17},{17,9},{25,1},{2,26},{10... | collective-permute-start | bytes 393224 | tf_op jit(solution)/shard_map/ppermute | solution.py:488
  37.0 7.6 %collective-permute-start.10 = (f32[4,64,128]{2,1,0:T(8,128)S(1)}, f32[4,64,128]{2,1,0:T(8,128)S(1)}, u32[]{:S(2)}, u32[]{:S(2)}) collective-permute-start(f32[4,64,128]{2,1,0:T(8,128)S(1)} %pad_maximum_fusion.refs_0_), channel_id=1, source_target_pairs={{0,16},{8,24},{16,0},{24,8},{1,17},{9,25},{17,1},{25,9},{2,18},{10... | collective-permute-start | bytes 393224 | tf_op jit(solution)/shard_map/ppermute | solution.py:488
  40.8 5.4 %collective-permute-start.9 = (f32[4,64,128]{2,1,0:T(8,128)S(1)}, f32[4,64,128]{2,1,0:T(8,128)S(1)}, u32[]{:S(2)}, u32[]{:S(2)}) collective-permute-start(f32[4,64,128]{2,1,0:T(8,128)S(1)} %pad_maximum_fusion.refs_0_), channel_id=1, source_target_pairs={{0,8},{8,0},{16,24},{24,16},{1,9},{9,1},{17,25},{25,17},{2,10},{10... | collective-permute-start | bytes 393224 | tf_op jit(solution)/shard_map/ppermute | solution.py:488
  41.8 4.4 %collective-permute-start.12 = (f32[4,64,128]{2,1,0:T(8,128)S(1)}, f32[4,64,128]{2,1,0:T(8,128)S(1)}, u32[]{:S(2)}, u32[]{:S(2)}) collective-permute-start(f32[4,64,128]{2,1,0:T(8,128)S(1)} %pad_maximum_fusion.refs_0_), channel_id=1, source_target_pairs={{0,4},{4,0},{1,5},{5,1},{2,6},{6,2},{3,7},{7,3},{8,12},{12,8},{9,1... | collective-permute-start | bytes 393224 | tf_op jit(solution)/shard_map/ppermute | solution.py:488
  41.8 4.4 %collective-permute-start.15 = (f32[4,64,128]{2,1,0:T(8,128)S(1)}, f32[4,64,128]{2,1,0:T(8,128)S(1)}, u32[]{:S(2)}, u32[]{:S(2)}) collective-permute-start(f32[4,64,128]{2,1,0:T(8,128)S(1)} %collective-permute-done.11.refs_3_), channel_id=1, source_target_pairs={{0,4},{4,0},{1,5},{5,1},{2,6},{6,2},{3,7},{7,3},{8,12},{12,8},{9,1... | collective-permute-start | bytes 393224 | tf_op jit(solution)/shard_map/ppermute | solution.py:488
  44.7 1.5 %collective-permute-start.14 = (f32[4,64,128]{2,1,0:T(8,128)S(1)}, f32[4,64,128]{2,1,0:T(8,128)S(1)}, u32[]{:S(2)}, u32[]{:S(2)}) collective-permute-start(f32[4,64,128]{2,1,0:T(8,128)S(1)} %collective-permute-done.10.refs_2_), channel_id=1, source_target_pairs={{0,4},{4,0},{1,5},{5,1},{2,6},{6,2},{3,7},{7,3},{8,12},{12,8},{9,1... | collective-permute-start | bytes 393224 | tf_op jit(solution)/shard_map/ppermute | solution.py:488
  46.1 1.3 %collective-permute-start.13 = (f32[4,64,128]{2,1,0:T(8,128)S(1)}, f32[4,64,128]{2,1,0:T(8,128)S(1)}, u32[]{:S(2)}, u32[]{:S(2)}) collective-permute-start(f32[4,64,128]{2,1,0:T(8,128)S(1)} %collective-permute-done.9.refs_1_), channel_id=1, source_target_pairs={{0,4},{4,0},{1,5},{5,1},{2,6},{6,2},{3,7},{7,3},{8,12},{12,8},{9,1... | collective-permute-start | bytes 393224 | tf_op jit(solution)/shard_map/ppermute | solution.py:488
  (12 other events, 108.9 us)

commit v5 on v4

--- a/solution.py
+++ b/solution.py
@@ -207,7 +207,7 @@
     return (solution, residual)
 
 
-HALO_Z = 7
+HALO_Z = 8
 HALO_Y = 8
 HALO_X = 8
 PAD = 3
@@ -258,7 +258,7 @@
     lax.fori_loop(0, (stop - start) // block, step, carry)
 
 
-def plane_faces(coef, faces, start, stop, link_y, link_x, source, update, block=2):
+def plane_faces(coef, faces, start, stop, link_y, link_x, source, update, block=4):
     face_z, face_y, face_x, diagonal, inverse = faces
     back_y = None if link_y is None else turned(link_y, 1, 1)
     back_x = None if link_x is None else turned(link_x, 1, 2)
@@ -290,7 +290,7 @@
     in_blocks(start, stop, block, body, 0.5 * below)
 
 
-def plane_sweep(faces, start, stop, field, finish, block=2):
+def plane_sweep(faces, start, stop, field, finish, block=4):
     face_z, face_y, face_x, diagonal, inverse = faces
 
     def body(here, after, below):
@@ -498,18 +498,23 @@
     return lax.broadcasted_iota(jnp.int32, shape, len(shape) - 1)
 
 
-def side_rows():
-    return pl.ds(pl.multiple_of(jnp.where(lax.axis_index("gy") == 0, 0, HALO_Y), HALO_Y), HALO_Y)
-
-
-def pack_x_kernel(source, coef, side_source, side_coef, x_a, x_b):
-    planes, own_y, _ = source.shape
+def start_kernel(source, coef, both, side):
+    own_y = source.shape[1]
+    first = jnp.where(lax.axis_index("gy") == 0, own_y - HALO_Y, 0)
+    rows = pl.ds(pl.multiple_of(first, HALO_Y), HALO_Y)
+    for which, ref in enumerate((source, coef)):
+        both[which] = ref[...]
+        side[which] = ref[:, rows]
+
+
+def pack_x_kernel(own, side, x_a, x_b):
+    _, planes, own_y, _ = own.shape
     x_even = lax.axis_index("gx") % 2 == 0
     lane = lanes_of((own_y + HALO_Y, 128))
-    for which, (ref, side) in enumerate(((source, side_source), (coef, side_coef))):
+    for which in range(2):
         right = left = jnp.zeros(lane.shape, F32)
         for plane in range(planes):
-            value = jnp.concatenate([ref[plane], side[plane, side_rows()]], axis=0)
+            value = jnp.concatenate([own[which, plane], side[which, plane]], axis=0)
             slot = (lane >= 8 * plane) & (lane < 8 * plane + 8)
             right = jnp.where(slot, turned(value, 8 * plane + 8, 1), right)
             left = jnp.where(slot, turned(value, 8 * plane, 1), left)
@@ -529,25 +534,25 @@
     return right, left
 
 
-def pack_z_kernel(x_count, source, coef, side_source, side_coef, x_a, x_b, z_a, z_b):
-    planes, own_y, _ = source.shape
+def pack_z_kernel(x_count, own, side, x_a, x_b, z_a, z_b):
+    _, planes, own_y, _ = own.shape
     z_even = lax.axis_index("gz") % 2 == 0
     lane = lanes_of((own_y + HALO_Y, 128))
     skip = 8 * (planes - HALO_Z)
-    for which, (ref, side) in enumerate(((source, side_source), (coef, side_coef))):
+    for which in range(2):
         right, left = x_halos(x_a, x_b, which, x_count)
         bottom = jnp.where(lane < 64, right, turned(left, 64, 1))
         top = jnp.where(lane < 64, turned(right, -skip, 1), turned(left, 64 - skip, 1))
         for target, is_top in ((z_a, z_even), (z_b, jnp.logical_not(z_even))):
             first = jnp.where(is_top, planes - HALO_Z, 0)
-            target[which, :HALO_Z, :own_y] = ref[pl.ds(first, HALO_Z)]
-            target[which, :HALO_Z, own_y:] = side[pl.ds(first, HALO_Z), side_rows()]
+            target[which, :HALO_Z, :own_y] = own[which, pl.ds(first, HALO_Z)]
+            target[which, :HALO_Z, own_y:] = side[which, pl.ds(first, HALO_Z)]
             target[which, HALO_Z] = jnp.where(is_top, top, bottom)
 
 
 def fill_window(own, side, got, source, coef, x_count, z_count):
     x_a, x_b, z_a, z_b = got
-    planes, own_y = own[0].shape[:2]
+    _, planes, own_y, _ = own.shape
     rows = own_y + HALO_Y
     z_index = lax.axis_index("gz")
     z_even = z_index % 2 == 0
@@ -559,8 +564,8 @@
         return jnp.where((lane < 8) | (lane >= 120), value, 0.0)
 
     for which, target in enumerate((source, coef)):
-        target[pl.ds(HALO_Z, planes), :own_y, :128] = own[which][...]
-        target[pl.ds(HALO_Z, planes), own_y:, :128] = side[which][:, side_rows()]
+        target[pl.ds(HALO_Z, planes), :own_y, :128] = own[which]
+        target[pl.ds(HALO_Z, planes), own_y:, :128] = side[which]
         right, left = x_halos(x_a, x_b, which, x_count)
         for plane in range(planes):
             target[HALO_Z + plane, :, 128:] = edges(right, left, 8 * plane, 8 * plane)
@@ -577,23 +582,15 @@
 
 
 def first_kernel(counts, *refs):
-    own, side, got = refs[:2], refs[2:4], refs[4:8]
-    left, right_source, right_coef, message = refs[8:12]
-    kept_out = refs[12:19]
-    source, estimate, *faces, coef, residual, update, pair_source, pair_coef, done = refs[19:]
+    own, side, got = refs[0], refs[1], refs[2:6]
+    left, right_source, right_coef, message, source, coef, estimate = refs[6:13]
+    *faces, residual, update, pair_source, pair_coef = refs[13:]
     fill_window(own, side, got, source, coef, *counts)
     planes, rows, lanes = source.shape
     own_y = rows - HALO_Y
-    copies = [
-        pltpu.make_async_copy(value, target, done.at[index])
-        for index, (value, target) in enumerate(zip((source, estimate, *faces), kept_out))
-    ]
     plane_faces(coef, faces, 0, planes, link_mask(rows, lanes), None, source, update)
-    for copy in copies[:1] + copies[2:]:
-        copy.start()
-    ranges = [(step + 2, planes - step - 2) for step in range(DEGREE - 1)]
+    ranges = [(2, planes - 2), (4, planes - 4)]
     plane_steps(faces, ranges, source, residual, update, estimate, True)
-    copies[1].start()
     plane_residual(faces, HALO_Z, planes - HALO_Z, residual, update)
     for pair in range((planes - 2 * HALO_Z) // 2):
         low = HALO_Z + 2 * pair
@@ -603,34 +600,30 @@
     message[...] = times_right(times_left(left[...], pair_source[...]), right_source[...]) + times_right(
         times_left(left[...], pair_coef[...]), right_coef[...]
     )
-    for copy in copies:
-        copy.wait()
 
 
 def second_kernel(counts, matrix_count, *refs):
     x_count, y_count, z_count = counts
     x_index, y_index, z_index = (lax.axis_index(axis) for axis in ("gx", "gy", "gz"))
     halves, refs = (refs[:x_count], refs[x_count : 2 * x_count]), refs[2 * x_count :]
-    brought, refs = refs[: 7 + matrix_count], refs[7 + matrix_count :]
+    (source, coef, estimate), refs = refs[:3], refs[3:]
+    brought, refs = refs[:matrix_count], refs[matrix_count:]
     (solution, residual_out), scratch = refs[:2], refs[2:]
-    held, scratch, done = scratch[: 7 + matrix_count], scratch[7 + matrix_count : -1], scratch[-1]
+    held, scratch, done = scratch[:matrix_count], scratch[matrix_count:-1], scratch[-1]
     copies = []
     for index, (value, target) in enumerate(zip(brought, held)):
-        if index == 7:
-            value = value.at[y_index]
-        if index == 8:
-            value = value.at[x_index]
+        if index < 2:
+            value = value.at[(y_index, x_index)[index]]
         copies.append(pltpu.make_async_copy(value, target, done.at[index]))
-    for copy in copies[7:] + copies[:7]:
+    for copy in copies:
         copy.start()
-    source, estimate = held[:2]
-    faces = held[2:7]
-    up_left, up_right = held[7:9]
-    mid_refs = held[9:13]
-    sheet_refs = held[13:]
+    up_left, up_right = held[:2]
+    mid_refs = held[2:6]
+    sheet_refs = held[6:]
     mid_source, mid_coef, mid_residual, mid_update, mid_estimate, mid_correction = scratch[:6]
     mid_faces = scratch[6:11]
-    pairs, wide, residual, update, current = scratch[11:]
+    pairs, wide, residual, update, current = scratch[11:16]
+    faces = scratch[16:]
 
     planes, rows, lanes = source.shape
     own_y = rows - HALO_Y
@@ -666,7 +659,7 @@
     plane_steps(mid_faces, ranges, mid_source, mid_residual, mid_update, mid_estimate, True)
     plane_residual(mid_faces, start, stop, mid_residual, mid_update)
 
-    for copy in copies[7:]:
+    for copy in copies:
         copy.wait()
     left_down, right_down, mid_left_up, mid_right_up = mid_refs
     sheets = []
@@ -698,13 +691,12 @@
 
     low, high = clipped(6)
     lax.fori_loop((low - PAD) // 2, (high - PAD) // 2, add_mid, 0)
-    plane_restart(mid_faces, *clipped(6), mid_source, mid_residual, mid_update, mid_estimate)
+    plane_restart(mid_faces, *clipped(8), mid_source, mid_residual, mid_update, mid_estimate)
     plane_steps(
         mid_faces, [clipped(4), clipped(4)], mid_source, mid_residual, mid_update, mid_estimate, False
     )
 
-    for copy in copies[:7]:
-        copy.wait()
+    plane_faces(coef, faces, 0, planes, link_mask(rows, lanes), None, source, update)
     coarse_planes = up_left.shape[1] // mid_y
     near = mid_estimate[pl.ds(z_index * 8, coarse_planes)].reshape(coarse_planes * mid_y, mid_x)
     raised = times_left(up_left[...], times_right(near, up_right[...]))
@@ -714,14 +706,16 @@
     def add_fine(place, carry):
         own = 0.75 * wide[place]
         for offset, other in ((0, place - 1), (1, place + 1)):
-            plane = 2 * place + 1 + offset
+            plane = 2 * place + HALO_Z - 2 * PAD + offset
             step = own + 0.25 * wide[other]
             current[plane] = estimate[plane] + jnp.where(inverse[plane] > 0.0, step, 0.0)
         return carry
 
     lax.fori_loop(1, coarse_planes - 1, add_fine, 0)
-    plane_restart(faces, HALO_Z - 3, planes - HALO_Z + 3, source, residual, update, current)
-    ranges = [(HALO_Z - 2, planes - HALO_Z + 2), (HALO_Z - 1, planes - HALO_Z + 1)]
+    for plane in (HALO_Z - 5, planes - HALO_Z + 4):
+        current[plane] = estimate[plane]
+    plane_restart(faces, HALO_Z - 4, planes - HALO_Z + 4, source, residual, update, current)
+    ranges = [(HALO_Z - 2, planes - HALO_Z + 2)] * 2
     plane_steps(faces, ranges, source, residual, update, current, False)
     plane_residual(faces, HALO_Z, planes - HALO_Z, residual, update)
     own_planes = pl.ds(HALO_Z, planes - 2 * HALO_Z)
@@ -737,22 +731,22 @@
     planes, rows, lanes = own_z + 2 * HALO_Z, own_y + HALO_Y, 2 * own_x
     vmem = pl.BlockSpec(memory_space=pltpu.VMEM)
 
-    def call(kernel, name, room, arguments, shapes, scratch, far_arguments=(), far_shapes=(), copies=0):
+    def call(kernel, name, room, arguments, shapes, scratch, far_arguments=()):
         far = pl.BlockSpec(memory_space=pltpu.HBM)
         return pl.pallas_call(
             kernel,
-            out_shape=tuple(jax.ShapeDtypeStruct(shape, F32) for shape in (*shapes, *far_shapes)),
+            out_shape=tuple(jax.ShapeDtypeStruct(shape, F32) for shape in shapes),
             in_specs=[vmem] * len(arguments) + [far] * len(far_arguments),
-            out_specs=(vmem,) * len(shapes) + (far,) * len(far_shapes),
-            scratch_shapes=[pltpu.VMEM(item, F32) if isinstance(item, tuple) else item for item in scratch]
-            + ([pltpu.SemaphoreType.DMA((copies,))] if copies else []),
+            out_specs=(vmem,) * len(shapes),
+            scratch_shapes=[pltpu.VMEM(item, F32) if isinstance(item, tuple) else item for item in scratch],
             compiler_params=pltpu.CompilerParams(vmem_limit_bytes=room * 1024 * 1024),
             name=name,
         )(*arguments, *far_arguments)
 
     core_pairs = swap_pairs(y_count, False)
-    blocks = (right_side, coefficient)
-    blocks += tuple(swapped(value, "gy", [core_pairs]) for value in blocks)
+    shapes = [(2, own_z, own_y, own_x), (2, own_z, HALO_Y, own_x)]
+    both, side = call(start_kernel, "start", 4, (right_side, coefficient), shapes, [])
+    blocks = (both, swapped(side, "gy", [core_pairs]))
     swaps = [[swap_pairs(count, odd) for odd in (False, True)] for count in (x_count, z_count)]
     sent = call(pack_x_kernel, "pack_x", 4, blocks, [(2, rows, 128)] * 2, [])
     got = [swapped(value, "gx", [pairs]) for value, pairs in zip(sent, swaps[0])]
@@ -768,10 +762,8 @@
         "first",
         12,
         (*blocks, *got, *down),
-        [(own_z * own_y // 4, own_x)],
-        [window] * 7 + [padded, window, padded] + [(own_z * own_y // 2, own_x)] * 2,
-        far_shapes=[window] * 7,
-        copies=7,
+        [(own_z * own_y // 4, own_x), window, padded, window],
+        [window] * 6 + [padded] + [(own_z * own_y // 2, own_x)] * 2,
     )
 
     def from_others(value, axis, count):
@@ -807,16 +799,16 @@
         functools.partial(second_kernel, counts, len(matrices)),
         "second",
         28,
-        parts,
+        (*parts, *windows),
         [(own_z, own_y, own_x)] * 2,
-        [window] * 7
-        + held
+        held
         + [mid_padded] * 5
         + [(mid[0] // 2 + 2, mid[1], mid[2])]
         + [mid_padded] * 5
-        + [(mid[0] // 2 * mid[1], mid[2]), (coarse_planes, rows, lanes), window, padded, padded],
-        far_arguments=(*windows, *(jnp.asarray(item) for item in matrices)),
-        copies=7 + len(matrices),
+        + [(mid[0] // 2 * mid[1], mid[2]), (coarse_planes, rows, lanes), window, padded, padded]
+        + [window] * 5
+        + [pltpu.SemaphoreType.DMA((len(matrices),))],
+        far_arguments=[jnp.asarray(item) for item in matrices],
     )
     return solution[None], residual[None]
 

time: 68.8 us -> 59.6 us (0.87)
  Pallas kernels: 29.5 us -> 20.5 us
    pallas_call x4 -> x5, Pallas kernels: 29.5 us -> 20.5 us  [call(): pl.pallas_call(kernel, out_shape=tuple((jax.ShapeDtypeStruct(shape, F32)...]
    ppermute x16 -> x15, waiting for transfers between devices: 14.7 us -> 14.6 us  [swapped(): return lax.ppermute(value, axes, list(enumerate(places)))]
    ppermute x16 -> x15, starting transfers between devices: 21.5 us -> 21.5 us  [swapped(): return lax.ppermute(value, axes, list(enumerate(places)))]
    unnamed x40 -> x36, local copies, waits for them, and re-layouts: 1.9 us -> 1.88 us
  transfers between devices with their start and end apart: 16 -> 15, of which waited for: 9 -> 8; matrix products, arithmetic and copies ran while one was open for 0% -> 0% of each run, Pallas kernels for 0% -> 0%
where the time goes in v5:
time: 59.6 us; the launch traced here: 59.3 us
  starting transfers between devices  21.5 us (36%)
  Pallas kernels  20.5 us (34%)
  waiting for transfers between devices  14.6 us (24%)
  local copies, waits for them, and re-layouts  1.88 us (3%)
  between operations  0.85 us (1%)
    ppermute x15, starting transfers between devices, swapped(): return lax.ppermute(value, axes, list(enumerate(places)))  21.5 us
    pallas_call x5, Pallas kernels, call(): pl.pallas_call(kernel, out_shape=tuple((jax.ShapeDtypeStruct(shape, F32)...  20.5 us
    ppermute x15, waiting for transfers between devices, swapped(): return lax.ppermute(value, axes, list(enumerate(places)))  14.6 us
    unnamed x36, local copies, waits for them, and re-layouts  1.88 us
  transfers between devices with their start and end apart: 15, of which 8 were waited for; matrix products, arithmetic and copies ran while one was open for 0% of the time, Pallas kernels for 0%

profile of v5, /device:TPU:0, one launch (start us, length us, event | category | flops | bytes accessed | tf_op | source)
XLA Modules:
  0.0 59.3 jit_solution(4273020411710950782)
XLA Ops:
  0.6 0.9 %copy-done.3 = f32[1,16,16,128]{3,2,1,0:T(8,128)S(1)} copy-done((f32[1,16,16,128]{3,2,1,0:T(8,128)S(1)}, f32[1,16,16,128]{3,2,1,0:T(8,128)}, u32[]{:S(2)}) %copy-start.3) | copy-done | bytes 131096
  1.5 0.9 %copy-done.4 = f32[16,16,128]{2,1,0:T(8,128)S(1)} copy-done((f32[16,16,128]{2,1,0:T(8,128)S(1)}, f32[16,16,128]{2,1,0:T(8,128)}, u32[]{:S(2)}) %copy-start.4) | copy-done | bytes 131096
  2.5 0.5 collective-permute-start
  3.0 1.0 %collective-permute-done.side.refs_1_ = f32[2,16,8,128]{3,2,1,0:T(8,128)S(1)} collective-permute-done((f32[2,16,8,128]{3,2,1,0:T(8,128)S(1)}, f32[2,16,8,128]{3,2,1,0:T(8,128)S(1)}, u32[]{:S(2)}, u32[]{:S(2)}) %collective-permute-start) | collective-permute-done | bytes 131104 | tf_op jit(solution)/shard_map/ppermute | solution.py:488
  4.2 2.9 %collective-permute-start.1 = (f32[2,24,128]{2,1,0:T(8,128)S(1)}, f32[2,24,128]{2,1,0:T(8,128)S(1)}, u32[]{:S(2)}, u32[]{:S(2)}) collective-permute-start(f32[2,24,128]{2,1,0:T(8,128)S(1)} %get-tuple-element.16), channel_id=1, source_target_pairs={{0,8},{8,0},{16,24},{24,16},{1,9},{9,1},{17,25},{25,17},{2,10},{10... | collective-permute-start | bytes 73736 | tf_op jit(solution)/shard_map/ppermute | solution.py:488
  7.2 0.8 %collective-permute-start.2 = (f32[2,24,128]{2,1,0:T(8,128)S(1)}, f32[2,24,128]{2,1,0:T(8,128)S(1)}, u32[]{:S(2)}, u32[]{:S(2)}) collective-permute-start(f32[2,24,128]{2,1,0:T(8,128)S(1)} %get-tuple-element.17), channel_id=1, source_target_pairs={{0,0},{8,16},{16,8},{24,24},{1,1},{9,17},{17,9},{25,25},{2,2},{10,... | collective-permute-start | bytes 73736 | tf_op jit(solution)/shard_map/ppermute | solution.py:488
  8.0 1.0 %collective-permute-done.1.x_a.refs_2_ = f32[2,24,128]{2,1,0:T(8,128)S(1)} collective-permute-done((f32[2,24,128]{2,1,0:T(8,128)S(1)}, f32[2,24,128]{2,1,0:T(8,128)S(1)}, u32[]{:S(2)}, u32[]{:S(2)}) %collective-permute-start.1) | collective-permute-done | bytes 24608 | tf_op jit(solution)/shard_map/ppermute | solution.py:488
  9.1 2.2 %collective-permute-start.3 = (f32[2,9,24,128]{3,2,1,0:T(8,128)S(1)}, f32[2,9,24,128]{3,2,1,0:T(8,128)S(1)}, u32[]{:S(2)}, u32[]{:S(2)}) collective-permute-start(f32[2,9,24,128]{3,2,1,0:T(8,128)S(1)} %get-tuple-element.18), channel_id=1, source_target_pairs={{0,1},{1,0},{2,3},{3,2},{4,5},{5,4},{6,7},{7,6},{8,9},{9,8},{10,11... | collective-permute-start | bytes 663560 | tf_op jit(solution)/shard_map/ppermute | solution.py:488
  11.2 0.8 %collective-permute-start.4 = (f32[2,9,24,128]{3,2,1,0:T(8,128)S(1)}, f32[2,9,24,128]{3,2,1,0:T(8,128)S(1)}, u32[]{:S(2)}, u32[]{:S(2)}) collective-permute-start(f32[2,9,24,128]{3,2,1,0:T(8,128)S(1)} %get-tuple-element.19), channel_id=1, source_target_pairs={{0,0},{1,2},{2,1},{3,3},{4,4},{5,6},{6,5},{7,7},{8,8},{9,10},{10,9... | collective-permute-start | bytes 663560 | tf_op jit(solution)/shard_map/ppermute | solution.py:488
  12.0 3.8 %collective-permute-done.3.refs_4_ = f32[2,9,24,128]{3,2,1,0:T(8,128)S(1)} collective-permute-done((f32[2,9,24,128]{3,2,1,0:T(8,128)S(1)}, f32[2,9,24,128]{3,2,1,0:T(8,128)S(1)}, u32[]{:S(2)}, u32[]{:S(2)}) %collective-permute-start.3) | collective-permute-done | bytes 221216 | tf_op jit(solution)/shard_map/ppermute | solution.py:488
  15.9 4.4 %first.1 = (f32[64,128]{1,0:T(8,128)S(1)}, f32[32,24,256]{2,1,0:T(8,128)S(1)}, f32[33,24,256]{2,1,0:T(8,128)S(1)}, f32[32,24,256]{2,1,0:T(8,128)S(1)}) custom-call(f32[2,16,16,128]{3,2,1,0:T(8,128)S(1)} %get-tuple-element.14.own.refs_0_, f32[2,16,8,128]{3,2,1,0:T(8,128)S(1)} %collective-permute-done.side.refs_1_, ...), custom_call_target="tpu_custom_call" | custom-call | tf_op jit(solution)/shard_map/first/pallas_call | solution.py:736
  20.3 3.8 %collective-permute-start.7 = (f32[64,128]{1,0:T(8,128)S(1)}, f32[64,128]{1,0:T(8,128)S(1)}, u32[]{:S(2)}, u32[]{:S(2)}) collective-permute-start(f32[64,128]{1,0:T(8,128)S(1)} %get-tuple-element.20), channel_id=1, source_target_pairs={{0,3},{1,2},{2,1},{3,0},{4,7},{5,6},{6,5},{7,4},{8,11},{9,10},{10,... | collective-permute-start | bytes 98312 | tf_op jit(solution)/shard_map/ppermute | solution.py:488
  24.1 2.6 %collective-permute-start.6 = (f32[64,128]{1,0:T(8,128)S(1)}, f32[64,128]{1,0:T(8,128)S(1)}, u32[]{:S(2)}, u32[]{:S(2)}) collective-permute-start(f32[64,128]{1,0:T(8,128)S(1)} %get-tuple-element.20), channel_id=1, source_target_pairs={{0,2},{1,3},{2,0},{3,1},{4,6},{5,7},{6,4},{7,5},{8,10},{9,11},{10,... | collective-permute-start | bytes 98312 | tf_op jit(solution)/shard_map/ppermute | solution.py:488
  26.7 0.3 collective-permute-start.5
  26.9 2.0 %collective-permute-done.6 = f32[64,128]{1,0:T(8,128)S(1)} collective-permute-done((f32[64,128]{1,0:T(8,128)S(1)}, f32[64,128]{1,0:T(8,128)S(1)}, u32[]{:S(2)}, u32[]{:S(2)}) %collective-permute-start.6) | collective-permute-done | bytes 32800 | tf_op jit(solution)/shard_map/ppermute | solution.py:488
  28.9 1.7 %collective-permute-done.5 = f32[64,128]{1,0:T(8,128)S(1)} collective-permute-done((f32[64,128]{1,0:T(8,128)S(1)}, f32[64,128]{1,0:T(8,128)S(1)}, u32[]{:S(2)}, u32[]{:S(2)}) %collective-permute-start.5) | collective-permute-done | bytes 32800 | tf_op jit(solution)/shard_map/ppermute | solution.py:488
  30.6 2.5 %collective-permute-start.10 = (f32[4,64,128]{2,1,0:T(8,128)S(1)}, f32[4,64,128]{2,1,0:T(8,128)S(1)}, u32[]{:S(2)}, u32[]{:S(2)}) collective-permute-start(f32[4,64,128]{2,1,0:T(8,128)S(1)} %pad_maximum_fusion.refs_0_), channel_id=1, source_target_pairs={{0,24},{8,16},{16,8},{24,0},{1,25},{9,17},{17,9},{25,1},{2,26},{10... | collective-permute-start | bytes 393224 | tf_op jit(solution)/shard_map/ppermute | solution.py:488
  33.1 3.7 %collective-permute-start.9 = (f32[4,64,128]{2,1,0:T(8,128)S(1)}, f32[4,64,128]{2,1,0:T(8,128)S(1)}, u32[]{:S(2)}, u32[]{:S(2)}) collective-permute-start(f32[4,64,128]{2,1,0:T(8,128)S(1)} %pad_maximum_fusion.refs_0_), channel_id=1, source_target_pairs={{0,16},{8,24},{16,0},{24,8},{1,17},{9,25},{17,1},{25,9},{2,18},{10... | collective-permute-start | bytes 393224 | tf_op jit(solution)/shard_map/ppermute | solution.py:488
  36.8 1.0 %collective-permute-start.8 = (f32[4,64,128]{2,1,0:T(8,128)S(1)}, f32[4,64,128]{2,1,0:T(8,128)S(1)}, u32[]{:S(2)}, u32[]{:S(2)}) collective-permute-start(f32[4,64,128]{2,1,0:T(8,128)S(1)} %pad_maximum_fusion.refs_0_), channel_id=1, source_target_pairs={{0,8},{8,0},{16,24},{24,16},{1,9},{9,1},{17,25},{25,17},{2,10},{10... | collective-permute-start | bytes 393224 | tf_op jit(solution)/shard_map/ppermute | solution.py:488
  37.8 0.5 collective-permute-start.14
  38.3 2.4 %collective-permute-done.9.refs_2_ = f32[4,64,128]{2,1,0:T(8,128)S(1)} collective-permute-done((f32[4,64,128]{2,1,0:T(8,128)S(1)}, f32[4,64,128]{2,1,0:T(8,128)S(1)}, u32[]{:S(2)}, u32[]{:S(2)}) %collective-permute-start.9) | collective-permute-done | bytes 131104 | tf_op jit(solution)/shard_map/ppermute | solution.py:488
  40.7 1.5 %collective-permute-done.8.refs_1_ = f32[4,64,128]{2,1,0:T(8,128)S(1)} collective-permute-done((f32[4,64,128]{2,1,0:T(8,128)S(1)}, f32[4,64,128]{2,1,0:T(8,128)S(1)}, u32[]{:S(2)}, u32[]{:S(2)}) %collective-permute-start.8) | collective-permute-done | bytes 131104 | tf_op jit(solution)/shard_map/ppermute | solution.py:488
  42.2 1.3 %collective-permute-done.12.refs_5_ = f32[4,64,128]{2,1,0:T(8,128)S(1)} collective-permute-done((f32[4,64,128]{2,1,0:T(8,128)S(1)}, f32[4,64,128]{2,1,0:T(8,128)S(1)}, u32[]{:S(2)}, u32[]{:S(2)}) %collective-permute-start.12) | collective-permute-done | bytes 131104 | tf_op jit(solution)/shard_map/ppermute | solution.py:488
  43.6 15.7 %second.1 = (f32[16,16,128]{2,1,0:T(8,128)}, f32[16,16,128]{2,1,0:T(8,128)}) custom-call(f32[4,64,128]{2,1,0:T(8,128)S(1)} %pad_maximum_fusion.refs_0_, f32[4,64,128]{2,1,0:T(8,128)S(1)} %collective-permute-done.8.refs_1_, f32[4,64,128]{2,1,0:T(8,128)S(1)} %collective-permute-done.9.refs_2_, f32[4,64,128]{2,1,0:T(8,128)S(1)} %collective-permute-done.10.refs_3_, ...), custom_call_target="tpu_custom_call" | custom-call | tf_op jit(solution)/shard_map/second/pallas_call | solution.py:736
  (48 shorter events, 0.5 us)
Async XLA Ops:
  2.5 1.5 %collective-permute-start = (f32[2,16,8,128]{3,2,1,0:T(8,128)S(1)}, f32[2,16,8,128]{3,2,1,0:T(8,128)S(1)}, u32[]{:S(2)}, u32[]{:S(2)}) collective-permute-start(f32[2,16,8,128]{3,2,1,0:T(8,128)S(1)} %get-tuple-element.15), channel_id=1, source_target_pairs={{0,4},{4,0},{1,5},{5,1},{2,6},{6,2},{3,7},{7,3},{8,12},{12,8},{9,1... | collective-permute-start | bytes 393224 | tf_op jit(solution)/shard_map/ppermute | solution.py:488
  4.2 4.7 %collective-permute-start.1 = (f32[2,24,128]{2,1,0:T(8,128)S(1)}, f32[2,24,128]{2,1,0:T(8,128)S(1)}, u32[]{:S(2)}, u32[]{:S(2)}) collective-permute-start(f32[2,24,128]{2,1,0:T(8,128)S(1)} %get-tuple-element.16), channel_id=1, source_target_pairs={{0,8},{8,0},{16,24},{24,16},{1,9},{9,1},{17,25},{25,17},{2,10},{10... | collective-permute-start | bytes 73736 | tf_op jit(solution)/shard_map/ppermute | solution.py:488
  7.2 1.8 %collective-permute-start.2 = (f32[2,24,128]{2,1,0:T(8,128)S(1)}, f32[2,24,128]{2,1,0:T(8,128)S(1)}, u32[]{:S(2)}, u32[]{:S(2)}) collective-permute-start(f32[2,24,128]{2,1,0:T(8,128)S(1)} %get-tuple-element.17), channel_id=1, source_target_pairs={{0,0},{8,16},{16,8},{24,24},{1,1},{9,17},{17,9},{25,25},{2,2},{10,... | collective-permute-start | bytes 73736 | tf_op jit(solution)/shard_map/ppermute | solution.py:488
  9.0 34.6 %copy-start.12 = (bf16[128,32]{1,0:T(8,128)(2,1)S(1)}, bf16[128,32]{1,0:T(8,128)(2,1)}, u32[]{:S(2)}) copy-start(bf16[128,32]{1,0:T(8,128)(2,1)} %constant.42.clone.refs_19_) | copy-start | bytes 24580
  9.0 34.6 %copy-start.16 = (bf16[32,128]{1,0:T(8,128)(2,1)S(1)}, bf16[32,128]{1,0:T(8,128)(2,1)}, u32[]{:S(2)}) copy-start(bf16[32,128]{1,0:T(8,128)(2,1)} %constant.41.clone.refs_17_) | copy-start | bytes 24580
  9.1 6.8 %collective-permute-start.3 = (f32[2,9,24,128]{3,2,1,0:T(8,128)S(1)}, f32[2,9,24,128]{3,2,1,0:T(8,128)S(1)}, u32[]{:S(2)}, u32[]{:S(2)}) collective-permute-start(f32[2,9,24,128]{3,2,1,0:T(8,128)S(1)} %get-tuple-element.18), channel_id=1, source_target_pairs={{0,1},{1,0},{2,3},{3,2},{4,5},{5,4},{6,7},{7,6},{8,9},{9,8},{10,11... | collective-permute-start | bytes 663560 | tf_op jit(solution)/shard_map/ppermute | solution.py:488
  11.2 32.3 %copy-start = (bf16[4,256,256]{2,1,0:T(8,128)(2,1)S(1)}, bf16[4,256,256]{2,1,0:T(8,128)(2,1)}, u32[]{:S(2)}) copy-start(bf16[4,256,256]{2,1,0:T(8,128)(2,1)} %constant.36.clone.refs_12_) | copy-start | bytes 1572868
  11.2 4.6 %collective-permute-start.4 = (f32[2,9,24,128]{3,2,1,0:T(8,128)S(1)}, f32[2,9,24,128]{3,2,1,0:T(8,128)S(1)}, u32[]{:S(2)}, u32[]{:S(2)}) collective-permute-start(f32[2,9,24,128]{3,2,1,0:T(8,128)S(1)} %get-tuple-element.19), channel_id=1, source_target_pairs={{0,0},{1,2},{2,1},{3,3},{4,4},{5,6},{6,5},{7,7},{8,8},{9,10},{10,9... | collective-permute-start | bytes 663560 | tf_op jit(solution)/shard_map/ppermute | solution.py:488
  15.9 27.7 %copy-start.1 = (bf16[2,336,224]{2,1,0:T(8,128)(2,1)S(1)}, bf16[2,336,224]{2,1,0:T(8,128)(2,1)}, u32[]{:S(2)}) copy-start(bf16[2,336,224]{2,1,0:T(8,128)(2,1)} %constant.35.clone.refs_11_) | copy-start | bytes 903172
  15.9 27.7 %copy-start.9 = (bf16[128,128]{1,0:T(8,128)(2,1)S(1)}, bf16[128,128]{1,0:T(8,128)(2,1)}, u32[]{:S(2)}) copy-start(bf16[128,128]{1,0:T(8,128)(2,1)} %constant.47.clone.refs_24_) | copy-start | bytes 98308
  15.9 27.7 %copy-start.10 = (bf16[128,128]{1,0:T(8,128)(2,1)S(1)}, bf16[128,128]{1,0:T(8,128)(2,1)}, u32[]{:S(2)}) copy-start(bf16[128,128]{1,0:T(8,128)(2,1)} %constant.45.clone.refs_22_) | copy-start | bytes 98308
  15.9 27.7 %copy-start.11 = (bf16[128,128]{1,0:T(8,128)(2,1)S(1)}, bf16[128,128]{1,0:T(8,128)(2,1)}, u32[]{:S(2)}) copy-start(bf16[128,128]{1,0:T(8,128)(2,1)} %constant.43.clone.refs_20_) | copy-start | bytes 98308
  15.9 27.7 %copy-start.17 = (bf16[8,32]{1,0:T(8,128)(2,1)S(1)}, bf16[8,32]{1,0:T(8,128)(2,1)}, u32[]{:S(2)}) copy-start(bf16[8,32]{1,0:T(8,128)(2,1)} %constant.44.clone.refs_21_) | copy-start | bytes 1540
  20.3 6.6 %collective-permute-start.7 = (f32[64,128]{1,0:T(8,128)S(1)}, f32[64,128]{1,0:T(8,128)S(1)}, u32[]{:S(2)}, u32[]{:S(2)}) collective-permute-start(f32[64,128]{1,0:T(8,128)S(1)} %get-tuple-element.20), channel_id=1, source_target_pairs={{0,3},{1,2},{2,1},{3,0},{4,7},{5,6},{6,5},{7,4},{8,11},{9,10},{10,... | collective-permute-start | bytes 98312 | tf_op jit(solution)/shard_map/ppermute | solution.py:488
  24.1 4.8 %collective-permute-start.6 = (f32[64,128]{1,0:T(8,128)S(1)}, f32[64,128]{1,0:T(8,128)S(1)}, u32[]{:S(2)}, u32[]{:S(2)}) collective-permute-start(f32[64,128]{1,0:T(8,128)S(1)} %get-tuple-element.20), channel_id=1, source_target_pairs={{0,2},{1,3},{2,0},{3,1},{4,6},{5,7},{6,4},{7,5},{8,10},{9,11},{10,... | collective-permute-start | bytes 98312 | tf_op jit(solution)/shard_map/ppermute | solution.py:488
  26.7 3.9 %collective-permute-start.5 = (f32[64,128]{1,0:T(8,128)S(1)}, f32[64,128]{1,0:T(8,128)S(1)}, u32[]{:S(2)}, u32[]{:S(2)}) collective-permute-start(f32[64,128]{1,0:T(8,128)S(1)} %get-tuple-element.20), channel_id=1, source_target_pairs={{0,1},{1,0},{2,3},{3,2},{4,5},{5,4},{6,7},{7,6},{8,9},{9,8},{10,11... | collective-permute-start | bytes 98312 | tf_op jit(solution)/shard_map/ppermute | solution.py:488
  30.6 13.0 %copy-start.8 = (bf16[128,256]{1,0:T(8,128)(2,1)S(1)}, bf16[128,256]{1,0:T(8,128)(2,1)}, u32[]{:S(2)}) copy-start(bf16[128,256]{1,0:T(8,128)(2,1)} %constant.37.clone.refs_13_) | copy-start | bytes 196612
  30.6 7.2 %collective-permute-start.10 = (f32[4,64,128]{2,1,0:T(8,128)S(1)}, f32[4,64,128]{2,1,0:T(8,128)S(1)}, u32[]{:S(2)}, u32[]{:S(2)}) collective-permute-start(f32[4,64,128]{2,1,0:T(8,128)S(1)} %pad_maximum_fusion.refs_0_), channel_id=1, source_target_pairs={{0,24},{8,16},{16,8},{24,0},{1,25},{9,17},{17,9},{25,1},{2,26},{10... | collective-permute-start | bytes 393224 | tf_op jit(solution)/shard_map/ppermute | solution.py:488
  33.1 7.6 %collective-permute-start.9 = (f32[4,64,128]{2,1,0:T(8,128)S(1)}, f32[4,64,128]{2,1,0:T(8,128)S(1)}, u32[]{:S(2)}, u32[]{:S(2)}) collective-permute-start(f32[4,64,128]{2,1,0:T(8,128)S(1)} %pad_maximum_fusion.refs_0_), channel_id=1, source_target_pairs={{0,16},{8,24},{16,0},{24,8},{1,17},{9,25},{17,1},{25,9},{2,18},{10... | collective-permute-start | bytes 393224 | tf_op jit(solution)/shard_map/ppermute | solution.py:488
  36.8 5.4 %collective-permute-start.8 = (f32[4,64,128]{2,1,0:T(8,128)S(1)}, f32[4,64,128]{2,1,0:T(8,128)S(1)}, u32[]{:S(2)}, u32[]{:S(2)}) collective-permute-start(f32[4,64,128]{2,1,0:T(8,128)S(1)} %pad_maximum_fusion.refs_0_), channel_id=1, source_target_pairs={{0,8},{8,0},{16,24},{24,16},{1,9},{9,1},{17,25},{25,17},{2,10},{10... | collective-permute-start | bytes 393224 | tf_op jit(solution)/shard_map/ppermute | solution.py:488
  37.8 4.4 %collective-permute-start.11 = (f32[4,64,128]{2,1,0:T(8,128)S(1)}, f32[4,64,128]{2,1,0:T(8,128)S(1)}, u32[]{:S(2)}, u32[]{:S(2)}) collective-permute-start(f32[4,64,128]{2,1,0:T(8,128)S(1)} %pad_maximum_fusion.refs_0_), channel_id=1, source_target_pairs={{0,4},{4,0},{1,5},{5,1},{2,6},{6,2},{3,7},{7,3},{8,12},{12,8},{9,1... | collective-permute-start | bytes 393224 | tf_op jit(solution)/shard_map/ppermute | solution.py:488
  37.8 4.4 %collective-permute-start.14 = (f32[4,64,128]{2,1,0:T(8,128)S(1)}, f32[4,64,128]{2,1,0:T(8,128)S(1)}, u32[]{:S(2)}, u32[]{:S(2)}) collective-permute-start(f32[4,64,128]{2,1,0:T(8,128)S(1)} %collective-permute-done.10.refs_3_), channel_id=1, source_target_pairs={{0,4},{4,0},{1,5},{5,1},{2,6},{6,2},{3,7},{7,3},{8,12},{12,8},{9,1... | collective-permute-start | bytes 393224 | tf_op jit(solution)/shard_map/ppermute | solution.py:488
  40.7 1.5 %collective-permute-start.13 = (f32[4,64,128]{2,1,0:T(8,128)S(1)}, f32[4,64,128]{2,1,0:T(8,128)S(1)}, u32[]{:S(2)}, u32[]{:S(2)}) collective-permute-start(f32[4,64,128]{2,1,0:T(8,128)S(1)} %collective-permute-done.9.refs_2_), channel_id=1, source_target_pairs={{0,4},{4,0},{1,5},{5,1},{2,6},{6,2},{3,7},{7,3},{8,12},{12,8},{9,1... | collective-permute-start | bytes 393224 | tf_op jit(solution)/shard_map/ppermute | solution.py:488
  42.2 1.3 %collective-permute-start.12 = (f32[4,64,128]{2,1,0:T(8,128)S(1)}, f32[4,64,128]{2,1,0:T(8,128)S(1)}, u32[]{:S(2)}, u32[]{:S(2)}) collective-permute-start(f32[4,64,128]{2,1,0:T(8,128)S(1)} %collective-permute-done.8.refs_1_), channel_id=1, source_target_pairs={{0,4},{4,0},{1,5},{5,1},{2,6},{6,2},{3,7},{7,3},{8,12},{12,8},{9,1... | collective-permute-start | bytes 393224 | tf_op jit(solution)/shard_map/ppermute | solution.py:488
  (9 other events, 79.9 us)

commit v6 on v5

--- a/solution.py
+++ b/solution.py
@@ -208,6 +208,7 @@
 
 
 HALO_Z = 8
+SENT_Z = (6, 7)
 HALO_Y = 8
 HALO_X = 8
 PAD = 3
@@ -364,32 +365,41 @@
     plane_sweep(faces, start, stop, update, finish)
 
 
-def sheet_faces(coef, shape):
-    z_cells, y_cells, x_cells = shape
-    row = lax.broadcasted_iota(jnp.int32, coef.shape, 0)
-    lane = lax.broadcasted_iota(jnp.int32, coef.shape, 1)
-    links = (
-        (row < (z_cells - 1) * y_cells, y_cells, 0),
-        (row % y_cells < y_cells - 1, 1, 0),
-        (lane < x_cells - 1, 1, 1),
-    )
-    inside = lane < x_cells
+def moved(value, shift, axis):
+    if axis:
+        return turned(value, -shift, axis)
+    return jnp.concatenate([value[shift:], value[:shift]], axis=0)
+
+
+def places(shape, axis):
+    return lax.broadcasted_iota(jnp.int32, shape, axis)
+
+
+def up_to(shape, axis, stop):
+    return jnp.where(places(shape, axis) < stop, 1.0, 0.0)
+
+
+def sheet_faces(coef, stride):
     total = 3.0 * coef
     faces = []
-    for link, shift, axis in links:
-        above = jnp.where(link, turned(coef, -shift, axis), 0.0)
-        below = turned(jnp.where(link, coef, 0.0), shift, axis)
-        faces.append((jnp.where(link, 0.5 * (coef + above), 0.0), shift, axis))
+    for axis, count in enumerate(coef.shape):
+        link = up_to(coef.shape, axis, count - stride)
+        above = link * moved(coef, stride, axis)
+        below = moved(link * coef, -stride, axis)
+        faces.append((link * (0.5 * (coef + above)), axis))
         total = total + 0.5 * (above + below)
+    inside = coef > 0.0
+    for axis in range(3):
+        inside = inside & (places(coef.shape, axis) % stride == 0)
     inverse = jnp.where(inside, 1.0 / jnp.where(inside, total, 1.0), 0.0)
-    return faces, total, inverse
+    return faces, total, inverse, stride
 
 
 def sheet_apply(field, face_set):
-    faces, diagonal, _ = face_set
+    faces, diagonal, _, stride = face_set
     value = diagonal * field
-    for face, shift, axis in faces:
-        value = value - (face * turned(field, -shift, axis) + turned(face * field, shift, axis))
+    for face, axis in faces:
+        value = value - (face * moved(field, stride, axis) + moved(face * field, -stride, axis))
     return value
 
 
@@ -404,18 +414,30 @@
     return estimate, residual, update
 
 
-def sheet_cycle(source, coef, shape, depth, matrices):
-    face_set = sheet_faces(coef, shape)
+def sheet_down(value, stride):
+    for axis in range(3):
+        value = value + moved(value, stride, axis)
+    return value
+
+
+def sheet_up(value, stride):
+    for axis, count in enumerate(value.shape):
+        far = moved(value * up_to(value.shape, axis, count - 2 * stride), -2 * stride, axis)
+        near = moved(value, stride, axis) * up_to(value.shape, axis, count - stride)
+        value = 0.75 * (value + moved(value, -stride, axis)) + 0.25 * (far + near)
+    return value
+
+
+def sheet_cycle(source, coef, depth):
+    stride = 1 << (depth - 2)
+    face_set = sheet_faces(coef, stride)
     estimate, residual, update = sheet_smooth(source, face_set)
     if depth == LEVELS - 1:
         return estimate
     residual = residual - sheet_apply(update, face_set)
-    left_down, right_down, left_up, right_up = (ref[...] for ref in matrices[0])
-    coarse_source = 4.0 * times_right(times_left(left_down, residual), right_down)
-    coarse_coef = times_right(times_left(left_down, coef), right_down)
-    coarse_shape = tuple(count // 2 for count in shape)
-    correction = sheet_cycle(coarse_source, coarse_coef, coarse_shape, depth + 1, matrices[1:])
-    estimate = estimate + times_left(left_up, times_right(correction, right_up))
+    coarse_source = (4.0 / 8.0) * sheet_down(residual, stride)
+    correction = sheet_cycle(coarse_source, 0.125 * sheet_down(coef, stride), depth + 1)
+    estimate = estimate + sheet_up(correction, stride)
     return sheet_smooth(source - sheet_apply(estimate, face_set), face_set, estimate)[0]
 
 
@@ -427,22 +449,6 @@
 
 def table(shape):
     return np.arange(shape[0])[:, None], np.arange(shape[1])[None, :]
-
-
-def sheet_matrices(fine_shape, lanes):
-    z_cells, y_cells, x_cells = fine_shape
-    rows, coarse_rows = z_cells * y_cells, z_cells * y_cells // 4
-    half = y_cells // 2
-    coarse, fine = table((coarse_rows, rows))
-    same_z = coarse // half == fine // y_cells // 2
-    left_down = np.where(same_z & (coarse % half == fine % y_cells // 2), 0.25, 0.0)
-    fine, coarse = table((lanes, 128))
-    right_down = np.where((fine // 2 == coarse) & (fine < x_cells), 0.5, 0.0)
-    fine, coarse = table((rows, coarse_rows))
-    left_up = weight(fine // y_cells, coarse // half) * weight(fine % y_cells, coarse % half)
-    coarse, fine = table((128, lanes))
-    right_up = np.where((fine < x_cells) & (coarse < x_cells // 2), weight(fine, coarse), 0.0)
-    return [matrix.astype(BF16) for matrix in (left_down, right_down, left_up, right_up)]
 
 
 def pair_rows_matrix(z_pairs, y_cells):
@@ -498,23 +504,25 @@
     return lax.broadcasted_iota(jnp.int32, shape, len(shape) - 1)
 
 
-def start_kernel(source, coef, both, side):
-    own_y = source.shape[1]
-    first = jnp.where(lax.axis_index("gy") == 0, own_y - HALO_Y, 0)
-    rows = pl.ds(pl.multiple_of(first, HALO_Y), HALO_Y)
-    for which, ref in enumerate((source, coef)):
-        both[which] = ref[...]
-        side[which] = ref[:, rows]
-
-
-def pack_x_kernel(own, side, x_a, x_b):
-    _, planes, own_y, _ = own.shape
+def near_rows(value):
+    first = jnp.where(lax.axis_index("gy") == 0, 0, value.shape[-2] - HALO_Y)
+    return pl.ds(pl.multiple_of(first, HALO_Y), HALO_Y)
+
+
+def start_kernel(source, coef, both, x_a, x_b, done):
+    _, planes, own_y, _ = both.shape
+    copies = [
+        pltpu.make_async_copy(ref, both.at[which], done.at[which]) for which, ref in enumerate((source, coef))
+    ]
+    for copy in copies:
+        copy.start()
     x_even = lax.axis_index("gx") % 2 == 0
-    lane = lanes_of((own_y + HALO_Y, 128))
-    for which in range(2):
+    lane = lanes_of((own_y, 128))
+    for which, copy in enumerate(copies):
+        copy.wait()
         right = left = jnp.zeros(lane.shape, F32)
         for plane in range(planes):
-            value = jnp.concatenate([own[which, plane], side[which, plane]], axis=0)
+            value = both[which, plane]
             slot = (lane >= 8 * plane) & (lane < 8 * plane + 8)
             right = jnp.where(slot, turned(value, 8 * plane + 8, 1), right)
             left = jnp.where(slot, turned(value, 8 * plane, 1), left)
@@ -526,66 +534,80 @@
     return jnp.where(flag, value, 0.0)
 
 
-def x_halos(x_a, x_b, which, x_count):
+def x_halos(x_a, x_b, x_count):
     x_index = lax.axis_index("gx")
     x_even = x_index % 2 == 0
-    right = kept(x_index < x_count - 1, jnp.where(x_even, x_a[which], x_b[which]))
-    left = kept(x_index > 0, jnp.where(x_even, x_b[which], x_a[which]))
+    right = kept(x_index < x_count - 1, jnp.where(x_even, x_a, x_b))
+    left = kept(x_index > 0, jnp.where(x_even, x_b, x_a))
     return right, left
 
 
-def pack_z_kernel(x_count, own, side, x_a, x_b, z_a, z_b):
+def pack_z_kernel(x_count, own, x_a, x_b, z_a, z_b):
     _, planes, own_y, _ = own.shape
     z_even = lax.axis_index("gz") % 2 == 0
-    lane = lanes_of((own_y + HALO_Y, 128))
+    lane = lanes_of((own_y, 128))
     skip = 8 * (planes - HALO_Z)
-    for which in range(2):
-        right, left = x_halos(x_a, x_b, which, x_count)
+    at = 0
+    for which, count in enumerate(SENT_Z):
+        right, left = x_halos(x_a[which], x_b[which], x_count)
         bottom = jnp.where(lane < 64, right, turned(left, 64, 1))
         top = jnp.where(lane < 64, turned(right, -skip, 1), turned(left, 64 - skip, 1))
         for target, is_top in ((z_a, z_even), (z_b, jnp.logical_not(z_even))):
-            first = jnp.where(is_top, planes - HALO_Z, 0)
-            target[which, :HALO_Z, :own_y] = own[which, pl.ds(first, HALO_Z)]
-            target[which, :HALO_Z, own_y:] = side[which, pl.ds(first, HALO_Z)]
-            target[which, HALO_Z] = jnp.where(is_top, top, bottom)
-
-
-def fill_window(own, side, got, source, coef, x_count, z_count):
-    x_a, x_b, z_a, z_b = got
+            first = jnp.where(is_top, planes - count, 0)
+            target[pl.ds(at, count)] = own[which, pl.ds(first, count)]
+            target[sum(SENT_Z) + which] = jnp.where(is_top, top, bottom)
+        at += count
+
+
+def fill_window(own, got, far, source, coef, x_count, z_count):
     _, planes, own_y, _ = own.shape
     rows = own_y + HALO_Y
     z_index = lax.axis_index("gz")
     z_even = z_index % 2 == 0
-    above_at, below_at = HALO_Z + planes, 0
+    above_at = HALO_Z + planes
     lane = lanes_of((rows, 128))
+    window = source.shape[1:]
+
+    def joined(ref, other, place):
+        return jnp.concatenate([ref[place], other[(*place, near_rows(other))]], axis=0)
 
     def edges(right, left, right_shift, left_shift):
         value = jnp.where(lane < 8, turned(right, -right_shift, 1), turned(left, 120 - left_shift, 1))
         return jnp.where((lane < 8) | (lane >= 120), value, 0.0)
 
-    for which, target in enumerate((source, coef)):
+    sent_at = 0
+    for which, (target, count) in enumerate(zip((source, coef), SENT_Z)):
         target[pl.ds(HALO_Z, planes), :own_y, :128] = own[which]
-        target[pl.ds(HALO_Z, planes), own_y:, :128] = side[which]
-        right, left = x_halos(x_a, x_b, which, x_count)
+        target[pl.ds(HALO_Z, planes), own_y:, :128] = far[0][which, :, near_rows(far[0])]
+        x_a, x_b = (joined(got[index], far[1 + index], (which,)) for index in (0, 1))
+        right, left = x_halos(x_a, x_b, x_count)
         for plane in range(planes):
             target[HALO_Z + plane, :, 128:] = edges(right, left, 8 * plane, 8 * plane)
-        for at, flag, is_a in (
-            (above_at, z_index < z_count - 1, z_even),
-            (below_at, z_index > 0, jnp.logical_not(z_even)),
+        for is_above, flag, is_a in (
+            (True, z_index < z_count - 1, z_even),
+            (False, z_index > 0, jnp.logical_not(z_even)),
         ):
-            for plane in range(HALO_Z):
-                target[at + plane, :, :128] = kept(flag, jnp.where(is_a, z_a[which, plane], z_b[which, plane]))
-            packed = kept(flag, jnp.where(is_a, z_a[which, HALO_Z], z_b[which, HALO_Z]))
-            for plane in range(HALO_Z):
-                target[at + plane, :, 128:] = edges(packed, packed, 8 * plane, 64 + 8 * plane)
-    coef[pl.ds(above_at + HALO_Z, 1)] = jnp.zeros((1,) + coef.shape[1:], F32)
+
+            def taken(place):
+                by_a, by_b = (joined(got[index], far[1 + index], (place,)) for index in (2, 3))
+                return kept(flag, jnp.where(is_a, by_a, by_b))
+
+            packed = taken(sum(SENT_Z) + which)
+            for plane in range(count):
+                slot = plane if is_above else HALO_Z - count + plane
+                at = above_at + slot if is_above else slot
+                target[at, :, :128] = taken(sent_at + plane)
+                target[at, :, 128:] = edges(packed, packed, 8 * slot, 64 + 8 * slot)
+        for at in (*range(HALO_Z - count), *range(above_at + count, target.shape[0])):
+            target[at] = jnp.zeros(window, F32)
+        sent_at += count
 
 
 def first_kernel(counts, *refs):
-    own, side, got = refs[0], refs[1], refs[2:6]
-    left, right_source, right_coef, message, source, coef, estimate = refs[6:13]
-    *faces, residual, update, pair_source, pair_coef = refs[13:]
-    fill_window(own, side, got, source, coef, *counts)
+    own, got, far = refs[0], refs[1:5], refs[5:10]
+    left, right_source, right_coef, message, source, coef, estimate = refs[10:17]
+    *faces, residual, update, pair_source, pair_coef = refs[17:]
+    fill_window(own, got, far, source, coef, *counts)
     planes, rows, lanes = source.shape
     own_y = rows - HALO_Y
     plane_faces(coef, faces, 0, planes, link_mask(rows, lanes), None, source, update)
@@ -618,8 +640,7 @@
     for copy in copies:
         copy.start()
     up_left, up_right = held[:2]
-    mid_refs = held[2:6]
-    sheet_refs = held[6:]
+    mid_refs = held[2:]
     mid_source, mid_coef, mid_residual, mid_update, mid_estimate, mid_correction = scratch[:6]
     mid_faces = scratch[6:11]
     pairs, wide, residual, update, current = scratch[11:16]
@@ -669,8 +690,8 @@
             pairs[pl.ds(pair * mid_y, mid_y)] = ref[low] + ref[low + 1]
         sheets.append(scale * times_right(times_left(left_down[...], pairs[...]), right_down[...]))
     shape = (mid_z // 2, mid_y // 2, mid_x // 2)
-    matrices = [sheet_refs[index : index + 4] for index in range(0, len(sheet_refs), 4)]
-    correction = sheet_cycle(sheets[0], sheets[1], shape, 2, matrices)
+    correction = sheet_cycle(sheets[0].reshape(shape), sheets[1].reshape(shape), 2)
+    correction = correction.reshape(mid_z * mid_y // 4, mid_x // 2)
 
     raised = times_left(mid_left_up[...], times_right(correction, mid_right_up[...]))
     mid_correction[pl.ds(1, mid_z // 2)] = raised.reshape(mid_z // 2, mid_y, mid_x)
@@ -744,16 +765,21 @@
         )(*arguments, *far_arguments)
 
     core_pairs = swap_pairs(y_count, False)
-    shapes = [(2, own_z, own_y, own_x), (2, own_z, HALO_Y, own_x)]
-    both, side = call(start_kernel, "start", 4, (right_side, coefficient), shapes, [])
-    blocks = (both, swapped(side, "gy", [core_pairs]))
     swaps = [[swap_pairs(count, odd) for odd in (False, True)] for count in (x_count, z_count)]
-    sent = call(pack_x_kernel, "pack_x", 4, blocks, [(2, rows, 128)] * 2, [])
+    both, *sent = call(
+        start_kernel,
+        "start",
+        4,
+        (),
+        [(2, own_z, own_y, own_x)] + [(2, own_y, 128)] * 2,
+        [pltpu.SemaphoreType.DMA((2,))],
+        (right_side, coefficient),
+    )
     got = [swapped(value, "gx", [pairs]) for value, pairs in zip(sent, swaps[0])]
-    sent = call(
-        functools.partial(pack_z_kernel, x_count), "pack_z", 4, blocks + tuple(got), [(2, HALO_Z + 1, rows, 128)] * 2, []
-    )
+    z_shape = (sum(SENT_Z) + 2, own_y, 128)
+    sent = call(functools.partial(pack_z_kernel, x_count), "pack_z", 4, (both, *got), [z_shape] * 2, [])
     got += [swapped(value, "gz", [pairs]) for value, pairs in zip(sent, swaps[1])]
+    far = [swapped(value, "gy", [core_pairs]) for value in (both, *got)]
 
     window, padded = (planes, rows, lanes), (planes + 1, rows, lanes)
     down = own_down_matrices(own_z // 2, own_y, own_x)
@@ -761,7 +787,7 @@
         functools.partial(first_kernel, (x_count, z_count)),
         "first",
         12,
-        (*blocks, *got, *down),
+        (both, *got, *far, *down),
         [(own_z * own_y // 4, own_x), window, padded, window],
         [window] * 6 + [padded] + [(own_z * own_y // 2, own_x)] * 2,
     )
@@ -787,13 +813,8 @@
     mid_up = plane_up_matrices(
         mid[0] // 2, np.arange(mid[1]), mid[1] // 2, np.arange(mid[2]), mid[2] // 2
     )
-    shape = tuple(count // 2 for count in mid)
-    sheets = []
-    for level in range(2, LEVELS - 1):
-        sheets += sheet_matrices(shape, 128)
-        shape = tuple(count // 2 for count in shape)
     mid_padded = (mid[0] + 2 * PAD, mid[1], mid[2])
-    matrices = [*up, *mid_down, *mid_up, *sheets]
+    matrices = [*up, *mid_down, *mid_up]
     held = [pltpu.VMEM(item.shape[1 if item.ndim == 3 else 0 :], BF16) for item in matrices]
     solution, residual = call(
         functools.partial(second_kernel, counts, len(matrices)),

time: 59.6 us -> 58 us (0.973)
  waiting for transfers between devices: 14.6 us -> 13 us
  starting transfers between devices: 21.5 us -> 22.5 us
  Pallas kernels: 20.5 us -> 19.6 us
    ppermute x15 -> x19, waiting for transfers between devices: 14.6 us -> 13 us  [swapped(): return lax.ppermute(value, axes, list(enumerate(places)))]
    ppermute x15 -> x19, starting transfers between devices: 21.5 us -> 22.5 us  [swapped(): return lax.ppermute(value, axes, list(enumerate(places)))]
    pallas_call x5 -> x4, Pallas kernels: 20.5 us -> 19.6 us  [call(): pl.pallas_call(kernel, out_shape=tuple((jax.ShapeDtypeStruct(shape, F32)...]
    unnamed x36 -> x22, local copies, waits for them, and re-layouts: 1.88 us -> 1.85 us
  transfers between devices with their start and end apart: 15 -> 19, of which waited for: 8 -> 9; matrix products, arithmetic and copies ran while one was open for 0% -> 0% of each run, Pallas kernels for 0% -> 0%
where the time goes in v6:
time: 58 us; the launch traced here: 57.9 us
  starting transfers between devices  22.5 us (39%)
  Pallas kernels  19.6 us (34%)
  waiting for transfers between devices  13 us (22%)
  local copies, waits for them, and re-layouts  1.85 us (3%)
  between operations  0.8 us (1%)
    ppermute x19, starting transfers between devices, swapped(): return lax.ppermute(value, axes, list(enumerate(places)))  22.5 us
    pallas_call x4, Pallas kernels, call(): pl.pallas_call(kernel, out_shape=tuple((jax.ShapeDtypeStruct(shape, F32)...  19.6 us
    ppermute x19, waiting for transfers between devices, swapped(): return lax.ppermute(value, axes, list(enumerate(places)))  13 us
    unnamed x22, local copies, waits for them, and re-layouts  1.85 us
  transfers between devices with their start and end apart: 19, of which 9 were waited for; matrix products, arithmetic and copies ran while one was open for 0% of the time, Pallas kernels for 0%

profile of v6, /device:TPU:0, one launch (start us, length us, event | category | flops | bytes accessed | tf_op | source)
XLA Modules:
  0.0 57.9 jit_solution(15219686884567844407)
XLA Ops:
  0.6 0.9 %copy-done.2 = f32[1,16,16,128]{3,2,1,0:T(8,128)S(1)} copy-done((f32[1,16,16,128]{3,2,1,0:T(8,128)S(1)}, f32[1,16,16,128]{3,2,1,0:T(8,128)}, u32[]{:S(2)}) %copy-start.2) | copy-done | bytes 131096
  1.5 0.9 %copy-done.3 = f32[16,16,128]{2,1,0:T(8,128)S(1)} copy-done((f32[16,16,128]{2,1,0:T(8,128)S(1)}, f32[16,16,128]{2,1,0:T(8,128)}, u32[]{:S(2)}) %copy-start.3) | copy-done | bytes 131096
  2.4 0.6 %start.1 = (f32[2,16,16,128]{3,2,1,0:T(8,128)S(1)}, f32[2,16,128]{2,1,0:T(8,128)S(1)}, f32[2,16,128]{2,1,0:T(8,128)S(1)}) custom-call(f32[16,16,128]{2,1,0:T(8,128)S(1)} %bitcast.7, f32[16,16,128]{2,1,0:T(8,128)S(1)} %copy-done.3), custom_call_target="tpu_custom_call" | custom-call | tf_op jit(solution)/shard_map/start/pallas_call | solution.py:757
  3.0 3.0 %collective-permute-start = (f32[2,16,128]{2,1,0:T(8,128)S(1)}, f32[2,16,128]{2,1,0:T(8,128)S(1)}, u32[]{:S(2)}, u32[]{:S(2)}) collective-permute-start(f32[2,16,128]{2,1,0:T(8,128)S(1)} %get-tuple-element.14), channel_id=1, source_target_pairs={{0,8},{8,0},{16,24},{24,16},{1,9},{9,1},{17,25},{25,17},{2,10},{10... | collective-permute-start | bytes 49160 | tf_op jit(solution)/shard_map/ppermute | solution.py:494
  6.0 0.7 %collective-permute-start.1 = (f32[2,16,128]{2,1,0:T(8,128)S(1)}, f32[2,16,128]{2,1,0:T(8,128)S(1)}, u32[]{:S(2)}, u32[]{:S(2)}) collective-permute-start(f32[2,16,128]{2,1,0:T(8,128)S(1)} %get-tuple-element.15), channel_id=1, source_target_pairs={{0,0},{8,16},{16,8},{24,24},{1,1},{9,17},{17,9},{25,25},{2,2},{10,... | collective-permute-start | bytes 49160 | tf_op jit(solution)/shard_map/ppermute | solution.py:494
  6.8 0.9 %collective-permute-done.x_a.refs_1_ = f32[2,16,128]{2,1,0:T(8,128)S(1)} collective-permute-done((f32[2,16,128]{2,1,0:T(8,128)S(1)}, f32[2,16,128]{2,1,0:T(8,128)S(1)}, u32[]{:S(2)}, u32[]{:S(2)}) %collective-permute-start) | collective-permute-done | bytes 16416 | tf_op jit(solution)/shard_map/ppermute | solution.py:494
  7.9 2.1 %collective-permute-start.2 = (f32[15,16,128]{2,1,0:T(8,128)S(1)}, f32[15,16,128]{2,1,0:T(8,128)S(1)}, u32[]{:S(2)}, u32[]{:S(2)}) collective-permute-start(f32[15,16,128]{2,1,0:T(8,128)S(1)} %get-tuple-element.16), channel_id=1, source_target_pairs={{0,1},{1,0},{2,3},{3,2},{4,5},{5,4},{6,7},{7,6},{8,9},{9,8},{10,11... | collective-permute-start | bytes 368648 | tf_op jit(solution)/shard_map/ppermute | solution.py:494
  10.0 0.8 %collective-permute-start.3 = (f32[15,16,128]{2,1,0:T(8,128)S(1)}, f32[15,16,128]{2,1,0:T(8,128)S(1)}, u32[]{:S(2)}, u32[]{:S(2)}) collective-permute-start(f32[15,16,128]{2,1,0:T(8,128)S(1)} %get-tuple-element.17), channel_id=1, source_target_pairs={{0,0},{1,2},{2,1},{3,3},{4,4},{5,6},{6,5},{7,7},{8,8},{9,10},{10,9... | collective-permute-start | bytes 368648 | tf_op jit(solution)/shard_map/ppermute | solution.py:494
  10.8 2.1 %collective-permute-done.2.refs_3_ = f32[15,16,128]{2,1,0:T(8,128)S(1)} collective-permute-done((f32[15,16,128]{2,1,0:T(8,128)S(1)}, f32[15,16,128]{2,1,0:T(8,128)S(1)}, u32[]{:S(2)}, u32[]{:S(2)}) %collective-permute-start.2) | collective-permute-done | bytes 122912 | tf_op jit(solution)/shard_map/ppermute | solution.py:494
  13.9 0.7 %collective-permute-done.5.refs_6_ = f32[2,16,128]{2,1,0:T(8,128)S(1)} collective-permute-done((f32[2,16,128]{2,1,0:T(8,128)S(1)}, f32[2,16,128]{2,1,0:T(8,128)S(1)}, u32[]{:S(2)}, u32[]{:S(2)}) %collective-permute-start.5) | collective-permute-done | bytes 16416 | tf_op jit(solution)/shard_map/ppermute | solution.py:494
  14.8 4.4 %first.1 = (f32[64,128]{1,0:T(8,128)S(1)}, f32[32,24,256]{2,1,0:T(8,128)S(1)}, f32[33,24,256]{2,1,0:T(8,128)S(1)}, f32[32,24,256]{2,1,0:T(8,128)S(1)}) custom-call(f32[2,16,16,128]{3,2,1,0:T(8,128)S(1)} %get-tuple-element.13.own.refs_0_, f32[2,16,128]{2,1,0:T(8,128)S(1)} %collective-permute-done.x_a.refs_1_, ...), custom_call_target="tpu_custom_call" | custom-call | tf_op jit(solution)/shard_map/first/pallas_call | solution.py:757
  19.1 4.1 %collective-permute-start.11 = (f32[64,128]{1,0:T(8,128)S(1)}, f32[64,128]{1,0:T(8,128)S(1)}, u32[]{:S(2)}, u32[]{:S(2)}) collective-permute-start(f32[64,128]{1,0:T(8,128)S(1)} %get-tuple-element.18), channel_id=1, source_target_pairs={{0,3},{1,2},{2,1},{3,0},{4,7},{5,6},{6,5},{7,4},{8,11},{9,10},{10,... | collective-permute-start | bytes 98312 | tf_op jit(solution)/shard_map/ppermute | solution.py:494
  23.2 2.5 %collective-permute-start.10 = (f32[64,128]{1,0:T(8,128)S(1)}, f32[64,128]{1,0:T(8,128)S(1)}, u32[]{:S(2)}, u32[]{:S(2)}) collective-permute-start(f32[64,128]{1,0:T(8,128)S(1)} %get-tuple-element.18), channel_id=1, source_target_pairs={{0,2},{1,3},{2,0},{3,1},{4,6},{5,7},{6,4},{7,5},{8,10},{9,11},{10,... | collective-permute-start | bytes 98312 | tf_op jit(solution)/shard_map/ppermute | solution.py:494
  25.6 0.5 collective-permute-start.9
  26.2 1.8 %collective-permute-done.10 = f32[64,128]{1,0:T(8,128)S(1)} collective-permute-done((f32[64,128]{1,0:T(8,128)S(1)}, f32[64,128]{1,0:T(8,128)S(1)}, u32[]{:S(2)}, u32[]{:S(2)}) %collective-permute-start.10) | collective-permute-done | bytes 32800 | tf_op jit(solution)/shard_map/ppermute | solution.py:494
  28.0 1.5 %collective-permute-done.9 = f32[64,128]{1,0:T(8,128)S(1)} collective-permute-done((f32[64,128]{1,0:T(8,128)S(1)}, f32[64,128]{1,0:T(8,128)S(1)}, u32[]{:S(2)}, u32[]{:S(2)}) %collective-permute-start.9) | collective-permute-done | bytes 32800 | tf_op jit(solution)/shard_map/ppermute | solution.py:494
  29.6 2.5 %collective-permute-start.14 = (f32[4,64,128]{2,1,0:T(8,128)S(1)}, f32[4,64,128]{2,1,0:T(8,128)S(1)}, u32[]{:S(2)}, u32[]{:S(2)}) collective-permute-start(f32[4,64,128]{2,1,0:T(8,128)S(1)} %pad_maximum_fusion.refs_0_), channel_id=1, source_target_pairs={{0,24},{8,16},{16,8},{24,0},{1,25},{9,17},{17,9},{25,1},{2,26},{10... | collective-permute-start | bytes 393224 | tf_op jit(solution)/shard_map/ppermute | solution.py:494
  32.1 3.8 %collective-permute-start.13 = (f32[4,64,128]{2,1,0:T(8,128)S(1)}, f32[4,64,128]{2,1,0:T(8,128)S(1)}, u32[]{:S(2)}, u32[]{:S(2)}) collective-permute-start(f32[4,64,128]{2,1,0:T(8,128)S(1)} %pad_maximum_fusion.refs_0_), channel_id=1, source_target_pairs={{0,16},{8,24},{16,0},{24,8},{1,17},{9,25},{17,1},{25,9},{2,18},{10... | collective-permute-start | bytes 393224 | tf_op jit(solution)/shard_map/ppermute | solution.py:494
  35.9 1.0 %collective-permute-start.12 = (f32[4,64,128]{2,1,0:T(8,128)S(1)}, f32[4,64,128]{2,1,0:T(8,128)S(1)}, u32[]{:S(2)}, u32[]{:S(2)}) collective-permute-start(f32[4,64,128]{2,1,0:T(8,128)S(1)} %pad_maximum_fusion.refs_0_), channel_id=1, source_target_pairs={{0,8},{8,0},{16,24},{24,16},{1,9},{9,1},{17,25},{25,17},{2,10},{10... | collective-permute-start | bytes 393224 | tf_op jit(solution)/shard_map/ppermute | solution.py:494
  36.9 0.5 collective-permute-start.18
  37.4 2.7 %collective-permute-done.13.refs_2_ = f32[4,64,128]{2,1,0:T(8,128)S(1)} collective-permute-done((f32[4,64,128]{2,1,0:T(8,128)S(1)}, f32[4,64,128]{2,1,0:T(8,128)S(1)}, u32[]{:S(2)}, u32[]{:S(2)}) %collective-permute-start.13) | collective-permute-done | bytes 131104 | tf_op jit(solution)/shard_map/ppermute | solution.py:494
  40.1 1.7 %collective-permute-done.12.refs_1_ = f32[4,64,128]{2,1,0:T(8,128)S(1)} collective-permute-done((f32[4,64,128]{2,1,0:T(8,128)S(1)}, f32[4,64,128]{2,1,0:T(8,128)S(1)}, u32[]{:S(2)}, u32[]{:S(2)}) %collective-permute-start.12) | collective-permute-done | bytes 131104 | tf_op jit(solution)/shard_map/ppermute | solution.py:494
  41.9 1.3 %collective-permute-done.16.refs_5_ = f32[4,64,128]{2,1,0:T(8,128)S(1)} collective-permute-done((f32[4,64,128]{2,1,0:T(8,128)S(1)}, f32[4,64,128]{2,1,0:T(8,128)S(1)}, u32[]{:S(2)}, u32[]{:S(2)}) %collective-permute-start.16) | collective-permute-done | bytes 131104 | tf_op jit(solution)/shard_map/ppermute | solution.py:494
  43.3 14.6 %second.1 = (f32[16,16,128]{2,1,0:T(8,128)}, f32[16,16,128]{2,1,0:T(8,128)}) custom-call(f32[4,64,128]{2,1,0:T(8,128)S(1)} %pad_maximum_fusion.refs_0_, f32[4,64,128]{2,1,0:T(8,128)S(1)} %collective-permute-done.12.refs_1_, f32[4,64,128]{2,1,0:T(8,128)S(1)} %collective-permute-done.13.refs_2_, f32[4,64,128]{2,1,0:T(8,128)S(1)} %collective-permute-done.14.refs_3_, ...), custom_call_target="tpu_custom_call" | custom-call | tf_op jit(solution)/shard_map/second/pallas_call | solution.py:757
  (41 shorter events, 1.4 us)
Async XLA Ops:
  3.0 4.7 %collective-permute-start = (f32[2,16,128]{2,1,0:T(8,128)S(1)}, f32[2,16,128]{2,1,0:T(8,128)S(1)}, u32[]{:S(2)}, u32[]{:S(2)}) collective-permute-start(f32[2,16,128]{2,1,0:T(8,128)S(1)} %get-tuple-element.14), channel_id=1, source_target_pairs={{0,8},{8,0},{16,24},{24,16},{1,9},{9,1},{17,25},{25,17},{2,10},{10... | collective-permute-start | bytes 49160 | tf_op jit(solution)/shard_map/ppermute | solution.py:494
  6.0 1.7 %collective-permute-start.1 = (f32[2,16,128]{2,1,0:T(8,128)S(1)}, f32[2,16,128]{2,1,0:T(8,128)S(1)}, u32[]{:S(2)}, u32[]{:S(2)}) collective-permute-start(f32[2,16,128]{2,1,0:T(8,128)S(1)} %get-tuple-element.15), channel_id=1, source_target_pairs={{0,0},{8,16},{16,8},{24,24},{1,1},{9,17},{17,9},{25,25},{2,2},{10,... | collective-permute-start | bytes 49160 | tf_op jit(solution)/shard_map/ppermute | solution.py:494
  6.7 8.0 %collective-permute-start.4 = (f32[2,16,16,128]{3,2,1,0:T(8,128)S(1)}, f32[2,16,16,128]{3,2,1,0:T(8,128)S(1)}, u32[]{:S(2)}, u32[]{:S(2)}) collective-permute-start(f32[2,16,16,128]{3,2,1,0:T(8,128)S(1)} %get-tuple-element.13.own.refs_0_), channel_id=1, source_target_pairs={{0,4},{4,0},{1,5},{5,1},{2,6},{6,2},{3,7},{7,3},{8,12},{12,8},{9,1... | collective-permute-start | bytes 786440 | tf_op jit(solution)/shard_map/ppermute | solution.py:494
  7.9 5.0 %collective-permute-start.2 = (f32[15,16,128]{2,1,0:T(8,128)S(1)}, f32[15,16,128]{2,1,0:T(8,128)S(1)}, u32[]{:S(2)}, u32[]{:S(2)}) collective-permute-start(f32[15,16,128]{2,1,0:T(8,128)S(1)} %get-tuple-element.16), channel_id=1, source_target_pairs={{0,1},{1,0},{2,3},{3,2},{4,5},{5,4},{6,7},{7,6},{8,9},{9,8},{10,11... | collective-permute-start | bytes 368648 | tf_op jit(solution)/shard_map/ppermute | solution.py:494
  10.0 33.2 %copy-start = (bf16[4,256,256]{2,1,0:T(8,128)(2,1)S(1)}, bf16[4,256,256]{2,1,0:T(8,128)(2,1)}, u32[]{:S(2)}) copy-start(bf16[4,256,256]{2,1,0:T(8,128)(2,1)} %constant.22.clone.refs_12_) | copy-start | bytes 1572868
  10.0 2.9 %collective-permute-start.3 = (f32[15,16,128]{2,1,0:T(8,128)S(1)}, f32[15,16,128]{2,1,0:T(8,128)S(1)}, u32[]{:S(2)}, u32[]{:S(2)}) collective-permute-start(f32[15,16,128]{2,1,0:T(8,128)S(1)} %get-tuple-element.17), channel_id=1, source_target_pairs={{0,0},{1,2},{2,1},{3,3},{4,4},{5,6},{6,5},{7,7},{8,8},{9,10},{10,9... | collective-permute-start | bytes 368648 | tf_op jit(solution)/shard_map/ppermute | solution.py:494
  12.8 1.9 %collective-permute-start.7 = (f32[15,16,128]{2,1,0:T(8,128)S(1)}, f32[15,16,128]{2,1,0:T(8,128)S(1)}, u32[]{:S(2)}, u32[]{:S(2)}) collective-permute-start(f32[15,16,128]{2,1,0:T(8,128)S(1)} %collective-permute-done.2.refs_3_), channel_id=1, source_target_pairs={{0,4},{4,0},{1,5},{5,1},{2,6},{6,2},{3,7},{7,3},{8,12},{12,8},{9,1... | collective-permute-start | bytes 368648 | tf_op jit(solution)/shard_map/ppermute | solution.py:494
  12.9 1.9 %collective-permute-start.8 = (f32[15,16,128]{2,1,0:T(8,128)S(1)}, f32[15,16,128]{2,1,0:T(8,128)S(1)}, u32[]{:S(2)}, u32[]{:S(2)}) collective-permute-start(f32[15,16,128]{2,1,0:T(8,128)S(1)} %collective-permute-done.3.refs_4_), channel_id=1, source_target_pairs={{0,4},{4,0},{1,5},{5,1},{2,6},{6,2},{3,7},{7,3},{8,12},{12,8},{9,1... | collective-permute-start | bytes 368648 | tf_op jit(solution)/shard_map/ppermute | solution.py:494
  13.4 1.2 %collective-permute-start.5 = (f32[2,16,128]{2,1,0:T(8,128)S(1)}, f32[2,16,128]{2,1,0:T(8,128)S(1)}, u32[]{:S(2)}, u32[]{:S(2)}) collective-permute-start(f32[2,16,128]{2,1,0:T(8,128)S(1)} %collective-permute-done.x_a.refs_1_), channel_id=1, source_target_pairs={{0,4},{4,0},{1,5},{5,1},{2,6},{6,2},{3,7},{7,3},{8,12},{12,8},{9,1... | collective-permute-start | bytes 49160 | tf_op jit(solution)/shard_map/ppermute | solution.py:494
  13.4 1.3 %collective-permute-start.6 = (f32[2,16,128]{2,1,0:T(8,128)S(1)}, f32[2,16,128]{2,1,0:T(8,128)S(1)}, u32[]{:S(2)}, u32[]{:S(2)}) collective-permute-start(f32[2,16,128]{2,1,0:T(8,128)S(1)} %collective-permute-done.1.x_b.refs_2_), channel_id=1, source_target_pairs={{0,4},{4,0},{1,5},{5,1},{2,6},{6,2},{3,7},{7,3},{8,12},{12,8},{9,1... | collective-permute-start | bytes 49160 | tf_op jit(solution)/shard_map/ppermute | solution.py:494
  14.8 28.5 %copy-start.1 = (bf16[2,336,224]{2,1,0:T(8,128)(2,1)S(1)}, bf16[2,336,224]{2,1,0:T(8,128)(2,1)}, u32[]{:S(2)}) copy-start(bf16[2,336,224]{2,1,0:T(8,128)(2,1)} %constant.21.clone.refs_11_) | copy-start | bytes 903172
  19.1 7.0 %collective-permute-start.11 = (f32[64,128]{1,0:T(8,128)S(1)}, f32[64,128]{1,0:T(8,128)S(1)}, u32[]{:S(2)}, u32[]{:S(2)}) collective-permute-start(f32[64,128]{1,0:T(8,128)S(1)} %get-tuple-element.18), channel_id=1, source_target_pairs={{0,3},{1,2},{2,1},{3,0},{4,7},{5,6},{6,5},{7,4},{8,11},{9,10},{10,... | collective-permute-start | bytes 98312 | tf_op jit(solution)/shard_map/ppermute | solution.py:494
  23.2 4.8 %collective-permute-start.10 = (f32[64,128]{1,0:T(8,128)S(1)}, f32[64,128]{1,0:T(8,128)S(1)}, u32[]{:S(2)}, u32[]{:S(2)}) collective-permute-start(f32[64,128]{1,0:T(8,128)S(1)} %get-tuple-element.18), channel_id=1, source_target_pairs={{0,2},{1,3},{2,0},{3,1},{4,6},{5,7},{6,4},{7,5},{8,10},{9,11},{10,... | collective-permute-start | bytes 98312 | tf_op jit(solution)/shard_map/ppermute | solution.py:494
  25.6 3.9 %collective-permute-start.9 = (f32[64,128]{1,0:T(8,128)S(1)}, f32[64,128]{1,0:T(8,128)S(1)}, u32[]{:S(2)}, u32[]{:S(2)}) collective-permute-start(f32[64,128]{1,0:T(8,128)S(1)} %get-tuple-element.18), channel_id=1, source_target_pairs={{0,1},{1,0},{2,3},{3,2},{4,5},{5,4},{6,7},{7,6},{8,9},{9,8},{10,11... | collective-permute-start | bytes 98312 | tf_op jit(solution)/shard_map/ppermute | solution.py:494
  29.6 13.7 %copy-start.5 = (bf16[256,128]{1,0:T(8,128)(2,1)S(1)}, bf16[256,128]{1,0:T(8,128)(2,1)}, u32[]{:S(2)}) copy-start(bf16[256,128]{1,0:T(8,128)(2,1)} %constant.25.clone.refs_15_) | copy-start | bytes 196612
  29.6 13.7 %copy-start.6 = (bf16[256,128]{1,0:T(8,128)(2,1)S(1)}, bf16[256,128]{1,0:T(8,128)(2,1)}, u32[]{:S(2)}) copy-start(bf16[256,128]{1,0:T(8,128)(2,1)} %constant.24.clone.refs_14_) | copy-start | bytes 196612
  29.6 13.7 %copy-start.7 = (bf16[128,256]{1,0:T(8,128)(2,1)S(1)}, bf16[128,256]{1,0:T(8,128)(2,1)}, u32[]{:S(2)}) copy-start(bf16[128,256]{1,0:T(8,128)(2,1)} %constant.23.clone.refs_13_) | copy-start | bytes 196612
  29.6 7.3 %collective-permute-start.14 = (f32[4,64,128]{2,1,0:T(8,128)S(1)}, f32[4,64,128]{2,1,0:T(8,128)S(1)}, u32[]{:S(2)}, u32[]{:S(2)}) collective-permute-start(f32[4,64,128]{2,1,0:T(8,128)S(1)} %pad_maximum_fusion.refs_0_), channel_id=1, source_target_pairs={{0,24},{8,16},{16,8},{24,0},{1,25},{9,17},{17,9},{25,1},{2,26},{10... | collective-permute-start | bytes 393224 | tf_op jit(solution)/shard_map/ppermute | solution.py:494
  32.1 8.0 %collective-permute-start.13 = (f32[4,64,128]{2,1,0:T(8,128)S(1)}, f32[4,64,128]{2,1,0:T(8,128)S(1)}, u32[]{:S(2)}, u32[]{:S(2)}) collective-permute-start(f32[4,64,128]{2,1,0:T(8,128)S(1)} %pad_maximum_fusion.refs_0_), channel_id=1, source_target_pairs={{0,16},{8,24},{16,0},{24,8},{1,17},{9,25},{17,1},{25,9},{2,18},{10... | collective-permute-start | bytes 393224 | tf_op jit(solution)/shard_map/ppermute | solution.py:494
  35.9 5.9 %collective-permute-start.12 = (f32[4,64,128]{2,1,0:T(8,128)S(1)}, f32[4,64,128]{2,1,0:T(8,128)S(1)}, u32[]{:S(2)}, u32[]{:S(2)}) collective-permute-start(f32[4,64,128]{2,1,0:T(8,128)S(1)} %pad_maximum_fusion.refs_0_), channel_id=1, source_target_pairs={{0,8},{8,0},{16,24},{24,16},{1,9},{9,1},{17,25},{25,17},{2,10},{10... | collective-permute-start | bytes 393224 | tf_op jit(solution)/shard_map/ppermute | solution.py:494
  36.9 5.0 %collective-permute-start.15 = (f32[4,64,128]{2,1,0:T(8,128)S(1)}, f32[4,64,128]{2,1,0:T(8,128)S(1)}, u32[]{:S(2)}, u32[]{:S(2)}) collective-permute-start(f32[4,64,128]{2,1,0:T(8,128)S(1)} %pad_maximum_fusion.refs_0_), channel_id=1, source_target_pairs={{0,4},{4,0},{1,5},{5,1},{2,6},{6,2},{3,7},{7,3},{8,12},{12,8},{9,1... | collective-permute-start | bytes 393224 | tf_op jit(solution)/shard_map/ppermute | solution.py:494
  36.9 5.0 %collective-permute-start.18 = (f32[4,64,128]{2,1,0:T(8,128)S(1)}, f32[4,64,128]{2,1,0:T(8,128)S(1)}, u32[]{:S(2)}, u32[]{:S(2)}) collective-permute-start(f32[4,64,128]{2,1,0:T(8,128)S(1)} %collective-permute-done.14.refs_3_), channel_id=1, source_target_pairs={{0,4},{4,0},{1,5},{5,1},{2,6},{6,2},{3,7},{7,3},{8,12},{12,8},{9,1... | collective-permute-start | bytes 393224 | tf_op jit(solution)/shard_map/ppermute | solution.py:494
  40.1 1.7 %collective-permute-start.17 = (f32[4,64,128]{2,1,0:T(8,128)S(1)}, f32[4,64,128]{2,1,0:T(8,128)S(1)}, u32[]{:S(2)}, u32[]{:S(2)}) collective-permute-start(f32[4,64,128]{2,1,0:T(8,128)S(1)} %collective-permute-done.13.refs_2_), channel_id=1, source_target_pairs={{0,4},{4,0},{1,5},{5,1},{2,6},{6,2},{3,7},{7,3},{8,12},{12,8},{9,1... | collective-permute-start | bytes 393224 | tf_op jit(solution)/shard_map/ppermute | solution.py:494
  41.9 1.3 %collective-permute-start.16 = (f32[4,64,128]{2,1,0:T(8,128)S(1)}, f32[4,64,128]{2,1,0:T(8,128)S(1)}, u32[]{:S(2)}, u32[]{:S(2)}) collective-permute-start(f32[4,64,128]{2,1,0:T(8,128)S(1)} %collective-permute-done.12.refs_1_), channel_id=1, source_target_pairs={{0,4},{4,0},{1,5},{5,1},{2,6},{6,2},{3,7},{7,3},{8,12},{12,8},{9,1... | collective-permute-start | bytes 393224 | tf_op jit(solution)/shard_map/ppermute | solution.py:494
  (6 other events, 39.5 us)

commit v7 on v6

--- a/solution.py
+++ b/solution.py
@@ -259,7 +259,7 @@
     lax.fori_loop(0, (stop - start) // block, step, carry)
 
 
-def plane_faces(coef, faces, start, stop, link_y, link_x, source, update, block=4):
+def plane_faces(coef, faces, start, stop, link_y, link_x, source=None, update=None, block=4):
     face_z, face_y, face_x, diagonal, inverse = faces
     back_y = None if link_y is None else turned(link_y, 1, 1)
     back_x = None if link_x is None else turned(link_x, 1, 2)
@@ -276,13 +276,13 @@
         down_x = 0.5 * (own + masked(turned(own, 1, 2), back_x))
         total = above + shifted_in(below, above) + up_y + down_y + up_x + down_x
         over = jnp.where(own > 0.0, 1.0 / jnp.where(own > 0.0, total, 1.0), 0.0)
-        first = source[here] * over * first_scale
+        if update is not None:
+            update[here] = source[here] * over * first_scale
         face_z[here] = above
         face_y[here] = masked(up_y, link_y)
         face_x[here] = masked(up_x, link_x)
         diagonal[here] = total
         inverse[here] = over
-        update[here] = first
         return above[-1:]
 
     below = coef[pl.ds(start, 1)]
@@ -542,14 +542,14 @@
     return right, left
 
 
-def pack_z_kernel(x_count, own, x_a, x_b, z_a, z_b):
+def pack_z_kernel(x_count, own, x_edges, z_a, z_b):
     _, planes, own_y, _ = own.shape
     z_even = lax.axis_index("gz") % 2 == 0
     lane = lanes_of((own_y, 128))
     skip = 8 * (planes - HALO_Z)
     at = 0
     for which, count in enumerate(SENT_Z):
-        right, left = x_halos(x_a[which], x_b[which], x_count)
+        right, left = x_halos(x_edges[0, which], x_edges[1, which], x_count)
         bottom = jnp.where(lane < 64, right, turned(left, 64, 1))
         top = jnp.where(lane < 64, turned(right, -skip, 1), turned(left, 64 - skip, 1))
         for target, is_top in ((z_a, z_even), (z_b, jnp.logical_not(z_even))):
@@ -579,7 +579,7 @@
     for which, (target, count) in enumerate(zip((source, coef), SENT_Z)):
         target[pl.ds(HALO_Z, planes), :own_y, :128] = own[which]
         target[pl.ds(HALO_Z, planes), own_y:, :128] = far[0][which, :, near_rows(far[0])]
-        x_a, x_b = (joined(got[index], far[1 + index], (which,)) for index in (0, 1))
+        x_a, x_b = (joined(got[0], far[1], (index, which)) for index in (0, 1))
         right, left = x_halos(x_a, x_b, x_count)
         for plane in range(planes):
             target[HALO_Z + plane, :, 128:] = edges(right, left, 8 * plane, 8 * plane)
@@ -589,7 +589,7 @@
         ):
 
             def taken(place):
-                by_a, by_b = (joined(got[index], far[1 + index], (place,)) for index in (2, 3))
+                by_a, by_b = (joined(got[index], far[1 + index], (place,)) for index in (1, 2))
                 return kept(flag, jnp.where(is_a, by_a, by_b))
 
             packed = taken(sum(SENT_Z) + which)
@@ -604,9 +604,9 @@
 
 
 def first_kernel(counts, *refs):
-    own, got, far = refs[0], refs[1:5], refs[5:10]
-    left, right_source, right_coef, message, source, coef, estimate = refs[10:17]
-    *faces, residual, update, pair_source, pair_coef = refs[17:]
+    own, got, far = refs[0], refs[1:4], refs[4:8]
+    left, right_source, right_coef, message, source, coef, estimate = refs[8:15]
+    *faces, residual, update, pair_source, pair_coef = refs[15:]
     fill_window(own, got, far, source, coef, *counts)
     planes, rows, lanes = source.shape
     own_y = rows - HALO_Y
@@ -624,11 +624,16 @@
     )
 
 
+def faces_kernel(coef, late, *faces):
+    planes, rows, lanes = faces[0].shape
+    plane_faces(coef, faces, 0, planes, link_mask(rows, lanes), None)
+
+
 def second_kernel(counts, matrix_count, *refs):
     x_count, y_count, z_count = counts
     x_index, y_index, z_index = (lax.axis_index(axis) for axis in ("gx", "gy", "gz"))
     halves, refs = (refs[:x_count], refs[x_count : 2 * x_count]), refs[2 * x_count :]
-    (source, coef, estimate), refs = refs[:3], refs[3:]
+    (source, estimate, *faces), refs = refs[:7], refs[7:]
     brought, refs = refs[:matrix_count], refs[matrix_count:]
     (solution, residual_out), scratch = refs[:2], refs[2:]
     held, scratch, done = scratch[:matrix_count], scratch[matrix_count:-1], scratch[-1]
@@ -644,7 +649,6 @@
     mid_source, mid_coef, mid_residual, mid_update, mid_estimate, mid_correction = scratch[:6]
     mid_faces = scratch[6:11]
     pairs, wide, residual, update, current = scratch[11:16]
-    faces = scratch[16:]
 
     planes, rows, lanes = source.shape
     own_y = rows - HALO_Y
@@ -717,7 +721,6 @@
         mid_faces, [clipped(4), clipped(4)], mid_source, mid_residual, mid_update, mid_estimate, False
     )
 
-    plane_faces(coef, faces, 0, planes, link_mask(rows, lanes), None, source, update)
     coarse_planes = up_left.shape[1] // mid_y
     near = mid_estimate[pl.ds(z_index * 8, coarse_planes)].reshape(coarse_planes * mid_y, mid_x)
     raised = times_left(up_left[...], times_right(near, up_right[...]))
@@ -760,30 +763,32 @@
             in_specs=[vmem] * len(arguments) + [far] * len(far_arguments),
             out_specs=(vmem,) * len(shapes),
             scratch_shapes=[pltpu.VMEM(item, F32) if isinstance(item, tuple) else item for item in scratch],
-            compiler_params=pltpu.CompilerParams(vmem_limit_bytes=room * 1024 * 1024),
+            compiler_params=pltpu.CompilerParams(vmem_limit_bytes=int(room * 1024 * 1024)),
             name=name,
         )(*arguments, *far_arguments)
 
     core_pairs = swap_pairs(y_count, False)
-    swaps = [[swap_pairs(count, odd) for odd in (False, True)] for count in (x_count, z_count)]
+    z_swaps = [swap_pairs(z_count, odd) for odd in (False, True)]
     both, *sent = call(
         start_kernel,
         "start",
-        4,
+        60.1,
         (),
         [(2, own_z, own_y, own_x)] + [(2, own_y, 128)] * 2,
         [pltpu.SemaphoreType.DMA((2,))],
         (right_side, coefficient),
     )
-    got = [swapped(value, "gx", [pairs]) for value, pairs in zip(sent, swaps[0])]
+    passed = swapped(sent[1], "gx", [[index ^ 2 for index in range(x_count)]])
+    edges = swapped(jnp.stack([sent[0], passed]), "gx", [swap_pairs(x_count, False)])
+    got = [edges]
     z_shape = (sum(SENT_Z) + 2, own_y, 128)
     sent = call(functools.partial(pack_z_kernel, x_count), "pack_z", 4, (both, *got), [z_shape] * 2, [])
-    got += [swapped(value, "gz", [pairs]) for value, pairs in zip(sent, swaps[1])]
+    got += [swapped(value, "gz", [pairs]) for value, pairs in zip(sent, z_swaps)]
     far = [swapped(value, "gy", [core_pairs]) for value in (both, *got)]
 
     window, padded = (planes, rows, lanes), (planes + 1, rows, lanes)
     down = own_down_matrices(own_z // 2, own_y, own_x)
-    message, *windows = call(
+    message, source, coef, estimate = call(
         functools.partial(first_kernel, (x_count, z_count)),
         "first",
         12,
@@ -798,6 +803,7 @@
         ]
 
     mine = jnp.stack([message] + from_others(message, "gz", z_count))
+    faces = call(faces_kernel, "faces", 4, (coef, mine[1, :8]), [window] * 5, [])
     parts = [mine] + from_others(mine, "gx", x_count)
     parts += [swapped(part, "gy", [core_pairs]) for part in parts]
 
@@ -820,14 +826,13 @@
         functools.partial(second_kernel, counts, len(matrices)),
         "second",
         28,
-        (*parts, *windows),
+        (*parts, source, estimate, *faces),
         [(own_z, own_y, own_x)] * 2,
         held
         + [mid_padded] * 5
         + [(mid[0] // 2 + 2, mid[1], mid[2])]
         + [mid_padded] * 5
         + [(mid[0] // 2 * mid[1], mid[2]), (coarse_planes, rows, lanes), window, padded, padded]
-        + [window] * 5
         + [pltpu.SemaphoreType.DMA((len(matrices),))],
         far_arguments=[jnp.asarray(item) for item in matrices],
     )

time: 58 us -> 60.7 us (1.047)
  waiting for transfers between devices: 13 us -> 17.2 us
  starting transfers between devices: 22.5 us -> 20 us
  Pallas kernels: 19.6 us -> 20.7 us
  local copies, waits for them, and re-layouts: 1.85 us -> 0.99 us
  other arithmetic: 0.01 us -> 0.74 us
    ppermute x19 -> x18, waiting for transfers between devices: 13 us -> 17.2 us  [swapped(): return lax.ppermute(value, axes, list(enumerate(places)))]
    ppermute x19 -> x18, starting transfers between devices: 22.5 us -> 20 us  [swapped(): return lax.ppermute(value, axes, list(enumerate(places)))]
    pallas_call x4 -> x5, Pallas kernels: 19.6 us -> 20.7 us  [call(): pl.pallas_call(kernel, out_shape=tuple((jax.ShapeDtypeStruct(shape, F32)...]
    unnamed x22, local copies, waits for them, and re-layouts: 1.85 us -> 0.99 us
    another operation x0 -> x1, other arithmetic: none -> 0.73 us  [near_local(): jnp.stack([sent[0], passed])]
  transfers between devices with their start and end apart: 19 -> 18, of which waited for: 9 -> 8; matrix products, arithmetic and copies ran while one was open for 0% -> 0% of each run, Pallas kernels for 0% -> 2%
where the time goes in v7:
time: 60.7 us; the launch traced here: 60.4 us
  Pallas kernels  20.7 us (34%)
  starting transfers between devices  20 us (33%)
  waiting for transfers between devices  17.2 us (28%)
  local copies, waits for them, and re-layouts  0.99 us (2%)
  between operations  0.81 us (1%)
  other arithmetic  0.74 us (1%)
    pallas_call x5, Pallas kernels, call(): pl.pallas_call(kernel, out_shape=tuple((jax.ShapeDtypeStruct(shape, F32)...  20.7 us
    ppermute x18, starting transfers between devices, swapped(): return lax.ppermute(value, axes, list(enumerate(places)))  20 us
    ppermute x18, waiting for transfers between devices, swapped(): return lax.ppermute(value, axes, list(enumerate(places)))  17.2 us
  transfers between devices with their start and end apart: 18, of which 8 were waited for; matrix products, arithmetic and copies ran while one was open for 0% of the time, Pallas kernels for 2%

profile of v7, /device:TPU:0, one launch (start us, length us, event | category | flops | bytes accessed | tf_op | source)
XLA Modules:
  0.0 60.4 jit_solution(2916622881341560516)
XLA Ops:
  0.6 1.8 %start.1 = (f32[2,16,16,128]{3,2,1,0:T(8,128)}, f32[2,16,128]{2,1,0:T(8,128)}, f32[2,16,128]{2,1,0:T(8,128)}) custom-call(f32[16,16,128]{2,1,0:T(8,128)} %bitcast.12, f32[16,16,128]{2,1,0:T(8,128)} %coef.1), custom_call_target="tpu_custom_call" | custom-call | tf_op jit(solution)/shard_map/start/pallas_call | solution.py:760
  2.4 3.0 %collective-permute-start = (f32[2,16,128]{2,1,0:T(8,128)}, f32[2,16,128]{2,1,0:T(8,128)S(1)}, u32[]{:S(2)}, u32[]{:S(2)}) collective-permute-start(f32[2,16,128]{2,1,0:T(8,128)} %get-tuple-element.20), channel_id=1, source_target_pairs={{0,16},{8,24},{16,0},{24,8},{1,17},{9,25},{17,1},{25,9},{2,18},{10... | collective-permute-start | bytes 49160 | tf_op jit(solution)/shard_map/ppermute | solution.py:494
  5.5 1.9 %collective-permute-done = f32[2,16,128]{2,1,0:T(8,128)S(1)} collective-permute-done((f32[2,16,128]{2,1,0:T(8,128)}, f32[2,16,128]{2,1,0:T(8,128)S(1)}, u32[]{:S(2)}, u32[]{:S(2)}) %collective-permute-start) | collective-permute-done | bytes 16416 | tf_op jit(solution)/shard_map/ppermute | solution.py:494
  7.4 0.7 %pad_maximum_fusion.1 = f32[2,2,16,128]{3,2,1,0:T(8,128)S(1)} fusion(f32[1,2,16,128]{3,2,1,0:T(8,128)S(1)} %bitcast.18, f32[1,2,16,128]{3,2,1,0:T(8,128)} %bitcast.17), kind=kLoop, calls=%fused_computation.1 | loop fusion | flops 8192 | bytes 65536 | tf_op jit(solution)/shard_map/stack | solution.py:782
  8.1 2.0 %collective-permute-start.1 = (f32[2,2,16,128]{3,2,1,0:T(8,128)S(1)}, f32[2,2,16,128]{3,2,1,0:T(8,128)S(1)}, u32[]{:S(2)}, u32[]{:S(2)}) collective-permute-start(f32[2,2,16,128]{3,2,1,0:T(8,128)S(1)} %pad_maximum_fusion.1), channel_id=1, source_target_pairs={{0,8},{8,0},{16,24},{24,16},{1,9},{9,1},{17,25},{25,17},{2,10},{10... | collective-permute-start | bytes 98312 | tf_op jit(solution)/shard_map/ppermute | solution.py:494
  10.1 1.9 %collective-permute-done.1.x_edges.refs_1_ = f32[2,2,16,128]{3,2,1,0:T(8,128)S(1)} collective-permute-done((f32[2,2,16,128]{3,2,1,0:T(8,128)S(1)}, f32[2,2,16,128]{3,2,1,0:T(8,128)S(1)}, u32[]{:S(2)}, u32[]{:S(2)}) %collective-permute-start.1) | collective-permute-done | bytes 32800 | tf_op jit(solution)/shard_map/ppermute | solution.py:494
  12.0 0.9 %copy-done = f32[2,16,16,128]{3,2,1,0:T(8,128)S(1)} copy-done((f32[2,16,16,128]{3,2,1,0:T(8,128)S(1)}, f32[2,16,16,128]{3,2,1,0:T(8,128)}, u32[]{:S(2)}) %copy-start) | copy-done | bytes 262168
  13.1 2.1 %collective-permute-start.2 = (f32[15,16,128]{2,1,0:T(8,128)S(1)}, f32[15,16,128]{2,1,0:T(8,128)S(1)}, u32[]{:S(2)}, u32[]{:S(2)}) collective-permute-start(f32[15,16,128]{2,1,0:T(8,128)S(1)} %get-tuple-element.21), channel_id=1, source_target_pairs={{0,1},{1,0},{2,3},{3,2},{4,5},{5,4},{6,7},{7,6},{8,9},{9,8},{10,11... | collective-permute-start | bytes 368648 | tf_op jit(solution)/shard_map/ppermute | solution.py:494
  15.2 0.7 %collective-permute-start.3 = (f32[15,16,128]{2,1,0:T(8,128)S(1)}, f32[15,16,128]{2,1,0:T(8,128)S(1)}, u32[]{:S(2)}, u32[]{:S(2)}) collective-permute-start(f32[15,16,128]{2,1,0:T(8,128)S(1)} %get-tuple-element.22), channel_id=1, source_target_pairs={{0,0},{1,2},{2,1},{3,3},{4,4},{5,6},{6,5},{7,7},{8,8},{9,10},{10,9... | collective-permute-start | bytes 368648 | tf_op jit(solution)/shard_map/ppermute | solution.py:494
  15.8 2.2 %collective-permute-done.2.refs_2_ = f32[15,16,128]{2,1,0:T(8,128)S(1)} collective-permute-done((f32[15,16,128]{2,1,0:T(8,128)S(1)}, f32[15,16,128]{2,1,0:T(8,128)S(1)}, u32[]{:S(2)}, u32[]{:S(2)}) %collective-permute-start.2) | collective-permute-done | bytes 122912 | tf_op jit(solution)/shard_map/ppermute | solution.py:494
  18.0 0.5 collective-permute-start.7
  18.6 1.2 %collective-permute-done.5.refs_5_ = f32[2,2,16,128]{3,2,1,0:T(8,128)S(1)} collective-permute-done((f32[2,2,16,128]{3,2,1,0:T(8,128)S(1)}, f32[2,2,16,128]{3,2,1,0:T(8,128)S(1)}, u32[]{:S(2)}, u32[]{:S(2)}) %collective-permute-start.5) | collective-permute-done | bytes 32800 | tf_op jit(solution)/shard_map/ppermute | solution.py:494
  19.8 4.3 %first.1 = (f32[64,128]{1,0:T(8,128)S(1)}, f32[32,24,256]{2,1,0:T(8,128)S(1)}, f32[33,24,256]{2,1,0:T(8,128)S(1)}, f32[32,24,256]{2,1,0:T(8,128)S(1)}) custom-call(f32[2,16,16,128]{3,2,1,0:T(8,128)S(1)} %copy-done.1, f32[2,2,16,128]{3,2,1,0:T(8,128)S(1)} %collective-permute-done.1.x_edges.refs_1_, f32[15,16,128]{2,1,0:T(8,128)S(1)} %collective-permute-done.2.refs_2_, ...), custom_call_target="tpu_custom_call" | custom-call | tf_op jit(solution)/shard_map/first/pallas_call | solution.py:760
  24.2 4.7 %collective-permute-start.8 = (f32[64,128]{1,0:T(8,128)S(1)}, f32[64,128]{1,0:T(8,128)S(1)}, u32[]{:S(2)}, u32[]{:S(2)}) collective-permute-start(f32[64,128]{1,0:T(8,128)S(1)} %get-tuple-element.23), channel_id=1, source_target_pairs={{0,1},{1,0},{2,3},{3,2},{4,5},{5,4},{6,7},{7,6},{8,9},{9,8},{10,11... | collective-permute-start | bytes 98312 | tf_op jit(solution)/shard_map/ppermute | solution.py:494
  28.9 1.5 %collective-permute-start.9 = (f32[64,128]{1,0:T(8,128)S(1)}, f32[64,128]{1,0:T(8,128)S(1)}, u32[]{:S(2)}, u32[]{:S(2)}) collective-permute-start(f32[64,128]{1,0:T(8,128)S(1)} %get-tuple-element.23), channel_id=1, source_target_pairs={{0,2},{1,3},{2,0},{3,1},{4,6},{5,7},{6,4},{7,5},{8,10},{9,11},{10,... | collective-permute-start | bytes 98312 | tf_op jit(solution)/shard_map/ppermute | solution.py:494
  30.4 1.4 %collective-permute-start.10 = (f32[64,128]{1,0:T(8,128)S(1)}, f32[64,128]{1,0:T(8,128)S(1)}, u32[]{:S(2)}, u32[]{:S(2)}) collective-permute-start(f32[64,128]{1,0:T(8,128)S(1)} %get-tuple-element.23), channel_id=1, source_target_pairs={{0,3},{1,2},{2,1},{3,0},{4,7},{5,6},{6,5},{7,4},{8,11},{9,10},{10,... | collective-permute-start | bytes 98312 | tf_op jit(solution)/shard_map/ppermute | solution.py:494
  31.8 2.0 %collective-permute-done.9 = f32[64,128]{1,0:T(8,128)S(1)} collective-permute-done((f32[64,128]{1,0:T(8,128)S(1)}, f32[64,128]{1,0:T(8,128)S(1)}, u32[]{:S(2)}, u32[]{:S(2)}) %collective-permute-start.9) | collective-permute-done | bytes 32800 | tf_op jit(solution)/shard_map/ppermute | solution.py:494
  33.8 2.3 %collective-permute-done.10 = f32[64,128]{1,0:T(8,128)S(1)} collective-permute-done((f32[64,128]{1,0:T(8,128)S(1)}, f32[64,128]{1,0:T(8,128)S(1)}, u32[]{:S(2)}, u32[]{:S(2)}) %collective-permute-start.10) | collective-permute-done | bytes 32800 | tf_op jit(solution)/shard_map/ppermute | solution.py:494
  36.1 1.6 %collective-permute-start.11 = (f32[4,64,128]{2,1,0:T(8,128)S(1)}, f32[4,64,128]{2,1,0:T(8,128)S(1)}, u32[]{:S(2)}, u32[]{:S(2)}) collective-permute-start(f32[4,64,128]{2,1,0:T(8,128)S(1)} %pad_maximum_fusion.refs_0_), channel_id=1, source_target_pairs={{0,8},{8,0},{16,24},{24,16},{1,9},{9,1},{17,25},{25,17},{2,10},{10... | collective-permute-start | bytes 393224 | tf_op jit(solution)/shard_map/ppermute | solution.py:494
  37.7 1.5 %collective-permute-start.12 = (f32[4,64,128]{2,1,0:T(8,128)S(1)}, f32[4,64,128]{2,1,0:T(8,128)S(1)}, u32[]{:S(2)}, u32[]{:S(2)}) collective-permute-start(f32[4,64,128]{2,1,0:T(8,128)S(1)} %pad_maximum_fusion.refs_0_), channel_id=1, source_target_pairs={{0,16},{8,24},{16,0},{24,8},{1,17},{9,25},{17,1},{25,9},{2,18},{10... | collective-permute-start | bytes 393224 | tf_op jit(solution)/shard_map/ppermute | solution.py:494
  39.7 2.5 %collective-permute-done.11.refs_1_ = f32[4,64,128]{2,1,0:T(8,128)S(1)} collective-permute-done((f32[4,64,128]{2,1,0:T(8,128)S(1)}, f32[4,64,128]{2,1,0:T(8,128)S(1)}, u32[]{:S(2)}, u32[]{:S(2)}) %collective-permute-start.11) | collective-permute-done | bytes 131104 | tf_op jit(solution)/shard_map/ppermute | solution.py:494
  42.2 3.1 %collective-permute-done.12.refs_2_ = f32[4,64,128]{2,1,0:T(8,128)S(1)} collective-permute-done((f32[4,64,128]{2,1,0:T(8,128)S(1)}, f32[4,64,128]{2,1,0:T(8,128)S(1)}, u32[]{:S(2)}, u32[]{:S(2)}) %collective-permute-start.12) | collective-permute-done | bytes 131104 | tf_op jit(solution)/shard_map/ppermute | solution.py:494
  45.9 1.2 %faces.1 = (f32[32,24,256]{2,1,0:T(8,128)S(1)}, f32[32,24,256]{2,1,0:T(8,128)S(1)}, f32[32,24,256]{2,1,0:T(8,128)S(1)}, f32[32,24,256]{2,1,0:T(8,128)S(1)}, f32[32,24,256]{2,1,0:T(8,128)S(1)}) custom-call(f32[33,24,256]{2,1,0:T(8,128)S(1)} %get-tuple-element.26.coef, f32[8,128]{1,0:T(8,128)S(1)} %slice_bitcast_fusion.late), custom_call_target="tpu_custom_call" | custom-call | tf_op jit(solution)/shard_map/faces/pallas_call | solution.py:760
  47.2 13.3 %second.1 = (f32[16,16,128]{2,1,0:T(8,128)}, f32[16,16,128]{2,1,0:T(8,128)}) custom-call(f32[4,64,128]{2,1,0:T(8,128)S(1)} %pad_maximum_fusion.refs_0_, f32[4,64,128]{2,1,0:T(8,128)S(1)} %collective-permute-done.11.refs_1_, f32[4,64,128]{2,1,0:T(8,128)S(1)} %collective-permute-done.12.refs_2_, f32[4,64,128]{2,1,0:T(8,128)S(1)} %collective-permute-done.13.refs_3_, ...), custom_call_target="tpu_custom_call" | custom-call | tf_op jit(solution)/shard_map/second/pallas_call | solution.py:760
  (42 shorter events, 1.2 us)
Async XLA Ops:
  2.4 5.0 %collective-permute-start = (f32[2,16,128]{2,1,0:T(8,128)}, f32[2,16,128]{2,1,0:T(8,128)S(1)}, u32[]{:S(2)}, u32[]{:S(2)}) collective-permute-start(f32[2,16,128]{2,1,0:T(8,128)} %get-tuple-element.20), channel_id=1, source_target_pairs={{0,16},{8,24},{16,0},{24,8},{1,17},{9,25},{17,1},{25,9},{2,18},{10... | collective-permute-start | bytes 49160 | tf_op jit(solution)/shard_map/ppermute | solution.py:494
  7.4 12.4 %copy-start.9 = (bf16[128,128]{1,0:T(8,128)(2,1)S(1)}, bf16[128,128]{1,0:T(8,128)(2,1)}, u32[]{:S(2)}) copy-start(bf16[128,128]{1,0:T(8,128)(2,1)} %constant.20.clone.refs_10_) | copy-start | bytes 98308
  7.4 12.4 %copy-start.10 = (bf16[64,128]{1,0:T(8,128)(2,1)S(1)}, bf16[64,128]{1,0:T(8,128)(2,1)}, u32[]{:S(2)}) copy-start(bf16[64,128]{1,0:T(8,128)(2,1)} %constant.18.clone.refs_8_) | copy-start | bytes 49156
  8.1 3.9 %collective-permute-start.1 = (f32[2,2,16,128]{3,2,1,0:T(8,128)S(1)}, f32[2,2,16,128]{3,2,1,0:T(8,128)S(1)}, u32[]{:S(2)}, u32[]{:S(2)}) collective-permute-start(f32[2,2,16,128]{3,2,1,0:T(8,128)S(1)} %pad_maximum_fusion.1), channel_id=1, source_target_pairs={{0,8},{8,0},{16,24},{24,16},{1,9},{9,1},{17,25},{25,17},{2,10},{10... | collective-permute-start | bytes 98312 | tf_op jit(solution)/shard_map/ppermute | solution.py:494
  10.1 9.7 %collective-permute-start.4 = (f32[2,16,16,128]{3,2,1,0:T(8,128)}, f32[2,16,16,128]{3,2,1,0:T(8,128)S(1)}, u32[]{:S(2)}, u32[]{:S(2)}) collective-permute-start(f32[2,16,16,128]{3,2,1,0:T(8,128)} %get-tuple-element.18.own.refs_0_), channel_id=1, source_target_pairs={{0,4},{4,0},{1,5},{5,1},{2,6},{6,2},{3,7},{7,3},{8,12},{12,8},{9,1... | collective-permute-start | bytes 786440 | tf_op jit(solution)/shard_map/ppermute | solution.py:494
  13.0 6.8 %copy-start.1 = (f32[2,16,16,128]{3,2,1,0:T(8,128)S(1)}, f32[2,16,16,128]{3,2,1,0:T(8,128)}, u32[]{:S(2)}) copy-start(f32[2,16,16,128]{3,2,1,0:T(8,128)} %get-tuple-element.18.own.refs_0_) | copy-start | bytes 786436
  13.0 6.8 %copy-start.8 = (bf16[128,128]{1,0:T(8,128)(2,1)S(1)}, bf16[128,128]{1,0:T(8,128)(2,1)}, u32[]{:S(2)}) copy-start(bf16[128,128]{1,0:T(8,128)(2,1)} %constant.19.clone.refs_9_) | copy-start | bytes 98308
  13.1 5.0 %collective-permute-start.2 = (f32[15,16,128]{2,1,0:T(8,128)S(1)}, f32[15,16,128]{2,1,0:T(8,128)S(1)}, u32[]{:S(2)}, u32[]{:S(2)}) collective-permute-start(f32[15,16,128]{2,1,0:T(8,128)S(1)} %get-tuple-element.21), channel_id=1, source_target_pairs={{0,1},{1,0},{2,3},{3,2},{4,5},{5,4},{6,7},{7,6},{8,9},{9,8},{10,11... | collective-permute-start | bytes 368648 | tf_op jit(solution)/shard_map/ppermute | solution.py:494
  15.2 2.9 %collective-permute-start.3 = (f32[15,16,128]{2,1,0:T(8,128)S(1)}, f32[15,16,128]{2,1,0:T(8,128)S(1)}, u32[]{:S(2)}, u32[]{:S(2)}) collective-permute-start(f32[15,16,128]{2,1,0:T(8,128)S(1)} %get-tuple-element.22), channel_id=1, source_target_pairs={{0,0},{1,2},{2,1},{3,3},{4,4},{5,6},{6,5},{7,7},{8,8},{9,10},{10,9... | collective-permute-start | bytes 368648 | tf_op jit(solution)/shard_map/ppermute | solution.py:494
  18.0 1.7 %collective-permute-start.6 = (f32[15,16,128]{2,1,0:T(8,128)S(1)}, f32[15,16,128]{2,1,0:T(8,128)S(1)}, u32[]{:S(2)}, u32[]{:S(2)}) collective-permute-start(f32[15,16,128]{2,1,0:T(8,128)S(1)} %collective-permute-done.2.refs_2_), channel_id=1, source_target_pairs={{0,4},{4,0},{1,5},{5,1},{2,6},{6,2},{3,7},{7,3},{8,12},{12,8},{9,1... | collective-permute-start | bytes 368648 | tf_op jit(solution)/shard_map/ppermute | solution.py:494
  18.0 1.7 %collective-permute-start.7 = (f32[15,16,128]{2,1,0:T(8,128)S(1)}, f32[15,16,128]{2,1,0:T(8,128)S(1)}, u32[]{:S(2)}, u32[]{:S(2)}) collective-permute-start(f32[15,16,128]{2,1,0:T(8,128)S(1)} %collective-permute-done.3.refs_3_), channel_id=1, source_target_pairs={{0,4},{4,0},{1,5},{5,1},{2,6},{6,2},{3,7},{7,3},{8,12},{12,8},{9,1... | collective-permute-start | bytes 368648 | tf_op jit(solution)/shard_map/ppermute | solution.py:494
  18.6 1.2 %collective-permute-start.5 = (f32[2,2,16,128]{3,2,1,0:T(8,128)S(1)}, f32[2,2,16,128]{3,2,1,0:T(8,128)S(1)}, u32[]{:S(2)}, u32[]{:S(2)}) collective-permute-start(f32[2,2,16,128]{3,2,1,0:T(8,128)S(1)} %collective-permute-done.1.x_edges.refs_1_), channel_id=1, source_target_pairs={{0,4},{4,0},{1,5},{5,1},{2,6},{6,2},{3,7},{7,3},{8,12},{12,8},{9,1... | collective-permute-start | bytes 98312 | tf_op jit(solution)/shard_map/ppermute | solution.py:494
  19.8 27.3 %copy-start.7 = (bf16[128,256]{1,0:T(8,128)(2,1)S(1)}, bf16[128,256]{1,0:T(8,128)(2,1)}, u32[]{:S(2)}) copy-start(bf16[128,256]{1,0:T(8,128)(2,1)} %constant.26.clone.refs_20_) | copy-start | bytes 196612
  24.2 7.6 %collective-permute-start.8 = (f32[64,128]{1,0:T(8,128)S(1)}, f32[64,128]{1,0:T(8,128)S(1)}, u32[]{:S(2)}, u32[]{:S(2)}) collective-permute-start(f32[64,128]{1,0:T(8,128)S(1)} %get-tuple-element.23), channel_id=1, source_target_pairs={{0,1},{1,0},{2,3},{3,2},{4,5},{5,4},{6,7},{7,6},{8,9},{9,8},{10,11... | collective-permute-start | bytes 98312 | tf_op jit(solution)/shard_map/ppermute | solution.py:494
  28.9 4.9 %collective-permute-start.9 = (f32[64,128]{1,0:T(8,128)S(1)}, f32[64,128]{1,0:T(8,128)S(1)}, u32[]{:S(2)}, u32[]{:S(2)}) collective-permute-start(f32[64,128]{1,0:T(8,128)S(1)} %get-tuple-element.23), channel_id=1, source_target_pairs={{0,2},{1,3},{2,0},{3,1},{4,6},{5,7},{6,4},{7,5},{8,10},{9,11},{10,... | collective-permute-start | bytes 98312 | tf_op jit(solution)/shard_map/ppermute | solution.py:494
  30.4 5.7 %collective-permute-start.10 = (f32[64,128]{1,0:T(8,128)S(1)}, f32[64,128]{1,0:T(8,128)S(1)}, u32[]{:S(2)}, u32[]{:S(2)}) collective-permute-start(f32[64,128]{1,0:T(8,128)S(1)} %get-tuple-element.23), channel_id=1, source_target_pairs={{0,3},{1,2},{2,1},{3,0},{4,7},{5,6},{6,5},{7,4},{8,11},{9,10},{10,... | collective-permute-start | bytes 98312 | tf_op jit(solution)/shard_map/ppermute | solution.py:494
  36.1 11.0 %copy-start.2 = (bf16[4,256,256]{2,1,0:T(8,128)(2,1)S(1)}, bf16[4,256,256]{2,1,0:T(8,128)(2,1)}, u32[]{:S(2)}) copy-start(bf16[4,256,256]{2,1,0:T(8,128)(2,1)} %constant.22.clone.refs_16_) | copy-start | bytes 1572868
  36.1 6.1 %collective-permute-start.11 = (f32[4,64,128]{2,1,0:T(8,128)S(1)}, f32[4,64,128]{2,1,0:T(8,128)S(1)}, u32[]{:S(2)}, u32[]{:S(2)}) collective-permute-start(f32[4,64,128]{2,1,0:T(8,128)S(1)} %pad_maximum_fusion.refs_0_), channel_id=1, source_target_pairs={{0,8},{8,0},{16,24},{24,16},{1,9},{9,1},{17,25},{25,17},{2,10},{10... | collective-permute-start | bytes 393224 | tf_op jit(solution)/shard_map/ppermute | solution.py:494
  37.7 7.7 %collective-permute-start.12 = (f32[4,64,128]{2,1,0:T(8,128)S(1)}, f32[4,64,128]{2,1,0:T(8,128)S(1)}, u32[]{:S(2)}, u32[]{:S(2)}) collective-permute-start(f32[4,64,128]{2,1,0:T(8,128)S(1)} %pad_maximum_fusion.refs_0_), channel_id=1, source_target_pairs={{0,16},{8,24},{16,0},{24,8},{1,17},{9,25},{17,1},{25,9},{2,18},{10... | collective-permute-start | bytes 393224 | tf_op jit(solution)/shard_map/ppermute | solution.py:494
  39.2 6.2 %collective-permute-start.13 = (f32[4,64,128]{2,1,0:T(8,128)S(1)}, f32[4,64,128]{2,1,0:T(8,128)S(1)}, u32[]{:S(2)}, u32[]{:S(2)}) collective-permute-start(f32[4,64,128]{2,1,0:T(8,128)S(1)} %pad_maximum_fusion.refs_0_), channel_id=1, source_target_pairs={{0,24},{8,16},{16,8},{24,0},{1,25},{9,17},{17,9},{25,1},{2,26},{10... | collective-permute-start | bytes 393224 | tf_op jit(solution)/shard_map/ppermute | solution.py:494
  39.7 7.4 %collective-permute-start.14 = (f32[4,64,128]{2,1,0:T(8,128)S(1)}, f32[4,64,128]{2,1,0:T(8,128)S(1)}, u32[]{:S(2)}, u32[]{:S(2)}) collective-permute-start(f32[4,64,128]{2,1,0:T(8,128)S(1)} %pad_maximum_fusion.refs_0_), channel_id=1, source_target_pairs={{0,4},{4,0},{1,5},{5,1},{2,6},{6,2},{3,7},{7,3},{8,12},{12,8},{9,1... | collective-permute-start | bytes 393224 | tf_op jit(solution)/shard_map/ppermute | solution.py:494
  42.2 4.9 %collective-permute-start.15 = (f32[4,64,128]{2,1,0:T(8,128)S(1)}, f32[4,64,128]{2,1,0:T(8,128)S(1)}, u32[]{:S(2)}, u32[]{:S(2)}) collective-permute-start(f32[4,64,128]{2,1,0:T(8,128)S(1)} %collective-permute-done.11.refs_1_), channel_id=1, source_target_pairs={{0,4},{4,0},{1,5},{5,1},{2,6},{6,2},{3,7},{7,3},{8,12},{12,8},{9,1... | collective-permute-start | bytes 393224 | tf_op jit(solution)/shard_map/ppermute | solution.py:494
  45.3 1.7 %collective-permute-start.16 = (f32[4,64,128]{2,1,0:T(8,128)S(1)}, f32[4,64,128]{2,1,0:T(8,128)S(1)}, u32[]{:S(2)}, u32[]{:S(2)}) collective-permute-start(f32[4,64,128]{2,1,0:T(8,128)S(1)} %collective-permute-done.12.refs_2_), channel_id=1, source_target_pairs={{0,4},{4,0},{1,5},{5,1},{2,6},{6,2},{3,7},{7,3},{8,12},{12,8},{9,1... | collective-permute-start | bytes 393224 | tf_op jit(solution)/shard_map/ppermute | solution.py:494
  45.3 1.7 %collective-permute-start.17 = (f32[4,64,128]{2,1,0:T(8,128)S(1)}, f32[4,64,128]{2,1,0:T(8,128)S(1)}, u32[]{:S(2)}, u32[]{:S(2)}) collective-permute-start(f32[4,64,128]{2,1,0:T(8,128)S(1)} %collective-permute-done.13.refs_3_), channel_id=1, source_target_pairs={{0,4},{4,0},{1,5},{5,1},{2,6},{6,2},{3,7},{7,3},{8,12},{12,8},{9,1... | collective-permute-start | bytes 393224 | tf_op jit(solution)/shard_map/ppermute | solution.py:494
  (5 other events, 6.1 us)

commit v8 on v6

--- a/solution.py
+++ b/solution.py
@@ -312,7 +312,7 @@
     in_blocks(start, stop, block, body, face_z[before] * field[before])
 
 
-def plane_steps(faces, ranges, source, residual, update, estimate, from_zero):
+def plane_steps(faces, ranges, source, residual, update, estimate, from_zero, block=4):
     inverse = faces[4]
     for step, ((keep, push), (start, stop)) in enumerate(zip(cheb_terms(), ranges)):
         fresh = from_zero and step == 0
@@ -331,7 +331,7 @@
 
             return store
 
-        plane_sweep(faces, start, stop, update, finish)
+        plane_sweep(faces, start, stop, update, finish, block)
 
 
 def plane_restart(faces, start, stop, source, residual, update, estimate):
@@ -353,7 +353,7 @@
     plane_sweep(faces, start, stop, estimate, finish)
 
 
-def plane_residual(faces, start, stop, residual, update):
+def plane_residual(faces, start, stop, residual, update, block=4):
     def finish(here, own):
         before = residual[here]
 
@@ -362,7 +362,7 @@
 
         return store
 
-    plane_sweep(faces, start, stop, update, finish)
+    plane_sweep(faces, start, stop, update, finish, block)
 
 
 def moved(value, shift, axis):
@@ -487,11 +487,21 @@
     return [pairs[index] for index in range(count)]
 
 
-def swapped(value, axes, partners):
-    places = [0]
-    for partner in partners:
-        places = [place * len(partner) + other for place in places for other in partner]
-    return lax.ppermute(value, axes, list(enumerate(places)))
+def swapped(value, axes, partner):
+    counts = [lax.axis_size(axis) for axis in axes]
+    pairs = [
+        (np.ravel_multi_index(place, counts), np.ravel_multi_index(partner(*place), counts))
+        for place in np.ndindex(*counts)
+    ]
+    return lax.ppermute(value, axes, [(int(source), int(target)) for source, target in pairs])
+
+
+def other_core(value):
+    return swapped(value, ("gy",), lambda y: (1 - y,))
+
+
+def above_first():
+    return (lax.axis_index("gz") % 2 == 0) == (lax.axis_index("gy") == 0)
 
 
 def link_mask(rows, lanes):
@@ -509,7 +519,7 @@
     return pl.ds(pl.multiple_of(first, HALO_Y), HALO_Y)
 
 
-def start_kernel(source, coef, both, x_a, x_b, done):
+def start_kernel(source, coef, both, x_b, x_a, done):
     _, planes, own_y, _ = both.shape
     copies = [
         pltpu.make_async_copy(ref, both.at[which], done.at[which]) for which, ref in enumerate((source, coef))
@@ -542,9 +552,9 @@
     return right, left
 
 
-def pack_z_kernel(x_count, own, x_a, x_b, z_a, z_b):
+def pack_z_kernel(x_count, own, x_b, x_a, z_first, z_second):
     _, planes, own_y, _ = own.shape
-    z_even = lax.axis_index("gz") % 2 == 0
+    above = above_first()
     lane = lanes_of((own_y, 128))
     skip = 8 * (planes - HALO_Z)
     at = 0
@@ -552,7 +562,7 @@
         right, left = x_halos(x_a[which], x_b[which], x_count)
         bottom = jnp.where(lane < 64, right, turned(left, 64, 1))
         top = jnp.where(lane < 64, turned(right, -skip, 1), turned(left, 64 - skip, 1))
-        for target, is_top in ((z_a, z_even), (z_b, jnp.logical_not(z_even))):
+        for target, is_top in ((z_first, above), (z_second, jnp.logical_not(above))):
             first = jnp.where(is_top, planes - count, 0)
             target[pl.ds(at, count)] = own[which, pl.ds(first, count)]
             target[sum(SENT_Z) + which] = jnp.where(is_top, top, bottom)
@@ -563,7 +573,7 @@
     _, planes, own_y, _ = own.shape
     rows = own_y + HALO_Y
     z_index = lax.axis_index("gz")
-    z_even = z_index % 2 == 0
+    first_above = above_first()
     above_at = HALO_Z + planes
     lane = lanes_of((rows, 128))
     window = source.shape[1:]
@@ -579,18 +589,18 @@
     for which, (target, count) in enumerate(zip((source, coef), SENT_Z)):
         target[pl.ds(HALO_Z, planes), :own_y, :128] = own[which]
         target[pl.ds(HALO_Z, planes), own_y:, :128] = far[0][which, :, near_rows(far[0])]
-        x_a, x_b = (joined(got[index], far[1 + index], (which,)) for index in (0, 1))
+        x_b, x_a = (joined(got[index], far[1 + index], (which,)) for index in (0, 1))
         right, left = x_halos(x_a, x_b, x_count)
         for plane in range(planes):
             target[HALO_Z + plane, :, 128:] = edges(right, left, 8 * plane, 8 * plane)
-        for is_above, flag, is_a in (
-            (True, z_index < z_count - 1, z_even),
-            (False, z_index > 0, jnp.logical_not(z_even)),
-        ):
+        for is_above, flag in ((True, z_index < z_count - 1), (False, z_index > 0)):
 
             def taken(place):
-                by_a, by_b = (joined(got[index], far[1 + index], (place,)) for index in (2, 3))
-                return kept(flag, jnp.where(is_a, by_a, by_b))
+                first = first_above if is_above else jnp.logical_not(first_above)
+                mine = jnp.where(first, got[2][place], got[3][place])
+                near = near_rows(far[3])
+                other = jnp.where(first, far[4][place, near], far[3][place, near])
+                return kept(flag, jnp.concatenate([mine, other], axis=0))
 
             packed = taken(sum(SENT_Z) + which)
             for plane in range(count):
@@ -662,8 +672,12 @@
         for x_pair in range(x_count // 2):
             x_lanes = pl.ds(pl.multiple_of(((x_index // 2) ^ x_pair) * 128, 128), 128)
             for z_block in range(z_count):
-                mine = blocks[2 * x_pair][z_block]
-                partner = blocks[2 * x_pair + 1][z_block]
+                if x_pair == 0:
+                    mine = blocks[0][z_block]
+                    partner = jnp.where(y_block == 0, blocks[1][z_block], blocks[2][z_block])
+                else:
+                    mine = jnp.where(y_block == 0, blocks[2][z_block], blocks[1][z_block])
+                    partner = blocks[3][z_block]
                 even = jnp.where(x_even, mine, partner)
                 odd = jnp.where(x_even, partner, mine)
                 where = (pl.ds(PAD + (z_index ^ z_block) * 8, 8), y_rows, x_lanes)
@@ -677,8 +691,8 @@
     start, stop = PAD, PAD + mid_z
     plane_faces(mid_coef, mid_faces, start, stop, link_y, link_x, mid_source, mid_update)
     ranges = [(start, stop)] * (DEGREE - 1)
-    plane_steps(mid_faces, ranges, mid_source, mid_residual, mid_update, mid_estimate, True)
-    plane_residual(mid_faces, start, stop, mid_residual, mid_update)
+    plane_steps(mid_faces, ranges, mid_source, mid_residual, mid_update, mid_estimate, True, 8)
+    plane_residual(mid_faces, start, stop, mid_residual, mid_update, 8)
 
     for copy in copies:
         copy.wait()
@@ -764,8 +778,8 @@
             name=name,
         )(*arguments, *far_arguments)
 
-    core_pairs = swap_pairs(y_count, False)
-    swaps = [[swap_pairs(count, odd) for odd in (False, True)] for count in (x_count, z_count)]
+    x_a, x_b = swap_pairs(x_count, False), swap_pairs(x_count, True)
+    z_pairs = swap_pairs(z_count, False), swap_pairs(z_count, True)
     both, *sent = call(
         start_kernel,
         "start",
@@ -775,11 +789,14 @@
         [pltpu.SemaphoreType.DMA((2,))],
         (right_side, coefficient),
     )
-    got = [swapped(value, "gx", [pairs]) for value, pairs in zip(sent, swaps[0])]
+    got = [
+        swapped(value, ("gx",), lambda x, pairs=pairs: (pairs[x],)) for value, pairs in zip(sent, (x_b, x_a))
+    ]
     z_shape = (sum(SENT_Z) + 2, own_y, 128)
     sent = call(functools.partial(pack_z_kernel, x_count), "pack_z", 4, (both, *got), [z_shape] * 2, [])
-    got += [swapped(value, "gz", [pairs]) for value, pairs in zip(sent, swaps[1])]
-    far = [swapped(value, "gy", [core_pairs]) for value in (both, *got)]
+    got.append(swapped(sent[0], ("gy", "gz"), lambda y, z: (y, z_pairs[y][z])))
+    got.append(swapped(sent[1], ("gy", "gz"), lambda y, z: (y, z_pairs[1 - y][z])))
+    far = [other_core(value) for value in (both, *got)]
 
     window, padded = (planes, rows, lanes), (planes + 1, rows, lanes)
     down = own_down_matrices(own_z // 2, own_y, own_x)
@@ -792,14 +809,12 @@
         [window] * 6 + [padded] + [(own_z * own_y // 2, own_x)] * 2,
     )
 
-    def from_others(value, axis, count):
-        return [
-            swapped(value, axis, [[index ^ distance for index in range(count)]]) for distance in range(1, count)
-        ]
-
-    mine = jnp.stack([message] + from_others(message, "gz", z_count))
-    parts = [mine] + from_others(mine, "gx", x_count)
-    parts += [swapped(part, "gy", [core_pairs]) for part in parts]
+    others = [swapped(message, ("gz",), lambda z, step=step: (z ^ step,)) for step in range(1, z_count)]
+    mine = jnp.stack([message] + others)
+    parts = [mine]
+    for steps in ((1, 2), (2, 1), (3, 3)):
+        parts.append(swapped(mine, ("gx", "gy"), lambda x, y, steps=steps: (x ^ steps[y], y)))
+    parts += [other_core(part) for part in parts]
 
     mid = (own_z * z_count // 2, own_y * y_count // 2, own_x * x_count // 2)
     row, lane = np.arange(rows), np.arange(lanes)

time: 58 us -> 58.6 us (1.010)
  waiting for transfers between devices: 13 us -> 14.7 us
  Pallas kernels: 19.6 us -> 19 us
    ppermute x19, waiting for transfers between devices: 13 us -> 14.7 us  [swapped(): lax.ppermute(value, axes, [(int(source), int(target)) for source, target...]
    pallas_call x4, Pallas kernels: 19.6 us -> 19 us  [call(): pl.pallas_call(kernel, out_shape=tuple((jax.ShapeDtypeStruct(shape, F32)...]
  transfers between devices with their start and end apart: 19 -> 19, of which waited for: 9 -> 10; matrix products, arithmetic and copies ran while one was open for 0% -> 0% of each run, Pallas kernels for 0% -> 0%
where the time goes in v8:
time: 58.6 us; the launch traced here: 58.4 us
  starting transfers between devices  22 us (38%)
  Pallas kernels  19 us (32%)
  waiting for transfers between devices  14.7 us (25%)
  local copies, waits for them, and re-layouts  1.84 us (3%)
  between operations  0.79 us (1%)
    ppermute x19, starting transfers between devices, swapped(): lax.ppermute(value, axes, [(int(source), int(target)) for source, target...  22 us
    pallas_call x4, Pallas kernels, call(): pl.pallas_call(kernel, out_shape=tuple((jax.ShapeDtypeStruct(shape, F32)...  19 us
    ppermute x19, waiting for transfers between devices, swapped(): lax.ppermute(value, axes, [(int(source), int(target)) for source, target...  14.7 us
    unnamed x22, local copies, waits for them, and re-layouts  1.84 us
  transfers between devices with their start and end apart: 19, of which 10 were waited for; matrix products, arithmetic and copies ran while one was open for 0% of the time, Pallas kernels for 0%

profile of v8, /device:TPU:0, one launch (start us, length us, event | category | flops | bytes accessed | tf_op | source)
XLA Modules:
  0.0 58.4 jit_solution(11264191224895663468)
XLA Ops:
  0.6 0.9 %copy-done.2 = f32[1,16,16,128]{3,2,1,0:T(8,128)S(1)} copy-done((f32[1,16,16,128]{3,2,1,0:T(8,128)S(1)}, f32[1,16,16,128]{3,2,1,0:T(8,128)}, u32[]{:S(2)}) %copy-start.2) | copy-done | bytes 131096
  1.5 0.9 %copy-done.3 = f32[16,16,128]{2,1,0:T(8,128)S(1)} copy-done((f32[16,16,128]{2,1,0:T(8,128)S(1)}, f32[16,16,128]{2,1,0:T(8,128)}, u32[]{:S(2)}) %copy-start.3) | copy-done | bytes 131096
  2.4 0.6 %start.1 = (f32[2,16,16,128]{3,2,1,0:T(8,128)S(1)}, f32[2,16,128]{2,1,0:T(8,128)S(1)}, f32[2,16,128]{2,1,0:T(8,128)S(1)}) custom-call(f32[16,16,128]{2,1,0:T(8,128)S(1)} %bitcast.7, f32[16,16,128]{2,1,0:T(8,128)S(1)} %copy-done.3), custom_call_target="tpu_custom_call" | custom-call | tf_op jit(solution)/shard_map/start/pallas_call | solution.py:771
  3.0 0.7 %collective-permute-start = (f32[2,16,128]{2,1,0:T(8,128)S(1)}, f32[2,16,128]{2,1,0:T(8,128)S(1)}, u32[]{:S(2)}, u32[]{:S(2)}) collective-permute-start(f32[2,16,128]{2,1,0:T(8,128)S(1)} %get-tuple-element.14), channel_id=1, source_target_pairs={{0,0},{8,16},{16,8},{24,24},{1,1},{9,17},{17,9},{25,25},{2,2},{10,... | collective-permute-start | bytes 49160 | tf_op jit(solution)/shard_map/ppermute | solution.py:496
  3.7 5.7 %collective-permute-start.1 = (f32[2,16,128]{2,1,0:T(8,128)S(1)}, f32[2,16,128]{2,1,0:T(8,128)S(1)}, u32[]{:S(2)}, u32[]{:S(2)}) collective-permute-start(f32[2,16,128]{2,1,0:T(8,128)S(1)} %get-tuple-element.15), channel_id=1, source_target_pairs={{0,8},{8,0},{16,24},{24,16},{1,9},{9,1},{17,25},{25,17},{2,10},{10... | collective-permute-start | bytes 49160 | tf_op jit(solution)/shard_map/ppermute | solution.py:496
  9.5 1.8 %collective-permute-done.1.x_a.refs_2_ = f32[2,16,128]{2,1,0:T(8,128)S(1)} collective-permute-done((f32[2,16,128]{2,1,0:T(8,128)S(1)}, f32[2,16,128]{2,1,0:T(8,128)S(1)}, u32[]{:S(2)}, u32[]{:S(2)}) %collective-permute-start.1) | collective-permute-done | bytes 16416 | tf_op jit(solution)/shard_map/ppermute | solution.py:496
  11.3 3.5 %collective-permute-start.2 = (f32[15,16,128]{2,1,0:T(8,128)S(1)}, f32[15,16,128]{2,1,0:T(8,128)S(1)}, u32[]{:S(2)}, u32[]{:S(2)}) collective-permute-start(f32[15,16,128]{2,1,0:T(8,128)S(1)} %get-tuple-element.16), channel_id=1, source_target_pairs={{0,1},{1,0},{2,3},{3,2},{4,4},{5,6},{6,5},{7,7},{8,9},{9,8},{10,11... | collective-permute-start | bytes 368648 | tf_op jit(solution)/shard_map/ppermute | solution.py:496
  14.8 0.8 %collective-permute-start.3 = (f32[15,16,128]{2,1,0:T(8,128)S(1)}, f32[15,16,128]{2,1,0:T(8,128)S(1)}, u32[]{:S(2)}, u32[]{:S(2)}) collective-permute-start(f32[15,16,128]{2,1,0:T(8,128)S(1)} %get-tuple-element.17), channel_id=1, source_target_pairs={{0,0},{1,2},{2,1},{3,3},{4,5},{5,4},{6,7},{7,6},{8,8},{9,10},{10,9... | collective-permute-start | bytes 368648 | tf_op jit(solution)/shard_map/ppermute | solution.py:496
  15.6 2.8 %collective-permute-done.2.refs_3_ = f32[15,16,128]{2,1,0:T(8,128)S(1)} collective-permute-done((f32[15,16,128]{2,1,0:T(8,128)S(1)}, f32[15,16,128]{2,1,0:T(8,128)S(1)}, u32[]{:S(2)}, u32[]{:S(2)}) %collective-permute-start.2) | collective-permute-done | bytes 122912 | tf_op jit(solution)/shard_map/ppermute | solution.py:496
  18.5 0.8 %collective-permute-start.8 = (f32[15,16,128]{2,1,0:T(8,128)S(1)}, f32[15,16,128]{2,1,0:T(8,128)S(1)}, u32[]{:S(2)}, u32[]{:S(2)}) collective-permute-start(f32[15,16,128]{2,1,0:T(8,128)S(1)} %collective-permute-done.3.refs_4_), channel_id=1, source_target_pairs={{0,4},{4,0},{1,5},{5,1},{2,6},{6,2},{3,7},{7,3},{8,12},{12,8},{9,1... | collective-permute-start | bytes 368648 | tf_op jit(solution)/shard_map/ppermute | solution.py:496
  19.2 0.5 collective-permute-start.6
  19.8 0.7 %collective-permute-done.5.refs_6_ = f32[2,16,128]{2,1,0:T(8,128)S(1)} collective-permute-done((f32[2,16,128]{2,1,0:T(8,128)S(1)}, f32[2,16,128]{2,1,0:T(8,128)S(1)}, u32[]{:S(2)}, u32[]{:S(2)}) %collective-permute-start.5) | collective-permute-done | bytes 16416 | tf_op jit(solution)/shard_map/ppermute | solution.py:496
  20.6 4.4 %first.1 = (f32[64,128]{1,0:T(8,128)S(1)}, f32[32,24,256]{2,1,0:T(8,128)S(1)}, f32[33,24,256]{2,1,0:T(8,128)S(1)}, f32[32,24,256]{2,1,0:T(8,128)S(1)}) custom-call(f32[2,16,16,128]{3,2,1,0:T(8,128)S(1)} %get-tuple-element.13.own.refs_0_, f32[2,16,128]{2,1,0:T(8,128)S(1)} %collective-permute-done.x_b.refs_1_, ...), custom_call_target="tpu_custom_call" | custom-call | tf_op jit(solution)/shard_map/first/pallas_call | solution.py:771
  25.0 3.0 %collective-permute-start.11 = (f32[64,128]{1,0:T(8,128)S(1)}, f32[64,128]{1,0:T(8,128)S(1)}, u32[]{:S(2)}, u32[]{:S(2)}) collective-permute-start(f32[64,128]{1,0:T(8,128)S(1)} %get-tuple-element.18), channel_id=1, source_target_pairs={{0,3},{1,2},{2,1},{3,0},{4,7},{5,6},{6,5},{7,4},{8,11},{9,10},{10,... | collective-permute-start | bytes 98312 | tf_op jit(solution)/shard_map/ppermute | solution.py:496
  28.0 2.5 %collective-permute-start.10 = (f32[64,128]{1,0:T(8,128)S(1)}, f32[64,128]{1,0:T(8,128)S(1)}, u32[]{:S(2)}, u32[]{:S(2)}) collective-permute-start(f32[64,128]{1,0:T(8,128)S(1)} %get-tuple-element.18), channel_id=1, source_target_pairs={{0,2},{1,3},{2,0},{3,1},{4,6},{5,7},{6,4},{7,5},{8,10},{9,11},{10,... | collective-permute-start | bytes 98312 | tf_op jit(solution)/shard_map/ppermute | solution.py:496
  30.5 0.5 collective-permute-start.9
  31.0 1.8 %collective-permute-done.10 = f32[64,128]{1,0:T(8,128)S(1)} collective-permute-done((f32[64,128]{1,0:T(8,128)S(1)}, f32[64,128]{1,0:T(8,128)S(1)}, u32[]{:S(2)}, u32[]{:S(2)}) %collective-permute-start.10) | collective-permute-done | bytes 32800 | tf_op jit(solution)/shard_map/ppermute | solution.py:496
  32.9 1.5 %collective-permute-done.9 = f32[64,128]{1,0:T(8,128)S(1)} collective-permute-done((f32[64,128]{1,0:T(8,128)S(1)}, f32[64,128]{1,0:T(8,128)S(1)}, u32[]{:S(2)}, u32[]{:S(2)}) %collective-permute-start.9) | collective-permute-done | bytes 32800 | tf_op jit(solution)/shard_map/ppermute | solution.py:496
  34.4 1.5 %collective-permute-start.14 = (f32[4,64,128]{2,1,0:T(8,128)S(1)}, f32[4,64,128]{2,1,0:T(8,128)S(1)}, u32[]{:S(2)}, u32[]{:S(2)}) collective-permute-start(f32[4,64,128]{2,1,0:T(8,128)S(1)} %pad_maximum_fusion.refs_0_), channel_id=1, source_target_pairs={{0,24},{4,28},{8,16},{12,20},{16,8},{20,12},{24,0},{28,4},{1,25},{... | collective-permute-start | bytes 393224 | tf_op jit(solution)/shard_map/ppermute | solution.py:496
  35.9 2.0 %collective-permute-start.13 = (f32[4,64,128]{2,1,0:T(8,128)S(1)}, f32[4,64,128]{2,1,0:T(8,128)S(1)}, u32[]{:S(2)}, u32[]{:S(2)}) collective-permute-start(f32[4,64,128]{2,1,0:T(8,128)S(1)} %pad_maximum_fusion.refs_0_), channel_id=1, source_target_pairs={{0,16},{4,12},{8,24},{12,4},{16,0},{20,28},{24,8},{28,20},{1,17},{... | collective-permute-start | bytes 393224 | tf_op jit(solution)/shard_map/ppermute | solution.py:496
  38.0 3.3 %collective-permute-done.14.refs_3_ = f32[4,64,128]{2,1,0:T(8,128)S(1)} collective-permute-done((f32[4,64,128]{2,1,0:T(8,128)S(1)}, f32[4,64,128]{2,1,0:T(8,128)S(1)}, u32[]{:S(2)}, u32[]{:S(2)}) %collective-permute-start.14) | collective-permute-done | bytes 131104 | tf_op jit(solution)/shard_map/ppermute | solution.py:496
  41.3 1.6 %collective-permute-done.13.refs_2_ = f32[4,64,128]{2,1,0:T(8,128)S(1)} collective-permute-done((f32[4,64,128]{2,1,0:T(8,128)S(1)}, f32[4,64,128]{2,1,0:T(8,128)S(1)}, u32[]{:S(2)}, u32[]{:S(2)}) %collective-permute-start.13) | collective-permute-done | bytes 131104 | tf_op jit(solution)/shard_map/ppermute | solution.py:496
  43.4 0.8 %collective-permute-done.17.refs_6_ = f32[4,64,128]{2,1,0:T(8,128)S(1)} collective-permute-done((f32[4,64,128]{2,1,0:T(8,128)S(1)}, f32[4,64,128]{2,1,0:T(8,128)S(1)}, u32[]{:S(2)}, u32[]{:S(2)}) %collective-permute-start.17) | collective-permute-done | bytes 131104 | tf_op jit(solution)/shard_map/ppermute | solution.py:496
  44.4 13.9 %second.1 = (f32[16,16,128]{2,1,0:T(8,128)}, f32[16,16,128]{2,1,0:T(8,128)}) custom-call(f32[4,64,128]{2,1,0:T(8,128)S(1)} %pad_maximum_fusion.refs_0_, f32[4,64,128]{2,1,0:T(8,128)S(1)} %collective-permute-done.12.refs_1_, f32[4,64,128]{2,1,0:T(8,128)S(1)} %collective-permute-done.13.refs_2_, f32[4,64,128]{2,1,0:T(8,128)S(1)} %collective-permute-done.14.refs_3_, ...), custom_call_target="tpu_custom_call" | custom-call | tf_op jit(solution)/shard_map/second/pallas_call | solution.py:771
  (41 shorter events, 1.1 us)
Async XLA Ops:
  3.0 6.4 %collective-permute-start = (f32[2,16,128]{2,1,0:T(8,128)S(1)}, f32[2,16,128]{2,1,0:T(8,128)S(1)}, u32[]{:S(2)}, u32[]{:S(2)}) collective-permute-start(f32[2,16,128]{2,1,0:T(8,128)S(1)} %get-tuple-element.14), channel_id=1, source_target_pairs={{0,0},{8,16},{16,8},{24,24},{1,1},{9,17},{17,9},{25,25},{2,2},{10,... | collective-permute-start | bytes 49160 | tf_op jit(solution)/shard_map/ppermute | solution.py:496
  3.7 7.5 %collective-permute-start.1 = (f32[2,16,128]{2,1,0:T(8,128)S(1)}, f32[2,16,128]{2,1,0:T(8,128)S(1)}, u32[]{:S(2)}, u32[]{:S(2)}) collective-permute-start(f32[2,16,128]{2,1,0:T(8,128)S(1)} %get-tuple-element.15), channel_id=1, source_target_pairs={{0,8},{8,0},{16,24},{24,16},{1,9},{9,1},{17,25},{25,17},{2,10},{10... | collective-permute-start | bytes 49160 | tf_op jit(solution)/shard_map/ppermute | solution.py:496
  9.5 11.1 %copy-start.8 = (bf16[128,128]{1,0:T(8,128)(2,1)S(1)}, bf16[128,128]{1,0:T(8,128)(2,1)}, u32[]{:S(2)}) copy-start(bf16[128,128]{1,0:T(8,128)(2,1)} %constant.20.clone.refs_12_) | copy-start | bytes 98308
  9.5 11.2 %copy-start.9 = (bf16[128,128]{1,0:T(8,128)(2,1)S(1)}, bf16[128,128]{1,0:T(8,128)(2,1)}, u32[]{:S(2)}) copy-start(bf16[128,128]{1,0:T(8,128)(2,1)} %constant.19.clone.refs_11_) | copy-start | bytes 98308
  9.5 11.2 %copy-start.10 = (bf16[64,128]{1,0:T(8,128)(2,1)S(1)}, bf16[64,128]{1,0:T(8,128)(2,1)}, u32[]{:S(2)}) copy-start(bf16[64,128]{1,0:T(8,128)(2,1)} %constant.18.clone.refs_10_) | copy-start | bytes 49156
  9.5 11.1 %collective-permute-start.4 = (f32[2,16,16,128]{3,2,1,0:T(8,128)S(1)}, f32[2,16,16,128]{3,2,1,0:T(8,128)S(1)}, u32[]{:S(2)}, u32[]{:S(2)}) collective-permute-start(f32[2,16,16,128]{3,2,1,0:T(8,128)S(1)} %get-tuple-element.13.own.refs_0_), channel_id=1, source_target_pairs={{0,4},{4,0},{1,5},{5,1},{2,6},{6,2},{3,7},{7,3},{8,12},{12,8},{9,1... | collective-permute-start | bytes 786440 | tf_op jit(solution)/shard_map/ppermute | solution.py:496
  11.3 7.1 %collective-permute-start.2 = (f32[15,16,128]{2,1,0:T(8,128)S(1)}, f32[15,16,128]{2,1,0:T(8,128)S(1)}, u32[]{:S(2)}, u32[]{:S(2)}) collective-permute-start(f32[15,16,128]{2,1,0:T(8,128)S(1)} %get-tuple-element.16), channel_id=1, source_target_pairs={{0,1},{1,0},{2,3},{3,2},{4,4},{5,6},{6,5},{7,7},{8,9},{9,8},{10,11... | collective-permute-start | bytes 368648 | tf_op jit(solution)/shard_map/ppermute | solution.py:496
  14.8 29.6 %copy-start = (bf16[4,256,256]{2,1,0:T(8,128)(2,1)S(1)}, bf16[4,256,256]{2,1,0:T(8,128)(2,1)}, u32[]{:S(2)}) copy-start(bf16[4,256,256]{2,1,0:T(8,128)(2,1)} %constant.22.clone.refs_12_) | copy-start | bytes 1572868
  14.8 3.6 %collective-permute-start.3 = (f32[15,16,128]{2,1,0:T(8,128)S(1)}, f32[15,16,128]{2,1,0:T(8,128)S(1)}, u32[]{:S(2)}, u32[]{:S(2)}) collective-permute-start(f32[15,16,128]{2,1,0:T(8,128)S(1)} %get-tuple-element.17), channel_id=1, source_target_pairs={{0,0},{1,2},{2,1},{3,3},{4,5},{5,4},{6,7},{7,6},{8,8},{9,10},{10,9... | collective-permute-start | bytes 368648 | tf_op jit(solution)/shard_map/ppermute | solution.py:496
  18.5 2.1 %collective-permute-start.7 = (f32[15,16,128]{2,1,0:T(8,128)S(1)}, f32[15,16,128]{2,1,0:T(8,128)S(1)}, u32[]{:S(2)}, u32[]{:S(2)}) collective-permute-start(f32[15,16,128]{2,1,0:T(8,128)S(1)} %collective-permute-done.2.refs_3_), channel_id=1, source_target_pairs={{0,4},{4,0},{1,5},{5,1},{2,6},{6,2},{3,7},{7,3},{8,12},{12,8},{9,1... | collective-permute-start | bytes 368648 | tf_op jit(solution)/shard_map/ppermute | solution.py:496
  18.5 2.1 %collective-permute-start.8 = (f32[15,16,128]{2,1,0:T(8,128)S(1)}, f32[15,16,128]{2,1,0:T(8,128)S(1)}, u32[]{:S(2)}, u32[]{:S(2)}) collective-permute-start(f32[15,16,128]{2,1,0:T(8,128)S(1)} %collective-permute-done.3.refs_4_), channel_id=1, source_target_pairs={{0,4},{4,0},{1,5},{5,1},{2,6},{6,2},{3,7},{7,3},{8,12},{12,8},{9,1... | collective-permute-start | bytes 368648 | tf_op jit(solution)/shard_map/ppermute | solution.py:496
  19.2 1.2 %collective-permute-start.5 = (f32[2,16,128]{2,1,0:T(8,128)S(1)}, f32[2,16,128]{2,1,0:T(8,128)S(1)}, u32[]{:S(2)}, u32[]{:S(2)}) collective-permute-start(f32[2,16,128]{2,1,0:T(8,128)S(1)} %collective-permute-done.x_b.refs_1_), channel_id=1, source_target_pairs={{0,4},{4,0},{1,5},{5,1},{2,6},{6,2},{3,7},{7,3},{8,12},{12,8},{9,1... | collective-permute-start | bytes 49160 | tf_op jit(solution)/shard_map/ppermute | solution.py:496
  19.2 1.3 %collective-permute-start.6 = (f32[2,16,128]{2,1,0:T(8,128)S(1)}, f32[2,16,128]{2,1,0:T(8,128)S(1)}, u32[]{:S(2)}, u32[]{:S(2)}) collective-permute-start(f32[2,16,128]{2,1,0:T(8,128)S(1)} %collective-permute-done.1.x_a.refs_2_), channel_id=1, source_target_pairs={{0,4},{4,0},{1,5},{5,1},{2,6},{6,2},{3,7},{7,3},{8,12},{12,8},{9,1... | collective-permute-start | bytes 49160 | tf_op jit(solution)/shard_map/ppermute | solution.py:496
  20.6 23.8 %copy-start.1 = (bf16[2,336,224]{2,1,0:T(8,128)(2,1)S(1)}, bf16[2,336,224]{2,1,0:T(8,128)(2,1)}, u32[]{:S(2)}) copy-start(bf16[2,336,224]{2,1,0:T(8,128)(2,1)} %constant.21.clone.refs_11_) | copy-start | bytes 903172
  25.0 6.0 %collective-permute-start.11 = (f32[64,128]{1,0:T(8,128)S(1)}, f32[64,128]{1,0:T(8,128)S(1)}, u32[]{:S(2)}, u32[]{:S(2)}) collective-permute-start(f32[64,128]{1,0:T(8,128)S(1)} %get-tuple-element.18), channel_id=1, source_target_pairs={{0,3},{1,2},{2,1},{3,0},{4,7},{5,6},{6,5},{7,4},{8,11},{9,10},{10,... | collective-permute-start | bytes 98312 | tf_op jit(solution)/shard_map/ppermute | solution.py:496
  28.0 4.9 %collective-permute-start.10 = (f32[64,128]{1,0:T(8,128)S(1)}, f32[64,128]{1,0:T(8,128)S(1)}, u32[]{:S(2)}, u32[]{:S(2)}) collective-permute-start(f32[64,128]{1,0:T(8,128)S(1)} %get-tuple-element.18), channel_id=1, source_target_pairs={{0,2},{1,3},{2,0},{3,1},{4,6},{5,7},{6,4},{7,5},{8,10},{9,11},{10,... | collective-permute-start | bytes 98312 | tf_op jit(solution)/shard_map/ppermute | solution.py:496
  30.5 3.9 %collective-permute-start.9 = (f32[64,128]{1,0:T(8,128)S(1)}, f32[64,128]{1,0:T(8,128)S(1)}, u32[]{:S(2)}, u32[]{:S(2)}) collective-permute-start(f32[64,128]{1,0:T(8,128)S(1)} %get-tuple-element.18), channel_id=1, source_target_pairs={{0,1},{1,0},{2,3},{3,2},{4,5},{5,4},{6,7},{7,6},{8,9},{9,8},{10,11... | collective-permute-start | bytes 98312 | tf_op jit(solution)/shard_map/ppermute | solution.py:496
  34.4 6.8 %collective-permute-start.14 = (f32[4,64,128]{2,1,0:T(8,128)S(1)}, f32[4,64,128]{2,1,0:T(8,128)S(1)}, u32[]{:S(2)}, u32[]{:S(2)}) collective-permute-start(f32[4,64,128]{2,1,0:T(8,128)S(1)} %pad_maximum_fusion.refs_0_), channel_id=1, source_target_pairs={{0,24},{4,28},{8,16},{12,20},{16,8},{20,12},{24,0},{28,4},{1,25},{... | collective-permute-start | bytes 393224 | tf_op jit(solution)/shard_map/ppermute | solution.py:496
  35.9 6.9 %collective-permute-start.13 = (f32[4,64,128]{2,1,0:T(8,128)S(1)}, f32[4,64,128]{2,1,0:T(8,128)S(1)}, u32[]{:S(2)}, u32[]{:S(2)}) collective-permute-start(f32[4,64,128]{2,1,0:T(8,128)S(1)} %pad_maximum_fusion.refs_0_), channel_id=1, source_target_pairs={{0,16},{4,12},{8,24},{12,4},{16,0},{20,28},{24,8},{28,20},{1,17},{... | collective-permute-start | bytes 393224 | tf_op jit(solution)/shard_map/ppermute | solution.py:496
  37.9 5.0 %collective-permute-start.12 = (f32[4,64,128]{2,1,0:T(8,128)S(1)}, f32[4,64,128]{2,1,0:T(8,128)S(1)}, u32[]{:S(2)}, u32[]{:S(2)}) collective-permute-start(f32[4,64,128]{2,1,0:T(8,128)S(1)} %pad_maximum_fusion.refs_0_), channel_id=1, source_target_pairs={{0,8},{4,20},{8,0},{12,28},{16,24},{20,4},{24,16},{28,12},{1,9},{5... | collective-permute-start | bytes 393224 | tf_op jit(solution)/shard_map/ppermute | solution.py:496
  38.0 5.4 %collective-permute-start.15 = (f32[4,64,128]{2,1,0:T(8,128)S(1)}, f32[4,64,128]{2,1,0:T(8,128)S(1)}, u32[]{:S(2)}, u32[]{:S(2)}) collective-permute-start(f32[4,64,128]{2,1,0:T(8,128)S(1)} %pad_maximum_fusion.refs_0_), channel_id=1, source_target_pairs={{0,4},{4,0},{1,5},{5,1},{2,6},{6,2},{3,7},{7,3},{8,12},{12,8},{9,1... | collective-permute-start | bytes 393224 | tf_op jit(solution)/shard_map/ppermute | solution.py:496
  41.3 2.1 %collective-permute-start.18 = (f32[4,64,128]{2,1,0:T(8,128)S(1)}, f32[4,64,128]{2,1,0:T(8,128)S(1)}, u32[]{:S(2)}, u32[]{:S(2)}) collective-permute-start(f32[4,64,128]{2,1,0:T(8,128)S(1)} %collective-permute-done.14.refs_3_), channel_id=1, source_target_pairs={{0,4},{4,0},{1,5},{5,1},{2,6},{6,2},{3,7},{7,3},{8,12},{12,8},{9,1... | collective-permute-start | bytes 393224 | tf_op jit(solution)/shard_map/ppermute | solution.py:496
  42.9 1.3 %collective-permute-start.17 = (f32[4,64,128]{2,1,0:T(8,128)S(1)}, f32[4,64,128]{2,1,0:T(8,128)S(1)}, u32[]{:S(2)}, u32[]{:S(2)}) collective-permute-start(f32[4,64,128]{2,1,0:T(8,128)S(1)} %collective-permute-done.13.refs_2_), channel_id=1, source_target_pairs={{0,4},{4,0},{1,5},{5,1},{2,6},{6,2},{3,7},{7,3},{8,12},{12,8},{9,1... | collective-permute-start | bytes 393224 | tf_op jit(solution)/shard_map/ppermute | solution.py:496
  42.9 1.5 %collective-permute-start.16 = (f32[4,64,128]{2,1,0:T(8,128)S(1)}, f32[4,64,128]{2,1,0:T(8,128)S(1)}, u32[]{:S(2)}, u32[]{:S(2)}) collective-permute-start(f32[4,64,128]{2,1,0:T(8,128)S(1)} %collective-permute-done.12.refs_1_), channel_id=1, source_target_pairs={{0,4},{4,0},{1,5},{5,1},{2,6},{6,2},{3,7},{7,3},{8,12},{12,8},{9,1... | collective-permute-start | bytes 393224 | tf_op jit(solution)/shard_map/ppermute | solution.py:496
  (6 other events, 41.8 us)

commit v9 on v8

--- a/solution.py
+++ b/solution.py
@@ -498,10 +498,6 @@
 
 def other_core(value):
     return swapped(value, ("gy",), lambda y: (1 - y,))
-
-
-def above_first():
-    return (lax.axis_index("gz") % 2 == 0) == (lax.axis_index("gy") == 0)
 
 
 def link_mask(rows, lanes):
@@ -552,9 +548,10 @@
     return right, left
 
 
-def pack_z_kernel(x_count, own, x_b, x_a, z_first, z_second):
+def pack_z_kernel(x_count, own, x_b, x_a, edges, z_a, z_b):
     _, planes, own_y, _ = own.shape
-    above = above_first()
+    z_even = lax.axis_index("gz") % 2 == 0
+    edges[0], edges[1] = x_a[...], x_b[...]
     lane = lanes_of((own_y, 128))
     skip = 8 * (planes - HALO_Z)
     at = 0
@@ -562,7 +559,7 @@
         right, left = x_halos(x_a[which], x_b[which], x_count)
         bottom = jnp.where(lane < 64, right, turned(left, 64, 1))
         top = jnp.where(lane < 64, turned(right, -skip, 1), turned(left, 64 - skip, 1))
-        for target, is_top in ((z_first, above), (z_second, jnp.logical_not(above))):
+        for target, is_top in ((z_a, z_even), (z_b, jnp.logical_not(z_even))):
             first = jnp.where(is_top, planes - count, 0)
             target[pl.ds(at, count)] = own[which, pl.ds(first, count)]
             target[sum(SENT_Z) + which] = jnp.where(is_top, top, bottom)
@@ -573,7 +570,7 @@
     _, planes, own_y, _ = own.shape
     rows = own_y + HALO_Y
     z_index = lax.axis_index("gz")
-    first_above = above_first()
+    z_even = z_index % 2 == 0
     above_at = HALO_Z + planes
     lane = lanes_of((rows, 128))
     window = source.shape[1:]
@@ -589,18 +586,16 @@
     for which, (target, count) in enumerate(zip((source, coef), SENT_Z)):
         target[pl.ds(HALO_Z, planes), :own_y, :128] = own[which]
         target[pl.ds(HALO_Z, planes), own_y:, :128] = far[0][which, :, near_rows(far[0])]
-        x_b, x_a = (joined(got[index], far[1 + index], (which,)) for index in (0, 1))
+        x_a, x_b = (joined(got[0], far[1], (index, which)) for index in (0, 1))
         right, left = x_halos(x_a, x_b, x_count)
         for plane in range(planes):
             target[HALO_Z + plane, :, 128:] = edges(right, left, 8 * plane, 8 * plane)
         for is_above, flag in ((True, z_index < z_count - 1), (False, z_index > 0)):
 
             def taken(place):
-                first = first_above if is_above else jnp.logical_not(first_above)
-                mine = jnp.where(first, got[2][place], got[3][place])
-                near = near_rows(far[3])
-                other = jnp.where(first, far[4][place, near], far[3][place, near])
-                return kept(flag, jnp.concatenate([mine, other], axis=0))
+                is_a = z_even if is_above else jnp.logical_not(z_even)
+                by_a, by_b = (joined(got[index], far[1 + index], (place,)) for index in (1, 2))
+                return kept(flag, jnp.where(is_a, by_a, by_b))
 
             packed = taken(sum(SENT_Z) + which)
             for plane in range(count):
@@ -614,9 +609,9 @@
 
 
 def first_kernel(counts, *refs):
-    own, got, far = refs[0], refs[1:5], refs[5:10]
-    left, right_source, right_coef, message, source, coef, estimate = refs[10:17]
-    *faces, residual, update, pair_source, pair_coef = refs[17:]
+    own, got, far = refs[0], refs[1:4], refs[4:8]
+    left, right_source, right_coef, message, source, estimate, *faces = refs[8:19]
+    coef, residual, update, pair_source, pair_coef = refs[19:]
     fill_window(own, got, far, source, coef, *counts)
     planes, rows, lanes = source.shape
     own_y = rows - HALO_Y
@@ -638,7 +633,7 @@
     x_count, y_count, z_count = counts
     x_index, y_index, z_index = (lax.axis_index(axis) for axis in ("gx", "gy", "gz"))
     halves, refs = (refs[:x_count], refs[x_count : 2 * x_count]), refs[2 * x_count :]
-    (source, coef, estimate), refs = refs[:3], refs[3:]
+    (source, estimate, *faces), refs = refs[:7], refs[7:]
     brought, refs = refs[:matrix_count], refs[matrix_count:]
     (solution, residual_out), scratch = refs[:2], refs[2:]
     held, scratch, done = scratch[:matrix_count], scratch[matrix_count:-1], scratch[-1]
@@ -653,8 +648,7 @@
     mid_refs = held[2:]
     mid_source, mid_coef, mid_residual, mid_update, mid_estimate, mid_correction = scratch[:6]
     mid_faces = scratch[6:11]
-    pairs, wide, residual, update, current = scratch[11:16]
-    faces = scratch[16:]
+    pairs, wide, residual, update, current = scratch[11:]
 
     planes, rows, lanes = source.shape
     own_y = rows - HALO_Y
@@ -672,12 +666,8 @@
         for x_pair in range(x_count // 2):
             x_lanes = pl.ds(pl.multiple_of(((x_index // 2) ^ x_pair) * 128, 128), 128)
             for z_block in range(z_count):
-                if x_pair == 0:
-                    mine = blocks[0][z_block]
-                    partner = jnp.where(y_block == 0, blocks[1][z_block], blocks[2][z_block])
-                else:
-                    mine = jnp.where(y_block == 0, blocks[2][z_block], blocks[1][z_block])
-                    partner = blocks[3][z_block]
+                mine = blocks[2 * x_pair][z_block]
+                partner = blocks[2 * x_pair + 1][z_block]
                 even = jnp.where(x_even, mine, partner)
                 odd = jnp.where(x_even, partner, mine)
                 where = (pl.ds(PAD + (z_index ^ z_block) * 8, 8), y_rows, x_lanes)
@@ -731,7 +721,6 @@
         mid_faces, [clipped(4), clipped(4)], mid_source, mid_residual, mid_update, mid_estimate, False
     )
 
-    plane_faces(coef, faces, 0, planes, link_mask(rows, lanes), None, source, update)
     coarse_planes = up_left.shape[1] // mid_y
     near = mid_estimate[pl.ds(z_index * 8, coarse_planes)].reshape(coarse_planes * mid_y, mid_x)
     raised = times_left(up_left[...], times_right(near, up_right[...]))
@@ -793,9 +782,17 @@
         swapped(value, ("gx",), lambda x, pairs=pairs: (pairs[x],)) for value, pairs in zip(sent, (x_b, x_a))
     ]
     z_shape = (sum(SENT_Z) + 2, own_y, 128)
-    sent = call(functools.partial(pack_z_kernel, x_count), "pack_z", 4, (both, *got), [z_shape] * 2, [])
-    got.append(swapped(sent[0], ("gy", "gz"), lambda y, z: (y, z_pairs[y][z])))
-    got.append(swapped(sent[1], ("gy", "gz"), lambda y, z: (y, z_pairs[1 - y][z])))
+    edges, *sent = call(
+        functools.partial(pack_z_kernel, x_count),
+        "pack_z",
+        4,
+        (both, *got),
+        [(2, 2, own_y, 128)] + [z_shape] * 2,
+        [],
+    )
+    got = [edges] + [
+        swapped(value, ("gz",), lambda z, pairs=pairs: (pairs[z],)) for value, pairs in zip(sent, z_pairs)
+    ]
     far = [other_core(value) for value in (both, *got)]
 
     window, padded = (planes, rows, lanes), (planes + 1, rows, lanes)
@@ -805,15 +802,15 @@
         "first",
         12,
         (both, *got, *far, *down),
-        [(own_z * own_y // 4, own_x), window, padded, window],
-        [window] * 6 + [padded] + [(own_z * own_y // 2, own_x)] * 2,
+        [(own_z * own_y // 4, own_x)] + [window] * 7,
+        [padded, window, padded] + [(own_z * own_y // 2, own_x)] * 2,
     )
 
     others = [swapped(message, ("gz",), lambda z, step=step: (z ^ step,)) for step in range(1, z_count)]
     mine = jnp.stack([message] + others)
     parts = [mine]
-    for steps in ((1, 2), (2, 1), (3, 3)):
-        parts.append(swapped(mine, ("gx", "gy"), lambda x, y, steps=steps: (x ^ steps[y], y)))
+    for step in range(1, x_count):
+        parts.append(swapped(mine, ("gx",), lambda x, step=step: (x ^ step,)))
     parts += [other_core(part) for part in parts]
 
     mid = (own_z * z_count // 2, own_y * y_count // 2, own_x * x_count // 2)
@@ -842,7 +839,6 @@
         + [(mid[0] // 2 + 2, mid[1], mid[2])]
         + [mid_padded] * 5
         + [(mid[0] // 2 * mid[1], mid[2]), (coarse_planes, rows, lanes), window, padded, padded]
-        + [window] * 5
         + [pltpu.SemaphoreType.DMA((len(matrices),))],
         far_arguments=[jnp.asarray(item) for item in matrices],
     )

time: 58.6 us -> 55 us (0.939)
  starting transfers between devices: 22 us -> 19.1 us
  Pallas kernels: 19 us -> 17.7 us
  waiting for transfers between devices: 14.7 us -> 15.4 us
    ppermute x19 -> x18, starting transfers between devices: 22 us -> 19.1 us  [swapped(): lax.ppermute(value, axes, [(int(source), int(target)) for source, target...]
    pallas_call x4, Pallas kernels: 19 us -> 17.7 us  [call(): pl.pallas_call(kernel, out_shape=tuple((jax.ShapeDtypeStruct(shape, F32)...]
    ppermute x19 -> x18, waiting for transfers between devices: 14.7 us -> 15.4 us  [swapped(): lax.ppermute(value, axes, [(int(source), int(target)) for source, target...]
  transfers between devices with their start and end apart: 19 -> 18, of which waited for: 10 -> 10; matrix products, arithmetic and copies ran while one was open for 0% -> 0% of each run, Pallas kernels for 0% -> 0%
where the time goes in v9:
time: 55 us; the launch traced here: 54.8 us
  starting transfers between devices  19.1 us (35%)
  Pallas kernels  17.7 us (32%)
  waiting for transfers between devices  15.4 us (28%)
  local copies, waits for them, and re-layouts  1.84 us (3%)
  between operations  0.76 us (1%)
    ppermute x18, starting transfers between devices, swapped(): lax.ppermute(value, axes, [(int(source), int(target)) for source, target...  19.1 us
    pallas_call x4, Pallas kernels, call(): pl.pallas_call(kernel, out_shape=tuple((jax.ShapeDtypeStruct(shape, F32)...  17.7 us
    ppermute x18, waiting for transfers between devices, swapped(): lax.ppermute(value, axes, [(int(source), int(target)) for source, target...  15.4 us
    unnamed x22, local copies, waits for them, and re-layouts  1.84 us
  transfers between devices with their start and end apart: 18, of which 10 were waited for; matrix products, arithmetic and copies ran while one was open for 0% of the time, Pallas kernels for 0%

profile of v9, /device:TPU:0, one launch (start us, length us, event | category | flops | bytes accessed | tf_op | source)
XLA Modules:
  0.0 54.8 jit_solution(3266336763663597948)
XLA Ops:
  0.6 0.9 %copy-done.2 = f32[1,16,16,128]{3,2,1,0:T(8,128)S(1)} copy-done((f32[1,16,16,128]{3,2,1,0:T(8,128)S(1)}, f32[1,16,16,128]{3,2,1,0:T(8,128)}, u32[]{:S(2)}) %copy-start.2) | copy-done | bytes 131096
  1.5 0.9 %copy-done.3 = f32[16,16,128]{2,1,0:T(8,128)S(1)} copy-done((f32[16,16,128]{2,1,0:T(8,128)S(1)}, f32[16,16,128]{2,1,0:T(8,128)}, u32[]{:S(2)}) %copy-start.3) | copy-done | bytes 131096
  2.4 0.6 %start.1 = (f32[2,16,16,128]{3,2,1,0:T(8,128)S(1)}, f32[2,16,128]{2,1,0:T(8,128)S(1)}, f32[2,16,128]{2,1,0:T(8,128)S(1)}) custom-call(f32[16,16,128]{2,1,0:T(8,128)S(1)} %bitcast.7, f32[16,16,128]{2,1,0:T(8,128)S(1)} %copy-done.3), custom_call_target="tpu_custom_call" | custom-call | tf_op jit(solution)/shard_map/start/pallas_call | solution.py:760
  3.0 0.7 %collective-permute-start = (f32[2,16,128]{2,1,0:T(8,128)S(1)}, f32[2,16,128]{2,1,0:T(8,128)S(1)}, u32[]{:S(2)}, u32[]{:S(2)}) collective-permute-start(f32[2,16,128]{2,1,0:T(8,128)S(1)} %get-tuple-element.19), channel_id=1, source_target_pairs={{0,0},{8,16},{16,8},{24,24},{1,1},{9,17},{17,9},{25,25},{2,2},{10,... | collective-permute-start | bytes 49160 | tf_op jit(solution)/shard_map/ppermute | solution.py:496
  3.7 5.7 %collective-permute-start.1 = (f32[2,16,128]{2,1,0:T(8,128)S(1)}, f32[2,16,128]{2,1,0:T(8,128)S(1)}, u32[]{:S(2)}, u32[]{:S(2)}) collective-permute-start(f32[2,16,128]{2,1,0:T(8,128)S(1)} %get-tuple-element.20), channel_id=1, source_target_pairs={{0,8},{8,0},{16,24},{24,16},{1,9},{9,1},{17,25},{25,17},{2,10},{10... | collective-permute-start | bytes 49160 | tf_op jit(solution)/shard_map/ppermute | solution.py:496
  9.5 1.8 %collective-permute-done.1.x_a = f32[2,16,128]{2,1,0:T(8,128)S(1)} collective-permute-done((f32[2,16,128]{2,1,0:T(8,128)S(1)}, f32[2,16,128]{2,1,0:T(8,128)S(1)}, u32[]{:S(2)}, u32[]{:S(2)}) %collective-permute-start.1) | collective-permute-done | bytes 16416 | tf_op jit(solution)/shard_map/ppermute | solution.py:496
  11.3 1.6 %collective-permute-start.2 = (f32[15,16,128]{2,1,0:T(8,128)S(1)}, f32[15,16,128]{2,1,0:T(8,128)S(1)}, u32[]{:S(2)}, u32[]{:S(2)}) collective-permute-start(f32[15,16,128]{2,1,0:T(8,128)S(1)} %get-tuple-element.22), channel_id=1, source_target_pairs={{0,1},{1,0},{2,3},{3,2},{4,5},{5,4},{6,7},{7,6},{8,9},{9,8},{10,11... | collective-permute-start | bytes 368648 | tf_op jit(solution)/shard_map/ppermute | solution.py:496
  12.9 0.7 %collective-permute-start.3 = (f32[15,16,128]{2,1,0:T(8,128)S(1)}, f32[15,16,128]{2,1,0:T(8,128)S(1)}, u32[]{:S(2)}, u32[]{:S(2)}) collective-permute-start(f32[15,16,128]{2,1,0:T(8,128)S(1)} %get-tuple-element.23), channel_id=1, source_target_pairs={{0,0},{1,2},{2,1},{3,3},{4,4},{5,6},{6,5},{7,7},{8,8},{9,10},{10,9... | collective-permute-start | bytes 368648 | tf_op jit(solution)/shard_map/ppermute | solution.py:496
  13.6 2.6 %collective-permute-done.2.refs_2_ = f32[15,16,128]{2,1,0:T(8,128)S(1)} collective-permute-done((f32[15,16,128]{2,1,0:T(8,128)S(1)}, f32[15,16,128]{2,1,0:T(8,128)S(1)}, u32[]{:S(2)}, u32[]{:S(2)}) %collective-permute-start.2) | collective-permute-done | bytes 122912 | tf_op jit(solution)/shard_map/ppermute | solution.py:496
  16.8 1.1 %collective-permute-done.5.refs_5_ = f32[2,2,16,128]{3,2,1,0:T(8,128)S(1)} collective-permute-done((f32[2,2,16,128]{3,2,1,0:T(8,128)S(1)}, f32[2,2,16,128]{3,2,1,0:T(8,128)S(1)}, u32[]{:S(2)}, u32[]{:S(2)}) %collective-permute-start.5) | collective-permute-done | bytes 32800 | tf_op jit(solution)/shard_map/ppermute | solution.py:496
  18.0 4.4 %first.1 = (f32[64,128]{1,0:T(8,128)S(1)}, f32[32,24,256]{2,1,0:T(8,128)S(1)}, f32[32,24,256]{2,1,0:T(8,128)S(1)}, f32[32,24,256]{2,1,0:T(8,128)S(1)}, f32[32,24...) custom-call(f32[2,16,16,128]{3,2,1,0:T(8,128)S(1)} %get-tuple-element.1, ...), custom_call_target="tpu_custom_call" | custom-call | tf_op jit(solution)/shard_map/first/pallas_call | solution.py:760
  22.5 3.6 %collective-permute-start.10 = (f32[64,128]{1,0:T(8,128)S(1)}, f32[64,128]{1,0:T(8,128)S(1)}, u32[]{:S(2)}, u32[]{:S(2)}) collective-permute-start(f32[64,128]{1,0:T(8,128)S(1)} %get-tuple-element.24), channel_id=1, source_target_pairs={{0,3},{1,2},{2,1},{3,0},{4,7},{5,6},{6,5},{7,4},{8,11},{9,10},{10,... | collective-permute-start | bytes 98312 | tf_op jit(solution)/shard_map/ppermute | solution.py:496
  26.1 2.1 %collective-permute-start.9 = (f32[64,128]{1,0:T(8,128)S(1)}, f32[64,128]{1,0:T(8,128)S(1)}, u32[]{:S(2)}, u32[]{:S(2)}) collective-permute-start(f32[64,128]{1,0:T(8,128)S(1)} %get-tuple-element.24), channel_id=1, source_target_pairs={{0,2},{1,3},{2,0},{3,1},{4,6},{5,7},{6,4},{7,5},{8,10},{9,11},{10,... | collective-permute-start | bytes 98312 | tf_op jit(solution)/shard_map/ppermute | solution.py:496
  28.2 0.5 collective-permute-start.8
  28.8 2.1 %collective-permute-done.9 = f32[64,128]{1,0:T(8,128)S(1)} collective-permute-done((f32[64,128]{1,0:T(8,128)S(1)}, f32[64,128]{1,0:T(8,128)S(1)}, u32[]{:S(2)}, u32[]{:S(2)}) %collective-permute-start.9) | collective-permute-done | bytes 32800 | tf_op jit(solution)/shard_map/ppermute | solution.py:496
  30.9 1.2 %collective-permute-done.8 = f32[64,128]{1,0:T(8,128)S(1)} collective-permute-done((f32[64,128]{1,0:T(8,128)S(1)}, f32[64,128]{1,0:T(8,128)S(1)}, u32[]{:S(2)}, u32[]{:S(2)}) %collective-permute-start.8) | collective-permute-done | bytes 32800 | tf_op jit(solution)/shard_map/ppermute | solution.py:496
  32.2 1.5 %collective-permute-start.13 = (f32[4,64,128]{2,1,0:T(8,128)S(1)}, f32[4,64,128]{2,1,0:T(8,128)S(1)}, u32[]{:S(2)}, u32[]{:S(2)}) collective-permute-start(f32[4,64,128]{2,1,0:T(8,128)S(1)} %pad_maximum_fusion.refs_0_), channel_id=1, source_target_pairs={{0,24},{8,16},{16,8},{24,0},{1,25},{9,17},{17,9},{25,1},{2,26},{10... | collective-permute-start | bytes 393224 | tf_op jit(solution)/shard_map/ppermute | solution.py:496
  33.7 2.0 %collective-permute-start.12 = (f32[4,64,128]{2,1,0:T(8,128)S(1)}, f32[4,64,128]{2,1,0:T(8,128)S(1)}, u32[]{:S(2)}, u32[]{:S(2)}) collective-permute-start(f32[4,64,128]{2,1,0:T(8,128)S(1)} %pad_maximum_fusion.refs_0_), channel_id=1, source_target_pairs={{0,16},{8,24},{16,0},{24,8},{1,17},{9,25},{17,1},{25,9},{2,18},{10... | collective-permute-start | bytes 393224 | tf_op jit(solution)/shard_map/ppermute | solution.py:496
  35.7 3.4 %collective-permute-done.13.refs_3_ = f32[4,64,128]{2,1,0:T(8,128)S(1)} collective-permute-done((f32[4,64,128]{2,1,0:T(8,128)S(1)}, f32[4,64,128]{2,1,0:T(8,128)S(1)}, u32[]{:S(2)}, u32[]{:S(2)}) %collective-permute-start.13) | collective-permute-done | bytes 131104 | tf_op jit(solution)/shard_map/ppermute | solution.py:496
  39.2 1.1 %collective-permute-done.12.refs_2_ = f32[4,64,128]{2,1,0:T(8,128)S(1)} collective-permute-done((f32[4,64,128]{2,1,0:T(8,128)S(1)}, f32[4,64,128]{2,1,0:T(8,128)S(1)}, u32[]{:S(2)}, u32[]{:S(2)}) %collective-permute-start.12) | collective-permute-done | bytes 131104 | tf_op jit(solution)/shard_map/ppermute | solution.py:496
  40.3 0.5 collective-permute-done.11.refs_1_
  40.8 0.8 %collective-permute-done.16.refs_6_ = f32[4,64,128]{2,1,0:T(8,128)S(1)} collective-permute-done((f32[4,64,128]{2,1,0:T(8,128)S(1)}, f32[4,64,128]{2,1,0:T(8,128)S(1)}, u32[]{:S(2)}, u32[]{:S(2)}) %collective-permute-start.16) | collective-permute-done | bytes 131104 | tf_op jit(solution)/shard_map/ppermute | solution.py:496
  41.6 0.5 collective-permute-done.15.refs_5_
  42.2 12.6 %second.1 = (f32[16,16,128]{2,1,0:T(8,128)}, f32[16,16,128]{2,1,0:T(8,128)}) custom-call(f32[4,64,128]{2,1,0:T(8,128)S(1)} %pad_maximum_fusion.refs_0_, f32[4,64,128]{2,1,0:T(8,128)S(1)} %collective-permute-done.11.refs_1_, f32[4,64,128]{2,1,0:T(8,128)S(1)} %collective-permute-done.12.refs_2_, f32[4,64,128]{2,1,0:T(8,128)S(1)} %collective-permute-done.13.refs_3_, ...), custom_call_target="tpu_custom_call" | custom-call | tf_op jit(solution)/shard_map/second/pallas_call | solution.py:760
  (39 shorter events, 0.8 us)
Async XLA Ops:
  3.0 6.4 %collective-permute-start = (f32[2,16,128]{2,1,0:T(8,128)S(1)}, f32[2,16,128]{2,1,0:T(8,128)S(1)}, u32[]{:S(2)}, u32[]{:S(2)}) collective-permute-start(f32[2,16,128]{2,1,0:T(8,128)S(1)} %get-tuple-element.19), channel_id=1, source_target_pairs={{0,0},{8,16},{16,8},{24,24},{1,1},{9,17},{17,9},{25,25},{2,2},{10,... | collective-permute-start | bytes 49160 | tf_op jit(solution)/shard_map/ppermute | solution.py:496
  3.7 7.5 %collective-permute-start.1 = (f32[2,16,128]{2,1,0:T(8,128)S(1)}, f32[2,16,128]{2,1,0:T(8,128)S(1)}, u32[]{:S(2)}, u32[]{:S(2)}) collective-permute-start(f32[2,16,128]{2,1,0:T(8,128)S(1)} %get-tuple-element.20), channel_id=1, source_target_pairs={{0,8},{8,0},{16,24},{24,16},{1,9},{9,1},{17,25},{25,17},{2,10},{10... | collective-permute-start | bytes 49160 | tf_op jit(solution)/shard_map/ppermute | solution.py:496
  9.5 8.5 %collective-permute-start.4 = (f32[2,16,16,128]{3,2,1,0:T(8,128)S(1)}, f32[2,16,16,128]{3,2,1,0:T(8,128)S(1)}, u32[]{:S(2)}, u32[]{:S(2)}) collective-permute-start(f32[2,16,16,128]{3,2,1,0:T(8,128)S(1)} %get-tuple-element.18.own.refs_0_), channel_id=1, source_target_pairs={{0,4},{4,0},{1,5},{5,1},{2,6},{6,2},{3,7},{7,3},{8,12},{12,8},{9,1... | collective-permute-start | bytes 786440 | tf_op jit(solution)/shard_map/ppermute | solution.py:496
  11.3 4.9 %collective-permute-start.2 = (f32[15,16,128]{2,1,0:T(8,128)S(1)}, f32[15,16,128]{2,1,0:T(8,128)S(1)}, u32[]{:S(2)}, u32[]{:S(2)}) collective-permute-start(f32[15,16,128]{2,1,0:T(8,128)S(1)} %get-tuple-element.22), channel_id=1, source_target_pairs={{0,1},{1,0},{2,3},{3,2},{4,5},{5,4},{6,7},{7,6},{8,9},{9,8},{10,11... | collective-permute-start | bytes 368648 | tf_op jit(solution)/shard_map/ppermute | solution.py:496
  12.9 3.3 %collective-permute-start.3 = (f32[15,16,128]{2,1,0:T(8,128)S(1)}, f32[15,16,128]{2,1,0:T(8,128)S(1)}, u32[]{:S(2)}, u32[]{:S(2)}) collective-permute-start(f32[15,16,128]{2,1,0:T(8,128)S(1)} %get-tuple-element.23), channel_id=1, source_target_pairs={{0,0},{1,2},{2,1},{3,3},{4,4},{5,6},{6,5},{7,7},{8,8},{9,10},{10,9... | collective-permute-start | bytes 368648 | tf_op jit(solution)/shard_map/ppermute | solution.py:496
  16.3 1.7 %collective-permute-start.6 = (f32[15,16,128]{2,1,0:T(8,128)S(1)}, f32[15,16,128]{2,1,0:T(8,128)S(1)}, u32[]{:S(2)}, u32[]{:S(2)}) collective-permute-start(f32[15,16,128]{2,1,0:T(8,128)S(1)} %collective-permute-done.2.refs_2_), channel_id=1, source_target_pairs={{0,4},{4,0},{1,5},{5,1},{2,6},{6,2},{3,7},{7,3},{8,12},{12,8},{9,1... | collective-permute-start | bytes 368648 | tf_op jit(solution)/shard_map/ppermute | solution.py:496
  16.3 1.7 %collective-permute-start.7 = (f32[15,16,128]{2,1,0:T(8,128)S(1)}, f32[15,16,128]{2,1,0:T(8,128)S(1)}, u32[]{:S(2)}, u32[]{:S(2)}) collective-permute-start(f32[15,16,128]{2,1,0:T(8,128)S(1)} %collective-permute-done.3.refs_3_), channel_id=1, source_target_pairs={{0,4},{4,0},{1,5},{5,1},{2,6},{6,2},{3,7},{7,3},{8,12},{12,8},{9,1... | collective-permute-start | bytes 368648 | tf_op jit(solution)/shard_map/ppermute | solution.py:496
  16.8 25.4 %copy-start = (bf16[4,256,256]{2,1,0:T(8,128)(2,1)S(1)}, bf16[4,256,256]{2,1,0:T(8,128)(2,1)}, u32[]{:S(2)}) copy-start(bf16[4,256,256]{2,1,0:T(8,128)(2,1)} %constant.22.clone.refs_16_) | copy-start | bytes 1572868
  16.8 1.2 %collective-permute-start.5 = (f32[2,2,16,128]{3,2,1,0:T(8,128)S(1)}, f32[2,2,16,128]{3,2,1,0:T(8,128)S(1)}, u32[]{:S(2)}, u32[]{:S(2)}) collective-permute-start(f32[2,2,16,128]{3,2,1,0:T(8,128)S(1)} %get-tuple-element.21.refs_1_), channel_id=1, source_target_pairs={{0,4},{4,0},{1,5},{5,1},{2,6},{6,2},{3,7},{7,3},{8,12},{12,8},{9,1... | collective-permute-start | bytes 98312 | tf_op jit(solution)/shard_map/ppermute | solution.py:496
  18.0 24.2 %copy-start.1 = (bf16[2,336,224]{2,1,0:T(8,128)(2,1)S(1)}, bf16[2,336,224]{2,1,0:T(8,128)(2,1)}, u32[]{:S(2)}) copy-start(bf16[2,336,224]{2,1,0:T(8,128)(2,1)} %constant.21.clone.refs_15_) | copy-start | bytes 903172
  22.5 6.3 %collective-permute-start.10 = (f32[64,128]{1,0:T(8,128)S(1)}, f32[64,128]{1,0:T(8,128)S(1)}, u32[]{:S(2)}, u32[]{:S(2)}) collective-permute-start(f32[64,128]{1,0:T(8,128)S(1)} %get-tuple-element.24), channel_id=1, source_target_pairs={{0,3},{1,2},{2,1},{3,0},{4,7},{5,6},{6,5},{7,4},{8,11},{9,10},{10,... | collective-permute-start | bytes 98312 | tf_op jit(solution)/shard_map/ppermute | solution.py:496
  26.1 4.8 %collective-permute-start.9 = (f32[64,128]{1,0:T(8,128)S(1)}, f32[64,128]{1,0:T(8,128)S(1)}, u32[]{:S(2)}, u32[]{:S(2)}) collective-permute-start(f32[64,128]{1,0:T(8,128)S(1)} %get-tuple-element.24), channel_id=1, source_target_pairs={{0,2},{1,3},{2,0},{3,1},{4,6},{5,7},{6,4},{7,5},{8,10},{9,11},{10,... | collective-permute-start | bytes 98312 | tf_op jit(solution)/shard_map/ppermute | solution.py:496
  28.2 3.9 %collective-permute-start.8 = (f32[64,128]{1,0:T(8,128)S(1)}, f32[64,128]{1,0:T(8,128)S(1)}, u32[]{:S(2)}, u32[]{:S(2)}) collective-permute-start(f32[64,128]{1,0:T(8,128)S(1)} %get-tuple-element.24), channel_id=1, source_target_pairs={{0,1},{1,0},{2,3},{3,2},{4,5},{5,4},{6,7},{7,6},{8,9},{9,8},{10,11... | collective-permute-start | bytes 98312 | tf_op jit(solution)/shard_map/ppermute | solution.py:496
  32.2 10.0 %copy-start.4 = (bf16[128,256]{1,0:T(8,128)(2,1)S(1)}, bf16[128,256]{1,0:T(8,128)(2,1)}, u32[]{:S(2)}) copy-start(bf16[128,256]{1,0:T(8,128)(2,1)} %constant.26.clone.refs_20_) | copy-start | bytes 196612
  32.2 10.0 %copy-start.5 = (bf16[256,128]{1,0:T(8,128)(2,1)S(1)}, bf16[256,128]{1,0:T(8,128)(2,1)}, u32[]{:S(2)}) copy-start(bf16[256,128]{1,0:T(8,128)(2,1)} %constant.25.clone.refs_19_) | copy-start | bytes 196612
  32.2 10.0 %copy-start.6 = (bf16[256,128]{1,0:T(8,128)(2,1)S(1)}, bf16[256,128]{1,0:T(8,128)(2,1)}, u32[]{:S(2)}) copy-start(bf16[256,128]{1,0:T(8,128)(2,1)} %constant.24.clone.refs_18_) | copy-start | bytes 196612
  32.2 10.0 %copy-start.7 = (bf16[128,256]{1,0:T(8,128)(2,1)S(1)}, bf16[128,256]{1,0:T(8,128)(2,1)}, u32[]{:S(2)}) copy-start(bf16[128,256]{1,0:T(8,128)(2,1)} %constant.23.clone.refs_17_) | copy-start | bytes 196612
  32.2 7.0 %collective-permute-start.13 = (f32[4,64,128]{2,1,0:T(8,128)S(1)}, f32[4,64,128]{2,1,0:T(8,128)S(1)}, u32[]{:S(2)}, u32[]{:S(2)}) collective-permute-start(f32[4,64,128]{2,1,0:T(8,128)S(1)} %pad_maximum_fusion.refs_0_), channel_id=1, source_target_pairs={{0,24},{8,16},{16,8},{24,0},{1,25},{9,17},{17,9},{25,1},{2,26},{10... | collective-permute-start | bytes 393224 | tf_op jit(solution)/shard_map/ppermute | solution.py:496
  33.7 6.6 %collective-permute-start.12 = (f32[4,64,128]{2,1,0:T(8,128)S(1)}, f32[4,64,128]{2,1,0:T(8,128)S(1)}, u32[]{:S(2)}, u32[]{:S(2)}) collective-permute-start(f32[4,64,128]{2,1,0:T(8,128)S(1)} %pad_maximum_fusion.refs_0_), channel_id=1, source_target_pairs={{0,16},{8,24},{16,0},{24,8},{1,17},{9,25},{17,1},{25,9},{2,18},{10... | collective-permute-start | bytes 393224 | tf_op jit(solution)/shard_map/ppermute | solution.py:496
  35.7 5.2 %collective-permute-start.11 = (f32[4,64,128]{2,1,0:T(8,128)S(1)}, f32[4,64,128]{2,1,0:T(8,128)S(1)}, u32[]{:S(2)}, u32[]{:S(2)}) collective-permute-start(f32[4,64,128]{2,1,0:T(8,128)S(1)} %pad_maximum_fusion.refs_0_), channel_id=1, source_target_pairs={{0,8},{8,0},{16,24},{24,16},{1,9},{9,1},{17,25},{25,17},{2,10},{10... | collective-permute-start | bytes 393224 | tf_op jit(solution)/shard_map/ppermute | solution.py:496
  35.7 5.1 %collective-permute-start.14 = (f32[4,64,128]{2,1,0:T(8,128)S(1)}, f32[4,64,128]{2,1,0:T(8,128)S(1)}, u32[]{:S(2)}, u32[]{:S(2)}) collective-permute-start(f32[4,64,128]{2,1,0:T(8,128)S(1)} %pad_maximum_fusion.refs_0_), channel_id=1, source_target_pairs={{0,4},{4,0},{1,5},{5,1},{2,6},{6,2},{3,7},{7,3},{8,12},{12,8},{9,1... | collective-permute-start | bytes 393224 | tf_op jit(solution)/shard_map/ppermute | solution.py:496
  39.2 1.7 %collective-permute-start.17 = (f32[4,64,128]{2,1,0:T(8,128)S(1)}, f32[4,64,128]{2,1,0:T(8,128)S(1)}, u32[]{:S(2)}, u32[]{:S(2)}) collective-permute-start(f32[4,64,128]{2,1,0:T(8,128)S(1)} %collective-permute-done.13.refs_3_), channel_id=1, source_target_pairs={{0,4},{4,0},{1,5},{5,1},{2,6},{6,2},{3,7},{7,3},{8,12},{12,8},{9,1... | collective-permute-start | bytes 393224 | tf_op jit(solution)/shard_map/ppermute | solution.py:496
  40.3 1.3 %collective-permute-start.16 = (f32[4,64,128]{2,1,0:T(8,128)S(1)}, f32[4,64,128]{2,1,0:T(8,128)S(1)}, u32[]{:S(2)}, u32[]{:S(2)}) collective-permute-start(f32[4,64,128]{2,1,0:T(8,128)S(1)} %collective-permute-done.12.refs_2_), channel_id=1, source_target_pairs={{0,4},{4,0},{1,5},{5,1},{2,6},{6,2},{3,7},{7,3},{8,12},{12,8},{9,1... | collective-permute-start | bytes 393224 | tf_op jit(solution)/shard_map/ppermute | solution.py:496
  40.8 1.3 %collective-permute-start.15 = (f32[4,64,128]{2,1,0:T(8,128)S(1)}, f32[4,64,128]{2,1,0:T(8,128)S(1)}, u32[]{:S(2)}, u32[]{:S(2)}) collective-permute-start(f32[4,64,128]{2,1,0:T(8,128)S(1)} %collective-permute-done.11.refs_1_), channel_id=1, source_target_pairs={{0,4},{4,0},{1,5},{5,1},{2,6},{6,2},{3,7},{7,3},{8,12},{12,8},{9,1... | collective-permute-start | bytes 393224 | tf_op jit(solution)/shard_map/ppermute | solution.py:496
  (5 other events, 25.6 us)

commit v10 on v9

--- a/solution.py
+++ b/solution.py
@@ -379,27 +379,31 @@
     return jnp.where(places(shape, axis) < stop, 1.0, 0.0)
 
 
+def strides_of(stride):
+    return 1, stride, stride
+
+
 def sheet_faces(coef, stride):
     total = 3.0 * coef
     faces = []
-    for axis, count in enumerate(coef.shape):
-        link = up_to(coef.shape, axis, count - stride)
-        above = link * moved(coef, stride, axis)
-        below = moved(link * coef, -stride, axis)
+    for axis, step in enumerate(strides_of(stride)):
+        link = up_to(coef.shape, axis, coef.shape[axis] - step)
+        above = link * moved(coef, step, axis)
+        below = moved(link * coef, -step, axis)
         faces.append((link * (0.5 * (coef + above)), axis))
         total = total + 0.5 * (above + below)
     inside = coef > 0.0
-    for axis in range(3):
+    for axis in (1, 2):
         inside = inside & (places(coef.shape, axis) % stride == 0)
     inverse = jnp.where(inside, 1.0 / jnp.where(inside, total, 1.0), 0.0)
-    return faces, total, inverse, stride
+    return faces, total, inverse, strides_of(stride)
 
 
 def sheet_apply(field, face_set):
-    faces, diagonal, _, stride = face_set
+    faces, diagonal, _, steps = face_set
     value = diagonal * field
-    for face, axis in faces:
-        value = value - (face * moved(field, stride, axis) + moved(face * field, -stride, axis))
+    for (face, axis), step in zip(faces, steps):
+        value = value - (face * moved(field, step, axis) + moved(face * field, -step, axis))
     return value
 
 
@@ -415,17 +419,27 @@
 
 
 def sheet_down(value, stride):
-    for axis in range(3):
+    pairs = value.reshape((value.shape[0] // 2, 2) + value.shape[1:])
+    value = pairs[:, 0] + pairs[:, 1]
+    for axis in (1, 2):
         value = value + moved(value, stride, axis)
     return value
 
 
 def sheet_up(value, stride):
-    for axis, count in enumerate(value.shape):
+    for axis in (1, 2):
+        count = value.shape[axis]
         far = moved(value * up_to(value.shape, axis, count - 2 * stride), -2 * stride, axis)
         near = moved(value, stride, axis) * up_to(value.shape, axis, count - stride)
         value = 0.75 * (value + moved(value, -stride, axis)) + 0.25 * (far + near)
-    return value
+    return planes_up(value, jnp.zeros_like(value[:1]), jnp.zeros_like(value[:1]))
+
+
+def planes_up(value, before, after):
+    own, low = 0.75 * value, 0.25 * jnp.concatenate([before, value[:-1]], axis=0)
+    high = 0.25 * jnp.concatenate([value[1:], after], axis=0)
+    pairs = jnp.stack([own + low, own + high], axis=1)
+    return pairs.reshape((2 * value.shape[0],) + value.shape[1:])
 
 
 def sheet_cycle(source, coef, depth):
@@ -528,10 +542,10 @@
         copy.wait()
         right = left = jnp.zeros(lane.shape, F32)
         for plane in range(planes):
-            value = both[which, plane]
-            slot = (lane >= 8 * plane) & (lane < 8 * plane + 8)
-            right = jnp.where(slot, turned(value, 8 * plane + 8, 1), right)
-            left = jnp.where(slot, turned(value, 8 * plane, 1), left)
+            value = turned(both[which, plane], 8 * plane + 8, 1)
+            right = jnp.where(lane // 8 == plane, value, right)
+            left = jnp.where(lane // 8 == (plane + 1) % 16, value, left)
+        left = turned(left, -8, 1)
         x_a[which] = jnp.where(x_even, right, left)
         x_b[which] = jnp.where(x_even, left, right)
 
@@ -578,18 +592,22 @@
     def joined(ref, other, place):
         return jnp.concatenate([ref[place], other[(*place, near_rows(other))]], axis=0)
 
-    def edges(right, left, right_shift, left_shift):
-        value = jnp.where(lane < 8, turned(right, -right_shift, 1), turned(left, 120 - left_shift, 1))
-        return jnp.where((lane < 8) | (lane >= 120), value, 0.0)
+    def edge_packs(right, left):
+        left = turned(left, -8, 1)
+        odd_slot = lane // 8 % 2 == 1
+        return jnp.where(odd_slot, left, right), jnp.where(odd_slot, right, left)
+
+    def edges(packs, plane):
+        return jnp.where((lane < 8) | (lane >= 120), turned(packs[plane % 2], -8 * plane, 1), 0.0)
 
     sent_at = 0
     for which, (target, count) in enumerate(zip((source, coef), SENT_Z)):
         target[pl.ds(HALO_Z, planes), :own_y, :128] = own[which]
         target[pl.ds(HALO_Z, planes), own_y:, :128] = far[0][which, :, near_rows(far[0])]
         x_a, x_b = (joined(got[0], far[1], (index, which)) for index in (0, 1))
-        right, left = x_halos(x_a, x_b, x_count)
+        packs = edge_packs(*x_halos(x_a, x_b, x_count))
         for plane in range(planes):
-            target[HALO_Z + plane, :, 128:] = edges(right, left, 8 * plane, 8 * plane)
+            target[HALO_Z + plane, :, 128:] = edges(packs, plane)
         for is_above, flag in ((True, z_index < z_count - 1), (False, z_index > 0)):
 
             def taken(place):
@@ -598,11 +616,12 @@
                 return kept(flag, jnp.where(is_a, by_a, by_b))
 
             packed = taken(sum(SENT_Z) + which)
+            packs = edge_packs(packed, turned(packed, 64, 1))
             for plane in range(count):
                 slot = plane if is_above else HALO_Z - count + plane
                 at = above_at + slot if is_above else slot
                 target[at, :, :128] = taken(sent_at + plane)
-                target[at, :, 128:] = edges(packed, packed, 8 * slot, 64 + 8 * slot)
+                target[at, :, 128:] = edges(packs, slot)
         for at in (*range(HALO_Z - count), *range(above_at + count, target.shape[0])):
             target[at] = jnp.zeros(window, F32)
         sent_at += count
@@ -648,7 +667,7 @@
     mid_refs = held[2:]
     mid_source, mid_coef, mid_residual, mid_update, mid_estimate, mid_correction = scratch[:6]
     mid_faces = scratch[6:11]
-    pairs, wide, residual, update, current = scratch[11:]
+    residual_pairs, coef_pairs, wide, residual, update, current = scratch[11:]
 
     planes, rows, lanes = source.shape
     own_y = rows - HALO_Y
@@ -682,17 +701,27 @@
     plane_faces(mid_coef, mid_faces, start, stop, link_y, link_x, mid_source, mid_update)
     ranges = [(start, stop)] * (DEGREE - 1)
     plane_steps(mid_faces, ranges, mid_source, mid_residual, mid_update, mid_estimate, True, 8)
-    plane_residual(mid_faces, start, stop, mid_residual, mid_update, 8)
+
+    def finish_pairs(here, own):
+        before = mid_residual[here]
+        rows_here = pl.ds((here.start - PAD) // 2 * mid_y, 4 * mid_y)
+
+        def store(value):
+            left = (before - value).reshape(4, 2, mid_y, mid_x)
+            residual_pairs[rows_here] = (left[:, 0] + left[:, 1]).reshape(4 * mid_y, mid_x)
+            own_coef = mid_coef[here].reshape(4, 2, mid_y, mid_x)
+            coef_pairs[rows_here] = (own_coef[:, 0] + own_coef[:, 1]).reshape(4 * mid_y, mid_x)
+
+        return store
+
+    plane_sweep(mid_faces, start, stop, mid_update, finish_pairs, 8)
 
     for copy in copies:
         copy.wait()
     left_down, right_down, mid_left_up, mid_right_up = mid_refs
     sheets = []
-    for ref, scale in ((mid_residual, 4.0), (mid_coef, 1.0)):
-        for pair in range(mid_z // 2):
-            low = PAD + 2 * pair
-            pairs[pl.ds(pair * mid_y, mid_y)] = ref[low] + ref[low + 1]
-        sheets.append(scale * times_right(times_left(left_down[...], pairs[...]), right_down[...]))
+    for ref, scale in ((residual_pairs, 4.0), (coef_pairs, 1.0)):
+        sheets.append(scale * times_right(times_left(left_down[...], ref[...]), right_down[...]))
     shape = (mid_z // 2, mid_y // 2, mid_x // 2)
     correction = sheet_cycle(sheets[0].reshape(shape), sheets[1].reshape(shape), 2)
     correction = correction.reshape(mid_z * mid_y // 4, mid_x // 2)
@@ -702,11 +731,13 @@
     mid_correction[pl.ds(0, 1)] = zero[:1]
     mid_correction[pl.ds(1 + mid_z // 2, 1)] = zero[:1]
 
-    def add_mid(pair, carry):
-        own = 0.75 * mid_correction[pair + 1]
-        low = PAD + 2 * pair
-        mid_estimate[low] = mid_estimate[low] + (own + 0.25 * mid_correction[pair])
-        mid_estimate[low + 1] = mid_estimate[low + 1] + (own + 0.25 * mid_correction[pair + 2])
+    def add_mid(index, carry):
+        first = carry + 4 * index
+        here, last = pl.ds(PAD + 2 * first, 8), first + 4
+        step = planes_up(
+            mid_correction[pl.ds(first + 1, 4)], mid_correction[pl.ds(first, 1)], mid_correction[pl.ds(last + 1, 1)]
+        )
+        mid_estimate[here] = mid_estimate[here] + step
         return carry
 
     def clipped(margin):
@@ -714,8 +745,8 @@
         high = jnp.minimum(z_index * 8 + 8 + margin, mid_z)
         return PAD + low, PAD + high
 
-    low, high = clipped(6)
-    lax.fori_loop((low - PAD) // 2, (high - PAD) // 2, add_mid, 0)
+    low, high = clipped(8)
+    lax.fori_loop(0, (high - low) // 8, add_mid, (low - PAD) // 2)
     plane_restart(mid_faces, *clipped(8), mid_source, mid_residual, mid_update, mid_estimate)
     plane_steps(
         mid_faces, [clipped(4), clipped(4)], mid_source, mid_residual, mid_update, mid_estimate, False
@@ -727,15 +758,10 @@
     wide[...] = raised.reshape(coarse_planes, rows, lanes)
     inverse = faces[4]
 
-    def add_fine(place, carry):
-        own = 0.75 * wide[place]
-        for offset, other in ((0, place - 1), (1, place + 1)):
-            plane = 2 * place + HALO_Z - 2 * PAD + offset
-            step = own + 0.25 * wide[other]
-            current[plane] = estimate[plane] + jnp.where(inverse[plane] > 0.0, step, 0.0)
-        return carry
-
-    lax.fori_loop(1, coarse_planes - 1, add_fine, 0)
+    for first in range(1, coarse_planes - 1, 4):
+        here = pl.ds(2 * first + HALO_Z - 2 * PAD, 8)
+        step = planes_up(wide[pl.ds(first, 4)], wide[pl.ds(first - 1, 1)], wide[pl.ds(first + 4, 1)])
+        current[here] = estimate[here] + jnp.where(inverse[here] > 0.0, step, 0.0)
     for plane in (HALO_Z - 5, planes - HALO_Z + 4):
         current[plane] = estimate[plane]
     plane_restart(faces, HALO_Z - 4, planes - HALO_Z + 4, source, residual, update, current)
@@ -838,7 +864,8 @@
         + [mid_padded] * 5
         + [(mid[0] // 2 + 2, mid[1], mid[2])]
         + [mid_padded] * 5
-        + [(mid[0] // 2 * mid[1], mid[2]), (coarse_planes, rows, lanes), window, padded, padded]
+        + [(mid[0] // 2 * mid[1], mid[2])] * 2
+        + [(coarse_planes, rows, lanes), window, padded, padded]
         + [pltpu.SemaphoreType.DMA((len(matrices),))],
         far_arguments=[jnp.asarray(item) for item in matrices],
     )

time: 55 us -> 54.6 us (level)
  no operation moved by 1% of the time
where the time goes in v10:
time: 54.6 us; the launch traced here: 54.4 us
  starting transfers between devices  19.1 us (35%)
  Pallas kernels  17.3 us (32%)
  waiting for transfers between devices  15.4 us (28%)
  local copies, waits for them, and re-layouts  1.84 us (3%)
  between operations  0.76 us (1%)
    ppermute x18, starting transfers between devices, swapped(): lax.ppermute(value, axes, [(int(source), int(target)) for source, target...  19.1 us
    pallas_call x4, Pallas kernels, call(): pl.pallas_call(kernel, out_shape=tuple((jax.ShapeDtypeStruct(shape, F32)...  17.3 us
    ppermute x18, waiting for transfers between devices, swapped(): lax.ppermute(value, axes, [(int(source), int(target)) for source, target...  15.4 us
    unnamed x22, local copies, waits for them, and re-layouts  1.84 us
  transfers between devices with their start and end apart: 18, of which 10 were waited for; matrix products, arithmetic and copies ran while one was open for 0% of the time, Pallas kernels for 0%

profile of v10, /device:TPU:0, one launch (start us, length us, event | category | flops | bytes accessed | tf_op | source)
XLA Modules:
  0.0 54.4 jit_solution(211615630711332317)
XLA Ops:
  0.6 0.9 %copy-done.2 = f32[1,16,16,128]{3,2,1,0:T(8,128)S(1)} copy-done((f32[1,16,16,128]{3,2,1,0:T(8,128)S(1)}, f32[1,16,16,128]{3,2,1,0:T(8,128)}, u32[]{:S(2)}) %copy-start.2) | copy-done | bytes 131096
  1.5 0.9 %copy-done.3 = f32[16,16,128]{2,1,0:T(8,128)S(1)} copy-done((f32[16,16,128]{2,1,0:T(8,128)S(1)}, f32[16,16,128]{2,1,0:T(8,128)}, u32[]{:S(2)}) %copy-start.3) | copy-done | bytes 131096
  2.4 0.7 %start.1 = (f32[2,16,16,128]{3,2,1,0:T(8,128)S(1)}, f32[2,16,128]{2,1,0:T(8,128)S(1)}, f32[2,16,128]{2,1,0:T(8,128)S(1)}) custom-call(f32[16,16,128]{2,1,0:T(8,128)S(1)} %bitcast.7, f32[16,16,128]{2,1,0:T(8,128)S(1)} %copy-done.3), custom_call_target="tpu_custom_call" | custom-call | tf_op jit(solution)/shard_map/start/pallas_call | solution.py:786
  3.1 0.7 %collective-permute-start = (f32[2,16,128]{2,1,0:T(8,128)S(1)}, f32[2,16,128]{2,1,0:T(8,128)S(1)}, u32[]{:S(2)}, u32[]{:S(2)}) collective-permute-start(f32[2,16,128]{2,1,0:T(8,128)S(1)} %get-tuple-element.19), channel_id=1, source_target_pairs={{0,0},{8,16},{16,8},{24,24},{1,1},{9,17},{17,9},{25,25},{2,2},{10,... | collective-permute-start | bytes 49160 | tf_op jit(solution)/shard_map/ppermute | solution.py:510
  3.8 5.7 %collective-permute-start.1 = (f32[2,16,128]{2,1,0:T(8,128)S(1)}, f32[2,16,128]{2,1,0:T(8,128)S(1)}, u32[]{:S(2)}, u32[]{:S(2)}) collective-permute-start(f32[2,16,128]{2,1,0:T(8,128)S(1)} %get-tuple-element.20), channel_id=1, source_target_pairs={{0,8},{8,0},{16,24},{24,16},{1,9},{9,1},{17,25},{25,17},{2,10},{10... | collective-permute-start | bytes 49160 | tf_op jit(solution)/shard_map/ppermute | solution.py:510
  9.5 1.8 %collective-permute-done.1.x_a = f32[2,16,128]{2,1,0:T(8,128)S(1)} collective-permute-done((f32[2,16,128]{2,1,0:T(8,128)S(1)}, f32[2,16,128]{2,1,0:T(8,128)S(1)}, u32[]{:S(2)}, u32[]{:S(2)}) %collective-permute-start.1) | collective-permute-done | bytes 16416 | tf_op jit(solution)/shard_map/ppermute | solution.py:510
  11.4 1.6 %collective-permute-start.2 = (f32[15,16,128]{2,1,0:T(8,128)S(1)}, f32[15,16,128]{2,1,0:T(8,128)S(1)}, u32[]{:S(2)}, u32[]{:S(2)}) collective-permute-start(f32[15,16,128]{2,1,0:T(8,128)S(1)} %get-tuple-element.22), channel_id=1, source_target_pairs={{0,1},{1,0},{2,3},{3,2},{4,5},{5,4},{6,7},{7,6},{8,9},{9,8},{10,11... | collective-permute-start | bytes 368648 | tf_op jit(solution)/shard_map/ppermute | solution.py:510
  13.0 0.7 %collective-permute-start.3 = (f32[15,16,128]{2,1,0:T(8,128)S(1)}, f32[15,16,128]{2,1,0:T(8,128)S(1)}, u32[]{:S(2)}, u32[]{:S(2)}) collective-permute-start(f32[15,16,128]{2,1,0:T(8,128)S(1)} %get-tuple-element.23), channel_id=1, source_target_pairs={{0,0},{1,2},{2,1},{3,3},{4,4},{5,6},{6,5},{7,7},{8,8},{9,10},{10,9... | collective-permute-start | bytes 368648 | tf_op jit(solution)/shard_map/ppermute | solution.py:510
  13.7 2.6 %collective-permute-done.2.refs_2_ = f32[15,16,128]{2,1,0:T(8,128)S(1)} collective-permute-done((f32[15,16,128]{2,1,0:T(8,128)S(1)}, f32[15,16,128]{2,1,0:T(8,128)S(1)}, u32[]{:S(2)}, u32[]{:S(2)}) %collective-permute-start.2) | collective-permute-done | bytes 122912 | tf_op jit(solution)/shard_map/ppermute | solution.py:510
  16.9 1.1 %collective-permute-done.5.refs_5_ = f32[2,2,16,128]{3,2,1,0:T(8,128)S(1)} collective-permute-done((f32[2,2,16,128]{3,2,1,0:T(8,128)S(1)}, f32[2,2,16,128]{3,2,1,0:T(8,128)S(1)}, u32[]{:S(2)}, u32[]{:S(2)}) %collective-permute-start.5) | collective-permute-done | bytes 32800 | tf_op jit(solution)/shard_map/ppermute | solution.py:510
  18.1 4.3 %first.1 = (f32[64,128]{1,0:T(8,128)S(1)}, f32[32,24,256]{2,1,0:T(8,128)S(1)}, f32[32,24,256]{2,1,0:T(8,128)S(1)}, f32[32,24,256]{2,1,0:T(8,128)S(1)}, f32[32,24...) custom-call(f32[2,16,16,128]{3,2,1,0:T(8,128)S(1)} %get-tuple-element.1, ...), custom_call_target="tpu_custom_call" | custom-call | tf_op jit(solution)/shard_map/first/pallas_call | solution.py:786
  22.4 3.6 %collective-permute-start.10 = (f32[64,128]{1,0:T(8,128)S(1)}, f32[64,128]{1,0:T(8,128)S(1)}, u32[]{:S(2)}, u32[]{:S(2)}) collective-permute-start(f32[64,128]{1,0:T(8,128)S(1)} %get-tuple-element.24), channel_id=1, source_target_pairs={{0,3},{1,2},{2,1},{3,0},{4,7},{5,6},{6,5},{7,4},{8,11},{9,10},{10,... | collective-permute-start | bytes 98312 | tf_op jit(solution)/shard_map/ppermute | solution.py:510
  26.1 2.1 %collective-permute-start.9 = (f32[64,128]{1,0:T(8,128)S(1)}, f32[64,128]{1,0:T(8,128)S(1)}, u32[]{:S(2)}, u32[]{:S(2)}) collective-permute-start(f32[64,128]{1,0:T(8,128)S(1)} %get-tuple-element.24), channel_id=1, source_target_pairs={{0,2},{1,3},{2,0},{3,1},{4,6},{5,7},{6,4},{7,5},{8,10},{9,11},{10,... | collective-permute-start | bytes 98312 | tf_op jit(solution)/shard_map/ppermute | solution.py:510
  28.2 0.5 collective-permute-start.8
  28.7 2.1 %collective-permute-done.9 = f32[64,128]{1,0:T(8,128)S(1)} collective-permute-done((f32[64,128]{1,0:T(8,128)S(1)}, f32[64,128]{1,0:T(8,128)S(1)}, u32[]{:S(2)}, u32[]{:S(2)}) %collective-permute-start.9) | collective-permute-done | bytes 32800 | tf_op jit(solution)/shard_map/ppermute | solution.py:510
  30.9 1.2 %collective-permute-done.8 = f32[64,128]{1,0:T(8,128)S(1)} collective-permute-done((f32[64,128]{1,0:T(8,128)S(1)}, f32[64,128]{1,0:T(8,128)S(1)}, u32[]{:S(2)}, u32[]{:S(2)}) %collective-permute-start.8) | collective-permute-done | bytes 32800 | tf_op jit(solution)/shard_map/ppermute | solution.py:510
  32.1 1.5 %collective-permute-start.13 = (f32[4,64,128]{2,1,0:T(8,128)S(1)}, f32[4,64,128]{2,1,0:T(8,128)S(1)}, u32[]{:S(2)}, u32[]{:S(2)}) collective-permute-start(f32[4,64,128]{2,1,0:T(8,128)S(1)} %pad_maximum_fusion.refs_0_), channel_id=1, source_target_pairs={{0,24},{8,16},{16,8},{24,0},{1,25},{9,17},{17,9},{25,1},{2,26},{10... | collective-permute-start | bytes 393224 | tf_op jit(solution)/shard_map/ppermute | solution.py:510
  33.6 2.0 %collective-permute-start.12 = (f32[4,64,128]{2,1,0:T(8,128)S(1)}, f32[4,64,128]{2,1,0:T(8,128)S(1)}, u32[]{:S(2)}, u32[]{:S(2)}) collective-permute-start(f32[4,64,128]{2,1,0:T(8,128)S(1)} %pad_maximum_fusion.refs_0_), channel_id=1, source_target_pairs={{0,16},{8,24},{16,0},{24,8},{1,17},{9,25},{17,1},{25,9},{2,18},{10... | collective-permute-start | bytes 393224 | tf_op jit(solution)/shard_map/ppermute | solution.py:510
  35.7 3.4 %collective-permute-done.13.refs_3_ = f32[4,64,128]{2,1,0:T(8,128)S(1)} collective-permute-done((f32[4,64,128]{2,1,0:T(8,128)S(1)}, f32[4,64,128]{2,1,0:T(8,128)S(1)}, u32[]{:S(2)}, u32[]{:S(2)}) %collective-permute-start.13) | collective-permute-done | bytes 131104 | tf_op jit(solution)/shard_map/ppermute | solution.py:510
  39.1 1.1 %collective-permute-done.12.refs_2_ = f32[4,64,128]{2,1,0:T(8,128)S(1)} collective-permute-done((f32[4,64,128]{2,1,0:T(8,128)S(1)}, f32[4,64,128]{2,1,0:T(8,128)S(1)}, u32[]{:S(2)}, u32[]{:S(2)}) %collective-permute-start.12) | collective-permute-done | bytes 131104 | tf_op jit(solution)/shard_map/ppermute | solution.py:510
  40.2 0.5 collective-permute-done.11.refs_1_
  40.8 0.8 %collective-permute-done.16.refs_6_ = f32[4,64,128]{2,1,0:T(8,128)S(1)} collective-permute-done((f32[4,64,128]{2,1,0:T(8,128)S(1)}, f32[4,64,128]{2,1,0:T(8,128)S(1)}, u32[]{:S(2)}, u32[]{:S(2)}) %collective-permute-start.16) | collective-permute-done | bytes 131104 | tf_op jit(solution)/shard_map/ppermute | solution.py:510
  41.6 0.5 collective-permute-done.15.refs_5_
  42.2 12.2 %second.1 = (f32[16,16,128]{2,1,0:T(8,128)}, f32[16,16,128]{2,1,0:T(8,128)}) custom-call(f32[4,64,128]{2,1,0:T(8,128)S(1)} %pad_maximum_fusion.refs_0_, f32[4,64,128]{2,1,0:T(8,128)S(1)} %collective-permute-done.11.refs_1_, f32[4,64,128]{2,1,0:T(8,128)S(1)} %collective-permute-done.12.refs_2_, f32[4,64,128]{2,1,0:T(8,128)S(1)} %collective-permute-done.13.refs_3_, ...), custom_call_target="tpu_custom_call" | custom-call | tf_op jit(solution)/shard_map/second/pallas_call | solution.py:786
  (39 shorter events, 0.8 us)
Async XLA Ops:
  3.1 6.4 %collective-permute-start = (f32[2,16,128]{2,1,0:T(8,128)S(1)}, f32[2,16,128]{2,1,0:T(8,128)S(1)}, u32[]{:S(2)}, u32[]{:S(2)}) collective-permute-start(f32[2,16,128]{2,1,0:T(8,128)S(1)} %get-tuple-element.19), channel_id=1, source_target_pairs={{0,0},{8,16},{16,8},{24,24},{1,1},{9,17},{17,9},{25,25},{2,2},{10,... | collective-permute-start | bytes 49160 | tf_op jit(solution)/shard_map/ppermute | solution.py:510
  3.8 7.5 %collective-permute-start.1 = (f32[2,16,128]{2,1,0:T(8,128)S(1)}, f32[2,16,128]{2,1,0:T(8,128)S(1)}, u32[]{:S(2)}, u32[]{:S(2)}) collective-permute-start(f32[2,16,128]{2,1,0:T(8,128)S(1)} %get-tuple-element.20), channel_id=1, source_target_pairs={{0,8},{8,0},{16,24},{24,16},{1,9},{9,1},{17,25},{25,17},{2,10},{10... | collective-permute-start | bytes 49160 | tf_op jit(solution)/shard_map/ppermute | solution.py:510
  9.5 8.5 %collective-permute-start.4 = (f32[2,16,16,128]{3,2,1,0:T(8,128)S(1)}, f32[2,16,16,128]{3,2,1,0:T(8,128)S(1)}, u32[]{:S(2)}, u32[]{:S(2)}) collective-permute-start(f32[2,16,16,128]{3,2,1,0:T(8,128)S(1)} %get-tuple-element.18.own.refs_0_), channel_id=1, source_target_pairs={{0,4},{4,0},{1,5},{5,1},{2,6},{6,2},{3,7},{7,3},{8,12},{12,8},{9,1... | collective-permute-start | bytes 786440 | tf_op jit(solution)/shard_map/ppermute | solution.py:510
  11.4 4.9 %collective-permute-start.2 = (f32[15,16,128]{2,1,0:T(8,128)S(1)}, f32[15,16,128]{2,1,0:T(8,128)S(1)}, u32[]{:S(2)}, u32[]{:S(2)}) collective-permute-start(f32[15,16,128]{2,1,0:T(8,128)S(1)} %get-tuple-element.22), channel_id=1, source_target_pairs={{0,1},{1,0},{2,3},{3,2},{4,5},{5,4},{6,7},{7,6},{8,9},{9,8},{10,11... | collective-permute-start | bytes 368648 | tf_op jit(solution)/shard_map/ppermute | solution.py:510
  13.0 3.3 %collective-permute-start.3 = (f32[15,16,128]{2,1,0:T(8,128)S(1)}, f32[15,16,128]{2,1,0:T(8,128)S(1)}, u32[]{:S(2)}, u32[]{:S(2)}) collective-permute-start(f32[15,16,128]{2,1,0:T(8,128)S(1)} %get-tuple-element.23), channel_id=1, source_target_pairs={{0,0},{1,2},{2,1},{3,3},{4,4},{5,6},{6,5},{7,7},{8,8},{9,10},{10,9... | collective-permute-start | bytes 368648 | tf_op jit(solution)/shard_map/ppermute | solution.py:510
  16.3 1.7 %collective-permute-start.6 = (f32[15,16,128]{2,1,0:T(8,128)S(1)}, f32[15,16,128]{2,1,0:T(8,128)S(1)}, u32[]{:S(2)}, u32[]{:S(2)}) collective-permute-start(f32[15,16,128]{2,1,0:T(8,128)S(1)} %collective-permute-done.2.refs_2_), channel_id=1, source_target_pairs={{0,4},{4,0},{1,5},{5,1},{2,6},{6,2},{3,7},{7,3},{8,12},{12,8},{9,1... | collective-permute-start | bytes 368648 | tf_op jit(solution)/shard_map/ppermute | solution.py:510
  16.3 1.7 %collective-permute-start.7 = (f32[15,16,128]{2,1,0:T(8,128)S(1)}, f32[15,16,128]{2,1,0:T(8,128)S(1)}, u32[]{:S(2)}, u32[]{:S(2)}) collective-permute-start(f32[15,16,128]{2,1,0:T(8,128)S(1)} %collective-permute-done.3.refs_3_), channel_id=1, source_target_pairs={{0,4},{4,0},{1,5},{5,1},{2,6},{6,2},{3,7},{7,3},{8,12},{12,8},{9,1... | collective-permute-start | bytes 368648 | tf_op jit(solution)/shard_map/ppermute | solution.py:510
  16.8 25.3 %copy-start = (bf16[4,256,256]{2,1,0:T(8,128)(2,1)S(1)}, bf16[4,256,256]{2,1,0:T(8,128)(2,1)}, u32[]{:S(2)}) copy-start(bf16[4,256,256]{2,1,0:T(8,128)(2,1)} %constant.22.clone.refs_16_) | copy-start | bytes 1572868
  16.8 1.2 %collective-permute-start.5 = (f32[2,2,16,128]{3,2,1,0:T(8,128)S(1)}, f32[2,2,16,128]{3,2,1,0:T(8,128)S(1)}, u32[]{:S(2)}, u32[]{:S(2)}) collective-permute-start(f32[2,2,16,128]{3,2,1,0:T(8,128)S(1)} %get-tuple-element.21.refs_1_), channel_id=1, source_target_pairs={{0,4},{4,0},{1,5},{5,1},{2,6},{6,2},{3,7},{7,3},{8,12},{12,8},{9,1... | collective-permute-start | bytes 98312 | tf_op jit(solution)/shard_map/ppermute | solution.py:510
  18.1 24.0 %copy-start.1 = (bf16[2,336,224]{2,1,0:T(8,128)(2,1)S(1)}, bf16[2,336,224]{2,1,0:T(8,128)(2,1)}, u32[]{:S(2)}) copy-start(bf16[2,336,224]{2,1,0:T(8,128)(2,1)} %constant.21.clone.refs_15_) | copy-start | bytes 903172
  22.4 6.3 %collective-permute-start.10 = (f32[64,128]{1,0:T(8,128)S(1)}, f32[64,128]{1,0:T(8,128)S(1)}, u32[]{:S(2)}, u32[]{:S(2)}) collective-permute-start(f32[64,128]{1,0:T(8,128)S(1)} %get-tuple-element.24), channel_id=1, source_target_pairs={{0,3},{1,2},{2,1},{3,0},{4,7},{5,6},{6,5},{7,4},{8,11},{9,10},{10,... | collective-permute-start | bytes 98312 | tf_op jit(solution)/shard_map/ppermute | solution.py:510
  26.1 4.8 %collective-permute-start.9 = (f32[64,128]{1,0:T(8,128)S(1)}, f32[64,128]{1,0:T(8,128)S(1)}, u32[]{:S(2)}, u32[]{:S(2)}) collective-permute-start(f32[64,128]{1,0:T(8,128)S(1)} %get-tuple-element.24), channel_id=1, source_target_pairs={{0,2},{1,3},{2,0},{3,1},{4,6},{5,7},{6,4},{7,5},{8,10},{9,11},{10,... | collective-permute-start | bytes 98312 | tf_op jit(solution)/shard_map/ppermute | solution.py:510
  28.2 3.9 %collective-permute-start.8 = (f32[64,128]{1,0:T(8,128)S(1)}, f32[64,128]{1,0:T(8,128)S(1)}, u32[]{:S(2)}, u32[]{:S(2)}) collective-permute-start(f32[64,128]{1,0:T(8,128)S(1)} %get-tuple-element.24), channel_id=1, source_target_pairs={{0,1},{1,0},{2,3},{3,2},{4,5},{5,4},{6,7},{7,6},{8,9},{9,8},{10,11... | collective-permute-start | bytes 98312 | tf_op jit(solution)/shard_map/ppermute | solution.py:510
  32.1 10.0 %copy-start.4 = (bf16[128,256]{1,0:T(8,128)(2,1)S(1)}, bf16[128,256]{1,0:T(8,128)(2,1)}, u32[]{:S(2)}) copy-start(bf16[128,256]{1,0:T(8,128)(2,1)} %constant.26.clone.refs_20_) | copy-start | bytes 196612
  32.1 10.0 %copy-start.5 = (bf16[256,128]{1,0:T(8,128)(2,1)S(1)}, bf16[256,128]{1,0:T(8,128)(2,1)}, u32[]{:S(2)}) copy-start(bf16[256,128]{1,0:T(8,128)(2,1)} %constant.25.clone.refs_19_) | copy-start | bytes 196612
  32.1 10.0 %copy-start.6 = (bf16[256,128]{1,0:T(8,128)(2,1)S(1)}, bf16[256,128]{1,0:T(8,128)(2,1)}, u32[]{:S(2)}) copy-start(bf16[256,128]{1,0:T(8,128)(2,1)} %constant.24.clone.refs_18_) | copy-start | bytes 196612
  32.1 10.0 %copy-start.7 = (bf16[128,256]{1,0:T(8,128)(2,1)S(1)}, bf16[128,256]{1,0:T(8,128)(2,1)}, u32[]{:S(2)}) copy-start(bf16[128,256]{1,0:T(8,128)(2,1)} %constant.23.clone.refs_17_) | copy-start | bytes 196612
  32.1 7.0 %collective-permute-start.13 = (f32[4,64,128]{2,1,0:T(8,128)S(1)}, f32[4,64,128]{2,1,0:T(8,128)S(1)}, u32[]{:S(2)}, u32[]{:S(2)}) collective-permute-start(f32[4,64,128]{2,1,0:T(8,128)S(1)} %pad_maximum_fusion.refs_0_), channel_id=1, source_target_pairs={{0,24},{8,16},{16,8},{24,0},{1,25},{9,17},{17,9},{25,1},{2,26},{10... | collective-permute-start | bytes 393224 | tf_op jit(solution)/shard_map/ppermute | solution.py:510
  33.6 6.6 %collective-permute-start.12 = (f32[4,64,128]{2,1,0:T(8,128)S(1)}, f32[4,64,128]{2,1,0:T(8,128)S(1)}, u32[]{:S(2)}, u32[]{:S(2)}) collective-permute-start(f32[4,64,128]{2,1,0:T(8,128)S(1)} %pad_maximum_fusion.refs_0_), channel_id=1, source_target_pairs={{0,16},{8,24},{16,0},{24,8},{1,17},{9,25},{17,1},{25,9},{2,18},{10... | collective-permute-start | bytes 393224 | tf_op jit(solution)/shard_map/ppermute | solution.py:510
  35.6 5.2 %collective-permute-start.11 = (f32[4,64,128]{2,1,0:T(8,128)S(1)}, f32[4,64,128]{2,1,0:T(8,128)S(1)}, u32[]{:S(2)}, u32[]{:S(2)}) collective-permute-start(f32[4,64,128]{2,1,0:T(8,128)S(1)} %pad_maximum_fusion.refs_0_), channel_id=1, source_target_pairs={{0,8},{8,0},{16,24},{24,16},{1,9},{9,1},{17,25},{25,17},{2,10},{10... | collective-permute-start | bytes 393224 | tf_op jit(solution)/shard_map/ppermute | solution.py:510
  35.7 5.1 %collective-permute-start.14 = (f32[4,64,128]{2,1,0:T(8,128)S(1)}, f32[4,64,128]{2,1,0:T(8,128)S(1)}, u32[]{:S(2)}, u32[]{:S(2)}) collective-permute-start(f32[4,64,128]{2,1,0:T(8,128)S(1)} %pad_maximum_fusion.refs_0_), channel_id=1, source_target_pairs={{0,4},{4,0},{1,5},{5,1},{2,6},{6,2},{3,7},{7,3},{8,12},{12,8},{9,1... | collective-permute-start | bytes 393224 | tf_op jit(solution)/shard_map/ppermute | solution.py:510
  39.1 1.7 %collective-permute-start.17 = (f32[4,64,128]{2,1,0:T(8,128)S(1)}, f32[4,64,128]{2,1,0:T(8,128)S(1)}, u32[]{:S(2)}, u32[]{:S(2)}) collective-permute-start(f32[4,64,128]{2,1,0:T(8,128)S(1)} %collective-permute-done.13.refs_3_), channel_id=1, source_target_pairs={{0,4},{4,0},{1,5},{5,1},{2,6},{6,2},{3,7},{7,3},{8,12},{12,8},{9,1... | collective-permute-start | bytes 393224 | tf_op jit(solution)/shard_map/ppermute | solution.py:510
  40.2 1.3 %collective-permute-start.16 = (f32[4,64,128]{2,1,0:T(8,128)S(1)}, f32[4,64,128]{2,1,0:T(8,128)S(1)}, u32[]{:S(2)}, u32[]{:S(2)}) collective-permute-start(f32[4,64,128]{2,1,0:T(8,128)S(1)} %collective-permute-done.12.refs_2_), channel_id=1, source_target_pairs={{0,4},{4,0},{1,5},{5,1},{2,6},{6,2},{3,7},{7,3},{8,12},{12,8},{9,1... | collective-permute-start | bytes 393224 | tf_op jit(solution)/shard_map/ppermute | solution.py:510
  40.8 1.3 %collective-permute-start.15 = (f32[4,64,128]{2,1,0:T(8,128)S(1)}, f32[4,64,128]{2,1,0:T(8,128)S(1)}, u32[]{:S(2)}, u32[]{:S(2)}) collective-permute-start(f32[4,64,128]{2,1,0:T(8,128)S(1)} %collective-permute-done.11.refs_1_), channel_id=1, source_target_pairs={{0,4},{4,0},{1,5},{5,1},{2,6},{6,2},{3,7},{7,3},{8,12},{12,8},{9,1... | collective-permute-start | bytes 393224 | tf_op jit(solution)/shard_map/ppermute | solution.py:510
  (5 other events, 25.6 us)

commit v11 on v10

--- a/solution.py
+++ b/solution.py
@@ -529,10 +529,10 @@
     return pl.ds(pl.multiple_of(first, HALO_Y), HALO_Y)
 
 
-def start_kernel(source, coef, both, x_b, x_a, done):
-    _, planes, own_y, _ = both.shape
+def start_kernel(source, coef, x_b, x_a, blocks, done):
+    _, planes, own_y, _ = blocks.shape
     copies = [
-        pltpu.make_async_copy(ref, both.at[which], done.at[which]) for which, ref in enumerate((source, coef))
+        pltpu.make_async_copy(ref, blocks.at[which], done.at[which]) for which, ref in enumerate((source, coef))
     ]
     for copy in copies:
         copy.start()
@@ -542,10 +542,10 @@
         copy.wait()
         right = left = jnp.zeros(lane.shape, F32)
         for plane in range(planes):
-            value = turned(both[which, plane], 8 * plane + 8, 1)
-            right = jnp.where(lane // 8 == plane, value, right)
-            left = jnp.where(lane // 8 == (plane + 1) % 16, value, left)
-        left = turned(left, -8, 1)
+            value = blocks[which, plane]
+            slot = (lane >= 8 * plane) & (lane < 8 * plane + 8)
+            right = jnp.where(slot, turned(value, 8 * plane + 8, 1), right)
+            left = jnp.where(slot, turned(value, 8 * plane, 1), left)
         x_a[which] = jnp.where(x_even, right, left)
         x_b[which] = jnp.where(x_even, left, right)
 
@@ -795,13 +795,14 @@
 
     x_a, x_b = swap_pairs(x_count, False), swap_pairs(x_count, True)
     z_pairs = swap_pairs(z_count, False), swap_pairs(z_count, True)
-    both, *sent = call(
+    both = jnp.stack([right_side, coefficient])
+    sent = call(
         start_kernel,
         "start",
-        4,
+        60,
         (),
-        [(2, own_z, own_y, own_x)] + [(2, own_y, 128)] * 2,
-        [pltpu.SemaphoreType.DMA((2,))],
+        [(2, own_y, 128)] * 2,
+        [(2, own_z, own_y, own_x), pltpu.SemaphoreType.DMA((2,))],
         (right_side, coefficient),
     )
     got = [

time: 54.6 us -> 54.3 us (level)
  local copies, waits for them, and re-layouts: 1.84 us -> 0.05 us
  Pallas kernels: 17.3 us -> 18.5 us
    unnamed x22, local copies, waits for them, and re-layouts: 1.84 us -> 0.05 us
    pallas_call x4, Pallas kernels: 17.3 us -> 18.5 us  [call(): pl.pallas_call(kernel, out_shape=tuple((jax.ShapeDtypeStruct(shape, F32)...]
where the time goes in v11:
time: 54.3 us; the launch traced here: 54 us
  starting transfers between devices  19.2 us (35%)
  Pallas kernels  18.5 us (34%)
  waiting for transfers between devices  15.5 us (29%)
  between operations  0.8 us (1%)
    ppermute x18, starting transfers between devices, swapped(): lax.ppermute(value, axes, [(int(source), int(target)) for source, target...  19.2 us
    pallas_call x4, Pallas kernels, call(): pl.pallas_call(kernel, out_shape=tuple((jax.ShapeDtypeStruct(shape, F32)...  18.5 us
    ppermute x18, waiting for transfers between devices, swapped(): lax.ppermute(value, axes, [(int(source), int(target)) for source, target...  15.5 us
  transfers between devices with their start and end apart: 18, of which 10 were waited for; matrix products, arithmetic and copies ran while one was open for 0% of the time, Pallas kernels for 0%

profile of v11, /device:TPU:0, one launch (start us, length us, event | category | flops | bytes accessed | tf_op | source)
XLA Modules:
  0.0 54.0 jit_solution(11402270948619828910)
XLA Ops:
  0.6 1.9 %start.1 = (f32[2,16,128]{2,1,0:T(8,128)}, f32[2,16,128]{2,1,0:T(8,128)}) custom-call(f32[16,16,128]{2,1,0:T(8,128)} %bitcast.10, f32[16,16,128]{2,1,0:T(8,128)} %coef.1), custom_call_target="tpu_custom_call" | custom-call | tf_op jit(solution)/shard_map/start/pallas_call | solution.py:786
  2.5 1.4 %collective-permute-start = (f32[2,16,128]{2,1,0:T(8,128)}, f32[2,16,128]{2,1,0:T(8,128)S(1)}, u32[]{:S(2)}, u32[]{:S(2)}) collective-permute-start(f32[2,16,128]{2,1,0:T(8,128)} %get-tuple-element.17), channel_id=1, source_target_pairs={{0,0},{8,16},{16,8},{24,24},{1,1},{9,17},{17,9},{25,25},{2,2},{10,... | collective-permute-start | bytes 49160 | tf_op jit(solution)/shard_map/ppermute | solution.py:510
  3.9 5.0 %collective-permute-start.1 = (f32[2,16,128]{2,1,0:T(8,128)}, f32[2,16,128]{2,1,0:T(8,128)S(1)}, u32[]{:S(2)}, u32[]{:S(2)}) collective-permute-start(f32[2,16,128]{2,1,0:T(8,128)} %get-tuple-element.18), channel_id=1, source_target_pairs={{0,8},{8,0},{16,24},{24,16},{1,9},{9,1},{17,25},{25,17},{2,10},{10... | collective-permute-start | bytes 49160 | tf_op jit(solution)/shard_map/ppermute | solution.py:510
  9.1 1.9 %collective-permute-done.1.x_a = f32[2,16,128]{2,1,0:T(8,128)S(1)} collective-permute-done((f32[2,16,128]{2,1,0:T(8,128)}, f32[2,16,128]{2,1,0:T(8,128)S(1)}, u32[]{:S(2)}, u32[]{:S(2)}) %collective-permute-start.1) | collective-permute-done | bytes 16416 | tf_op jit(solution)/shard_map/ppermute | solution.py:510
  11.0 1.6 %collective-permute-start.2 = (f32[15,16,128]{2,1,0:T(8,128)S(1)}, f32[15,16,128]{2,1,0:T(8,128)S(1)}, u32[]{:S(2)}, u32[]{:S(2)}) collective-permute-start(f32[15,16,128]{2,1,0:T(8,128)S(1)} %get-tuple-element.20), channel_id=1, source_target_pairs={{0,1},{1,0},{2,3},{3,2},{4,5},{5,4},{6,7},{7,6},{8,9},{9,8},{10,11... | collective-permute-start | bytes 368648 | tf_op jit(solution)/shard_map/ppermute | solution.py:510
  12.6 0.7 %collective-permute-start.3 = (f32[15,16,128]{2,1,0:T(8,128)S(1)}, f32[15,16,128]{2,1,0:T(8,128)S(1)}, u32[]{:S(2)}, u32[]{:S(2)}) collective-permute-start(f32[15,16,128]{2,1,0:T(8,128)S(1)} %get-tuple-element.21), channel_id=1, source_target_pairs={{0,0},{1,2},{2,1},{3,3},{4,4},{5,6},{6,5},{7,7},{8,8},{9,10},{10,9... | collective-permute-start | bytes 368648 | tf_op jit(solution)/shard_map/ppermute | solution.py:510
  13.3 2.6 %collective-permute-done.2.refs_2_ = f32[15,16,128]{2,1,0:T(8,128)S(1)} collective-permute-done((f32[15,16,128]{2,1,0:T(8,128)S(1)}, f32[15,16,128]{2,1,0:T(8,128)S(1)}, u32[]{:S(2)}, u32[]{:S(2)}) %collective-permute-start.2) | collective-permute-done | bytes 122912 | tf_op jit(solution)/shard_map/ppermute | solution.py:510
  15.9 0.5 collective-permute-start.7
  16.5 1.1 %collective-permute-done.5.refs_5_ = f32[2,2,16,128]{3,2,1,0:T(8,128)S(1)} collective-permute-done((f32[2,2,16,128]{3,2,1,0:T(8,128)S(1)}, f32[2,2,16,128]{3,2,1,0:T(8,128)S(1)}, u32[]{:S(2)}, u32[]{:S(2)}) %collective-permute-start.5) | collective-permute-done | bytes 32800 | tf_op jit(solution)/shard_map/ppermute | solution.py:510
  17.7 4.3 %first.1 = (f32[64,128]{1,0:T(8,128)S(1)}, f32[32,24,256]{2,1,0:T(8,128)S(1)}, f32[32,24,256]{2,1,0:T(8,128)S(1)}, f32[32,24,256]{2,1,0:T(8,128)S(1)}, f32[32,24...) custom-call(f32[2,16,16,128]{3,2,1,0:T(8,128)S(1)} %pad_maximum_fusion., ...), custom_call_target="tpu_custom_call" | custom-call | tf_op jit(solution)/shard_map/first/pallas_call | solution.py:786
  22.0 3.6 %collective-permute-start.10 = (f32[64,128]{1,0:T(8,128)S(1)}, f32[64,128]{1,0:T(8,128)S(1)}, u32[]{:S(2)}, u32[]{:S(2)}) collective-permute-start(f32[64,128]{1,0:T(8,128)S(1)} %get-tuple-element.22), channel_id=1, source_target_pairs={{0,3},{1,2},{2,1},{3,0},{4,7},{5,6},{6,5},{7,4},{8,11},{9,10},{10,... | collective-permute-start | bytes 98312 | tf_op jit(solution)/shard_map/ppermute | solution.py:510
  25.7 2.1 %collective-permute-start.9 = (f32[64,128]{1,0:T(8,128)S(1)}, f32[64,128]{1,0:T(8,128)S(1)}, u32[]{:S(2)}, u32[]{:S(2)}) collective-permute-start(f32[64,128]{1,0:T(8,128)S(1)} %get-tuple-element.22), channel_id=1, source_target_pairs={{0,2},{1,3},{2,0},{3,1},{4,6},{5,7},{6,4},{7,5},{8,10},{9,11},{10,... | collective-permute-start | bytes 98312 | tf_op jit(solution)/shard_map/ppermute | solution.py:510
  27.8 0.5 collective-permute-start.8
  28.3 2.1 %collective-permute-done.9 = f32[64,128]{1,0:T(8,128)S(1)} collective-permute-done((f32[64,128]{1,0:T(8,128)S(1)}, f32[64,128]{1,0:T(8,128)S(1)}, u32[]{:S(2)}, u32[]{:S(2)}) %collective-permute-start.9) | collective-permute-done | bytes 32800 | tf_op jit(solution)/shard_map/ppermute | solution.py:510
  30.5 1.2 %collective-permute-done.8 = f32[64,128]{1,0:T(8,128)S(1)} collective-permute-done((f32[64,128]{1,0:T(8,128)S(1)}, f32[64,128]{1,0:T(8,128)S(1)}, u32[]{:S(2)}, u32[]{:S(2)}) %collective-permute-start.8) | collective-permute-done | bytes 32800 | tf_op jit(solution)/shard_map/ppermute | solution.py:510
  31.8 1.5 %collective-permute-start.13 = (f32[4,64,128]{2,1,0:T(8,128)S(1)}, f32[4,64,128]{2,1,0:T(8,128)S(1)}, u32[]{:S(2)}, u32[]{:S(2)}) collective-permute-start(f32[4,64,128]{2,1,0:T(8,128)S(1)} %pad_maximum_fusion.1.refs_0_), channel_id=1, source_target_pairs={{0,24},{8,16},{16,8},{24,0},{1,25},{9,17},{17,9},{25,1},{2,26},{10... | collective-permute-start | bytes 393224 | tf_op jit(solution)/shard_map/ppermute | solution.py:510
  33.3 2.0 %collective-permute-start.12 = (f32[4,64,128]{2,1,0:T(8,128)S(1)}, f32[4,64,128]{2,1,0:T(8,128)S(1)}, u32[]{:S(2)}, u32[]{:S(2)}) collective-permute-start(f32[4,64,128]{2,1,0:T(8,128)S(1)} %pad_maximum_fusion.1.refs_0_), channel_id=1, source_target_pairs={{0,16},{8,24},{16,0},{24,8},{1,17},{9,25},{17,1},{25,9},{2,18},{10... | collective-permute-start | bytes 393224 | tf_op jit(solution)/shard_map/ppermute | solution.py:510
  35.2 0.1 collective-permute-start.11
  35.3 3.4 %collective-permute-done.13.refs_3_ = f32[4,64,128]{2,1,0:T(8,128)S(1)} collective-permute-done((f32[4,64,128]{2,1,0:T(8,128)S(1)}, f32[4,64,128]{2,1,0:T(8,128)S(1)}, u32[]{:S(2)}, u32[]{:S(2)}) %collective-permute-start.13) | collective-permute-done | bytes 131104 | tf_op jit(solution)/shard_map/ppermute | solution.py:510
  38.7 1.1 %collective-permute-done.12.refs_2_ = f32[4,64,128]{2,1,0:T(8,128)S(1)} collective-permute-done((f32[4,64,128]{2,1,0:T(8,128)S(1)}, f32[4,64,128]{2,1,0:T(8,128)S(1)}, u32[]{:S(2)}, u32[]{:S(2)}) %collective-permute-start.12) | collective-permute-done | bytes 131104 | tf_op jit(solution)/shard_map/ppermute | solution.py:510
  39.9 0.5 collective-permute-done.11.refs_1_
  40.4 0.8 %collective-permute-done.16.refs_6_ = f32[4,64,128]{2,1,0:T(8,128)S(1)} collective-permute-done((f32[4,64,128]{2,1,0:T(8,128)S(1)}, f32[4,64,128]{2,1,0:T(8,128)S(1)}, u32[]{:S(2)}, u32[]{:S(2)}) %collective-permute-start.16) | collective-permute-done | bytes 131104 | tf_op jit(solution)/shard_map/ppermute | solution.py:510
  41.2 0.5 collective-permute-done.15.refs_5_
  41.8 12.2 %second.1 = (f32[16,16,128]{2,1,0:T(8,128)}, f32[16,16,128]{2,1,0:T(8,128)}) custom-call(f32[4,64,128]{2,1,0:T(8,128)S(1)} %pad_maximum_fusion.1.refs_0_, f32[4,64,128]{2,1,0:T(8,128)S(1)} %collective-permute-done.11.refs_1_, f32[4,64,128]{2,1,0:T(8,128)S(1)} %collective-permute-done.12.refs_2_, f32[4,64,128]{2,1,0:T(8,128)S(1)} %collective-permute-done.13.refs_3_, ...), custom_call_target="tpu_custom_call" | custom-call | tf_op jit(solution)/shard_map/second/pallas_call | solution.py:786
  (40 shorter events, 0.3 us)
Async XLA Ops:
  2.5 6.5 %collective-permute-start = (f32[2,16,128]{2,1,0:T(8,128)}, f32[2,16,128]{2,1,0:T(8,128)S(1)}, u32[]{:S(2)}, u32[]{:S(2)}) collective-permute-start(f32[2,16,128]{2,1,0:T(8,128)} %get-tuple-element.17), channel_id=1, source_target_pairs={{0,0},{8,16},{16,8},{24,24},{1,1},{9,17},{17,9},{25,25},{2,2},{10,... | collective-permute-start | bytes 49160 | tf_op jit(solution)/shard_map/ppermute | solution.py:510
  3.9 7.0 %collective-permute-start.1 = (f32[2,16,128]{2,1,0:T(8,128)}, f32[2,16,128]{2,1,0:T(8,128)S(1)}, u32[]{:S(2)}, u32[]{:S(2)}) collective-permute-start(f32[2,16,128]{2,1,0:T(8,128)} %get-tuple-element.18), channel_id=1, source_target_pairs={{0,8},{8,0},{16,24},{24,16},{1,9},{9,1},{17,25},{25,17},{2,10},{10... | collective-permute-start | bytes 49160 | tf_op jit(solution)/shard_map/ppermute | solution.py:510
  9.0 8.7 %collective-permute-start.4 = (f32[2,16,16,128]{3,2,1,0:T(8,128)S(1)}, f32[2,16,16,128]{3,2,1,0:T(8,128)S(1)}, u32[]{:S(2)}, u32[]{:S(2)}) collective-permute-start(f32[2,16,16,128]{3,2,1,0:T(8,128)S(1)} %pad_maximum_fusion.own.refs_0_), channel_id=1, source_target_pairs={{0,4},{4,0},{1,5},{5,1},{2,6},{6,2},{3,7},{7,3},{8,12},{12,8},{9,1... | collective-permute-start | bytes 786440 | tf_op jit(solution)/shard_map/ppermute | solution.py:510
  11.0 4.9 %collective-permute-start.2 = (f32[15,16,128]{2,1,0:T(8,128)S(1)}, f32[15,16,128]{2,1,0:T(8,128)S(1)}, u32[]{:S(2)}, u32[]{:S(2)}) collective-permute-start(f32[15,16,128]{2,1,0:T(8,128)S(1)} %get-tuple-element.20), channel_id=1, source_target_pairs={{0,1},{1,0},{2,3},{3,2},{4,5},{5,4},{6,7},{7,6},{8,9},{9,8},{10,11... | collective-permute-start | bytes 368648 | tf_op jit(solution)/shard_map/ppermute | solution.py:510
  12.6 3.3 %collective-permute-start.3 = (f32[15,16,128]{2,1,0:T(8,128)S(1)}, f32[15,16,128]{2,1,0:T(8,128)S(1)}, u32[]{:S(2)}, u32[]{:S(2)}) collective-permute-start(f32[15,16,128]{2,1,0:T(8,128)S(1)} %get-tuple-element.21), channel_id=1, source_target_pairs={{0,0},{1,2},{2,1},{3,3},{4,4},{5,6},{6,5},{7,7},{8,8},{9,10},{10,9... | collective-permute-start | bytes 368648 | tf_op jit(solution)/shard_map/ppermute | solution.py:510
  15.9 1.7 %collective-permute-start.6 = (f32[15,16,128]{2,1,0:T(8,128)S(1)}, f32[15,16,128]{2,1,0:T(8,128)S(1)}, u32[]{:S(2)}, u32[]{:S(2)}) collective-permute-start(f32[15,16,128]{2,1,0:T(8,128)S(1)} %collective-permute-done.2.refs_2_), channel_id=1, source_target_pairs={{0,4},{4,0},{1,5},{5,1},{2,6},{6,2},{3,7},{7,3},{8,12},{12,8},{9,1... | collective-permute-start | bytes 368648 | tf_op jit(solution)/shard_map/ppermute | solution.py:510
  15.9 1.7 %collective-permute-start.7 = (f32[15,16,128]{2,1,0:T(8,128)S(1)}, f32[15,16,128]{2,1,0:T(8,128)S(1)}, u32[]{:S(2)}, u32[]{:S(2)}) collective-permute-start(f32[15,16,128]{2,1,0:T(8,128)S(1)} %collective-permute-done.3.refs_3_), channel_id=1, source_target_pairs={{0,4},{4,0},{1,5},{5,1},{2,6},{6,2},{3,7},{7,3},{8,12},{12,8},{9,1... | collective-permute-start | bytes 368648 | tf_op jit(solution)/shard_map/ppermute | solution.py:510
  16.4 25.3 %copy-start = (bf16[4,256,256]{2,1,0:T(8,128)(2,1)S(1)}, bf16[4,256,256]{2,1,0:T(8,128)(2,1)}, u32[]{:S(2)}) copy-start(bf16[4,256,256]{2,1,0:T(8,128)(2,1)} %constant.22.clone.refs_16_) | copy-start | bytes 1572868
  16.4 1.2 %collective-permute-start.5 = (f32[2,2,16,128]{3,2,1,0:T(8,128)S(1)}, f32[2,2,16,128]{3,2,1,0:T(8,128)S(1)}, u32[]{:S(2)}, u32[]{:S(2)}) collective-permute-start(f32[2,2,16,128]{3,2,1,0:T(8,128)S(1)} %get-tuple-element.19.refs_1_), channel_id=1, source_target_pairs={{0,4},{4,0},{1,5},{5,1},{2,6},{6,2},{3,7},{7,3},{8,12},{12,8},{9,1... | collective-permute-start | bytes 98312 | tf_op jit(solution)/shard_map/ppermute | solution.py:510
  17.7 24.0 %copy-start.1 = (bf16[2,336,224]{2,1,0:T(8,128)(2,1)S(1)}, bf16[2,336,224]{2,1,0:T(8,128)(2,1)}, u32[]{:S(2)}) copy-start(bf16[2,336,224]{2,1,0:T(8,128)(2,1)} %constant.21.clone.refs_15_) | copy-start | bytes 903172
  22.0 6.3 %collective-permute-start.10 = (f32[64,128]{1,0:T(8,128)S(1)}, f32[64,128]{1,0:T(8,128)S(1)}, u32[]{:S(2)}, u32[]{:S(2)}) collective-permute-start(f32[64,128]{1,0:T(8,128)S(1)} %get-tuple-element.22), channel_id=1, source_target_pairs={{0,3},{1,2},{2,1},{3,0},{4,7},{5,6},{6,5},{7,4},{8,11},{9,10},{10,... | collective-permute-start | bytes 98312 | tf_op jit(solution)/shard_map/ppermute | solution.py:510
  25.7 4.8 %collective-permute-start.9 = (f32[64,128]{1,0:T(8,128)S(1)}, f32[64,128]{1,0:T(8,128)S(1)}, u32[]{:S(2)}, u32[]{:S(2)}) collective-permute-start(f32[64,128]{1,0:T(8,128)S(1)} %get-tuple-element.22), channel_id=1, source_target_pairs={{0,2},{1,3},{2,0},{3,1},{4,6},{5,7},{6,4},{7,5},{8,10},{9,11},{10,... | collective-permute-start | bytes 98312 | tf_op jit(solution)/shard_map/ppermute | solution.py:510
  27.8 3.9 %collective-permute-start.8 = (f32[64,128]{1,0:T(8,128)S(1)}, f32[64,128]{1,0:T(8,128)S(1)}, u32[]{:S(2)}, u32[]{:S(2)}) collective-permute-start(f32[64,128]{1,0:T(8,128)S(1)} %get-tuple-element.22), channel_id=1, source_target_pairs={{0,1},{1,0},{2,3},{3,2},{4,5},{5,4},{6,7},{7,6},{8,9},{9,8},{10,11... | collective-permute-start | bytes 98312 | tf_op jit(solution)/shard_map/ppermute | solution.py:510
  31.7 10.0 %copy-start.2 = (bf16[128,256]{1,0:T(8,128)(2,1)S(1)}, bf16[128,256]{1,0:T(8,128)(2,1)}, u32[]{:S(2)}) copy-start(bf16[128,256]{1,0:T(8,128)(2,1)} %constant.26.clone.refs_20_) | copy-start | bytes 196612
  31.7 10.0 %copy-start.3 = (bf16[256,128]{1,0:T(8,128)(2,1)S(1)}, bf16[256,128]{1,0:T(8,128)(2,1)}, u32[]{:S(2)}) copy-start(bf16[256,128]{1,0:T(8,128)(2,1)} %constant.25.clone.refs_19_) | copy-start | bytes 196612
  31.7 10.0 %copy-start.4 = (bf16[256,128]{1,0:T(8,128)(2,1)S(1)}, bf16[256,128]{1,0:T(8,128)(2,1)}, u32[]{:S(2)}) copy-start(bf16[256,128]{1,0:T(8,128)(2,1)} %constant.24.clone.refs_18_) | copy-start | bytes 196612
  31.7 10.0 %copy-start.5 = (bf16[128,256]{1,0:T(8,128)(2,1)S(1)}, bf16[128,256]{1,0:T(8,128)(2,1)}, u32[]{:S(2)}) copy-start(bf16[128,256]{1,0:T(8,128)(2,1)} %constant.23.clone.refs_17_) | copy-start | bytes 196612
  31.8 7.0 %collective-permute-start.13 = (f32[4,64,128]{2,1,0:T(8,128)S(1)}, f32[4,64,128]{2,1,0:T(8,128)S(1)}, u32[]{:S(2)}, u32[]{:S(2)}) collective-permute-start(f32[4,64,128]{2,1,0:T(8,128)S(1)} %pad_maximum_fusion.1.refs_0_), channel_id=1, source_target_pairs={{0,24},{8,16},{16,8},{24,0},{1,25},{9,17},{17,9},{25,1},{2,26},{10... | collective-permute-start | bytes 393224 | tf_op jit(solution)/shard_map/ppermute | solution.py:510
  33.3 6.6 %collective-permute-start.12 = (f32[4,64,128]{2,1,0:T(8,128)S(1)}, f32[4,64,128]{2,1,0:T(8,128)S(1)}, u32[]{:S(2)}, u32[]{:S(2)}) collective-permute-start(f32[4,64,128]{2,1,0:T(8,128)S(1)} %pad_maximum_fusion.1.refs_0_), channel_id=1, source_target_pairs={{0,16},{8,24},{16,0},{24,8},{1,17},{9,25},{17,1},{25,9},{2,18},{10... | collective-permute-start | bytes 393224 | tf_op jit(solution)/shard_map/ppermute | solution.py:510
  35.2 5.2 %collective-permute-start.11 = (f32[4,64,128]{2,1,0:T(8,128)S(1)}, f32[4,64,128]{2,1,0:T(8,128)S(1)}, u32[]{:S(2)}, u32[]{:S(2)}) collective-permute-start(f32[4,64,128]{2,1,0:T(8,128)S(1)} %pad_maximum_fusion.1.refs_0_), channel_id=1, source_target_pairs={{0,8},{8,0},{16,24},{24,16},{1,9},{9,1},{17,25},{25,17},{2,10},{10... | collective-permute-start | bytes 393224 | tf_op jit(solution)/shard_map/ppermute | solution.py:510
  35.3 5.1 %collective-permute-start.14 = (f32[4,64,128]{2,1,0:T(8,128)S(1)}, f32[4,64,128]{2,1,0:T(8,128)S(1)}, u32[]{:S(2)}, u32[]{:S(2)}) collective-permute-start(f32[4,64,128]{2,1,0:T(8,128)S(1)} %pad_maximum_fusion.1.refs_0_), channel_id=1, source_target_pairs={{0,4},{4,0},{1,5},{5,1},{2,6},{6,2},{3,7},{7,3},{8,12},{12,8},{9,1... | collective-permute-start | bytes 393224 | tf_op jit(solution)/shard_map/ppermute | solution.py:510
  38.7 1.7 %collective-permute-start.17 = (f32[4,64,128]{2,1,0:T(8,128)S(1)}, f32[4,64,128]{2,1,0:T(8,128)S(1)}, u32[]{:S(2)}, u32[]{:S(2)}) collective-permute-start(f32[4,64,128]{2,1,0:T(8,128)S(1)} %collective-permute-done.13.refs_3_), channel_id=1, source_target_pairs={{0,4},{4,0},{1,5},{5,1},{2,6},{6,2},{3,7},{7,3},{8,12},{12,8},{9,1... | collective-permute-start | bytes 393224 | tf_op jit(solution)/shard_map/ppermute | solution.py:510
  39.9 1.3 %collective-permute-start.16 = (f32[4,64,128]{2,1,0:T(8,128)S(1)}, f32[4,64,128]{2,1,0:T(8,128)S(1)}, u32[]{:S(2)}, u32[]{:S(2)}) collective-permute-start(f32[4,64,128]{2,1,0:T(8,128)S(1)} %collective-permute-done.12.refs_2_), channel_id=1, source_target_pairs={{0,4},{4,0},{1,5},{5,1},{2,6},{6,2},{3,7},{7,3},{8,12},{12,8},{9,1... | collective-permute-start | bytes 393224 | tf_op jit(solution)/shard_map/ppermute | solution.py:510
  40.4 1.3 %collective-permute-start.15 = (f32[4,64,128]{2,1,0:T(8,128)S(1)}, f32[4,64,128]{2,1,0:T(8,128)S(1)}, u32[]{:S(2)}, u32[]{:S(2)}) collective-permute-start(f32[4,64,128]{2,1,0:T(8,128)S(1)} %collective-permute-done.11.refs_1_), channel_id=1, source_target_pairs={{0,4},{4,0},{1,5},{5,1},{2,6},{6,2},{3,7},{7,3},{8,12},{12,8},{9,1... | collective-permute-start | bytes 393224 | tf_op jit(solution)/shard_map/ppermute | solution.py:510
  (5 other events, 40.8 us)

commit v12 on v11

--- a/solution.py
+++ b/solution.py
@@ -312,9 +312,9 @@
     in_blocks(start, stop, block, body, face_z[before] * field[before])
 
 
-def plane_steps(faces, ranges, source, residual, update, estimate, from_zero, block=4):
+def plane_steps(faces, ranges, source, residual, update, estimate, from_zero, blocks):
     inverse = faces[4]
-    for step, ((keep, push), (start, stop)) in enumerate(zip(cheb_terms(), ranges)):
+    for step, ((keep, push), (start, stop), block) in enumerate(zip(cheb_terms(), ranges, blocks)):
         fresh = from_zero and step == 0
 
         def finish(here, own, keep=keep, push=push, fresh=fresh):
@@ -334,7 +334,7 @@
         plane_sweep(faces, start, stop, update, finish, block)
 
 
-def plane_restart(faces, start, stop, source, residual, update, estimate):
+def plane_restart(faces, start, stop, source, residual, update, estimate, block=8):
     inverse = faces[4]
 
     def finish(here, own):
@@ -350,7 +350,7 @@
 
         return store
 
-    plane_sweep(faces, start, stop, estimate, finish)
+    plane_sweep(faces, start, stop, estimate, finish, block)
 
 
 def plane_residual(faces, start, stop, residual, update, block=4):
@@ -636,8 +636,8 @@
     own_y = rows - HALO_Y
     plane_faces(coef, faces, 0, planes, link_mask(rows, lanes), None, source, update)
     ranges = [(2, planes - 2), (4, planes - 4)]
-    plane_steps(faces, ranges, source, residual, update, estimate, True)
-    plane_residual(faces, HALO_Z, planes - HALO_Z, residual, update)
+    plane_steps(faces, ranges, source, residual, update, estimate, True, (7, 8))
+    plane_residual(faces, HALO_Z, planes - HALO_Z, residual, update, 8)
     for pair in range((planes - 2 * HALO_Z) // 2):
         low = HALO_Z + 2 * pair
         target = pl.ds(pair * own_y, own_y)
@@ -698,9 +698,9 @@
     link_y = jnp.where(row == mid_y - 1, 0.0, 1.0)
     link_x = jnp.where(lane == mid_x - 1, 0.0, 1.0)
     start, stop = PAD, PAD + mid_z
-    plane_faces(mid_coef, mid_faces, start, stop, link_y, link_x, mid_source, mid_update)
+    plane_faces(mid_coef, mid_faces, start, stop, link_y, link_x, mid_source, mid_update, 8)
     ranges = [(start, stop)] * (DEGREE - 1)
-    plane_steps(mid_faces, ranges, mid_source, mid_residual, mid_update, mid_estimate, True, 8)
+    plane_steps(mid_faces, ranges, mid_source, mid_residual, mid_update, mid_estimate, True, (8, 8))
 
     def finish_pairs(here, own):
         before = mid_residual[here]
@@ -749,7 +749,7 @@
     lax.fori_loop(0, (high - low) // 8, add_mid, (low - PAD) // 2)
     plane_restart(mid_faces, *clipped(8), mid_source, mid_residual, mid_update, mid_estimate)
     plane_steps(
-        mid_faces, [clipped(4), clipped(4)], mid_source, mid_residual, mid_update, mid_estimate, False
+        mid_faces, [clipped(4), clipped(4)], mid_source, mid_residual, mid_update, mid_estimate, False, (4, 4)
     )
 
     coarse_planes = up_left.shape[1] // mid_y
@@ -766,8 +766,8 @@
         current[plane] = estimate[plane]
     plane_restart(faces, HALO_Z - 4, planes - HALO_Z + 4, source, residual, update, current)
     ranges = [(HALO_Z - 2, planes - HALO_Z + 2)] * 2
-    plane_steps(faces, ranges, source, residual, update, current, False)
-    plane_residual(faces, HALO_Z, planes - HALO_Z, residual, update)
+    plane_steps(faces, ranges, source, residual, update, current, False, (5, 5))
+    plane_residual(faces, HALO_Z, planes - HALO_Z, residual, update, 8)
     own_planes = pl.ds(HALO_Z, planes - 2 * HALO_Z)
     residual_out[...] = residual[own_planes, :own_y, :128]
     solution[...] = current[own_planes, :own_y, :128]

time: 54.3 us -> 53.3 us (0.982)
  Pallas kernels: 18.5 us -> 17.5 us
    pallas_call x4, Pallas kernels: 18.5 us -> 17.5 us  [call(): pl.pallas_call(kernel, out_shape=tuple((jax.ShapeDtypeStruct(shape, F32)...]
where the time goes in v12:
time: 53.3 us; the launch traced here: 53 us
  starting transfers between devices  19.2 us (36%)
  Pallas kernels  17.5 us (33%)
  waiting for transfers between devices  15.5 us (29%)
  between operations  0.8 us (2%)
    ppermute x18, starting transfers between devices, swapped(): lax.ppermute(value, axes, [(int(source), int(target)) for source, target...  19.2 us
    pallas_call x4, Pallas kernels, call(): pl.pallas_call(kernel, out_shape=tuple((jax.ShapeDtypeStruct(shape, F32)...  17.5 us
    ppermute x18, waiting for transfers between devices, swapped(): lax.ppermute(value, axes, [(int(source), int(target)) for source, target...  15.5 us
  transfers between devices with their start and end apart: 18, of which 10 were waited for; matrix products, arithmetic and copies ran while one was open for 0% of the time, Pallas kernels for 0%

profile of v12, /device:TPU:0, one launch (start us, length us, event | category | flops | bytes accessed | tf_op | source)
XLA Modules:
  0.0 53.0 jit_solution(1708815302271473483)
XLA Ops:
  0.6 1.9 %start.1 = (f32[2,16,128]{2,1,0:T(8,128)}, f32[2,16,128]{2,1,0:T(8,128)}) custom-call(f32[16,16,128]{2,1,0:T(8,128)} %bitcast.10, f32[16,16,128]{2,1,0:T(8,128)} %coef.1), custom_call_target="tpu_custom_call" | custom-call | tf_op jit(solution)/shard_map/start/pallas_call | solution.py:786
  2.5 1.4 %collective-permute-start = (f32[2,16,128]{2,1,0:T(8,128)}, f32[2,16,128]{2,1,0:T(8,128)S(1)}, u32[]{:S(2)}, u32[]{:S(2)}) collective-permute-start(f32[2,16,128]{2,1,0:T(8,128)} %get-tuple-element.17), channel_id=1, source_target_pairs={{0,0},{8,16},{16,8},{24,24},{1,1},{9,17},{17,9},{25,25},{2,2},{10,... | collective-permute-start | bytes 49160 | tf_op jit(solution)/shard_map/ppermute | solution.py:510
  3.9 5.0 %collective-permute-start.1 = (f32[2,16,128]{2,1,0:T(8,128)}, f32[2,16,128]{2,1,0:T(8,128)S(1)}, u32[]{:S(2)}, u32[]{:S(2)}) collective-permute-start(f32[2,16,128]{2,1,0:T(8,128)} %get-tuple-element.18), channel_id=1, source_target_pairs={{0,8},{8,0},{16,24},{24,16},{1,9},{9,1},{17,25},{25,17},{2,10},{10... | collective-permute-start | bytes 49160 | tf_op jit(solution)/shard_map/ppermute | solution.py:510
  9.1 1.9 %collective-permute-done.1.x_a = f32[2,16,128]{2,1,0:T(8,128)S(1)} collective-permute-done((f32[2,16,128]{2,1,0:T(8,128)}, f32[2,16,128]{2,1,0:T(8,128)S(1)}, u32[]{:S(2)}, u32[]{:S(2)}) %collective-permute-start.1) | collective-permute-done | bytes 16416 | tf_op jit(solution)/shard_map/ppermute | solution.py:510
  11.0 1.6 %collective-permute-start.2 = (f32[15,16,128]{2,1,0:T(8,128)S(1)}, f32[15,16,128]{2,1,0:T(8,128)S(1)}, u32[]{:S(2)}, u32[]{:S(2)}) collective-permute-start(f32[15,16,128]{2,1,0:T(8,128)S(1)} %get-tuple-element.20), channel_id=1, source_target_pairs={{0,1},{1,0},{2,3},{3,2},{4,5},{5,4},{6,7},{7,6},{8,9},{9,8},{10,11... | collective-permute-start | bytes 368648 | tf_op jit(solution)/shard_map/ppermute | solution.py:510
  12.6 0.7 %collective-permute-start.3 = (f32[15,16,128]{2,1,0:T(8,128)S(1)}, f32[15,16,128]{2,1,0:T(8,128)S(1)}, u32[]{:S(2)}, u32[]{:S(2)}) collective-permute-start(f32[15,16,128]{2,1,0:T(8,128)S(1)} %get-tuple-element.21), channel_id=1, source_target_pairs={{0,0},{1,2},{2,1},{3,3},{4,4},{5,6},{6,5},{7,7},{8,8},{9,10},{10,9... | collective-permute-start | bytes 368648 | tf_op jit(solution)/shard_map/ppermute | solution.py:510
  13.3 2.6 %collective-permute-done.2.refs_2_ = f32[15,16,128]{2,1,0:T(8,128)S(1)} collective-permute-done((f32[15,16,128]{2,1,0:T(8,128)S(1)}, f32[15,16,128]{2,1,0:T(8,128)S(1)}, u32[]{:S(2)}, u32[]{:S(2)}) %collective-permute-start.2) | collective-permute-done | bytes 122912 | tf_op jit(solution)/shard_map/ppermute | solution.py:510
  15.9 0.5 collective-permute-start.7
  16.5 1.1 %collective-permute-done.5.refs_5_ = f32[2,2,16,128]{3,2,1,0:T(8,128)S(1)} collective-permute-done((f32[2,2,16,128]{3,2,1,0:T(8,128)S(1)}, f32[2,2,16,128]{3,2,1,0:T(8,128)S(1)}, u32[]{:S(2)}, u32[]{:S(2)}) %collective-permute-start.5) | collective-permute-done | bytes 32800 | tf_op jit(solution)/shard_map/ppermute | solution.py:510
  17.7 4.1 %first.1 = (f32[64,128]{1,0:T(8,128)S(1)}, f32[32,24,256]{2,1,0:T(8,128)S(1)}, f32[32,24,256]{2,1,0:T(8,128)S(1)}, f32[32,24,256]{2,1,0:T(8,128)S(1)}, f32[32,24...) custom-call(f32[2,16,16,128]{3,2,1,0:T(8,128)S(1)} %pad_maximum_fusion., ...), custom_call_target="tpu_custom_call" | custom-call | tf_op jit(solution)/shard_map/first/pallas_call | solution.py:786
  21.8 3.6 %collective-permute-start.10 = (f32[64,128]{1,0:T(8,128)S(1)}, f32[64,128]{1,0:T(8,128)S(1)}, u32[]{:S(2)}, u32[]{:S(2)}) collective-permute-start(f32[64,128]{1,0:T(8,128)S(1)} %get-tuple-element.22), channel_id=1, source_target_pairs={{0,3},{1,2},{2,1},{3,0},{4,7},{5,6},{6,5},{7,4},{8,11},{9,10},{10,... | collective-permute-start | bytes 98312 | tf_op jit(solution)/shard_map/ppermute | solution.py:510
  25.4 2.1 %collective-permute-start.9 = (f32[64,128]{1,0:T(8,128)S(1)}, f32[64,128]{1,0:T(8,128)S(1)}, u32[]{:S(2)}, u32[]{:S(2)}) collective-permute-start(f32[64,128]{1,0:T(8,128)S(1)} %get-tuple-element.22), channel_id=1, source_target_pairs={{0,2},{1,3},{2,0},{3,1},{4,6},{5,7},{6,4},{7,5},{8,10},{9,11},{10,... | collective-permute-start | bytes 98312 | tf_op jit(solution)/shard_map/ppermute | solution.py:510
  27.6 0.5 collective-permute-start.8
  28.1 2.1 %collective-permute-done.9 = f32[64,128]{1,0:T(8,128)S(1)} collective-permute-done((f32[64,128]{1,0:T(8,128)S(1)}, f32[64,128]{1,0:T(8,128)S(1)}, u32[]{:S(2)}, u32[]{:S(2)}) %collective-permute-start.9) | collective-permute-done | bytes 32800 | tf_op jit(solution)/shard_map/ppermute | solution.py:510
  30.2 1.2 %collective-permute-done.8 = f32[64,128]{1,0:T(8,128)S(1)} collective-permute-done((f32[64,128]{1,0:T(8,128)S(1)}, f32[64,128]{1,0:T(8,128)S(1)}, u32[]{:S(2)}, u32[]{:S(2)}) %collective-permute-start.8) | collective-permute-done | bytes 32800 | tf_op jit(solution)/shard_map/ppermute | solution.py:510
  31.5 1.5 %collective-permute-start.13 = (f32[4,64,128]{2,1,0:T(8,128)S(1)}, f32[4,64,128]{2,1,0:T(8,128)S(1)}, u32[]{:S(2)}, u32[]{:S(2)}) collective-permute-start(f32[4,64,128]{2,1,0:T(8,128)S(1)} %pad_maximum_fusion.1.refs_0_), channel_id=1, source_target_pairs={{0,24},{8,16},{16,8},{24,0},{1,25},{9,17},{17,9},{25,1},{2,26},{10... | collective-permute-start | bytes 393224 | tf_op jit(solution)/shard_map/ppermute | solution.py:510
  33.0 2.0 %collective-permute-start.12 = (f32[4,64,128]{2,1,0:T(8,128)S(1)}, f32[4,64,128]{2,1,0:T(8,128)S(1)}, u32[]{:S(2)}, u32[]{:S(2)}) collective-permute-start(f32[4,64,128]{2,1,0:T(8,128)S(1)} %pad_maximum_fusion.1.refs_0_), channel_id=1, source_target_pairs={{0,16},{8,24},{16,0},{24,8},{1,17},{9,25},{17,1},{25,9},{2,18},{10... | collective-permute-start | bytes 393224 | tf_op jit(solution)/shard_map/ppermute | solution.py:510
  35.0 0.1 collective-permute-start.11
  35.1 3.4 %collective-permute-done.13.refs_3_ = f32[4,64,128]{2,1,0:T(8,128)S(1)} collective-permute-done((f32[4,64,128]{2,1,0:T(8,128)S(1)}, f32[4,64,128]{2,1,0:T(8,128)S(1)}, u32[]{:S(2)}, u32[]{:S(2)}) %collective-permute-start.13) | collective-permute-done | bytes 131104 | tf_op jit(solution)/shard_map/ppermute | solution.py:510
  38.5 1.1 %collective-permute-done.12.refs_2_ = f32[4,64,128]{2,1,0:T(8,128)S(1)} collective-permute-done((f32[4,64,128]{2,1,0:T(8,128)S(1)}, f32[4,64,128]{2,1,0:T(8,128)S(1)}, u32[]{:S(2)}, u32[]{:S(2)}) %collective-permute-start.12) | collective-permute-done | bytes 131104 | tf_op jit(solution)/shard_map/ppermute | solution.py:510
  39.6 0.5 %collective-permute-done.11.refs_1_ = f32[4,64,128]{2,1,0:T(8,128)S(1)} collective-permute-done((f32[4,64,128]{2,1,0:T(8,128)S(1)}, f32[4,64,128]{2,1,0:T(8,128)S(1)}, u32[]{:S(2)}, u32[]{:S(2)}) %collective-permute-start.11) | collective-permute-done | bytes 131104 | tf_op jit(solution)/shard_map/ppermute | solution.py:510
  40.1 0.8 %collective-permute-done.16.refs_6_ = f32[4,64,128]{2,1,0:T(8,128)S(1)} collective-permute-done((f32[4,64,128]{2,1,0:T(8,128)S(1)}, f32[4,64,128]{2,1,0:T(8,128)S(1)}, u32[]{:S(2)}, u32[]{:S(2)}) %collective-permute-start.16) | collective-permute-done | bytes 131104 | tf_op jit(solution)/shard_map/ppermute | solution.py:510
  40.9 0.5 %collective-permute-done.15.refs_5_ = f32[4,64,128]{2,1,0:T(8,128)S(1)} collective-permute-done((f32[4,64,128]{2,1,0:T(8,128)S(1)}, f32[4,64,128]{2,1,0:T(8,128)S(1)}, u32[]{:S(2)}, u32[]{:S(2)}) %collective-permute-start.15) | collective-permute-done | bytes 131104 | tf_op jit(solution)/shard_map/ppermute | solution.py:510
  41.5 11.5 %second.1 = (f32[16,16,128]{2,1,0:T(8,128)}, f32[16,16,128]{2,1,0:T(8,128)}) custom-call(f32[4,64,128]{2,1,0:T(8,128)S(1)} %pad_maximum_fusion.1.refs_0_, f32[4,64,128]{2,1,0:T(8,128)S(1)} %collective-permute-done.11.refs_1_, f32[4,64,128]{2,1,0:T(8,128)S(1)} %collective-permute-done.12.refs_2_, f32[4,64,128]{2,1,0:T(8,128)S(1)} %collective-permute-done.13.refs_3_, ...), custom_call_target="tpu_custom_call" | custom-call | tf_op jit(solution)/shard_map/second/pallas_call | solution.py:786
  (40 shorter events, 0.3 us)
Async XLA Ops:
  2.5 6.5 %collective-permute-start = (f32[2,16,128]{2,1,0:T(8,128)}, f32[2,16,128]{2,1,0:T(8,128)S(1)}, u32[]{:S(2)}, u32[]{:S(2)}) collective-permute-start(f32[2,16,128]{2,1,0:T(8,128)} %get-tuple-element.17), channel_id=1, source_target_pairs={{0,0},{8,16},{16,8},{24,24},{1,1},{9,17},{17,9},{25,25},{2,2},{10,... | collective-permute-start | bytes 49160 | tf_op jit(solution)/shard_map/ppermute | solution.py:510
  3.9 7.0 %collective-permute-start.1 = (f32[2,16,128]{2,1,0:T(8,128)}, f32[2,16,128]{2,1,0:T(8,128)S(1)}, u32[]{:S(2)}, u32[]{:S(2)}) collective-permute-start(f32[2,16,128]{2,1,0:T(8,128)} %get-tuple-element.18), channel_id=1, source_target_pairs={{0,8},{8,0},{16,24},{24,16},{1,9},{9,1},{17,25},{25,17},{2,10},{10... | collective-permute-start | bytes 49160 | tf_op jit(solution)/shard_map/ppermute | solution.py:510
  9.0 8.7 %collective-permute-start.4 = (f32[2,16,16,128]{3,2,1,0:T(8,128)S(1)}, f32[2,16,16,128]{3,2,1,0:T(8,128)S(1)}, u32[]{:S(2)}, u32[]{:S(2)}) collective-permute-start(f32[2,16,16,128]{3,2,1,0:T(8,128)S(1)} %pad_maximum_fusion.own.refs_0_), channel_id=1, source_target_pairs={{0,4},{4,0},{1,5},{5,1},{2,6},{6,2},{3,7},{7,3},{8,12},{12,8},{9,1... | collective-permute-start | bytes 786440 | tf_op jit(solution)/shard_map/ppermute | solution.py:510
  11.0 4.9 %collective-permute-start.2 = (f32[15,16,128]{2,1,0:T(8,128)S(1)}, f32[15,16,128]{2,1,0:T(8,128)S(1)}, u32[]{:S(2)}, u32[]{:S(2)}) collective-permute-start(f32[15,16,128]{2,1,0:T(8,128)S(1)} %get-tuple-element.20), channel_id=1, source_target_pairs={{0,1},{1,0},{2,3},{3,2},{4,5},{5,4},{6,7},{7,6},{8,9},{9,8},{10,11... | collective-permute-start | bytes 368648 | tf_op jit(solution)/shard_map/ppermute | solution.py:510
  12.6 3.3 %collective-permute-start.3 = (f32[15,16,128]{2,1,0:T(8,128)S(1)}, f32[15,16,128]{2,1,0:T(8,128)S(1)}, u32[]{:S(2)}, u32[]{:S(2)}) collective-permute-start(f32[15,16,128]{2,1,0:T(8,128)S(1)} %get-tuple-element.21), channel_id=1, source_target_pairs={{0,0},{1,2},{2,1},{3,3},{4,4},{5,6},{6,5},{7,7},{8,8},{9,10},{10,9... | collective-permute-start | bytes 368648 | tf_op jit(solution)/shard_map/ppermute | solution.py:510
  15.9 1.7 %collective-permute-start.6 = (f32[15,16,128]{2,1,0:T(8,128)S(1)}, f32[15,16,128]{2,1,0:T(8,128)S(1)}, u32[]{:S(2)}, u32[]{:S(2)}) collective-permute-start(f32[15,16,128]{2,1,0:T(8,128)S(1)} %collective-permute-done.2.refs_2_), channel_id=1, source_target_pairs={{0,4},{4,0},{1,5},{5,1},{2,6},{6,2},{3,7},{7,3},{8,12},{12,8},{9,1... | collective-permute-start | bytes 368648 | tf_op jit(solution)/shard_map/ppermute | solution.py:510
  15.9 1.7 %collective-permute-start.7 = (f32[15,16,128]{2,1,0:T(8,128)S(1)}, f32[15,16,128]{2,1,0:T(8,128)S(1)}, u32[]{:S(2)}, u32[]{:S(2)}) collective-permute-start(f32[15,16,128]{2,1,0:T(8,128)S(1)} %collective-permute-done.3.refs_3_), channel_id=1, source_target_pairs={{0,4},{4,0},{1,5},{5,1},{2,6},{6,2},{3,7},{7,3},{8,12},{12,8},{9,1... | collective-permute-start | bytes 368648 | tf_op jit(solution)/shard_map/ppermute | solution.py:510
  16.4 25.0 %copy-start = (bf16[4,256,256]{2,1,0:T(8,128)(2,1)S(1)}, bf16[4,256,256]{2,1,0:T(8,128)(2,1)}, u32[]{:S(2)}) copy-start(bf16[4,256,256]{2,1,0:T(8,128)(2,1)} %constant.22.clone.refs_16_) | copy-start | bytes 1572868
  16.4 1.2 %collective-permute-start.5 = (f32[2,2,16,128]{3,2,1,0:T(8,128)S(1)}, f32[2,2,16,128]{3,2,1,0:T(8,128)S(1)}, u32[]{:S(2)}, u32[]{:S(2)}) collective-permute-start(f32[2,2,16,128]{3,2,1,0:T(8,128)S(1)} %get-tuple-element.19.refs_1_), channel_id=1, source_target_pairs={{0,4},{4,0},{1,5},{5,1},{2,6},{6,2},{3,7},{7,3},{8,12},{12,8},{9,1... | collective-permute-start | bytes 98312 | tf_op jit(solution)/shard_map/ppermute | solution.py:510
  17.7 23.8 %copy-start.1 = (bf16[2,336,224]{2,1,0:T(8,128)(2,1)S(1)}, bf16[2,336,224]{2,1,0:T(8,128)(2,1)}, u32[]{:S(2)}) copy-start(bf16[2,336,224]{2,1,0:T(8,128)(2,1)} %constant.21.clone.refs_15_) | copy-start | bytes 903172
  21.8 6.3 %collective-permute-start.10 = (f32[64,128]{1,0:T(8,128)S(1)}, f32[64,128]{1,0:T(8,128)S(1)}, u32[]{:S(2)}, u32[]{:S(2)}) collective-permute-start(f32[64,128]{1,0:T(8,128)S(1)} %get-tuple-element.22), channel_id=1, source_target_pairs={{0,3},{1,2},{2,1},{3,0},{4,7},{5,6},{6,5},{7,4},{8,11},{9,10},{10,... | collective-permute-start | bytes 98312 | tf_op jit(solution)/shard_map/ppermute | solution.py:510
  25.4 4.8 %collective-permute-start.9 = (f32[64,128]{1,0:T(8,128)S(1)}, f32[64,128]{1,0:T(8,128)S(1)}, u32[]{:S(2)}, u32[]{:S(2)}) collective-permute-start(f32[64,128]{1,0:T(8,128)S(1)} %get-tuple-element.22), channel_id=1, source_target_pairs={{0,2},{1,3},{2,0},{3,1},{4,6},{5,7},{6,4},{7,5},{8,10},{9,11},{10,... | collective-permute-start | bytes 98312 | tf_op jit(solution)/shard_map/ppermute | solution.py:510
  27.6 3.9 %collective-permute-start.8 = (f32[64,128]{1,0:T(8,128)S(1)}, f32[64,128]{1,0:T(8,128)S(1)}, u32[]{:S(2)}, u32[]{:S(2)}) collective-permute-start(f32[64,128]{1,0:T(8,128)S(1)} %get-tuple-element.22), channel_id=1, source_target_pairs={{0,1},{1,0},{2,3},{3,2},{4,5},{5,4},{6,7},{7,6},{8,9},{9,8},{10,11... | collective-permute-start | bytes 98312 | tf_op jit(solution)/shard_map/ppermute | solution.py:510
  31.5 10.0 %copy-start.2 = (bf16[128,256]{1,0:T(8,128)(2,1)S(1)}, bf16[128,256]{1,0:T(8,128)(2,1)}, u32[]{:S(2)}) copy-start(bf16[128,256]{1,0:T(8,128)(2,1)} %constant.26.clone.refs_20_) | copy-start | bytes 196612
  31.5 10.0 %copy-start.3 = (bf16[256,128]{1,0:T(8,128)(2,1)S(1)}, bf16[256,128]{1,0:T(8,128)(2,1)}, u32[]{:S(2)}) copy-start(bf16[256,128]{1,0:T(8,128)(2,1)} %constant.25.clone.refs_19_) | copy-start | bytes 196612
  31.5 10.0 %copy-start.4 = (bf16[256,128]{1,0:T(8,128)(2,1)S(1)}, bf16[256,128]{1,0:T(8,128)(2,1)}, u32[]{:S(2)}) copy-start(bf16[256,128]{1,0:T(8,128)(2,1)} %constant.24.clone.refs_18_) | copy-start | bytes 196612
  31.5 10.0 %copy-start.5 = (bf16[128,256]{1,0:T(8,128)(2,1)S(1)}, bf16[128,256]{1,0:T(8,128)(2,1)}, u32[]{:S(2)}) copy-start(bf16[128,256]{1,0:T(8,128)(2,1)} %constant.23.clone.refs_17_) | copy-start | bytes 196612
  31.5 7.0 %collective-permute-start.13 = (f32[4,64,128]{2,1,0:T(8,128)S(1)}, f32[4,64,128]{2,1,0:T(8,128)S(1)}, u32[]{:S(2)}, u32[]{:S(2)}) collective-permute-start(f32[4,64,128]{2,1,0:T(8,128)S(1)} %pad_maximum_fusion.1.refs_0_), channel_id=1, source_target_pairs={{0,24},{8,16},{16,8},{24,0},{1,25},{9,17},{17,9},{25,1},{2,26},{10... | collective-permute-start | bytes 393224 | tf_op jit(solution)/shard_map/ppermute | solution.py:510
  33.0 6.6 %collective-permute-start.12 = (f32[4,64,128]{2,1,0:T(8,128)S(1)}, f32[4,64,128]{2,1,0:T(8,128)S(1)}, u32[]{:S(2)}, u32[]{:S(2)}) collective-permute-start(f32[4,64,128]{2,1,0:T(8,128)S(1)} %pad_maximum_fusion.1.refs_0_), channel_id=1, source_target_pairs={{0,16},{8,24},{16,0},{24,8},{1,17},{9,25},{17,1},{25,9},{2,18},{10... | collective-permute-start | bytes 393224 | tf_op jit(solution)/shard_map/ppermute | solution.py:510
  35.0 5.2 %collective-permute-start.11 = (f32[4,64,128]{2,1,0:T(8,128)S(1)}, f32[4,64,128]{2,1,0:T(8,128)S(1)}, u32[]{:S(2)}, u32[]{:S(2)}) collective-permute-start(f32[4,64,128]{2,1,0:T(8,128)S(1)} %pad_maximum_fusion.1.refs_0_), channel_id=1, source_target_pairs={{0,8},{8,0},{16,24},{24,16},{1,9},{9,1},{17,25},{25,17},{2,10},{10... | collective-permute-start | bytes 393224 | tf_op jit(solution)/shard_map/ppermute | solution.py:510
  35.1 5.1 %collective-permute-start.14 = (f32[4,64,128]{2,1,0:T(8,128)S(1)}, f32[4,64,128]{2,1,0:T(8,128)S(1)}, u32[]{:S(2)}, u32[]{:S(2)}) collective-permute-start(f32[4,64,128]{2,1,0:T(8,128)S(1)} %pad_maximum_fusion.1.refs_0_), channel_id=1, source_target_pairs={{0,4},{4,0},{1,5},{5,1},{2,6},{6,2},{3,7},{7,3},{8,12},{12,8},{9,1... | collective-permute-start | bytes 393224 | tf_op jit(solution)/shard_map/ppermute | solution.py:510
  38.5 1.7 %collective-permute-start.17 = (f32[4,64,128]{2,1,0:T(8,128)S(1)}, f32[4,64,128]{2,1,0:T(8,128)S(1)}, u32[]{:S(2)}, u32[]{:S(2)}) collective-permute-start(f32[4,64,128]{2,1,0:T(8,128)S(1)} %collective-permute-done.13.refs_3_), channel_id=1, source_target_pairs={{0,4},{4,0},{1,5},{5,1},{2,6},{6,2},{3,7},{7,3},{8,12},{12,8},{9,1... | collective-permute-start | bytes 393224 | tf_op jit(solution)/shard_map/ppermute | solution.py:510
  39.6 1.3 %collective-permute-start.16 = (f32[4,64,128]{2,1,0:T(8,128)S(1)}, f32[4,64,128]{2,1,0:T(8,128)S(1)}, u32[]{:S(2)}, u32[]{:S(2)}) collective-permute-start(f32[4,64,128]{2,1,0:T(8,128)S(1)} %collective-permute-done.12.refs_2_), channel_id=1, source_target_pairs={{0,4},{4,0},{1,5},{5,1},{2,6},{6,2},{3,7},{7,3},{8,12},{12,8},{9,1... | collective-permute-start | bytes 393224 | tf_op jit(solution)/shard_map/ppermute | solution.py:510
  40.1 1.3 %collective-permute-start.15 = (f32[4,64,128]{2,1,0:T(8,128)S(1)}, f32[4,64,128]{2,1,0:T(8,128)S(1)}, u32[]{:S(2)}, u32[]{:S(2)}) collective-permute-start(f32[4,64,128]{2,1,0:T(8,128)S(1)} %collective-permute-done.11.refs_1_), channel_id=1, source_target_pairs={{0,4},{4,0},{1,5},{5,1},{2,6},{6,2},{3,7},{7,3},{8,12},{12,8},{9,1... | collective-permute-start | bytes 393224 | tf_op jit(solution)/shard_map/ppermute | solution.py:510
  (5 other events, 40.8 us)

commit v13 on v12

--- a/solution.py
+++ b/solution.py
@@ -562,7 +562,7 @@
     return right, left
 
 
-def pack_z_kernel(x_count, own, x_b, x_a, edges, z_a, z_b):
+def pack_z_kernel(x_count, own, x_b, x_a, edges, z_b, z_a):
     _, planes, own_y, _ = own.shape
     z_even = lax.axis_index("gz") % 2 == 0
     edges[0], edges[1] = x_a[...], x_b[...]
@@ -612,7 +612,7 @@
 
             def taken(place):
                 is_a = z_even if is_above else jnp.logical_not(z_even)
-                by_a, by_b = (joined(got[index], far[1 + index], (place,)) for index in (1, 2))
+                by_b, by_a = (joined(got[index], far[1 + index], (place,)) for index in (1, 2))
                 return kept(flag, jnp.where(is_a, by_a, by_b))
 
             packed = taken(sum(SENT_Z) + which)
@@ -634,10 +634,10 @@
     fill_window(own, got, far, source, coef, *counts)
     planes, rows, lanes = source.shape
     own_y = rows - HALO_Y
-    plane_faces(coef, faces, 0, planes, link_mask(rows, lanes), None, source, update)
+    plane_faces(coef, faces, 0, planes, link_mask(rows, lanes), None, source, update, 8)
     ranges = [(2, planes - 2), (4, planes - 4)]
-    plane_steps(faces, ranges, source, residual, update, estimate, True, (7, 8))
-    plane_residual(faces, HALO_Z, planes - HALO_Z, residual, update, 8)
+    plane_steps(faces, ranges, source, residual, update, estimate, True, (14, 12))
+    plane_residual(faces, HALO_Z, planes - HALO_Z, residual, update, 16)
     for pair in range((planes - 2 * HALO_Z) // 2):
         low = HALO_Z + 2 * pair
         target = pl.ds(pair * own_y, own_y)
@@ -700,7 +700,7 @@
     start, stop = PAD, PAD + mid_z
     plane_faces(mid_coef, mid_faces, start, stop, link_y, link_x, mid_source, mid_update, 8)
     ranges = [(start, stop)] * (DEGREE - 1)
-    plane_steps(mid_faces, ranges, mid_source, mid_residual, mid_update, mid_estimate, True, (8, 8))
+    plane_steps(mid_faces, ranges, mid_source, mid_residual, mid_update, mid_estimate, True, (16, 16))
 
     def finish_pairs(here, own):
         before = mid_residual[here]
@@ -764,10 +764,10 @@
         current[here] = estimate[here] + jnp.where(inverse[here] > 0.0, step, 0.0)
     for plane in (HALO_Z - 5, planes - HALO_Z + 4):
         current[plane] = estimate[plane]
-    plane_restart(faces, HALO_Z - 4, planes - HALO_Z + 4, source, residual, update, current)
+    plane_restart(faces, HALO_Z - 4, planes - HALO_Z + 4, source, residual, update, current, 12)
     ranges = [(HALO_Z - 2, planes - HALO_Z + 2)] * 2
-    plane_steps(faces, ranges, source, residual, update, current, False, (5, 5))
-    plane_residual(faces, HALO_Z, planes - HALO_Z, residual, update, 8)
+    plane_steps(faces, ranges, source, residual, update, current, False, (10, 10))
+    plane_residual(faces, HALO_Z, planes - HALO_Z, residual, update, 16)
     own_planes = pl.ds(HALO_Z, planes - 2 * HALO_Z)
     residual_out[...] = residual[own_planes, :own_y, :128]
     solution[...] = current[own_planes, :own_y, :128]
@@ -794,7 +794,7 @@
         )(*arguments, *far_arguments)
 
     x_a, x_b = swap_pairs(x_count, False), swap_pairs(x_count, True)
-    z_pairs = swap_pairs(z_count, False), swap_pairs(z_count, True)
+    z_a, z_b = swap_pairs(z_count, False), swap_pairs(z_count, True)
     both = jnp.stack([right_side, coefficient])
     sent = call(
         start_kernel,
@@ -818,7 +818,7 @@
         [],
     )
     got = [edges] + [
-        swapped(value, ("gz",), lambda z, pairs=pairs: (pairs[z],)) for value, pairs in zip(sent, z_pairs)
+        swapped(value, ("gz",), lambda z, pairs=pairs: (pairs[z],)) for value, pairs in zip(sent, (z_b, z_a))
     ]
     far = [other_core(value) for value in (both, *got)]
 

time: 53.3 us -> 53.2 us (level)
  starting transfers between devices: 19.2 us -> 20.1 us
  Pallas kernels: 17.5 us -> 16.7 us
    ppermute x18, starting transfers between devices: 19.2 us -> 20.1 us  [swapped(): lax.ppermute(value, axes, [(int(source), int(target)) for source, target...]
    pallas_call x4, Pallas kernels: 17.5 us -> 16.7 us  [call(): pl.pallas_call(kernel, out_shape=tuple((jax.ShapeDtypeStruct(shape, F32)...]
  transfers between devices with their start and end apart: 18 -> 18, of which waited for: 10 -> 11; matrix products, arithmetic and copies ran while one was open for 0% -> 0% of each run, Pallas kernels for 0% -> 0%
where the time goes in v13:
time: 53.2 us; the launch traced here: 53 us
  starting transfers between devices  20.1 us (38%)
  Pallas kernels  16.7 us (31%)
  waiting for transfers between devices  15.4 us (29%)
  between operations  0.8 us (2%)
    ppermute x18, starting transfers between devices, swapped(): lax.ppermute(value, axes, [(int(source), int(target)) for source, target...  20.1 us
    pallas_call x4, Pallas kernels, call(): pl.pallas_call(kernel, out_shape=tuple((jax.ShapeDtypeStruct(shape, F32)...  16.7 us
    ppermute x18, waiting for transfers between devices, swapped(): lax.ppermute(value, axes, [(int(source), int(target)) for source, target...  15.4 us
  transfers between devices with their start and end apart: 18, of which 11 were waited for; matrix products, arithmetic and copies ran while one was open for 0% of the time, Pallas kernels for 0%

profile of v13, /device:TPU:0, one launch (start us, length us, event | category | flops | bytes accessed | tf_op | source)
XLA Modules:
  0.0 53.0 jit_solution(14395790322868621079)
XLA Ops:
  0.6 1.9 %start.1 = (f32[2,16,128]{2,1,0:T(8,128)}, f32[2,16,128]{2,1,0:T(8,128)}) custom-call(f32[16,16,128]{2,1,0:T(8,128)} %bitcast.10, f32[16,16,128]{2,1,0:T(8,128)} %coef.1), custom_call_target="tpu_custom_call" | custom-call | tf_op jit(solution)/shard_map/start/pallas_call | solution.py:786
  2.5 1.4 %collective-permute-start = (f32[2,16,128]{2,1,0:T(8,128)}, f32[2,16,128]{2,1,0:T(8,128)S(1)}, u32[]{:S(2)}, u32[]{:S(2)}) collective-permute-start(f32[2,16,128]{2,1,0:T(8,128)} %get-tuple-element.17), channel_id=1, source_target_pairs={{0,0},{8,16},{16,8},{24,24},{1,1},{9,17},{17,9},{25,25},{2,2},{10,... | collective-permute-start | bytes 49160 | tf_op jit(solution)/shard_map/ppermute | solution.py:510
  3.9 5.0 %collective-permute-start.1 = (f32[2,16,128]{2,1,0:T(8,128)}, f32[2,16,128]{2,1,0:T(8,128)S(1)}, u32[]{:S(2)}, u32[]{:S(2)}) collective-permute-start(f32[2,16,128]{2,1,0:T(8,128)} %get-tuple-element.18), channel_id=1, source_target_pairs={{0,8},{8,0},{16,24},{24,16},{1,9},{9,1},{17,25},{25,17},{2,10},{10... | collective-permute-start | bytes 49160 | tf_op jit(solution)/shard_map/ppermute | solution.py:510
  9.1 1.9 %collective-permute-done.1.x_a = f32[2,16,128]{2,1,0:T(8,128)S(1)} collective-permute-done((f32[2,16,128]{2,1,0:T(8,128)}, f32[2,16,128]{2,1,0:T(8,128)S(1)}, u32[]{:S(2)}, u32[]{:S(2)}) %collective-permute-start.1) | collective-permute-done | bytes 16416 | tf_op jit(solution)/shard_map/ppermute | solution.py:510
  11.0 0.7 %collective-permute-start.2 = (f32[15,16,128]{2,1,0:T(8,128)S(1)}, f32[15,16,128]{2,1,0:T(8,128)S(1)}, u32[]{:S(2)}, u32[]{:S(2)}) collective-permute-start(f32[15,16,128]{2,1,0:T(8,128)S(1)} %get-tuple-element.20), channel_id=1, source_target_pairs={{0,0},{1,2},{2,1},{3,3},{4,4},{5,6},{6,5},{7,7},{8,8},{9,10},{10,9... | collective-permute-start | bytes 368648 | tf_op jit(solution)/shard_map/ppermute | solution.py:510
  11.7 4.5 %collective-permute-start.3 = (f32[15,16,128]{2,1,0:T(8,128)S(1)}, f32[15,16,128]{2,1,0:T(8,128)S(1)}, u32[]{:S(2)}, u32[]{:S(2)}) collective-permute-start(f32[15,16,128]{2,1,0:T(8,128)S(1)} %get-tuple-element.21), channel_id=1, source_target_pairs={{0,1},{1,0},{2,3},{3,2},{4,5},{5,4},{6,7},{7,6},{8,9},{9,8},{10,11... | collective-permute-start | bytes 368648 | tf_op jit(solution)/shard_map/ppermute | solution.py:510
  16.2 2.9 %collective-permute-done.3.refs_3_ = f32[15,16,128]{2,1,0:T(8,128)S(1)} collective-permute-done((f32[15,16,128]{2,1,0:T(8,128)S(1)}, f32[15,16,128]{2,1,0:T(8,128)S(1)}, u32[]{:S(2)}, u32[]{:S(2)}) %collective-permute-start.3) | collective-permute-done | bytes 122912 | tf_op jit(solution)/shard_map/ppermute | solution.py:510
  19.0 0.5 collective-permute-start.5
  19.5 0.9 %collective-permute-done.5.refs_5_ = f32[2,2,16,128]{3,2,1,0:T(8,128)S(1)} collective-permute-done((f32[2,2,16,128]{3,2,1,0:T(8,128)S(1)}, f32[2,2,16,128]{3,2,1,0:T(8,128)S(1)}, u32[]{:S(2)}, u32[]{:S(2)}) %collective-permute-start.5) | collective-permute-done | bytes 32800 | tf_op jit(solution)/shard_map/ppermute | solution.py:510
  20.4 3.6 %first.1 = (f32[64,128]{1,0:T(8,128)S(1)}, f32[32,24,256]{2,1,0:T(8,128)S(1)}, f32[32,24,256]{2,1,0:T(8,128)S(1)}, f32[32,24,256]{2,1,0:T(8,128)S(1)}, f32[32,24...) custom-call(f32[2,16,16,128]{3,2,1,0:T(8,128)S(1)} %pad_maximum_fusion., ...), custom_call_target="tpu_custom_call" | custom-call | tf_op jit(solution)/shard_map/first/pallas_call | solution.py:786
  24.0 1.4 %collective-permute-start.10 = (f32[64,128]{1,0:T(8,128)S(1)}, f32[64,128]{1,0:T(8,128)S(1)}, u32[]{:S(2)}, u32[]{:S(2)}) collective-permute-start(f32[64,128]{1,0:T(8,128)S(1)} %get-tuple-element.22), channel_id=1, source_target_pairs={{0,3},{1,2},{2,1},{3,0},{4,7},{5,6},{6,5},{7,4},{8,11},{9,10},{10,... | collective-permute-start | bytes 98312 | tf_op jit(solution)/shard_map/ppermute | solution.py:510
  25.4 2.1 %collective-permute-start.9 = (f32[64,128]{1,0:T(8,128)S(1)}, f32[64,128]{1,0:T(8,128)S(1)}, u32[]{:S(2)}, u32[]{:S(2)}) collective-permute-start(f32[64,128]{1,0:T(8,128)S(1)} %get-tuple-element.22), channel_id=1, source_target_pairs={{0,2},{1,3},{2,0},{3,1},{4,6},{5,7},{6,4},{7,5},{8,10},{9,11},{10,... | collective-permute-start | bytes 98312 | tf_op jit(solution)/shard_map/ppermute | solution.py:510
  27.5 0.9 %collective-permute-start.8 = (f32[64,128]{1,0:T(8,128)S(1)}, f32[64,128]{1,0:T(8,128)S(1)}, u32[]{:S(2)}, u32[]{:S(2)}) collective-permute-start(f32[64,128]{1,0:T(8,128)S(1)} %get-tuple-element.22), channel_id=1, source_target_pairs={{0,1},{1,0},{2,3},{3,2},{4,5},{5,4},{6,7},{7,6},{8,9},{9,8},{10,11... | collective-permute-start | bytes 98312 | tf_op jit(solution)/shard_map/ppermute | solution.py:510
  28.4 1.6 %collective-permute-done.10 = f32[64,128]{1,0:T(8,128)S(1)} collective-permute-done((f32[64,128]{1,0:T(8,128)S(1)}, f32[64,128]{1,0:T(8,128)S(1)}, u32[]{:S(2)}, u32[]{:S(2)}) %collective-permute-start.10) | collective-permute-done | bytes 32800 | tf_op jit(solution)/shard_map/ppermute | solution.py:510
  30.0 1.2 %collective-permute-done.9 = f32[64,128]{1,0:T(8,128)S(1)} collective-permute-done((f32[64,128]{1,0:T(8,128)S(1)}, f32[64,128]{1,0:T(8,128)S(1)}, u32[]{:S(2)}, u32[]{:S(2)}) %collective-permute-start.9) | collective-permute-done | bytes 32800 | tf_op jit(solution)/shard_map/ppermute | solution.py:510
  31.2 0.3 collective-permute-done.8
  31.6 1.5 %collective-permute-start.13 = (f32[4,64,128]{2,1,0:T(8,128)S(1)}, f32[4,64,128]{2,1,0:T(8,128)S(1)}, u32[]{:S(2)}, u32[]{:S(2)}) collective-permute-start(f32[4,64,128]{2,1,0:T(8,128)S(1)} %pad_maximum_fusion.1.refs_0_), channel_id=1, source_target_pairs={{0,24},{8,16},{16,8},{24,0},{1,25},{9,17},{17,9},{25,1},{2,26},{10... | collective-permute-start | bytes 393224 | tf_op jit(solution)/shard_map/ppermute | solution.py:510
  33.1 2.0 %collective-permute-start.12 = (f32[4,64,128]{2,1,0:T(8,128)S(1)}, f32[4,64,128]{2,1,0:T(8,128)S(1)}, u32[]{:S(2)}, u32[]{:S(2)}) collective-permute-start(f32[4,64,128]{2,1,0:T(8,128)S(1)} %pad_maximum_fusion.1.refs_0_), channel_id=1, source_target_pairs={{0,16},{8,24},{16,0},{24,8},{1,17},{9,25},{17,1},{25,9},{2,18},{10... | collective-permute-start | bytes 393224 | tf_op jit(solution)/shard_map/ppermute | solution.py:510
  35.1 3.6 %collective-permute-done.13.refs_3_ = f32[4,64,128]{2,1,0:T(8,128)S(1)} collective-permute-done((f32[4,64,128]{2,1,0:T(8,128)S(1)}, f32[4,64,128]{2,1,0:T(8,128)S(1)}, u32[]{:S(2)}, u32[]{:S(2)}) %collective-permute-start.13) | collective-permute-done | bytes 131104 | tf_op jit(solution)/shard_map/ppermute | solution.py:510
  38.8 1.1 %collective-permute-done.12.refs_2_ = f32[4,64,128]{2,1,0:T(8,128)S(1)} collective-permute-done((f32[4,64,128]{2,1,0:T(8,128)S(1)}, f32[4,64,128]{2,1,0:T(8,128)S(1)}, u32[]{:S(2)}, u32[]{:S(2)}) %collective-permute-start.12) | collective-permute-done | bytes 131104 | tf_op jit(solution)/shard_map/ppermute | solution.py:510
  39.9 0.5 %collective-permute-done.11.refs_1_ = f32[4,64,128]{2,1,0:T(8,128)S(1)} collective-permute-done((f32[4,64,128]{2,1,0:T(8,128)S(1)}, f32[4,64,128]{2,1,0:T(8,128)S(1)}, u32[]{:S(2)}, u32[]{:S(2)}) %collective-permute-start.11) | collective-permute-done | bytes 131104 | tf_op jit(solution)/shard_map/ppermute | solution.py:510
  40.4 0.8 %collective-permute-done.16.refs_6_ = f32[4,64,128]{2,1,0:T(8,128)S(1)} collective-permute-done((f32[4,64,128]{2,1,0:T(8,128)S(1)}, f32[4,64,128]{2,1,0:T(8,128)S(1)}, u32[]{:S(2)}, u32[]{:S(2)}) %collective-permute-start.16) | collective-permute-done | bytes 131104 | tf_op jit(solution)/shard_map/ppermute | solution.py:510
  41.2 0.5 %collective-permute-done.15.refs_5_ = f32[4,64,128]{2,1,0:T(8,128)S(1)} collective-permute-done((f32[4,64,128]{2,1,0:T(8,128)S(1)}, f32[4,64,128]{2,1,0:T(8,128)S(1)}, u32[]{:S(2)}, u32[]{:S(2)}) %collective-permute-start.15) | collective-permute-done | bytes 131104 | tf_op jit(solution)/shard_map/ppermute | solution.py:510
  41.8 11.2 %second.1 = (f32[16,16,128]{2,1,0:T(8,128)}, f32[16,16,128]{2,1,0:T(8,128)}) custom-call(f32[4,64,128]{2,1,0:T(8,128)S(1)} %pad_maximum_fusion.1.refs_0_, f32[4,64,128]{2,1,0:T(8,128)S(1)} %collective-permute-done.11.refs_1_, f32[4,64,128]{2,1,0:T(8,128)S(1)} %collective-permute-done.12.refs_2_, f32[4,64,128]{2,1,0:T(8,128)S(1)} %collective-permute-done.13.refs_3_, ...), custom_call_target="tpu_custom_call" | custom-call | tf_op jit(solution)/shard_map/second/pallas_call | solution.py:786
  (40 shorter events, 0.4 us)
Async XLA Ops:
  2.5 6.5 %collective-permute-start = (f32[2,16,128]{2,1,0:T(8,128)}, f32[2,16,128]{2,1,0:T(8,128)S(1)}, u32[]{:S(2)}, u32[]{:S(2)}) collective-permute-start(f32[2,16,128]{2,1,0:T(8,128)} %get-tuple-element.17), channel_id=1, source_target_pairs={{0,0},{8,16},{16,8},{24,24},{1,1},{9,17},{17,9},{25,25},{2,2},{10,... | collective-permute-start | bytes 49160 | tf_op jit(solution)/shard_map/ppermute | solution.py:510
  3.9 7.0 %collective-permute-start.1 = (f32[2,16,128]{2,1,0:T(8,128)}, f32[2,16,128]{2,1,0:T(8,128)S(1)}, u32[]{:S(2)}, u32[]{:S(2)}) collective-permute-start(f32[2,16,128]{2,1,0:T(8,128)} %get-tuple-element.18), channel_id=1, source_target_pairs={{0,8},{8,0},{16,24},{24,16},{1,9},{9,1},{17,25},{25,17},{2,10},{10... | collective-permute-start | bytes 49160 | tf_op jit(solution)/shard_map/ppermute | solution.py:510
  9.0 11.5 %copy-start.6 = (bf16[128,128]{1,0:T(8,128)(2,1)S(1)}, bf16[128,128]{1,0:T(8,128)(2,1)}, u32[]{:S(2)}) copy-start(bf16[128,128]{1,0:T(8,128)(2,1)} %constant.20.clone.refs_10_) | copy-start | bytes 98308
  9.0 11.4 %copy-start.7 = (bf16[128,128]{1,0:T(8,128)(2,1)S(1)}, bf16[128,128]{1,0:T(8,128)(2,1)}, u32[]{:S(2)}) copy-start(bf16[128,128]{1,0:T(8,128)(2,1)} %constant.19.clone.refs_9_) | copy-start | bytes 98308
  9.0 11.4 %collective-permute-start.4 = (f32[2,16,16,128]{3,2,1,0:T(8,128)S(1)}, f32[2,16,16,128]{3,2,1,0:T(8,128)S(1)}, u32[]{:S(2)}, u32[]{:S(2)}) collective-permute-start(f32[2,16,16,128]{3,2,1,0:T(8,128)S(1)} %pad_maximum_fusion.own.refs_0_), channel_id=1, source_target_pairs={{0,4},{4,0},{1,5},{5,1},{2,6},{6,2},{3,7},{7,3},{8,12},{12,8},{9,1... | collective-permute-start | bytes 786440 | tf_op jit(solution)/shard_map/ppermute | solution.py:510
  11.0 5.1 %collective-permute-start.2 = (f32[15,16,128]{2,1,0:T(8,128)S(1)}, f32[15,16,128]{2,1,0:T(8,128)S(1)}, u32[]{:S(2)}, u32[]{:S(2)}) collective-permute-start(f32[15,16,128]{2,1,0:T(8,128)S(1)} %get-tuple-element.20), channel_id=1, source_target_pairs={{0,0},{1,2},{2,1},{3,3},{4,4},{5,6},{6,5},{7,7},{8,8},{9,10},{10,9... | collective-permute-start | bytes 368648 | tf_op jit(solution)/shard_map/ppermute | solution.py:510
  11.7 7.3 %collective-permute-start.3 = (f32[15,16,128]{2,1,0:T(8,128)S(1)}, f32[15,16,128]{2,1,0:T(8,128)S(1)}, u32[]{:S(2)}, u32[]{:S(2)}) collective-permute-start(f32[15,16,128]{2,1,0:T(8,128)S(1)} %get-tuple-element.21), channel_id=1, source_target_pairs={{0,1},{1,0},{2,3},{3,2},{4,5},{5,4},{6,7},{7,6},{8,9},{9,8},{10,11... | collective-permute-start | bytes 368648 | tf_op jit(solution)/shard_map/ppermute | solution.py:510
  16.1 4.2 %collective-permute-start.6 = (f32[15,16,128]{2,1,0:T(8,128)S(1)}, f32[15,16,128]{2,1,0:T(8,128)S(1)}, u32[]{:S(2)}, u32[]{:S(2)}) collective-permute-start(f32[15,16,128]{2,1,0:T(8,128)S(1)} %collective-permute-done.2.refs_2_), channel_id=1, source_target_pairs={{0,4},{4,0},{1,5},{5,1},{2,6},{6,2},{3,7},{7,3},{8,12},{12,8},{9,1... | collective-permute-start | bytes 368648 | tf_op jit(solution)/shard_map/ppermute | solution.py:510
  19.0 1.4 %collective-permute-start.7 = (f32[15,16,128]{2,1,0:T(8,128)S(1)}, f32[15,16,128]{2,1,0:T(8,128)S(1)}, u32[]{:S(2)}, u32[]{:S(2)}) collective-permute-start(f32[15,16,128]{2,1,0:T(8,128)S(1)} %collective-permute-done.3.refs_3_), channel_id=1, source_target_pairs={{0,4},{4,0},{1,5},{5,1},{2,6},{6,2},{3,7},{7,3},{8,12},{12,8},{9,1... | collective-permute-start | bytes 368648 | tf_op jit(solution)/shard_map/ppermute | solution.py:510
  19.0 22.8 %copy-start = (bf16[4,256,256]{2,1,0:T(8,128)(2,1)S(1)}, bf16[4,256,256]{2,1,0:T(8,128)(2,1)}, u32[]{:S(2)}) copy-start(bf16[4,256,256]{2,1,0:T(8,128)(2,1)} %constant.22.clone.refs_16_) | copy-start | bytes 1572868
  19.0 1.4 %collective-permute-start.5 = (f32[2,2,16,128]{3,2,1,0:T(8,128)S(1)}, f32[2,2,16,128]{3,2,1,0:T(8,128)S(1)}, u32[]{:S(2)}, u32[]{:S(2)}) collective-permute-start(f32[2,2,16,128]{3,2,1,0:T(8,128)S(1)} %get-tuple-element.19.refs_1_), channel_id=1, source_target_pairs={{0,4},{4,0},{1,5},{5,1},{2,6},{6,2},{3,7},{7,3},{8,12},{12,8},{9,1... | collective-permute-start | bytes 98312 | tf_op jit(solution)/shard_map/ppermute | solution.py:510
  20.4 21.3 %copy-start.1 = (bf16[2,336,224]{2,1,0:T(8,128)(2,1)S(1)}, bf16[2,336,224]{2,1,0:T(8,128)(2,1)}, u32[]{:S(2)}) copy-start(bf16[2,336,224]{2,1,0:T(8,128)(2,1)} %constant.21.clone.refs_15_) | copy-start | bytes 903172
  24.0 6.0 %collective-permute-start.10 = (f32[64,128]{1,0:T(8,128)S(1)}, f32[64,128]{1,0:T(8,128)S(1)}, u32[]{:S(2)}, u32[]{:S(2)}) collective-permute-start(f32[64,128]{1,0:T(8,128)S(1)} %get-tuple-element.22), channel_id=1, source_target_pairs={{0,3},{1,2},{2,1},{3,0},{4,7},{5,6},{6,5},{7,4},{8,11},{9,10},{10,... | collective-permute-start | bytes 98312 | tf_op jit(solution)/shard_map/ppermute | solution.py:510
  25.4 5.9 %collective-permute-start.9 = (f32[64,128]{1,0:T(8,128)S(1)}, f32[64,128]{1,0:T(8,128)S(1)}, u32[]{:S(2)}, u32[]{:S(2)}) collective-permute-start(f32[64,128]{1,0:T(8,128)S(1)} %get-tuple-element.22), channel_id=1, source_target_pairs={{0,2},{1,3},{2,0},{3,1},{4,6},{5,7},{6,4},{7,5},{8,10},{9,11},{10,... | collective-permute-start | bytes 98312 | tf_op jit(solution)/shard_map/ppermute | solution.py:510
  27.5 4.1 %collective-permute-start.8 = (f32[64,128]{1,0:T(8,128)S(1)}, f32[64,128]{1,0:T(8,128)S(1)}, u32[]{:S(2)}, u32[]{:S(2)}) collective-permute-start(f32[64,128]{1,0:T(8,128)S(1)} %get-tuple-element.22), channel_id=1, source_target_pairs={{0,1},{1,0},{2,3},{3,2},{4,5},{5,4},{6,7},{7,6},{8,9},{9,8},{10,11... | collective-permute-start | bytes 98312 | tf_op jit(solution)/shard_map/ppermute | solution.py:510
  31.6 10.2 %copy-start.4 = (bf16[256,128]{1,0:T(8,128)(2,1)S(1)}, bf16[256,128]{1,0:T(8,128)(2,1)}, u32[]{:S(2)}) copy-start(bf16[256,128]{1,0:T(8,128)(2,1)} %constant.24.clone.refs_18_) | copy-start | bytes 196612
  31.6 10.2 %copy-start.5 = (bf16[128,256]{1,0:T(8,128)(2,1)S(1)}, bf16[128,256]{1,0:T(8,128)(2,1)}, u32[]{:S(2)}) copy-start(bf16[128,256]{1,0:T(8,128)(2,1)} %constant.23.clone.refs_17_) | copy-start | bytes 196612
  31.6 7.2 %collective-permute-start.13 = (f32[4,64,128]{2,1,0:T(8,128)S(1)}, f32[4,64,128]{2,1,0:T(8,128)S(1)}, u32[]{:S(2)}, u32[]{:S(2)}) collective-permute-start(f32[4,64,128]{2,1,0:T(8,128)S(1)} %pad_maximum_fusion.1.refs_0_), channel_id=1, source_target_pairs={{0,24},{8,16},{16,8},{24,0},{1,25},{9,17},{17,9},{25,1},{2,26},{10... | collective-permute-start | bytes 393224 | tf_op jit(solution)/shard_map/ppermute | solution.py:510
  33.1 6.8 %collective-permute-start.12 = (f32[4,64,128]{2,1,0:T(8,128)S(1)}, f32[4,64,128]{2,1,0:T(8,128)S(1)}, u32[]{:S(2)}, u32[]{:S(2)}) collective-permute-start(f32[4,64,128]{2,1,0:T(8,128)S(1)} %pad_maximum_fusion.1.refs_0_), channel_id=1, source_target_pairs={{0,16},{8,24},{16,0},{24,8},{1,17},{9,25},{17,1},{25,9},{2,18},{10... | collective-permute-start | bytes 393224 | tf_op jit(solution)/shard_map/ppermute | solution.py:510
  35.0 5.4 %collective-permute-start.11 = (f32[4,64,128]{2,1,0:T(8,128)S(1)}, f32[4,64,128]{2,1,0:T(8,128)S(1)}, u32[]{:S(2)}, u32[]{:S(2)}) collective-permute-start(f32[4,64,128]{2,1,0:T(8,128)S(1)} %pad_maximum_fusion.1.refs_0_), channel_id=1, source_target_pairs={{0,8},{8,0},{16,24},{24,16},{1,9},{9,1},{17,25},{25,17},{2,10},{10... | collective-permute-start | bytes 393224 | tf_op jit(solution)/shard_map/ppermute | solution.py:510
  35.1 5.3 %collective-permute-start.14 = (f32[4,64,128]{2,1,0:T(8,128)S(1)}, f32[4,64,128]{2,1,0:T(8,128)S(1)}, u32[]{:S(2)}, u32[]{:S(2)}) collective-permute-start(f32[4,64,128]{2,1,0:T(8,128)S(1)} %pad_maximum_fusion.1.refs_0_), channel_id=1, source_target_pairs={{0,4},{4,0},{1,5},{5,1},{2,6},{6,2},{3,7},{7,3},{8,12},{12,8},{9,1... | collective-permute-start | bytes 393224 | tf_op jit(solution)/shard_map/ppermute | solution.py:510
  38.8 1.7 %collective-permute-start.17 = (f32[4,64,128]{2,1,0:T(8,128)S(1)}, f32[4,64,128]{2,1,0:T(8,128)S(1)}, u32[]{:S(2)}, u32[]{:S(2)}) collective-permute-start(f32[4,64,128]{2,1,0:T(8,128)S(1)} %collective-permute-done.13.refs_3_), channel_id=1, source_target_pairs={{0,4},{4,0},{1,5},{5,1},{2,6},{6,2},{3,7},{7,3},{8,12},{12,8},{9,1... | collective-permute-start | bytes 393224 | tf_op jit(solution)/shard_map/ppermute | solution.py:510
  39.9 1.3 %collective-permute-start.16 = (f32[4,64,128]{2,1,0:T(8,128)S(1)}, f32[4,64,128]{2,1,0:T(8,128)S(1)}, u32[]{:S(2)}, u32[]{:S(2)}) collective-permute-start(f32[4,64,128]{2,1,0:T(8,128)S(1)} %collective-permute-done.12.refs_2_), channel_id=1, source_target_pairs={{0,4},{4,0},{1,5},{5,1},{2,6},{6,2},{3,7},{7,3},{8,12},{12,8},{9,1... | collective-permute-start | bytes 393224 | tf_op jit(solution)/shard_map/ppermute | solution.py:510
  40.4 1.3 %collective-permute-start.15 = (f32[4,64,128]{2,1,0:T(8,128)S(1)}, f32[4,64,128]{2,1,0:T(8,128)S(1)}, u32[]{:S(2)}, u32[]{:S(2)}) collective-permute-start(f32[4,64,128]{2,1,0:T(8,128)S(1)} %collective-permute-done.11.refs_1_), channel_id=1, source_target_pairs={{0,4},{4,0},{1,5},{5,1},{2,6},{6,2},{3,7},{7,3},{8,12},{12,8},{9,1... | collective-permute-start | bytes 393224 | tf_op jit(solution)/shard_map/ppermute | solution.py:510
  (5 other events, 46.5 us)

commit v14 on v13

--- a/solution.py
+++ b/solution.py
@@ -562,7 +562,7 @@
     return right, left
 
 
-def pack_z_kernel(x_count, own, x_b, x_a, edges, z_b, z_a):
+def pack_z_kernel(x_count, own, x_b, x_a, edges, z_a, z_b):
     _, planes, own_y, _ = own.shape
     z_even = lax.axis_index("gz") % 2 == 0
     edges[0], edges[1] = x_a[...], x_b[...]
@@ -612,7 +612,7 @@
 
             def taken(place):
                 is_a = z_even if is_above else jnp.logical_not(z_even)
-                by_b, by_a = (joined(got[index], far[1 + index], (place,)) for index in (1, 2))
+                by_a, by_b = (joined(got[index], far[1 + index], (place,)) for index in (1, 2))
                 return kept(flag, jnp.where(is_a, by_a, by_b))
 
             packed = taken(sum(SENT_Z) + which)
@@ -634,9 +634,9 @@
     fill_window(own, got, far, source, coef, *counts)
     planes, rows, lanes = source.shape
     own_y = rows - HALO_Y
-    plane_faces(coef, faces, 0, planes, link_mask(rows, lanes), None, source, update, 8)
+    plane_faces(coef, faces, 0, planes, link_mask(rows, lanes), None, source, update, 16)
     ranges = [(2, planes - 2), (4, planes - 4)]
-    plane_steps(faces, ranges, source, residual, update, estimate, True, (14, 12))
+    plane_steps(faces, ranges, source, residual, update, estimate, True, (28, 24))
     plane_residual(faces, HALO_Z, planes - HALO_Z, residual, update, 16)
     for pair in range((planes - 2 * HALO_Z) // 2):
         low = HALO_Z + 2 * pair
@@ -698,9 +698,9 @@
     link_y = jnp.where(row == mid_y - 1, 0.0, 1.0)
     link_x = jnp.where(lane == mid_x - 1, 0.0, 1.0)
     start, stop = PAD, PAD + mid_z
-    plane_faces(mid_coef, mid_faces, start, stop, link_y, link_x, mid_source, mid_update, 8)
+    plane_faces(mid_coef, mid_faces, start, stop, link_y, link_x, mid_source, mid_update, 16)
     ranges = [(start, stop)] * (DEGREE - 1)
-    plane_steps(mid_faces, ranges, mid_source, mid_residual, mid_update, mid_estimate, True, (16, 16))
+    plane_steps(mid_faces, ranges, mid_source, mid_residual, mid_update, mid_estimate, True, (32, 32))
 
     def finish_pairs(here, own):
         before = mid_residual[here]
@@ -745,11 +745,15 @@
         high = jnp.minimum(z_index * 8 + 8 + margin, mid_z)
         return PAD + low, PAD + high
 
+    def about(count):
+        low = PAD + jnp.clip(z_index * 8 + 4 - count // 2, 0, mid_z - count)
+        return low, low + count
+
     low, high = clipped(8)
     lax.fori_loop(0, (high - low) // 8, add_mid, (low - PAD) // 2)
-    plane_restart(mid_faces, *clipped(8), mid_source, mid_residual, mid_update, mid_estimate)
+    plane_restart(mid_faces, *about(24), mid_source, mid_residual, mid_update, mid_estimate, 24)
     plane_steps(
-        mid_faces, [clipped(4), clipped(4)], mid_source, mid_residual, mid_update, mid_estimate, False, (4, 4)
+        mid_faces, [about(16), about(16)], mid_source, mid_residual, mid_update, mid_estimate, False, (16, 16)
     )
 
     coarse_planes = up_left.shape[1] // mid_y
@@ -764,9 +768,9 @@
         current[here] = estimate[here] + jnp.where(inverse[here] > 0.0, step, 0.0)
     for plane in (HALO_Z - 5, planes - HALO_Z + 4):
         current[plane] = estimate[plane]
-    plane_restart(faces, HALO_Z - 4, planes - HALO_Z + 4, source, residual, update, current, 12)
+    plane_restart(faces, HALO_Z - 4, planes - HALO_Z + 4, source, residual, update, current, 24)
     ranges = [(HALO_Z - 2, planes - HALO_Z + 2)] * 2
-    plane_steps(faces, ranges, source, residual, update, current, False, (10, 10))
+    plane_steps(faces, ranges, source, residual, update, current, False, (20, 20))
     plane_residual(faces, HALO_Z, planes - HALO_Z, residual, update, 16)
     own_planes = pl.ds(HALO_Z, planes - 2 * HALO_Z)
     residual_out[...] = residual[own_planes, :own_y, :128]
@@ -818,7 +822,7 @@
         [],
     )
     got = [edges] + [
-        swapped(value, ("gz",), lambda z, pairs=pairs: (pairs[z],)) for value, pairs in zip(sent, (z_b, z_a))
+        swapped(value, ("gz",), lambda z, pairs=pairs: (pairs[z],)) for value, pairs in zip(sent, (z_a, z_b))
     ]
     far = [other_core(value) for value in (both, *got)]
 

time: 53.2 us -> 50.6 us (0.951)
  Pallas kernels: 16.7 us -> 14.9 us
  starting transfers between devices: 20.1 us -> 19.2 us
    pallas_call x4, Pallas kernels: 16.7 us -> 14.9 us  [call(): pl.pallas_call(kernel, out_shape=tuple((jax.ShapeDtypeStruct(shape, F32)...]
    ppermute x18, starting transfers between devices: 20.1 us -> 19.2 us  [swapped(): lax.ppermute(value, axes, [(int(source), int(target)) for source, target...]
  transfers between devices with their start and end apart: 18 -> 18, of which waited for: 11 -> 10; matrix products, arithmetic and copies ran while one was open for 0% -> 0% of each run, Pallas kernels for 0% -> 0%
where the time goes in v14:
time: 50.6 us; the launch traced here: 50.4 us
  starting transfers between devices  19.2 us (38%)
  waiting for transfers between devices  15.5 us (31%)
  Pallas kernels  14.9 us (29%)
  between operations  0.8 us (2%)
    ppermute x18, starting transfers between devices, swapped(): lax.ppermute(value, axes, [(int(source), int(target)) for source, target...  19.2 us
    ppermute x18, waiting for transfers between devices, swapped(): lax.ppermute(value, axes, [(int(source), int(target)) for source, target...  15.5 us
    pallas_call x4, Pallas kernels, call(): pl.pallas_call(kernel, out_shape=tuple((jax.ShapeDtypeStruct(shape, F32)...  14.9 us
  transfers between devices with their start and end apart: 18, of which 10 were waited for; matrix products, arithmetic and copies ran while one was open for 0% of the time, Pallas kernels for 0%

profile of v14, /device:TPU:0, one launch (start us, length us, event | category | flops | bytes accessed | tf_op | source)
XLA Modules:
  0.0 50.4 jit_solution(17966966125411147815)
XLA Ops:
  0.6 1.9 %start.1 = (f32[2,16,128]{2,1,0:T(8,128)}, f32[2,16,128]{2,1,0:T(8,128)}) custom-call(f32[16,16,128]{2,1,0:T(8,128)} %bitcast.10, f32[16,16,128]{2,1,0:T(8,128)} %coef.1), custom_call_target="tpu_custom_call" | custom-call | tf_op jit(solution)/shard_map/start/pallas_call | solution.py:790
  2.5 1.4 %collective-permute-start = (f32[2,16,128]{2,1,0:T(8,128)}, f32[2,16,128]{2,1,0:T(8,128)S(1)}, u32[]{:S(2)}, u32[]{:S(2)}) collective-permute-start(f32[2,16,128]{2,1,0:T(8,128)} %get-tuple-element.17), channel_id=1, source_target_pairs={{0,0},{8,16},{16,8},{24,24},{1,1},{9,17},{17,9},{25,25},{2,2},{10,... | collective-permute-start | bytes 49160 | tf_op jit(solution)/shard_map/ppermute | solution.py:510
  3.9 5.0 %collective-permute-start.1 = (f32[2,16,128]{2,1,0:T(8,128)}, f32[2,16,128]{2,1,0:T(8,128)S(1)}, u32[]{:S(2)}, u32[]{:S(2)}) collective-permute-start(f32[2,16,128]{2,1,0:T(8,128)} %get-tuple-element.18), channel_id=1, source_target_pairs={{0,8},{8,0},{16,24},{24,16},{1,9},{9,1},{17,25},{25,17},{2,10},{10... | collective-permute-start | bytes 49160 | tf_op jit(solution)/shard_map/ppermute | solution.py:510
  9.1 1.9 %collective-permute-done.1.x_a = f32[2,16,128]{2,1,0:T(8,128)S(1)} collective-permute-done((f32[2,16,128]{2,1,0:T(8,128)}, f32[2,16,128]{2,1,0:T(8,128)S(1)}, u32[]{:S(2)}, u32[]{:S(2)}) %collective-permute-start.1) | collective-permute-done | bytes 16416 | tf_op jit(solution)/shard_map/ppermute | solution.py:510
  11.0 1.6 %collective-permute-start.2 = (f32[15,16,128]{2,1,0:T(8,128)S(1)}, f32[15,16,128]{2,1,0:T(8,128)S(1)}, u32[]{:S(2)}, u32[]{:S(2)}) collective-permute-start(f32[15,16,128]{2,1,0:T(8,128)S(1)} %get-tuple-element.20), channel_id=1, source_target_pairs={{0,1},{1,0},{2,3},{3,2},{4,5},{5,4},{6,7},{7,6},{8,9},{9,8},{10,11... | collective-permute-start | bytes 368648 | tf_op jit(solution)/shard_map/ppermute | solution.py:510
  12.6 0.7 %collective-permute-start.3 = (f32[15,16,128]{2,1,0:T(8,128)S(1)}, f32[15,16,128]{2,1,0:T(8,128)S(1)}, u32[]{:S(2)}, u32[]{:S(2)}) collective-permute-start(f32[15,16,128]{2,1,0:T(8,128)S(1)} %get-tuple-element.21), channel_id=1, source_target_pairs={{0,0},{1,2},{2,1},{3,3},{4,4},{5,6},{6,5},{7,7},{8,8},{9,10},{10,9... | collective-permute-start | bytes 368648 | tf_op jit(solution)/shard_map/ppermute | solution.py:510
  13.3 2.6 %collective-permute-done.2.refs_2_ = f32[15,16,128]{2,1,0:T(8,128)S(1)} collective-permute-done((f32[15,16,128]{2,1,0:T(8,128)S(1)}, f32[15,16,128]{2,1,0:T(8,128)S(1)}, u32[]{:S(2)}, u32[]{:S(2)}) %collective-permute-start.2) | collective-permute-done | bytes 122912 | tf_op jit(solution)/shard_map/ppermute | solution.py:510
  15.9 0.5 %collective-permute-start.7 = (f32[15,16,128]{2,1,0:T(8,128)S(1)}, f32[15,16,128]{2,1,0:T(8,128)S(1)}, u32[]{:S(2)}, u32[]{:S(2)}) collective-permute-start(f32[15,16,128]{2,1,0:T(8,128)S(1)} %collective-permute-done.3.refs_3_), channel_id=1, source_target_pairs={{0,4},{4,0},{1,5},{5,1},{2,6},{6,2},{3,7},{7,3},{8,12},{12,8},{9,1... | collective-permute-start | bytes 368648 | tf_op jit(solution)/shard_map/ppermute | solution.py:510
  16.5 1.1 %collective-permute-done.5.refs_5_ = f32[2,2,16,128]{3,2,1,0:T(8,128)S(1)} collective-permute-done((f32[2,2,16,128]{3,2,1,0:T(8,128)S(1)}, f32[2,2,16,128]{3,2,1,0:T(8,128)S(1)}, u32[]{:S(2)}, u32[]{:S(2)}) %collective-permute-start.5) | collective-permute-done | bytes 32800 | tf_op jit(solution)/shard_map/ppermute | solution.py:510
  17.7 3.0 %first.1 = (f32[64,128]{1,0:T(8,128)S(1)}, f32[32,24,256]{2,1,0:T(8,128)S(1)}, f32[32,24,256]{2,1,0:T(8,128)S(1)}, f32[32,24,256]{2,1,0:T(8,128)S(1)}, f32[32,24...) custom-call(f32[2,16,16,128]{3,2,1,0:T(8,128)S(1)} %pad_maximum_fusion., ...), custom_call_target="tpu_custom_call" | custom-call | tf_op jit(solution)/shard_map/first/pallas_call | solution.py:790
  20.7 3.6 %collective-permute-start.10 = (f32[64,128]{1,0:T(8,128)S(1)}, f32[64,128]{1,0:T(8,128)S(1)}, u32[]{:S(2)}, u32[]{:S(2)}) collective-permute-start(f32[64,128]{1,0:T(8,128)S(1)} %get-tuple-element.22), channel_id=1, source_target_pairs={{0,3},{1,2},{2,1},{3,0},{4,7},{5,6},{6,5},{7,4},{8,11},{9,10},{10,... | collective-permute-start | bytes 98312 | tf_op jit(solution)/shard_map/ppermute | solution.py:510
  24.3 2.1 %collective-permute-start.9 = (f32[64,128]{1,0:T(8,128)S(1)}, f32[64,128]{1,0:T(8,128)S(1)}, u32[]{:S(2)}, u32[]{:S(2)}) collective-permute-start(f32[64,128]{1,0:T(8,128)S(1)} %get-tuple-element.22), channel_id=1, source_target_pairs={{0,2},{1,3},{2,0},{3,1},{4,6},{5,7},{6,4},{7,5},{8,10},{9,11},{10,... | collective-permute-start | bytes 98312 | tf_op jit(solution)/shard_map/ppermute | solution.py:510
  26.4 0.5 %collective-permute-start.8 = (f32[64,128]{1,0:T(8,128)S(1)}, f32[64,128]{1,0:T(8,128)S(1)}, u32[]{:S(2)}, u32[]{:S(2)}) collective-permute-start(f32[64,128]{1,0:T(8,128)S(1)} %get-tuple-element.22), channel_id=1, source_target_pairs={{0,1},{1,0},{2,3},{3,2},{4,5},{5,4},{6,7},{7,6},{8,9},{9,8},{10,11... | collective-permute-start | bytes 98312 | tf_op jit(solution)/shard_map/ppermute | solution.py:510
  27.0 2.1 %collective-permute-done.9 = f32[64,128]{1,0:T(8,128)S(1)} collective-permute-done((f32[64,128]{1,0:T(8,128)S(1)}, f32[64,128]{1,0:T(8,128)S(1)}, u32[]{:S(2)}, u32[]{:S(2)}) %collective-permute-start.9) | collective-permute-done | bytes 32800 | tf_op jit(solution)/shard_map/ppermute | solution.py:510
  29.1 1.2 %collective-permute-done.8 = f32[64,128]{1,0:T(8,128)S(1)} collective-permute-done((f32[64,128]{1,0:T(8,128)S(1)}, f32[64,128]{1,0:T(8,128)S(1)}, u32[]{:S(2)}, u32[]{:S(2)}) %collective-permute-start.8) | collective-permute-done | bytes 32800 | tf_op jit(solution)/shard_map/ppermute | solution.py:510
  30.4 1.5 %collective-permute-start.13 = (f32[4,64,128]{2,1,0:T(8,128)S(1)}, f32[4,64,128]{2,1,0:T(8,128)S(1)}, u32[]{:S(2)}, u32[]{:S(2)}) collective-permute-start(f32[4,64,128]{2,1,0:T(8,128)S(1)} %pad_maximum_fusion.1.refs_0_), channel_id=1, source_target_pairs={{0,24},{8,16},{16,8},{24,0},{1,25},{9,17},{17,9},{25,1},{2,26},{10... | collective-permute-start | bytes 393224 | tf_op jit(solution)/shard_map/ppermute | solution.py:510
  31.9 2.0 %collective-permute-start.12 = (f32[4,64,128]{2,1,0:T(8,128)S(1)}, f32[4,64,128]{2,1,0:T(8,128)S(1)}, u32[]{:S(2)}, u32[]{:S(2)}) collective-permute-start(f32[4,64,128]{2,1,0:T(8,128)S(1)} %pad_maximum_fusion.1.refs_0_), channel_id=1, source_target_pairs={{0,16},{8,24},{16,0},{24,8},{1,17},{9,25},{17,1},{25,9},{2,18},{10... | collective-permute-start | bytes 393224 | tf_op jit(solution)/shard_map/ppermute | solution.py:510
  33.8 0.1 collective-permute-start.11
  33.9 3.4 %collective-permute-done.13.refs_3_ = f32[4,64,128]{2,1,0:T(8,128)S(1)} collective-permute-done((f32[4,64,128]{2,1,0:T(8,128)S(1)}, f32[4,64,128]{2,1,0:T(8,128)S(1)}, u32[]{:S(2)}, u32[]{:S(2)}) %collective-permute-start.13) | collective-permute-done | bytes 131104 | tf_op jit(solution)/shard_map/ppermute | solution.py:510
  37.4 1.1 %collective-permute-done.12.refs_2_ = f32[4,64,128]{2,1,0:T(8,128)S(1)} collective-permute-done((f32[4,64,128]{2,1,0:T(8,128)S(1)}, f32[4,64,128]{2,1,0:T(8,128)S(1)}, u32[]{:S(2)}, u32[]{:S(2)}) %collective-permute-start.12) | collective-permute-done | bytes 131104 | tf_op jit(solution)/shard_map/ppermute | solution.py:510
  38.5 0.5 %collective-permute-done.11.refs_1_ = f32[4,64,128]{2,1,0:T(8,128)S(1)} collective-permute-done((f32[4,64,128]{2,1,0:T(8,128)S(1)}, f32[4,64,128]{2,1,0:T(8,128)S(1)}, u32[]{:S(2)}, u32[]{:S(2)}) %collective-permute-start.11) | collective-permute-done | bytes 131104 | tf_op jit(solution)/shard_map/ppermute | solution.py:510
  39.0 0.8 %collective-permute-done.16.refs_6_ = f32[4,64,128]{2,1,0:T(8,128)S(1)} collective-permute-done((f32[4,64,128]{2,1,0:T(8,128)S(1)}, f32[4,64,128]{2,1,0:T(8,128)S(1)}, u32[]{:S(2)}, u32[]{:S(2)}) %collective-permute-start.16) | collective-permute-done | bytes 131104 | tf_op jit(solution)/shard_map/ppermute | solution.py:510
  39.8 0.5 %collective-permute-done.15.refs_5_ = f32[4,64,128]{2,1,0:T(8,128)S(1)} collective-permute-done((f32[4,64,128]{2,1,0:T(8,128)S(1)}, f32[4,64,128]{2,1,0:T(8,128)S(1)}, u32[]{:S(2)}, u32[]{:S(2)}) %collective-permute-start.15) | collective-permute-done | bytes 131104 | tf_op jit(solution)/shard_map/ppermute | solution.py:510
  40.4 10.0 %second.1 = (f32[16,16,128]{2,1,0:T(8,128)}, f32[16,16,128]{2,1,0:T(8,128)}) custom-call(f32[4,64,128]{2,1,0:T(8,128)S(1)} %pad_maximum_fusion.1.refs_0_, f32[4,64,128]{2,1,0:T(8,128)S(1)} %collective-permute-done.11.refs_1_, f32[4,64,128]{2,1,0:T(8,128)S(1)} %collective-permute-done.12.refs_2_, f32[4,64,128]{2,1,0:T(8,128)S(1)} %collective-permute-done.13.refs_3_, ...), custom_call_target="tpu_custom_call" | custom-call | tf_op jit(solution)/shard_map/second/pallas_call | solution.py:790
  (40 shorter events, 0.3 us)
Async XLA Ops:
  2.5 6.5 %collective-permute-start = (f32[2,16,128]{2,1,0:T(8,128)}, f32[2,16,128]{2,1,0:T(8,128)S(1)}, u32[]{:S(2)}, u32[]{:S(2)}) collective-permute-start(f32[2,16,128]{2,1,0:T(8,128)} %get-tuple-element.17), channel_id=1, source_target_pairs={{0,0},{8,16},{16,8},{24,24},{1,1},{9,17},{17,9},{25,25},{2,2},{10,... | collective-permute-start | bytes 49160 | tf_op jit(solution)/shard_map/ppermute | solution.py:510
  3.9 7.0 %collective-permute-start.1 = (f32[2,16,128]{2,1,0:T(8,128)}, f32[2,16,128]{2,1,0:T(8,128)S(1)}, u32[]{:S(2)}, u32[]{:S(2)}) collective-permute-start(f32[2,16,128]{2,1,0:T(8,128)} %get-tuple-element.18), channel_id=1, source_target_pairs={{0,8},{8,0},{16,24},{24,16},{1,9},{9,1},{17,25},{25,17},{2,10},{10... | collective-permute-start | bytes 49160 | tf_op jit(solution)/shard_map/ppermute | solution.py:510
  9.0 8.7 %collective-permute-start.4 = (f32[2,16,16,128]{3,2,1,0:T(8,128)S(1)}, f32[2,16,16,128]{3,2,1,0:T(8,128)S(1)}, u32[]{:S(2)}, u32[]{:S(2)}) collective-permute-start(f32[2,16,16,128]{3,2,1,0:T(8,128)S(1)} %pad_maximum_fusion.own.refs_0_), channel_id=1, source_target_pairs={{0,4},{4,0},{1,5},{5,1},{2,6},{6,2},{3,7},{7,3},{8,12},{12,8},{9,1... | collective-permute-start | bytes 786440 | tf_op jit(solution)/shard_map/ppermute | solution.py:510
  11.0 4.9 %collective-permute-start.2 = (f32[15,16,128]{2,1,0:T(8,128)S(1)}, f32[15,16,128]{2,1,0:T(8,128)S(1)}, u32[]{:S(2)}, u32[]{:S(2)}) collective-permute-start(f32[15,16,128]{2,1,0:T(8,128)S(1)} %get-tuple-element.20), channel_id=1, source_target_pairs={{0,1},{1,0},{2,3},{3,2},{4,5},{5,4},{6,7},{7,6},{8,9},{9,8},{10,11... | collective-permute-start | bytes 368648 | tf_op jit(solution)/shard_map/ppermute | solution.py:510
  12.6 3.3 %collective-permute-start.3 = (f32[15,16,128]{2,1,0:T(8,128)S(1)}, f32[15,16,128]{2,1,0:T(8,128)S(1)}, u32[]{:S(2)}, u32[]{:S(2)}) collective-permute-start(f32[15,16,128]{2,1,0:T(8,128)S(1)} %get-tuple-element.21), channel_id=1, source_target_pairs={{0,0},{1,2},{2,1},{3,3},{4,4},{5,6},{6,5},{7,7},{8,8},{9,10},{10,9... | collective-permute-start | bytes 368648 | tf_op jit(solution)/shard_map/ppermute | solution.py:510
  15.9 1.7 %collective-permute-start.6 = (f32[15,16,128]{2,1,0:T(8,128)S(1)}, f32[15,16,128]{2,1,0:T(8,128)S(1)}, u32[]{:S(2)}, u32[]{:S(2)}) collective-permute-start(f32[15,16,128]{2,1,0:T(8,128)S(1)} %collective-permute-done.2.refs_2_), channel_id=1, source_target_pairs={{0,4},{4,0},{1,5},{5,1},{2,6},{6,2},{3,7},{7,3},{8,12},{12,8},{9,1... | collective-permute-start | bytes 368648 | tf_op jit(solution)/shard_map/ppermute | solution.py:510
  15.9 1.7 %collective-permute-start.7 = (f32[15,16,128]{2,1,0:T(8,128)S(1)}, f32[15,16,128]{2,1,0:T(8,128)S(1)}, u32[]{:S(2)}, u32[]{:S(2)}) collective-permute-start(f32[15,16,128]{2,1,0:T(8,128)S(1)} %collective-permute-done.3.refs_3_), channel_id=1, source_target_pairs={{0,4},{4,0},{1,5},{5,1},{2,6},{6,2},{3,7},{7,3},{8,12},{12,8},{9,1... | collective-permute-start | bytes 368648 | tf_op jit(solution)/shard_map/ppermute | solution.py:510
  16.4 23.9 %copy-start = (bf16[4,256,256]{2,1,0:T(8,128)(2,1)S(1)}, bf16[4,256,256]{2,1,0:T(8,128)(2,1)}, u32[]{:S(2)}) copy-start(bf16[4,256,256]{2,1,0:T(8,128)(2,1)} %constant.22.clone.refs_16_) | copy-start | bytes 1572868
  16.4 1.2 %collective-permute-start.5 = (f32[2,2,16,128]{3,2,1,0:T(8,128)S(1)}, f32[2,2,16,128]{3,2,1,0:T(8,128)S(1)}, u32[]{:S(2)}, u32[]{:S(2)}) collective-permute-start(f32[2,2,16,128]{3,2,1,0:T(8,128)S(1)} %get-tuple-element.19.refs_1_), channel_id=1, source_target_pairs={{0,4},{4,0},{1,5},{5,1},{2,6},{6,2},{3,7},{7,3},{8,12},{12,8},{9,1... | collective-permute-start | bytes 98312 | tf_op jit(solution)/shard_map/ppermute | solution.py:510
  17.7 22.7 %copy-start.1 = (bf16[2,336,224]{2,1,0:T(8,128)(2,1)S(1)}, bf16[2,336,224]{2,1,0:T(8,128)(2,1)}, u32[]{:S(2)}) copy-start(bf16[2,336,224]{2,1,0:T(8,128)(2,1)} %constant.21.clone.refs_15_) | copy-start | bytes 903172
  20.7 6.3 %collective-permute-start.10 = (f32[64,128]{1,0:T(8,128)S(1)}, f32[64,128]{1,0:T(8,128)S(1)}, u32[]{:S(2)}, u32[]{:S(2)}) collective-permute-start(f32[64,128]{1,0:T(8,128)S(1)} %get-tuple-element.22), channel_id=1, source_target_pairs={{0,3},{1,2},{2,1},{3,0},{4,7},{5,6},{6,5},{7,4},{8,11},{9,10},{10,... | collective-permute-start | bytes 98312 | tf_op jit(solution)/shard_map/ppermute | solution.py:510
  24.3 4.8 %collective-permute-start.9 = (f32[64,128]{1,0:T(8,128)S(1)}, f32[64,128]{1,0:T(8,128)S(1)}, u32[]{:S(2)}, u32[]{:S(2)}) collective-permute-start(f32[64,128]{1,0:T(8,128)S(1)} %get-tuple-element.22), channel_id=1, source_target_pairs={{0,2},{1,3},{2,0},{3,1},{4,6},{5,7},{6,4},{7,5},{8,10},{9,11},{10,... | collective-permute-start | bytes 98312 | tf_op jit(solution)/shard_map/ppermute | solution.py:510
  26.4 3.9 %collective-permute-start.8 = (f32[64,128]{1,0:T(8,128)S(1)}, f32[64,128]{1,0:T(8,128)S(1)}, u32[]{:S(2)}, u32[]{:S(2)}) collective-permute-start(f32[64,128]{1,0:T(8,128)S(1)} %get-tuple-element.22), channel_id=1, source_target_pairs={{0,1},{1,0},{2,3},{3,2},{4,5},{5,4},{6,7},{7,6},{8,9},{9,8},{10,11... | collective-permute-start | bytes 98312 | tf_op jit(solution)/shard_map/ppermute | solution.py:510
  30.3 10.0 %copy-start.2 = (bf16[128,256]{1,0:T(8,128)(2,1)S(1)}, bf16[128,256]{1,0:T(8,128)(2,1)}, u32[]{:S(2)}) copy-start(bf16[128,256]{1,0:T(8,128)(2,1)} %constant.26.clone.refs_20_) | copy-start | bytes 196612
  30.3 10.0 %copy-start.3 = (bf16[256,128]{1,0:T(8,128)(2,1)S(1)}, bf16[256,128]{1,0:T(8,128)(2,1)}, u32[]{:S(2)}) copy-start(bf16[256,128]{1,0:T(8,128)(2,1)} %constant.25.clone.refs_19_) | copy-start | bytes 196612
  30.3 10.0 %copy-start.4 = (bf16[256,128]{1,0:T(8,128)(2,1)S(1)}, bf16[256,128]{1,0:T(8,128)(2,1)}, u32[]{:S(2)}) copy-start(bf16[256,128]{1,0:T(8,128)(2,1)} %constant.24.clone.refs_18_) | copy-start | bytes 196612
  30.4 10.0 %copy-start.5 = (bf16[128,256]{1,0:T(8,128)(2,1)S(1)}, bf16[128,256]{1,0:T(8,128)(2,1)}, u32[]{:S(2)}) copy-start(bf16[128,256]{1,0:T(8,128)(2,1)} %constant.23.clone.refs_17_) | copy-start | bytes 196612
  30.4 7.0 %collective-permute-start.13 = (f32[4,64,128]{2,1,0:T(8,128)S(1)}, f32[4,64,128]{2,1,0:T(8,128)S(1)}, u32[]{:S(2)}, u32[]{:S(2)}) collective-permute-start(f32[4,64,128]{2,1,0:T(8,128)S(1)} %pad_maximum_fusion.1.refs_0_), channel_id=1, source_target_pairs={{0,24},{8,16},{16,8},{24,0},{1,25},{9,17},{17,9},{25,1},{2,26},{10... | collective-permute-start | bytes 393224 | tf_op jit(solution)/shard_map/ppermute | solution.py:510
  31.9 6.6 %collective-permute-start.12 = (f32[4,64,128]{2,1,0:T(8,128)S(1)}, f32[4,64,128]{2,1,0:T(8,128)S(1)}, u32[]{:S(2)}, u32[]{:S(2)}) collective-permute-start(f32[4,64,128]{2,1,0:T(8,128)S(1)} %pad_maximum_fusion.1.refs_0_), channel_id=1, source_target_pairs={{0,16},{8,24},{16,0},{24,8},{1,17},{9,25},{17,1},{25,9},{2,18},{10... | collective-permute-start | bytes 393224 | tf_op jit(solution)/shard_map/ppermute | solution.py:510
  33.8 5.2 %collective-permute-start.11 = (f32[4,64,128]{2,1,0:T(8,128)S(1)}, f32[4,64,128]{2,1,0:T(8,128)S(1)}, u32[]{:S(2)}, u32[]{:S(2)}) collective-permute-start(f32[4,64,128]{2,1,0:T(8,128)S(1)} %pad_maximum_fusion.1.refs_0_), channel_id=1, source_target_pairs={{0,8},{8,0},{16,24},{24,16},{1,9},{9,1},{17,25},{25,17},{2,10},{10... | collective-permute-start | bytes 393224 | tf_op jit(solution)/shard_map/ppermute | solution.py:510
  33.9 5.1 %collective-permute-start.14 = (f32[4,64,128]{2,1,0:T(8,128)S(1)}, f32[4,64,128]{2,1,0:T(8,128)S(1)}, u32[]{:S(2)}, u32[]{:S(2)}) collective-permute-start(f32[4,64,128]{2,1,0:T(8,128)S(1)} %pad_maximum_fusion.1.refs_0_), channel_id=1, source_target_pairs={{0,4},{4,0},{1,5},{5,1},{2,6},{6,2},{3,7},{7,3},{8,12},{12,8},{9,1... | collective-permute-start | bytes 393224 | tf_op jit(solution)/shard_map/ppermute | solution.py:510
  37.4 1.7 %collective-permute-start.17 = (f32[4,64,128]{2,1,0:T(8,128)S(1)}, f32[4,64,128]{2,1,0:T(8,128)S(1)}, u32[]{:S(2)}, u32[]{:S(2)}) collective-permute-start(f32[4,64,128]{2,1,0:T(8,128)S(1)} %collective-permute-done.13.refs_3_), channel_id=1, source_target_pairs={{0,4},{4,0},{1,5},{5,1},{2,6},{6,2},{3,7},{7,3},{8,12},{12,8},{9,1... | collective-permute-start | bytes 393224 | tf_op jit(solution)/shard_map/ppermute | solution.py:510
  38.5 1.3 %collective-permute-start.16 = (f32[4,64,128]{2,1,0:T(8,128)S(1)}, f32[4,64,128]{2,1,0:T(8,128)S(1)}, u32[]{:S(2)}, u32[]{:S(2)}) collective-permute-start(f32[4,64,128]{2,1,0:T(8,128)S(1)} %collective-permute-done.12.refs_2_), channel_id=1, source_target_pairs={{0,4},{4,0},{1,5},{5,1},{2,6},{6,2},{3,7},{7,3},{8,12},{12,8},{9,1... | collective-permute-start | bytes 393224 | tf_op jit(solution)/shard_map/ppermute | solution.py:510
  39.0 1.3 %collective-permute-start.15 = (f32[4,64,128]{2,1,0:T(8,128)S(1)}, f32[4,64,128]{2,1,0:T(8,128)S(1)}, u32[]{:S(2)}, u32[]{:S(2)}) collective-permute-start(f32[4,64,128]{2,1,0:T(8,128)S(1)} %collective-permute-done.11.refs_1_), channel_id=1, source_target_pairs={{0,4},{4,0},{1,5},{5,1},{2,6},{6,2},{3,7},{7,3},{8,12},{12,8},{9,1... | collective-permute-start | bytes 393224 | tf_op jit(solution)/shard_map/ppermute | solution.py:510
  (5 other events, 40.8 us)

commit v15 on v14

--- a/solution.py
+++ b/solution.py
@@ -253,10 +253,9 @@
 
 
 def in_blocks(start, stop, block, body, carry):
-    def step(index, carry):
-        return body(pl.ds(start + index * block, block), pl.ds(start + index * block + 1, block), carry)
-
-    lax.fori_loop(0, (stop - start) // block, step, carry)
+    blocks = (stop - start) // block if isinstance(start, int) else 1
+    for index in range(blocks):
+        carry = body(pl.ds(start + index * block, block), pl.ds(start + index * block + 1, block), carry)
 
 
 def plane_faces(coef, faces, start, stop, link_y, link_x, source, update, block=4):
@@ -634,7 +633,7 @@
     fill_window(own, got, far, source, coef, *counts)
     planes, rows, lanes = source.shape
     own_y = rows - HALO_Y
-    plane_faces(coef, faces, 0, planes, link_mask(rows, lanes), None, source, update, 16)
+    plane_faces(coef, faces, 0, planes, link_mask(rows, lanes), None, source, update, 32)
     ranges = [(2, planes - 2), (4, planes - 4)]
     plane_steps(faces, ranges, source, residual, update, estimate, True, (28, 24))
     plane_residual(faces, HALO_Z, planes - HALO_Z, residual, update, 16)
@@ -698,23 +697,21 @@
     link_y = jnp.where(row == mid_y - 1, 0.0, 1.0)
     link_x = jnp.where(lane == mid_x - 1, 0.0, 1.0)
     start, stop = PAD, PAD + mid_z
-    plane_faces(mid_coef, mid_faces, start, stop, link_y, link_x, mid_source, mid_update, 16)
+    plane_faces(mid_coef, mid_faces, start, stop, link_y, link_x, mid_source, mid_update, mid_z)
     ranges = [(start, stop)] * (DEGREE - 1)
-    plane_steps(mid_faces, ranges, mid_source, mid_residual, mid_update, mid_estimate, True, (32, 32))
+    plane_steps(mid_faces, ranges, mid_source, mid_residual, mid_update, mid_estimate, True, (mid_z, mid_z))
 
     def finish_pairs(here, own):
         before = mid_residual[here]
-        rows_here = pl.ds((here.start - PAD) // 2 * mid_y, 4 * mid_y)
 
         def store(value):
-            left = (before - value).reshape(4, 2, mid_y, mid_x)
-            residual_pairs[rows_here] = (left[:, 0] + left[:, 1]).reshape(4 * mid_y, mid_x)
-            own_coef = mid_coef[here].reshape(4, 2, mid_y, mid_x)
-            coef_pairs[rows_here] = (own_coef[:, 0] + own_coef[:, 1]).reshape(4 * mid_y, mid_x)
+            for target, whole in ((residual_pairs, before - value), (coef_pairs, mid_coef[here])):
+                whole = whole.reshape(mid_z // 2, 2, mid_y, mid_x)
+                target[...] = (whole[:, 0] + whole[:, 1]).reshape(target.shape)
 
         return store
 
-    plane_sweep(mid_faces, start, stop, mid_update, finish_pairs, 8)
+    plane_sweep(mid_faces, start, stop, mid_update, finish_pairs, mid_z)
 
     for copy in copies:
         copy.wait()
@@ -731,26 +728,16 @@
     mid_correction[pl.ds(0, 1)] = zero[:1]
     mid_correction[pl.ds(1 + mid_z // 2, 1)] = zero[:1]
 
-    def add_mid(index, carry):
-        first = carry + 4 * index
-        here, last = pl.ds(PAD + 2 * first, 8), first + 4
-        step = planes_up(
-            mid_correction[pl.ds(first + 1, 4)], mid_correction[pl.ds(first, 1)], mid_correction[pl.ds(last + 1, 1)]
-        )
-        mid_estimate[here] = mid_estimate[here] + step
-        return carry
-
-    def clipped(margin):
-        low = jnp.maximum(z_index * 8 - margin, 0)
-        high = jnp.minimum(z_index * 8 + 8 + margin, mid_z)
-        return PAD + low, PAD + high
-
     def about(count):
         low = PAD + jnp.clip(z_index * 8 + 4 - count // 2, 0, mid_z - count)
         return low, low + count
 
-    low, high = clipped(8)
-    lax.fori_loop(0, (high - low) // 8, add_mid, (low - PAD) // 2)
+    low = about(24)[0]
+    first = (low - PAD) // 2
+    step = planes_up(
+        mid_correction[pl.ds(first + 1, 12)], mid_correction[pl.ds(first, 1)], mid_correction[pl.ds(first + 13, 1)]
+    )
+    mid_estimate[pl.ds(low, 24)] = mid_estimate[pl.ds(low, 24)] + step
     plane_restart(mid_faces, *about(24), mid_source, mid_residual, mid_update, mid_estimate, 24)
     plane_steps(
         mid_faces, [about(16), about(16)], mid_source, mid_residual, mid_update, mid_estimate, False, (16, 16)

time: 50.6 us -> 50.6 us (level)
  no operation moved by 1% of the time
where the time goes in v15:
time: 50.6 us; the launch traced here: 50.4 us
  starting transfers between devices  19.2 us (38%)
  waiting for transfers between devices  15.5 us (31%)
  Pallas kernels  14.9 us (29%)
  between operations  0.8 us (2%)
    ppermute x18, starting transfers between devices, swapped(): lax.ppermute(value, axes, [(int(source), int(target)) for source, target...  19.2 us
    ppermute x18, waiting for transfers between devices, swapped(): lax.ppermute(value, axes, [(int(source), int(target)) for source, target...  15.5 us
    pallas_call x4, Pallas kernels, call(): pl.pallas_call(kernel, out_shape=tuple((jax.ShapeDtypeStruct(shape, F32)...  14.9 us
  transfers between devices with their start and end apart: 18, of which 10 were waited for; matrix products, arithmetic and copies ran while one was open for 0% of the time, Pallas kernels for 0%

profile of v15, /device:TPU:0, one launch (start us, length us, event | category | flops | bytes accessed | tf_op | source)
XLA Modules:
  0.0 50.4 jit_solution(18161889849463967655)
XLA Ops:
  0.6 1.9 %start.1 = (f32[2,16,128]{2,1,0:T(8,128)}, f32[2,16,128]{2,1,0:T(8,128)}) custom-call(f32[16,16,128]{2,1,0:T(8,128)} %bitcast.10, f32[16,16,128]{2,1,0:T(8,128)} %coef.1), custom_call_target="tpu_custom_call" | custom-call | tf_op jit(solution)/shard_map/start/pallas_call | solution.py:777
  2.5 1.4 %collective-permute-start = (f32[2,16,128]{2,1,0:T(8,128)}, f32[2,16,128]{2,1,0:T(8,128)S(1)}, u32[]{:S(2)}, u32[]{:S(2)}) collective-permute-start(f32[2,16,128]{2,1,0:T(8,128)} %get-tuple-element.17), channel_id=1, source_target_pairs={{0,0},{8,16},{16,8},{24,24},{1,1},{9,17},{17,9},{25,25},{2,2},{10,... | collective-permute-start | bytes 49160 | tf_op jit(solution)/shard_map/ppermute | solution.py:509
  3.9 5.0 %collective-permute-start.1 = (f32[2,16,128]{2,1,0:T(8,128)}, f32[2,16,128]{2,1,0:T(8,128)S(1)}, u32[]{:S(2)}, u32[]{:S(2)}) collective-permute-start(f32[2,16,128]{2,1,0:T(8,128)} %get-tuple-element.18), channel_id=1, source_target_pairs={{0,8},{8,0},{16,24},{24,16},{1,9},{9,1},{17,25},{25,17},{2,10},{10... | collective-permute-start | bytes 49160 | tf_op jit(solution)/shard_map/ppermute | solution.py:509
  9.1 1.9 %collective-permute-done.1.x_a = f32[2,16,128]{2,1,0:T(8,128)S(1)} collective-permute-done((f32[2,16,128]{2,1,0:T(8,128)}, f32[2,16,128]{2,1,0:T(8,128)S(1)}, u32[]{:S(2)}, u32[]{:S(2)}) %collective-permute-start.1) | collective-permute-done | bytes 16416 | tf_op jit(solution)/shard_map/ppermute | solution.py:509
  11.0 1.6 %collective-permute-start.2 = (f32[15,16,128]{2,1,0:T(8,128)S(1)}, f32[15,16,128]{2,1,0:T(8,128)S(1)}, u32[]{:S(2)}, u32[]{:S(2)}) collective-permute-start(f32[15,16,128]{2,1,0:T(8,128)S(1)} %get-tuple-element.20), channel_id=1, source_target_pairs={{0,1},{1,0},{2,3},{3,2},{4,5},{5,4},{6,7},{7,6},{8,9},{9,8},{10,11... | collective-permute-start | bytes 368648 | tf_op jit(solution)/shard_map/ppermute | solution.py:509
  12.6 0.7 %collective-permute-start.3 = (f32[15,16,128]{2,1,0:T(8,128)S(1)}, f32[15,16,128]{2,1,0:T(8,128)S(1)}, u32[]{:S(2)}, u32[]{:S(2)}) collective-permute-start(f32[15,16,128]{2,1,0:T(8,128)S(1)} %get-tuple-element.21), channel_id=1, source_target_pairs={{0,0},{1,2},{2,1},{3,3},{4,4},{5,6},{6,5},{7,7},{8,8},{9,10},{10,9... | collective-permute-start | bytes 368648 | tf_op jit(solution)/shard_map/ppermute | solution.py:509
  13.3 2.6 %collective-permute-done.2.refs_2_ = f32[15,16,128]{2,1,0:T(8,128)S(1)} collective-permute-done((f32[15,16,128]{2,1,0:T(8,128)S(1)}, f32[15,16,128]{2,1,0:T(8,128)S(1)}, u32[]{:S(2)}, u32[]{:S(2)}) %collective-permute-start.2) | collective-permute-done | bytes 122912 | tf_op jit(solution)/shard_map/ppermute | solution.py:509
  15.9 0.5 %collective-permute-start.7 = (f32[15,16,128]{2,1,0:T(8,128)S(1)}, f32[15,16,128]{2,1,0:T(8,128)S(1)}, u32[]{:S(2)}, u32[]{:S(2)}) collective-permute-start(f32[15,16,128]{2,1,0:T(8,128)S(1)} %collective-permute-done.3.refs_3_), channel_id=1, source_target_pairs={{0,4},{4,0},{1,5},{5,1},{2,6},{6,2},{3,7},{7,3},{8,12},{12,8},{9,1... | collective-permute-start | bytes 368648 | tf_op jit(solution)/shard_map/ppermute | solution.py:509
  16.5 1.1 %collective-permute-done.5.refs_5_ = f32[2,2,16,128]{3,2,1,0:T(8,128)S(1)} collective-permute-done((f32[2,2,16,128]{3,2,1,0:T(8,128)S(1)}, f32[2,2,16,128]{3,2,1,0:T(8,128)S(1)}, u32[]{:S(2)}, u32[]{:S(2)}) %collective-permute-start.5) | collective-permute-done | bytes 32800 | tf_op jit(solution)/shard_map/ppermute | solution.py:509
  17.7 3.1 %first.1 = (f32[64,128]{1,0:T(8,128)S(1)}, f32[32,24,256]{2,1,0:T(8,128)S(1)}, f32[32,24,256]{2,1,0:T(8,128)S(1)}, f32[32,24,256]{2,1,0:T(8,128)S(1)}, f32[32,24...) custom-call(f32[2,16,16,128]{3,2,1,0:T(8,128)S(1)} %pad_maximum_fusion., ...), custom_call_target="tpu_custom_call" | custom-call | tf_op jit(solution)/shard_map/first/pallas_call | solution.py:777
  20.8 3.6 %collective-permute-start.10 = (f32[64,128]{1,0:T(8,128)S(1)}, f32[64,128]{1,0:T(8,128)S(1)}, u32[]{:S(2)}, u32[]{:S(2)}) collective-permute-start(f32[64,128]{1,0:T(8,128)S(1)} %get-tuple-element.22), channel_id=1, source_target_pairs={{0,3},{1,2},{2,1},{3,0},{4,7},{5,6},{6,5},{7,4},{8,11},{9,10},{10,... | collective-permute-start | bytes 98312 | tf_op jit(solution)/shard_map/ppermute | solution.py:509
  24.4 2.1 %collective-permute-start.9 = (f32[64,128]{1,0:T(8,128)S(1)}, f32[64,128]{1,0:T(8,128)S(1)}, u32[]{:S(2)}, u32[]{:S(2)}) collective-permute-start(f32[64,128]{1,0:T(8,128)S(1)} %get-tuple-element.22), channel_id=1, source_target_pairs={{0,2},{1,3},{2,0},{3,1},{4,6},{5,7},{6,4},{7,5},{8,10},{9,11},{10,... | collective-permute-start | bytes 98312 | tf_op jit(solution)/shard_map/ppermute | solution.py:509
  26.6 0.5 %collective-permute-start.8 = (f32[64,128]{1,0:T(8,128)S(1)}, f32[64,128]{1,0:T(8,128)S(1)}, u32[]{:S(2)}, u32[]{:S(2)}) collective-permute-start(f32[64,128]{1,0:T(8,128)S(1)} %get-tuple-element.22), channel_id=1, source_target_pairs={{0,1},{1,0},{2,3},{3,2},{4,5},{5,4},{6,7},{7,6},{8,9},{9,8},{10,11... | collective-permute-start | bytes 98312 | tf_op jit(solution)/shard_map/ppermute | solution.py:509
  27.1 2.1 %collective-permute-done.9 = f32[64,128]{1,0:T(8,128)S(1)} collective-permute-done((f32[64,128]{1,0:T(8,128)S(1)}, f32[64,128]{1,0:T(8,128)S(1)}, u32[]{:S(2)}, u32[]{:S(2)}) %collective-permute-start.9) | collective-permute-done | bytes 32800 | tf_op jit(solution)/shard_map/ppermute | solution.py:509
  29.2 1.2 %collective-permute-done.8 = f32[64,128]{1,0:T(8,128)S(1)} collective-permute-done((f32[64,128]{1,0:T(8,128)S(1)}, f32[64,128]{1,0:T(8,128)S(1)}, u32[]{:S(2)}, u32[]{:S(2)}) %collective-permute-start.8) | collective-permute-done | bytes 32800 | tf_op jit(solution)/shard_map/ppermute | solution.py:509
  30.5 1.5 %collective-permute-start.13 = (f32[4,64,128]{2,1,0:T(8,128)S(1)}, f32[4,64,128]{2,1,0:T(8,128)S(1)}, u32[]{:S(2)}, u32[]{:S(2)}) collective-permute-start(f32[4,64,128]{2,1,0:T(8,128)S(1)} %pad_maximum_fusion.1.refs_0_), channel_id=1, source_target_pairs={{0,24},{8,16},{16,8},{24,0},{1,25},{9,17},{17,9},{25,1},{2,26},{10... | collective-permute-start | bytes 393224 | tf_op jit(solution)/shard_map/ppermute | solution.py:509
  32.0 2.0 %collective-permute-start.12 = (f32[4,64,128]{2,1,0:T(8,128)S(1)}, f32[4,64,128]{2,1,0:T(8,128)S(1)}, u32[]{:S(2)}, u32[]{:S(2)}) collective-permute-start(f32[4,64,128]{2,1,0:T(8,128)S(1)} %pad_maximum_fusion.1.refs_0_), channel_id=1, source_target_pairs={{0,16},{8,24},{16,0},{24,8},{1,17},{9,25},{17,1},{25,9},{2,18},{10... | collective-permute-start | bytes 393224 | tf_op jit(solution)/shard_map/ppermute | solution.py:509
  34.0 0.1 collective-permute-start.11
  34.1 3.4 %collective-permute-done.13.refs_3_ = f32[4,64,128]{2,1,0:T(8,128)S(1)} collective-permute-done((f32[4,64,128]{2,1,0:T(8,128)S(1)}, f32[4,64,128]{2,1,0:T(8,128)S(1)}, u32[]{:S(2)}, u32[]{:S(2)}) %collective-permute-start.13) | collective-permute-done | bytes 131104 | tf_op jit(solution)/shard_map/ppermute | solution.py:509
  37.5 1.1 %collective-permute-done.12.refs_2_ = f32[4,64,128]{2,1,0:T(8,128)S(1)} collective-permute-done((f32[4,64,128]{2,1,0:T(8,128)S(1)}, f32[4,64,128]{2,1,0:T(8,128)S(1)}, u32[]{:S(2)}, u32[]{:S(2)}) %collective-permute-start.12) | collective-permute-done | bytes 131104 | tf_op jit(solution)/shard_map/ppermute | solution.py:509
  38.6 0.5 %collective-permute-done.11.refs_1_ = f32[4,64,128]{2,1,0:T(8,128)S(1)} collective-permute-done((f32[4,64,128]{2,1,0:T(8,128)S(1)}, f32[4,64,128]{2,1,0:T(8,128)S(1)}, u32[]{:S(2)}, u32[]{:S(2)}) %collective-permute-start.11) | collective-permute-done | bytes 131104 | tf_op jit(solution)/shard_map/ppermute | solution.py:509
  39.1 0.8 %collective-permute-done.16.refs_6_ = f32[4,64,128]{2,1,0:T(8,128)S(1)} collective-permute-done((f32[4,64,128]{2,1,0:T(8,128)S(1)}, f32[4,64,128]{2,1,0:T(8,128)S(1)}, u32[]{:S(2)}, u32[]{:S(2)}) %collective-permute-start.16) | collective-permute-done | bytes 131104 | tf_op jit(solution)/shard_map/ppermute | solution.py:509
  39.9 0.5 %collective-permute-done.15.refs_5_ = f32[4,64,128]{2,1,0:T(8,128)S(1)} collective-permute-done((f32[4,64,128]{2,1,0:T(8,128)S(1)}, f32[4,64,128]{2,1,0:T(8,128)S(1)}, u32[]{:S(2)}, u32[]{:S(2)}) %collective-permute-start.15) | collective-permute-done | bytes 131104 | tf_op jit(solution)/shard_map/ppermute | solution.py:509
  40.5 9.8 %second.1 = (f32[16,16,128]{2,1,0:T(8,128)}, f32[16,16,128]{2,1,0:T(8,128)}) custom-call(f32[4,64,128]{2,1,0:T(8,128)S(1)} %pad_maximum_fusion.1.refs_0_, f32[4,64,128]{2,1,0:T(8,128)S(1)} %collective-permute-done.11.refs_1_, f32[4,64,128]{2,1,0:T(8,128)S(1)} %collective-permute-done.12.refs_2_, f32[4,64,128]{2,1,0:T(8,128)S(1)} %collective-permute-done.13.refs_3_, ...), custom_call_target="tpu_custom_call" | custom-call | tf_op jit(solution)/shard_map/second/pallas_call | solution.py:777
  (40 shorter events, 0.3 us)
Async XLA Ops:
  2.5 6.5 %collective-permute-start = (f32[2,16,128]{2,1,0:T(8,128)}, f32[2,16,128]{2,1,0:T(8,128)S(1)}, u32[]{:S(2)}, u32[]{:S(2)}) collective-permute-start(f32[2,16,128]{2,1,0:T(8,128)} %get-tuple-element.17), channel_id=1, source_target_pairs={{0,0},{8,16},{16,8},{24,24},{1,1},{9,17},{17,9},{25,25},{2,2},{10,... | collective-permute-start | bytes 49160 | tf_op jit(solution)/shard_map/ppermute | solution.py:509
  3.9 7.0 %collective-permute-start.1 = (f32[2,16,128]{2,1,0:T(8,128)}, f32[2,16,128]{2,1,0:T(8,128)S(1)}, u32[]{:S(2)}, u32[]{:S(2)}) collective-permute-start(f32[2,16,128]{2,1,0:T(8,128)} %get-tuple-element.18), channel_id=1, source_target_pairs={{0,8},{8,0},{16,24},{24,16},{1,9},{9,1},{17,25},{25,17},{2,10},{10... | collective-permute-start | bytes 49160 | tf_op jit(solution)/shard_map/ppermute | solution.py:509
  9.0 8.7 %collective-permute-start.4 = (f32[2,16,16,128]{3,2,1,0:T(8,128)S(1)}, f32[2,16,16,128]{3,2,1,0:T(8,128)S(1)}, u32[]{:S(2)}, u32[]{:S(2)}) collective-permute-start(f32[2,16,16,128]{3,2,1,0:T(8,128)S(1)} %pad_maximum_fusion.own.refs_0_), channel_id=1, source_target_pairs={{0,4},{4,0},{1,5},{5,1},{2,6},{6,2},{3,7},{7,3},{8,12},{12,8},{9,1... | collective-permute-start | bytes 786440 | tf_op jit(solution)/shard_map/ppermute | solution.py:509
  11.0 4.9 %collective-permute-start.2 = (f32[15,16,128]{2,1,0:T(8,128)S(1)}, f32[15,16,128]{2,1,0:T(8,128)S(1)}, u32[]{:S(2)}, u32[]{:S(2)}) collective-permute-start(f32[15,16,128]{2,1,0:T(8,128)S(1)} %get-tuple-element.20), channel_id=1, source_target_pairs={{0,1},{1,0},{2,3},{3,2},{4,5},{5,4},{6,7},{7,6},{8,9},{9,8},{10,11... | collective-permute-start | bytes 368648 | tf_op jit(solution)/shard_map/ppermute | solution.py:509
  12.6 3.3 %collective-permute-start.3 = (f32[15,16,128]{2,1,0:T(8,128)S(1)}, f32[15,16,128]{2,1,0:T(8,128)S(1)}, u32[]{:S(2)}, u32[]{:S(2)}) collective-permute-start(f32[15,16,128]{2,1,0:T(8,128)S(1)} %get-tuple-element.21), channel_id=1, source_target_pairs={{0,0},{1,2},{2,1},{3,3},{4,4},{5,6},{6,5},{7,7},{8,8},{9,10},{10,9... | collective-permute-start | bytes 368648 | tf_op jit(solution)/shard_map/ppermute | solution.py:509
  15.9 1.7 %collective-permute-start.6 = (f32[15,16,128]{2,1,0:T(8,128)S(1)}, f32[15,16,128]{2,1,0:T(8,128)S(1)}, u32[]{:S(2)}, u32[]{:S(2)}) collective-permute-start(f32[15,16,128]{2,1,0:T(8,128)S(1)} %collective-permute-done.2.refs_2_), channel_id=1, source_target_pairs={{0,4},{4,0},{1,5},{5,1},{2,6},{6,2},{3,7},{7,3},{8,12},{12,8},{9,1... | collective-permute-start | bytes 368648 | tf_op jit(solution)/shard_map/ppermute | solution.py:509
  15.9 1.7 %collective-permute-start.7 = (f32[15,16,128]{2,1,0:T(8,128)S(1)}, f32[15,16,128]{2,1,0:T(8,128)S(1)}, u32[]{:S(2)}, u32[]{:S(2)}) collective-permute-start(f32[15,16,128]{2,1,0:T(8,128)S(1)} %collective-permute-done.3.refs_3_), channel_id=1, source_target_pairs={{0,4},{4,0},{1,5},{5,1},{2,6},{6,2},{3,7},{7,3},{8,12},{12,8},{9,1... | collective-permute-start | bytes 368648 | tf_op jit(solution)/shard_map/ppermute | solution.py:509
  16.4 24.0 %copy-start = (bf16[4,256,256]{2,1,0:T(8,128)(2,1)S(1)}, bf16[4,256,256]{2,1,0:T(8,128)(2,1)}, u32[]{:S(2)}) copy-start(bf16[4,256,256]{2,1,0:T(8,128)(2,1)} %constant.22.clone.refs_16_) | copy-start | bytes 1572868
  16.4 1.2 %collective-permute-start.5 = (f32[2,2,16,128]{3,2,1,0:T(8,128)S(1)}, f32[2,2,16,128]{3,2,1,0:T(8,128)S(1)}, u32[]{:S(2)}, u32[]{:S(2)}) collective-permute-start(f32[2,2,16,128]{3,2,1,0:T(8,128)S(1)} %get-tuple-element.19.refs_1_), channel_id=1, source_target_pairs={{0,4},{4,0},{1,5},{5,1},{2,6},{6,2},{3,7},{7,3},{8,12},{12,8},{9,1... | collective-permute-start | bytes 98312 | tf_op jit(solution)/shard_map/ppermute | solution.py:509
  17.7 22.8 %copy-start.1 = (bf16[2,336,224]{2,1,0:T(8,128)(2,1)S(1)}, bf16[2,336,224]{2,1,0:T(8,128)(2,1)}, u32[]{:S(2)}) copy-start(bf16[2,336,224]{2,1,0:T(8,128)(2,1)} %constant.21.clone.refs_15_) | copy-start | bytes 903172
  20.8 6.3 %collective-permute-start.10 = (f32[64,128]{1,0:T(8,128)S(1)}, f32[64,128]{1,0:T(8,128)S(1)}, u32[]{:S(2)}, u32[]{:S(2)}) collective-permute-start(f32[64,128]{1,0:T(8,128)S(1)} %get-tuple-element.22), channel_id=1, source_target_pairs={{0,3},{1,2},{2,1},{3,0},{4,7},{5,6},{6,5},{7,4},{8,11},{9,10},{10,... | collective-permute-start | bytes 98312 | tf_op jit(solution)/shard_map/ppermute | solution.py:509
  24.4 4.8 %collective-permute-start.9 = (f32[64,128]{1,0:T(8,128)S(1)}, f32[64,128]{1,0:T(8,128)S(1)}, u32[]{:S(2)}, u32[]{:S(2)}) collective-permute-start(f32[64,128]{1,0:T(8,128)S(1)} %get-tuple-element.22), channel_id=1, source_target_pairs={{0,2},{1,3},{2,0},{3,1},{4,6},{5,7},{6,4},{7,5},{8,10},{9,11},{10,... | collective-permute-start | bytes 98312 | tf_op jit(solution)/shard_map/ppermute | solution.py:509
  26.6 3.9 %collective-permute-start.8 = (f32[64,128]{1,0:T(8,128)S(1)}, f32[64,128]{1,0:T(8,128)S(1)}, u32[]{:S(2)}, u32[]{:S(2)}) collective-permute-start(f32[64,128]{1,0:T(8,128)S(1)} %get-tuple-element.22), channel_id=1, source_target_pairs={{0,1},{1,0},{2,3},{3,2},{4,5},{5,4},{6,7},{7,6},{8,9},{9,8},{10,11... | collective-permute-start | bytes 98312 | tf_op jit(solution)/shard_map/ppermute | solution.py:509
  30.5 10.0 %copy-start.2 = (bf16[128,256]{1,0:T(8,128)(2,1)S(1)}, bf16[128,256]{1,0:T(8,128)(2,1)}, u32[]{:S(2)}) copy-start(bf16[128,256]{1,0:T(8,128)(2,1)} %constant.26.clone.refs_20_) | copy-start | bytes 196612
  30.5 10.0 %copy-start.3 = (bf16[256,128]{1,0:T(8,128)(2,1)S(1)}, bf16[256,128]{1,0:T(8,128)(2,1)}, u32[]{:S(2)}) copy-start(bf16[256,128]{1,0:T(8,128)(2,1)} %constant.25.clone.refs_19_) | copy-start | bytes 196612
  30.5 10.0 %copy-start.4 = (bf16[256,128]{1,0:T(8,128)(2,1)S(1)}, bf16[256,128]{1,0:T(8,128)(2,1)}, u32[]{:S(2)}) copy-start(bf16[256,128]{1,0:T(8,128)(2,1)} %constant.24.clone.refs_18_) | copy-start | bytes 196612
  30.5 10.0 %copy-start.5 = (bf16[128,256]{1,0:T(8,128)(2,1)S(1)}, bf16[128,256]{1,0:T(8,128)(2,1)}, u32[]{:S(2)}) copy-start(bf16[128,256]{1,0:T(8,128)(2,1)} %constant.23.clone.refs_17_) | copy-start | bytes 196612
  30.5 7.0 %collective-permute-start.13 = (f32[4,64,128]{2,1,0:T(8,128)S(1)}, f32[4,64,128]{2,1,0:T(8,128)S(1)}, u32[]{:S(2)}, u32[]{:S(2)}) collective-permute-start(f32[4,64,128]{2,1,0:T(8,128)S(1)} %pad_maximum_fusion.1.refs_0_), channel_id=1, source_target_pairs={{0,24},{8,16},{16,8},{24,0},{1,25},{9,17},{17,9},{25,1},{2,26},{10... | collective-permute-start | bytes 393224 | tf_op jit(solution)/shard_map/ppermute | solution.py:509
  32.0 6.6 %collective-permute-start.12 = (f32[4,64,128]{2,1,0:T(8,128)S(1)}, f32[4,64,128]{2,1,0:T(8,128)S(1)}, u32[]{:S(2)}, u32[]{:S(2)}) collective-permute-start(f32[4,64,128]{2,1,0:T(8,128)S(1)} %pad_maximum_fusion.1.refs_0_), channel_id=1, source_target_pairs={{0,16},{8,24},{16,0},{24,8},{1,17},{9,25},{17,1},{25,9},{2,18},{10... | collective-permute-start | bytes 393224 | tf_op jit(solution)/shard_map/ppermute | solution.py:509
  34.0 5.2 %collective-permute-start.11 = (f32[4,64,128]{2,1,0:T(8,128)S(1)}, f32[4,64,128]{2,1,0:T(8,128)S(1)}, u32[]{:S(2)}, u32[]{:S(2)}) collective-permute-start(f32[4,64,128]{2,1,0:T(8,128)S(1)} %pad_maximum_fusion.1.refs_0_), channel_id=1, source_target_pairs={{0,8},{8,0},{16,24},{24,16},{1,9},{9,1},{17,25},{25,17},{2,10},{10... | collective-permute-start | bytes 393224 | tf_op jit(solution)/shard_map/ppermute | solution.py:509
  34.1 5.1 %collective-permute-start.14 = (f32[4,64,128]{2,1,0:T(8,128)S(1)}, f32[4,64,128]{2,1,0:T(8,128)S(1)}, u32[]{:S(2)}, u32[]{:S(2)}) collective-permute-start(f32[4,64,128]{2,1,0:T(8,128)S(1)} %pad_maximum_fusion.1.refs_0_), channel_id=1, source_target_pairs={{0,4},{4,0},{1,5},{5,1},{2,6},{6,2},{3,7},{7,3},{8,12},{12,8},{9,1... | collective-permute-start | bytes 393224 | tf_op jit(solution)/shard_map/ppermute | solution.py:509
  37.5 1.7 %collective-permute-start.17 = (f32[4,64,128]{2,1,0:T(8,128)S(1)}, f32[4,64,128]{2,1,0:T(8,128)S(1)}, u32[]{:S(2)}, u32[]{:S(2)}) collective-permute-start(f32[4,64,128]{2,1,0:T(8,128)S(1)} %collective-permute-done.13.refs_3_), channel_id=1, source_target_pairs={{0,4},{4,0},{1,5},{5,1},{2,6},{6,2},{3,7},{7,3},{8,12},{12,8},{9,1... | collective-permute-start | bytes 393224 | tf_op jit(solution)/shard_map/ppermute | solution.py:509
  38.6 1.3 %collective-permute-start.16 = (f32[4,64,128]{2,1,0:T(8,128)S(1)}, f32[4,64,128]{2,1,0:T(8,128)S(1)}, u32[]{:S(2)}, u32[]{:S(2)}) collective-permute-start(f32[4,64,128]{2,1,0:T(8,128)S(1)} %collective-permute-done.12.refs_2_), channel_id=1, source_target_pairs={{0,4},{4,0},{1,5},{5,1},{2,6},{6,2},{3,7},{7,3},{8,12},{12,8},{9,1... | collective-permute-start | bytes 393224 | tf_op jit(solution)/shard_map/ppermute | solution.py:509
  39.1 1.3 %collective-permute-start.15 = (f32[4,64,128]{2,1,0:T(8,128)S(1)}, f32[4,64,128]{2,1,0:T(8,128)S(1)}, u32[]{:S(2)}, u32[]{:S(2)}) collective-permute-start(f32[4,64,128]{2,1,0:T(8,128)S(1)} %collective-permute-done.11.refs_1_), channel_id=1, source_target_pairs={{0,4},{4,0},{1,5},{5,1},{2,6},{6,2},{3,7},{7,3},{8,12},{12,8},{9,1... | collective-permute-start | bytes 393224 | tf_op jit(solution)/shard_map/ppermute | solution.py:509
  (5 other events, 40.8 us)

commit v16 on v15

--- a/solution.py
+++ b/solution.py
@@ -633,9 +633,9 @@
     fill_window(own, got, far, source, coef, *counts)
     planes, rows, lanes = source.shape
     own_y = rows - HALO_Y
-    plane_faces(coef, faces, 0, planes, link_mask(rows, lanes), None, source, update, 32)
-    ranges = [(2, planes - 2), (4, planes - 4)]
-    plane_steps(faces, ranges, source, residual, update, estimate, True, (28, 24))
+    plane_faces(coef, faces, 2, planes - 2, link_mask(rows, lanes), None, source, update, planes // 2 - 2)
+    ranges = [(3, planes - 3), (4, planes - 4)]
+    plane_steps(faces, ranges, source, residual, update, estimate, True, (planes - 6, planes - 8))
     plane_residual(faces, HALO_Z, planes - HALO_Z, residual, update, 16)
     for pair in range((planes - 2 * HALO_Z) // 2):
         low = HALO_Z + 2 * pair
@@ -697,7 +697,7 @@
     link_y = jnp.where(row == mid_y - 1, 0.0, 1.0)
     link_x = jnp.where(lane == mid_x - 1, 0.0, 1.0)
     start, stop = PAD, PAD + mid_z
-    plane_faces(mid_coef, mid_faces, start, stop, link_y, link_x, mid_source, mid_update, mid_z)
+    plane_faces(mid_coef, mid_faces, start, stop, link_y, link_x, mid_source, mid_update, mid_z // 2)
     ranges = [(start, stop)] * (DEGREE - 1)
     plane_steps(mid_faces, ranges, mid_source, mid_residual, mid_update, mid_estimate, True, (mid_z, mid_z))
 
@@ -732,15 +732,15 @@
         low = PAD + jnp.clip(z_index * 8 + 4 - count // 2, 0, mid_z - count)
         return low, low + count
 
-    low = about(24)[0]
+    low = about(20)[0]
     first = (low - PAD) // 2
     step = planes_up(
-        mid_correction[pl.ds(first + 1, 12)], mid_correction[pl.ds(first, 1)], mid_correction[pl.ds(first + 13, 1)]
-    )
-    mid_estimate[pl.ds(low, 24)] = mid_estimate[pl.ds(low, 24)] + step
-    plane_restart(mid_faces, *about(24), mid_source, mid_residual, mid_update, mid_estimate, 24)
+        mid_correction[pl.ds(first + 1, 10)], mid_correction[pl.ds(first, 1)], mid_correction[pl.ds(first + 11, 1)]
+    )
+    mid_estimate[pl.ds(low, 20)] = mid_estimate[pl.ds(low, 20)] + step
+    plane_restart(mid_faces, *about(18), mid_source, mid_residual, mid_update, mid_estimate, 18)
     plane_steps(
-        mid_faces, [about(16), about(16)], mid_source, mid_residual, mid_update, mid_estimate, False, (16, 16)
+        mid_faces, [about(16), about(14)], mid_source, mid_residual, mid_update, mid_estimate, False, (16, 14)
     )
 
     coarse_planes = up_left.shape[1] // mid_y
@@ -753,11 +753,9 @@
         here = pl.ds(2 * first + HALO_Z - 2 * PAD, 8)
         step = planes_up(wide[pl.ds(first, 4)], wide[pl.ds(first - 1, 1)], wide[pl.ds(first + 4, 1)])
         current[here] = estimate[here] + jnp.where(inverse[here] > 0.0, step, 0.0)
-    for plane in (HALO_Z - 5, planes - HALO_Z + 4):
-        current[plane] = estimate[plane]
-    plane_restart(faces, HALO_Z - 4, planes - HALO_Z + 4, source, residual, update, current, 24)
-    ranges = [(HALO_Z - 2, planes - HALO_Z + 2)] * 2
-    plane_steps(faces, ranges, source, residual, update, current, False, (20, 20))
+    plane_restart(faces, HALO_Z - 3, planes - HALO_Z + 3, source, residual, update, current, 22)
+    ranges = [(HALO_Z - 2, planes - HALO_Z + 2), (HALO_Z - 1, planes - HALO_Z + 1)]
+    plane_steps(faces, ranges, source, residual, update, current, False, (20, 18))
     plane_residual(faces, HALO_Z, planes - HALO_Z, residual, update, 16)
     own_planes = pl.ds(HALO_Z, planes - 2 * HALO_Z)
     residual_out[...] = residual[own_planes, :own_y, :128]

time: 50.6 us -> 50.2 us (level)
  no operation moved by 1% of the time
where the time goes in v16:
time: 50.2 us; the launch traced here: 50 us
  starting transfers between devices  19.2 us (38%)
  waiting for transfers between devices  15.5 us (31%)
  Pallas kernels  14.5 us (29%)
  between operations  0.8 us (2%)
    ppermute x18, starting transfers between devices, swapped(): lax.ppermute(value, axes, [(int(source), int(target)) for source, target...  19.2 us
    ppermute x18, waiting for transfers between devices, swapped(): lax.ppermute(value, axes, [(int(source), int(target)) for source, target...  15.5 us
    pallas_call x4, Pallas kernels, call(): pl.pallas_call(kernel, out_shape=tuple((jax.ShapeDtypeStruct(shape, F32)...  14.5 us
  transfers between devices with their start and end apart: 18, of which 10 were waited for; matrix products, arithmetic and copies ran while one was open for 0% of the time, Pallas kernels for 0%

profile of v16, /device:TPU:0, one launch (start us, length us, event | category | flops | bytes accessed | tf_op | source)
XLA Modules:
  0.0 50.0 jit_solution(3317250540878243523)
XLA Ops:
  0.6 1.9 %start.1 = (f32[2,16,128]{2,1,0:T(8,128)}, f32[2,16,128]{2,1,0:T(8,128)}) custom-call(f32[16,16,128]{2,1,0:T(8,128)} %bitcast.10, f32[16,16,128]{2,1,0:T(8,128)} %coef.1), custom_call_target="tpu_custom_call" | custom-call | tf_op jit(solution)/shard_map/start/pallas_call | solution.py:775
  2.5 1.4 %collective-permute-start = (f32[2,16,128]{2,1,0:T(8,128)}, f32[2,16,128]{2,1,0:T(8,128)S(1)}, u32[]{:S(2)}, u32[]{:S(2)}) collective-permute-start(f32[2,16,128]{2,1,0:T(8,128)} %get-tuple-element.17), channel_id=1, source_target_pairs={{0,0},{8,16},{16,8},{24,24},{1,1},{9,17},{17,9},{25,25},{2,2},{10,... | collective-permute-start | bytes 49160 | tf_op jit(solution)/shard_map/ppermute | solution.py:509
  3.9 5.0 %collective-permute-start.1 = (f32[2,16,128]{2,1,0:T(8,128)}, f32[2,16,128]{2,1,0:T(8,128)S(1)}, u32[]{:S(2)}, u32[]{:S(2)}) collective-permute-start(f32[2,16,128]{2,1,0:T(8,128)} %get-tuple-element.18), channel_id=1, source_target_pairs={{0,8},{8,0},{16,24},{24,16},{1,9},{9,1},{17,25},{25,17},{2,10},{10... | collective-permute-start | bytes 49160 | tf_op jit(solution)/shard_map/ppermute | solution.py:509
  9.1 1.9 %collective-permute-done.1.x_a = f32[2,16,128]{2,1,0:T(8,128)S(1)} collective-permute-done((f32[2,16,128]{2,1,0:T(8,128)}, f32[2,16,128]{2,1,0:T(8,128)S(1)}, u32[]{:S(2)}, u32[]{:S(2)}) %collective-permute-start.1) | collective-permute-done | bytes 16416 | tf_op jit(solution)/shard_map/ppermute | solution.py:509
  11.0 1.6 %collective-permute-start.2 = (f32[15,16,128]{2,1,0:T(8,128)S(1)}, f32[15,16,128]{2,1,0:T(8,128)S(1)}, u32[]{:S(2)}, u32[]{:S(2)}) collective-permute-start(f32[15,16,128]{2,1,0:T(8,128)S(1)} %get-tuple-element.20), channel_id=1, source_target_pairs={{0,1},{1,0},{2,3},{3,2},{4,5},{5,4},{6,7},{7,6},{8,9},{9,8},{10,11... | collective-permute-start | bytes 368648 | tf_op jit(solution)/shard_map/ppermute | solution.py:509
  12.6 0.7 %collective-permute-start.3 = (f32[15,16,128]{2,1,0:T(8,128)S(1)}, f32[15,16,128]{2,1,0:T(8,128)S(1)}, u32[]{:S(2)}, u32[]{:S(2)}) collective-permute-start(f32[15,16,128]{2,1,0:T(8,128)S(1)} %get-tuple-element.21), channel_id=1, source_target_pairs={{0,0},{1,2},{2,1},{3,3},{4,4},{5,6},{6,5},{7,7},{8,8},{9,10},{10,9... | collective-permute-start | bytes 368648 | tf_op jit(solution)/shard_map/ppermute | solution.py:509
  13.3 2.6 %collective-permute-done.2.refs_2_ = f32[15,16,128]{2,1,0:T(8,128)S(1)} collective-permute-done((f32[15,16,128]{2,1,0:T(8,128)S(1)}, f32[15,16,128]{2,1,0:T(8,128)S(1)}, u32[]{:S(2)}, u32[]{:S(2)}) %collective-permute-start.2) | collective-permute-done | bytes 122912 | tf_op jit(solution)/shard_map/ppermute | solution.py:509
  15.9 0.5 %collective-permute-start.7 = (f32[15,16,128]{2,1,0:T(8,128)S(1)}, f32[15,16,128]{2,1,0:T(8,128)S(1)}, u32[]{:S(2)}, u32[]{:S(2)}) collective-permute-start(f32[15,16,128]{2,1,0:T(8,128)S(1)} %collective-permute-done.3.refs_3_), channel_id=1, source_target_pairs={{0,4},{4,0},{1,5},{5,1},{2,6},{6,2},{3,7},{7,3},{8,12},{12,8},{9,1... | collective-permute-start | bytes 368648 | tf_op jit(solution)/shard_map/ppermute | solution.py:509
  16.5 1.1 %collective-permute-done.5.refs_5_ = f32[2,2,16,128]{3,2,1,0:T(8,128)S(1)} collective-permute-done((f32[2,2,16,128]{3,2,1,0:T(8,128)S(1)}, f32[2,2,16,128]{3,2,1,0:T(8,128)S(1)}, u32[]{:S(2)}, u32[]{:S(2)}) %collective-permute-start.5) | collective-permute-done | bytes 32800 | tf_op jit(solution)/shard_map/ppermute | solution.py:509
  17.7 2.9 %first.1 = (f32[64,128]{1,0:T(8,128)S(1)}, f32[32,24,256]{2,1,0:T(8,128)S(1)}, f32[32,24,256]{2,1,0:T(8,128)S(1)}, f32[32,24,256]{2,1,0:T(8,128)S(1)}, f32[32,24...) custom-call(f32[2,16,16,128]{3,2,1,0:T(8,128)S(1)} %pad_maximum_fusion., ...), custom_call_target="tpu_custom_call" | custom-call | tf_op jit(solution)/shard_map/first/pallas_call | solution.py:775
  20.6 3.6 %collective-permute-start.10 = (f32[64,128]{1,0:T(8,128)S(1)}, f32[64,128]{1,0:T(8,128)S(1)}, u32[]{:S(2)}, u32[]{:S(2)}) collective-permute-start(f32[64,128]{1,0:T(8,128)S(1)} %get-tuple-element.22), channel_id=1, source_target_pairs={{0,3},{1,2},{2,1},{3,0},{4,7},{5,6},{6,5},{7,4},{8,11},{9,10},{10,... | collective-permute-start | bytes 98312 | tf_op jit(solution)/shard_map/ppermute | solution.py:509
  24.2 2.1 %collective-permute-start.9 = (f32[64,128]{1,0:T(8,128)S(1)}, f32[64,128]{1,0:T(8,128)S(1)}, u32[]{:S(2)}, u32[]{:S(2)}) collective-permute-start(f32[64,128]{1,0:T(8,128)S(1)} %get-tuple-element.22), channel_id=1, source_target_pairs={{0,2},{1,3},{2,0},{3,1},{4,6},{5,7},{6,4},{7,5},{8,10},{9,11},{10,... | collective-permute-start | bytes 98312 | tf_op jit(solution)/shard_map/ppermute | solution.py:509
  26.4 0.5 %collective-permute-start.8 = (f32[64,128]{1,0:T(8,128)S(1)}, f32[64,128]{1,0:T(8,128)S(1)}, u32[]{:S(2)}, u32[]{:S(2)}) collective-permute-start(f32[64,128]{1,0:T(8,128)S(1)} %get-tuple-element.22), channel_id=1, source_target_pairs={{0,1},{1,0},{2,3},{3,2},{4,5},{5,4},{6,7},{7,6},{8,9},{9,8},{10,11... | collective-permute-start | bytes 98312 | tf_op jit(solution)/shard_map/ppermute | solution.py:509
  26.9 2.1 %collective-permute-done.9 = f32[64,128]{1,0:T(8,128)S(1)} collective-permute-done((f32[64,128]{1,0:T(8,128)S(1)}, f32[64,128]{1,0:T(8,128)S(1)}, u32[]{:S(2)}, u32[]{:S(2)}) %collective-permute-start.9) | collective-permute-done | bytes 32800 | tf_op jit(solution)/shard_map/ppermute | solution.py:509
  29.1 1.2 %collective-permute-done.8 = f32[64,128]{1,0:T(8,128)S(1)} collective-permute-done((f32[64,128]{1,0:T(8,128)S(1)}, f32[64,128]{1,0:T(8,128)S(1)}, u32[]{:S(2)}, u32[]{:S(2)}) %collective-permute-start.8) | collective-permute-done | bytes 32800 | tf_op jit(solution)/shard_map/ppermute | solution.py:509
  30.3 1.5 %collective-permute-start.13 = (f32[4,64,128]{2,1,0:T(8,128)S(1)}, f32[4,64,128]{2,1,0:T(8,128)S(1)}, u32[]{:S(2)}, u32[]{:S(2)}) collective-permute-start(f32[4,64,128]{2,1,0:T(8,128)S(1)} %pad_maximum_fusion.1.refs_0_), channel_id=1, source_target_pairs={{0,24},{8,16},{16,8},{24,0},{1,25},{9,17},{17,9},{25,1},{2,26},{10... | collective-permute-start | bytes 393224 | tf_op jit(solution)/shard_map/ppermute | solution.py:509
  31.8 2.0 %collective-permute-start.12 = (f32[4,64,128]{2,1,0:T(8,128)S(1)}, f32[4,64,128]{2,1,0:T(8,128)S(1)}, u32[]{:S(2)}, u32[]{:S(2)}) collective-permute-start(f32[4,64,128]{2,1,0:T(8,128)S(1)} %pad_maximum_fusion.1.refs_0_), channel_id=1, source_target_pairs={{0,16},{8,24},{16,0},{24,8},{1,17},{9,25},{17,1},{25,9},{2,18},{10... | collective-permute-start | bytes 393224 | tf_op jit(solution)/shard_map/ppermute | solution.py:509
  33.8 0.1 collective-permute-start.11
  33.9 3.4 %collective-permute-done.13.refs_3_ = f32[4,64,128]{2,1,0:T(8,128)S(1)} collective-permute-done((f32[4,64,128]{2,1,0:T(8,128)S(1)}, f32[4,64,128]{2,1,0:T(8,128)S(1)}, u32[]{:S(2)}, u32[]{:S(2)}) %collective-permute-start.13) | collective-permute-done | bytes 131104 | tf_op jit(solution)/shard_map/ppermute | solution.py:509
  37.3 1.1 %collective-permute-done.12.refs_2_ = f32[4,64,128]{2,1,0:T(8,128)S(1)} collective-permute-done((f32[4,64,128]{2,1,0:T(8,128)S(1)}, f32[4,64,128]{2,1,0:T(8,128)S(1)}, u32[]{:S(2)}, u32[]{:S(2)}) %collective-permute-start.12) | collective-permute-done | bytes 131104 | tf_op jit(solution)/shard_map/ppermute | solution.py:509
  38.4 0.5 %collective-permute-done.11.refs_1_ = f32[4,64,128]{2,1,0:T(8,128)S(1)} collective-permute-done((f32[4,64,128]{2,1,0:T(8,128)S(1)}, f32[4,64,128]{2,1,0:T(8,128)S(1)}, u32[]{:S(2)}, u32[]{:S(2)}) %collective-permute-start.11) | collective-permute-done | bytes 131104 | tf_op jit(solution)/shard_map/ppermute | solution.py:509
  39.0 0.8 %collective-permute-done.16.refs_6_ = f32[4,64,128]{2,1,0:T(8,128)S(1)} collective-permute-done((f32[4,64,128]{2,1,0:T(8,128)S(1)}, f32[4,64,128]{2,1,0:T(8,128)S(1)}, u32[]{:S(2)}, u32[]{:S(2)}) %collective-permute-start.16) | collective-permute-done | bytes 131104 | tf_op jit(solution)/shard_map/ppermute | solution.py:509
  39.8 0.5 %collective-permute-done.15.refs_5_ = f32[4,64,128]{2,1,0:T(8,128)S(1)} collective-permute-done((f32[4,64,128]{2,1,0:T(8,128)S(1)}, f32[4,64,128]{2,1,0:T(8,128)S(1)}, u32[]{:S(2)}, u32[]{:S(2)}) %collective-permute-start.15) | collective-permute-done | bytes 131104 | tf_op jit(solution)/shard_map/ppermute | solution.py:509
  40.4 9.6 %second.1 = (f32[16,16,128]{2,1,0:T(8,128)}, f32[16,16,128]{2,1,0:T(8,128)}) custom-call(f32[4,64,128]{2,1,0:T(8,128)S(1)} %pad_maximum_fusion.1.refs_0_, f32[4,64,128]{2,1,0:T(8,128)S(1)} %collective-permute-done.11.refs_1_, f32[4,64,128]{2,1,0:T(8,128)S(1)} %collective-permute-done.12.refs_2_, f32[4,64,128]{2,1,0:T(8,128)S(1)} %collective-permute-done.13.refs_3_, ...), custom_call_target="tpu_custom_call" | custom-call | tf_op jit(solution)/shard_map/second/pallas_call | solution.py:775
  (40 shorter events, 0.3 us)
Async XLA Ops:
  2.5 6.5 %collective-permute-start = (f32[2,16,128]{2,1,0:T(8,128)}, f32[2,16,128]{2,1,0:T(8,128)S(1)}, u32[]{:S(2)}, u32[]{:S(2)}) collective-permute-start(f32[2,16,128]{2,1,0:T(8,128)} %get-tuple-element.17), channel_id=1, source_target_pairs={{0,0},{8,16},{16,8},{24,24},{1,1},{9,17},{17,9},{25,25},{2,2},{10,... | collective-permute-start | bytes 49160 | tf_op jit(solution)/shard_map/ppermute | solution.py:509
  3.9 7.0 %collective-permute-start.1 = (f32[2,16,128]{2,1,0:T(8,128)}, f32[2,16,128]{2,1,0:T(8,128)S(1)}, u32[]{:S(2)}, u32[]{:S(2)}) collective-permute-start(f32[2,16,128]{2,1,0:T(8,128)} %get-tuple-element.18), channel_id=1, source_target_pairs={{0,8},{8,0},{16,24},{24,16},{1,9},{9,1},{17,25},{25,17},{2,10},{10... | collective-permute-start | bytes 49160 | tf_op jit(solution)/shard_map/ppermute | solution.py:509
  9.0 8.7 %collective-permute-start.4 = (f32[2,16,16,128]{3,2,1,0:T(8,128)S(1)}, f32[2,16,16,128]{3,2,1,0:T(8,128)S(1)}, u32[]{:S(2)}, u32[]{:S(2)}) collective-permute-start(f32[2,16,16,128]{3,2,1,0:T(8,128)S(1)} %pad_maximum_fusion.own.refs_0_), channel_id=1, source_target_pairs={{0,4},{4,0},{1,5},{5,1},{2,6},{6,2},{3,7},{7,3},{8,12},{12,8},{9,1... | collective-permute-start | bytes 786440 | tf_op jit(solution)/shard_map/ppermute | solution.py:509
  11.0 4.9 %collective-permute-start.2 = (f32[15,16,128]{2,1,0:T(8,128)S(1)}, f32[15,16,128]{2,1,0:T(8,128)S(1)}, u32[]{:S(2)}, u32[]{:S(2)}) collective-permute-start(f32[15,16,128]{2,1,0:T(8,128)S(1)} %get-tuple-element.20), channel_id=1, source_target_pairs={{0,1},{1,0},{2,3},{3,2},{4,5},{5,4},{6,7},{7,6},{8,9},{9,8},{10,11... | collective-permute-start | bytes 368648 | tf_op jit(solution)/shard_map/ppermute | solution.py:509
  12.6 3.3 %collective-permute-start.3 = (f32[15,16,128]{2,1,0:T(8,128)S(1)}, f32[15,16,128]{2,1,0:T(8,128)S(1)}, u32[]{:S(2)}, u32[]{:S(2)}) collective-permute-start(f32[15,16,128]{2,1,0:T(8,128)S(1)} %get-tuple-element.21), channel_id=1, source_target_pairs={{0,0},{1,2},{2,1},{3,3},{4,4},{5,6},{6,5},{7,7},{8,8},{9,10},{10,9... | collective-permute-start | bytes 368648 | tf_op jit(solution)/shard_map/ppermute | solution.py:509
  15.9 1.7 %collective-permute-start.6 = (f32[15,16,128]{2,1,0:T(8,128)S(1)}, f32[15,16,128]{2,1,0:T(8,128)S(1)}, u32[]{:S(2)}, u32[]{:S(2)}) collective-permute-start(f32[15,16,128]{2,1,0:T(8,128)S(1)} %collective-permute-done.2.refs_2_), channel_id=1, source_target_pairs={{0,4},{4,0},{1,5},{5,1},{2,6},{6,2},{3,7},{7,3},{8,12},{12,8},{9,1... | collective-permute-start | bytes 368648 | tf_op jit(solution)/shard_map/ppermute | solution.py:509
  15.9 1.7 %collective-permute-start.7 = (f32[15,16,128]{2,1,0:T(8,128)S(1)}, f32[15,16,128]{2,1,0:T(8,128)S(1)}, u32[]{:S(2)}, u32[]{:S(2)}) collective-permute-start(f32[15,16,128]{2,1,0:T(8,128)S(1)} %collective-permute-done.3.refs_3_), channel_id=1, source_target_pairs={{0,4},{4,0},{1,5},{5,1},{2,6},{6,2},{3,7},{7,3},{8,12},{12,8},{9,1... | collective-permute-start | bytes 368648 | tf_op jit(solution)/shard_map/ppermute | solution.py:509
  16.4 23.9 %copy-start = (bf16[4,256,256]{2,1,0:T(8,128)(2,1)S(1)}, bf16[4,256,256]{2,1,0:T(8,128)(2,1)}, u32[]{:S(2)}) copy-start(bf16[4,256,256]{2,1,0:T(8,128)(2,1)} %constant.22.clone.refs_16_) | copy-start | bytes 1572868
  16.4 1.2 %collective-permute-start.5 = (f32[2,2,16,128]{3,2,1,0:T(8,128)S(1)}, f32[2,2,16,128]{3,2,1,0:T(8,128)S(1)}, u32[]{:S(2)}, u32[]{:S(2)}) collective-permute-start(f32[2,2,16,128]{3,2,1,0:T(8,128)S(1)} %get-tuple-element.19.refs_1_), channel_id=1, source_target_pairs={{0,4},{4,0},{1,5},{5,1},{2,6},{6,2},{3,7},{7,3},{8,12},{12,8},{9,1... | collective-permute-start | bytes 98312 | tf_op jit(solution)/shard_map/ppermute | solution.py:509
  17.7 22.6 %copy-start.1 = (bf16[2,336,224]{2,1,0:T(8,128)(2,1)S(1)}, bf16[2,336,224]{2,1,0:T(8,128)(2,1)}, u32[]{:S(2)}) copy-start(bf16[2,336,224]{2,1,0:T(8,128)(2,1)} %constant.21.clone.refs_15_) | copy-start | bytes 903172
  20.6 6.3 %collective-permute-start.10 = (f32[64,128]{1,0:T(8,128)S(1)}, f32[64,128]{1,0:T(8,128)S(1)}, u32[]{:S(2)}, u32[]{:S(2)}) collective-permute-start(f32[64,128]{1,0:T(8,128)S(1)} %get-tuple-element.22), channel_id=1, source_target_pairs={{0,3},{1,2},{2,1},{3,0},{4,7},{5,6},{6,5},{7,4},{8,11},{9,10},{10,... | collective-permute-start | bytes 98312 | tf_op jit(solution)/shard_map/ppermute | solution.py:509
  24.2 4.8 %collective-permute-start.9 = (f32[64,128]{1,0:T(8,128)S(1)}, f32[64,128]{1,0:T(8,128)S(1)}, u32[]{:S(2)}, u32[]{:S(2)}) collective-permute-start(f32[64,128]{1,0:T(8,128)S(1)} %get-tuple-element.22), channel_id=1, source_target_pairs={{0,2},{1,3},{2,0},{3,1},{4,6},{5,7},{6,4},{7,5},{8,10},{9,11},{10,... | collective-permute-start | bytes 98312 | tf_op jit(solution)/shard_map/ppermute | solution.py:509
  26.4 3.9 %collective-permute-start.8 = (f32[64,128]{1,0:T(8,128)S(1)}, f32[64,128]{1,0:T(8,128)S(1)}, u32[]{:S(2)}, u32[]{:S(2)}) collective-permute-start(f32[64,128]{1,0:T(8,128)S(1)} %get-tuple-element.22), channel_id=1, source_target_pairs={{0,1},{1,0},{2,3},{3,2},{4,5},{5,4},{6,7},{7,6},{8,9},{9,8},{10,11... | collective-permute-start | bytes 98312 | tf_op jit(solution)/shard_map/ppermute | solution.py:509
  30.3 10.0 %copy-start.2 = (bf16[128,256]{1,0:T(8,128)(2,1)S(1)}, bf16[128,256]{1,0:T(8,128)(2,1)}, u32[]{:S(2)}) copy-start(bf16[128,256]{1,0:T(8,128)(2,1)} %constant.26.clone.refs_20_) | copy-start | bytes 196612
  30.3 10.0 %copy-start.3 = (bf16[256,128]{1,0:T(8,128)(2,1)S(1)}, bf16[256,128]{1,0:T(8,128)(2,1)}, u32[]{:S(2)}) copy-start(bf16[256,128]{1,0:T(8,128)(2,1)} %constant.25.clone.refs_19_) | copy-start | bytes 196612
  30.3 10.0 %copy-start.4 = (bf16[256,128]{1,0:T(8,128)(2,1)S(1)}, bf16[256,128]{1,0:T(8,128)(2,1)}, u32[]{:S(2)}) copy-start(bf16[256,128]{1,0:T(8,128)(2,1)} %constant.24.clone.refs_18_) | copy-start | bytes 196612
  30.3 10.0 %copy-start.5 = (bf16[128,256]{1,0:T(8,128)(2,1)S(1)}, bf16[128,256]{1,0:T(8,128)(2,1)}, u32[]{:S(2)}) copy-start(bf16[128,256]{1,0:T(8,128)(2,1)} %constant.23.clone.refs_17_) | copy-start | bytes 196612
  30.3 7.0 %collective-permute-start.13 = (f32[4,64,128]{2,1,0:T(8,128)S(1)}, f32[4,64,128]{2,1,0:T(8,128)S(1)}, u32[]{:S(2)}, u32[]{:S(2)}) collective-permute-start(f32[4,64,128]{2,1,0:T(8,128)S(1)} %pad_maximum_fusion.1.refs_0_), channel_id=1, source_target_pairs={{0,24},{8,16},{16,8},{24,0},{1,25},{9,17},{17,9},{25,1},{2,26},{10... | collective-permute-start | bytes 393224 | tf_op jit(solution)/shard_map/ppermute | solution.py:509
  31.8 6.6 %collective-permute-start.12 = (f32[4,64,128]{2,1,0:T(8,128)S(1)}, f32[4,64,128]{2,1,0:T(8,128)S(1)}, u32[]{:S(2)}, u32[]{:S(2)}) collective-permute-start(f32[4,64,128]{2,1,0:T(8,128)S(1)} %pad_maximum_fusion.1.refs_0_), channel_id=1, source_target_pairs={{0,16},{8,24},{16,0},{24,8},{1,17},{9,25},{17,1},{25,9},{2,18},{10... | collective-permute-start | bytes 393224 | tf_op jit(solution)/shard_map/ppermute | solution.py:509
  33.8 5.2 %collective-permute-start.11 = (f32[4,64,128]{2,1,0:T(8,128)S(1)}, f32[4,64,128]{2,1,0:T(8,128)S(1)}, u32[]{:S(2)}, u32[]{:S(2)}) collective-permute-start(f32[4,64,128]{2,1,0:T(8,128)S(1)} %pad_maximum_fusion.1.refs_0_), channel_id=1, source_target_pairs={{0,8},{8,0},{16,24},{24,16},{1,9},{9,1},{17,25},{25,17},{2,10},{10... | collective-permute-start | bytes 393224 | tf_op jit(solution)/shard_map/ppermute | solution.py:509
  33.9 5.1 %collective-permute-start.14 = (f32[4,64,128]{2,1,0:T(8,128)S(1)}, f32[4,64,128]{2,1,0:T(8,128)S(1)}, u32[]{:S(2)}, u32[]{:S(2)}) collective-permute-start(f32[4,64,128]{2,1,0:T(8,128)S(1)} %pad_maximum_fusion.1.refs_0_), channel_id=1, source_target_pairs={{0,4},{4,0},{1,5},{5,1},{2,6},{6,2},{3,7},{7,3},{8,12},{12,8},{9,1... | collective-permute-start | bytes 393224 | tf_op jit(solution)/shard_map/ppermute | solution.py:509
  37.3 1.7 %collective-permute-start.17 = (f32[4,64,128]{2,1,0:T(8,128)S(1)}, f32[4,64,128]{2,1,0:T(8,128)S(1)}, u32[]{:S(2)}, u32[]{:S(2)}) collective-permute-start(f32[4,64,128]{2,1,0:T(8,128)S(1)} %collective-permute-done.13.refs_3_), channel_id=1, source_target_pairs={{0,4},{4,0},{1,5},{5,1},{2,6},{6,2},{3,7},{7,3},{8,12},{12,8},{9,1... | collective-permute-start | bytes 393224 | tf_op jit(solution)/shard_map/ppermute | solution.py:509
  38.4 1.3 %collective-permute-start.16 = (f32[4,64,128]{2,1,0:T(8,128)S(1)}, f32[4,64,128]{2,1,0:T(8,128)S(1)}, u32[]{:S(2)}, u32[]{:S(2)}) collective-permute-start(f32[4,64,128]{2,1,0:T(8,128)S(1)} %collective-permute-done.12.refs_2_), channel_id=1, source_target_pairs={{0,4},{4,0},{1,5},{5,1},{2,6},{6,2},{3,7},{7,3},{8,12},{12,8},{9,1... | collective-permute-start | bytes 393224 | tf_op jit(solution)/shard_map/ppermute | solution.py:509
  39.0 1.3 %collective-permute-start.15 = (f32[4,64,128]{2,1,0:T(8,128)S(1)}, f32[4,64,128]{2,1,0:T(8,128)S(1)}, u32[]{:S(2)}, u32[]{:S(2)}) collective-permute-start(f32[4,64,128]{2,1,0:T(8,128)S(1)} %collective-permute-done.11.refs_1_), channel_id=1, source_target_pairs={{0,4},{4,0},{1,5},{5,1},{2,6},{6,2},{3,7},{7,3},{8,12},{12,8},{9,1... | collective-permute-start | bytes 393224 | tf_op jit(solution)/shard_map/ppermute | solution.py:509
  (5 other events, 40.8 us)

commit v17 on v16

--- a/solution.py
+++ b/solution.py
@@ -352,16 +352,20 @@
     plane_sweep(faces, start, stop, estimate, finish, block)
 
 
-def plane_residual(faces, start, stop, residual, update, block=4):
-    def finish(here, own):
-        before = residual[here]
-
-        def store(value):
-            residual[here] = before - value
-
-        return store
-
-    plane_sweep(faces, start, stop, update, finish, block)
+def own_residual(faces, start, stop, residual, update, own_y):
+    face_z, face_y, face_x, diagonal, inverse = faces
+    here, after, before = (pl.ds(start + shift, stop - start) for shift in (0, 1, -1))
+
+    def own(ref, planes=here):
+        return ref[planes, :own_y, :128]
+
+    value = own(diagonal) * own(update) - own(face_z) * own(update, after) - own(face_z, before) * own(update, before)
+    for face, axis, places in ((face_y, 1, (here, slice(None), slice(0, 128))), (face_x, 2, (here, slice(0, own_y)))):
+        field = update[places]
+        above = turned(field, -1, axis)[:, :own_y, :128]
+        below = turned(face[places] * field, 1, axis)[:, :own_y, :128]
+        value = value - own(face) * above - below
+    return own(residual) - value
 
 
 def moved(value, shift, axis):
@@ -636,12 +640,11 @@
     plane_faces(coef, faces, 2, planes - 2, link_mask(rows, lanes), None, source, update, planes // 2 - 2)
     ranges = [(3, planes - 3), (4, planes - 4)]
     plane_steps(faces, ranges, source, residual, update, estimate, True, (planes - 6, planes - 8))
-    plane_residual(faces, HALO_Z, planes - HALO_Z, residual, update, 16)
-    for pair in range((planes - 2 * HALO_Z) // 2):
-        low = HALO_Z + 2 * pair
-        target = pl.ds(pair * own_y, own_y)
-        pair_source[target] = residual[low, :own_y, :128] + residual[low + 1, :own_y, :128]
-        pair_coef[target] = coef[low, :own_y, :128] + coef[low + 1, :own_y, :128]
+    left_over = own_residual(faces, HALO_Z, planes - HALO_Z, residual, update, own_y)
+    own_coef = coef[pl.ds(HALO_Z, planes - 2 * HALO_Z), :own_y, :128]
+    for target, whole in ((pair_source, left_over), (pair_coef, own_coef)):
+        whole = whole.reshape(planes // 2 - HALO_Z, 2, own_y, 128)
+        target[...] = (whole[:, 0] + whole[:, 1]).reshape(target.shape)
     message[...] = times_right(times_left(left[...], pair_source[...]), right_source[...]) + times_right(
         times_left(left[...], pair_coef[...]), right_coef[...]
     )
@@ -756,9 +759,8 @@
     plane_restart(faces, HALO_Z - 3, planes - HALO_Z + 3, source, residual, update, current, 22)
     ranges = [(HALO_Z - 2, planes - HALO_Z + 2), (HALO_Z - 1, planes - HALO_Z + 1)]
     plane_steps(faces, ranges, source, residual, update, current, False, (20, 18))
-    plane_residual(faces, HALO_Z, planes - HALO_Z, residual, update, 16)
     own_planes = pl.ds(HALO_Z, planes - 2 * HALO_Z)
-    residual_out[...] = residual[own_planes, :own_y, :128]
+    residual_out[...] = own_residual(faces, HALO_Z, planes - HALO_Z, residual, update, own_y)
     solution[...] = current[own_planes, :own_y, :128]
 
 

time: 50.2 us -> 50.2 us (level)
  no operation moved by 1% of the time
where the time goes in v17:
time: 50.2 us; the launch traced here: 50 us
  starting transfers between devices  19.2 us (38%)
  waiting for transfers between devices  15.5 us (31%)
  Pallas kernels  14.5 us (29%)
  between operations  0.8 us (2%)
    ppermute x18, starting transfers between devices, swapped(): lax.ppermute(value, axes, [(int(source), int(target)) for source, target...  19.2 us
    ppermute x18, waiting for transfers between devices, swapped(): lax.ppermute(value, axes, [(int(source), int(target)) for source, target...  15.5 us
    pallas_call x4, Pallas kernels, call(): pl.pallas_call(kernel, out_shape=tuple((jax.ShapeDtypeStruct(shape, F32)...  14.5 us
  transfers between devices with their start and end apart: 18, of which 10 were waited for; matrix products, arithmetic and copies ran while one was open for 0% of the time, Pallas kernels for 0%

profile of v17, /device:TPU:0, one launch (start us, length us, event | category | flops | bytes accessed | tf_op | source)
XLA Modules:
  0.0 50.0 jit_solution(13845573349452166329)
XLA Ops:
  0.6 1.9 %start.1 = (f32[2,16,128]{2,1,0:T(8,128)}, f32[2,16,128]{2,1,0:T(8,128)}) custom-call(f32[16,16,128]{2,1,0:T(8,128)} %bitcast.10, f32[16,16,128]{2,1,0:T(8,128)} %coef.1), custom_call_target="tpu_custom_call" | custom-call | tf_op jit(solution)/shard_map/start/pallas_call | solution.py:777
  2.5 1.4 %collective-permute-start = (f32[2,16,128]{2,1,0:T(8,128)}, f32[2,16,128]{2,1,0:T(8,128)S(1)}, u32[]{:S(2)}, u32[]{:S(2)}) collective-permute-start(f32[2,16,128]{2,1,0:T(8,128)} %get-tuple-element.17), channel_id=1, source_target_pairs={{0,0},{8,16},{16,8},{24,24},{1,1},{9,17},{17,9},{25,25},{2,2},{10,... | collective-permute-start | bytes 49160 | tf_op jit(solution)/shard_map/ppermute | solution.py:513
  3.9 5.0 %collective-permute-start.1 = (f32[2,16,128]{2,1,0:T(8,128)}, f32[2,16,128]{2,1,0:T(8,128)S(1)}, u32[]{:S(2)}, u32[]{:S(2)}) collective-permute-start(f32[2,16,128]{2,1,0:T(8,128)} %get-tuple-element.18), channel_id=1, source_target_pairs={{0,8},{8,0},{16,24},{24,16},{1,9},{9,1},{17,25},{25,17},{2,10},{10... | collective-permute-start | bytes 49160 | tf_op jit(solution)/shard_map/ppermute | solution.py:513
  9.1 1.9 %collective-permute-done.1.x_a = f32[2,16,128]{2,1,0:T(8,128)S(1)} collective-permute-done((f32[2,16,128]{2,1,0:T(8,128)}, f32[2,16,128]{2,1,0:T(8,128)S(1)}, u32[]{:S(2)}, u32[]{:S(2)}) %collective-permute-start.1) | collective-permute-done | bytes 16416 | tf_op jit(solution)/shard_map/ppermute | solution.py:513
  11.0 1.6 %collective-permute-start.2 = (f32[15,16,128]{2,1,0:T(8,128)S(1)}, f32[15,16,128]{2,1,0:T(8,128)S(1)}, u32[]{:S(2)}, u32[]{:S(2)}) collective-permute-start(f32[15,16,128]{2,1,0:T(8,128)S(1)} %get-tuple-element.20), channel_id=1, source_target_pairs={{0,1},{1,0},{2,3},{3,2},{4,5},{5,4},{6,7},{7,6},{8,9},{9,8},{10,11... | collective-permute-start | bytes 368648 | tf_op jit(solution)/shard_map/ppermute | solution.py:513
  12.6 0.7 %collective-permute-start.3 = (f32[15,16,128]{2,1,0:T(8,128)S(1)}, f32[15,16,128]{2,1,0:T(8,128)S(1)}, u32[]{:S(2)}, u32[]{:S(2)}) collective-permute-start(f32[15,16,128]{2,1,0:T(8,128)S(1)} %get-tuple-element.21), channel_id=1, source_target_pairs={{0,0},{1,2},{2,1},{3,3},{4,4},{5,6},{6,5},{7,7},{8,8},{9,10},{10,9... | collective-permute-start | bytes 368648 | tf_op jit(solution)/shard_map/ppermute | solution.py:513
  13.3 2.6 %collective-permute-done.2.refs_2_ = f32[15,16,128]{2,1,0:T(8,128)S(1)} collective-permute-done((f32[15,16,128]{2,1,0:T(8,128)S(1)}, f32[15,16,128]{2,1,0:T(8,128)S(1)}, u32[]{:S(2)}, u32[]{:S(2)}) %collective-permute-start.2) | collective-permute-done | bytes 122912 | tf_op jit(solution)/shard_map/ppermute | solution.py:513
  15.9 0.5 %collective-permute-start.7 = (f32[15,16,128]{2,1,0:T(8,128)S(1)}, f32[15,16,128]{2,1,0:T(8,128)S(1)}, u32[]{:S(2)}, u32[]{:S(2)}) collective-permute-start(f32[15,16,128]{2,1,0:T(8,128)S(1)} %collective-permute-done.3.refs_3_), channel_id=1, source_target_pairs={{0,4},{4,0},{1,5},{5,1},{2,6},{6,2},{3,7},{7,3},{8,12},{12,8},{9,1... | collective-permute-start | bytes 368648 | tf_op jit(solution)/shard_map/ppermute | solution.py:513
  16.5 1.1 %collective-permute-done.5.refs_5_ = f32[2,2,16,128]{3,2,1,0:T(8,128)S(1)} collective-permute-done((f32[2,2,16,128]{3,2,1,0:T(8,128)S(1)}, f32[2,2,16,128]{3,2,1,0:T(8,128)S(1)}, u32[]{:S(2)}, u32[]{:S(2)}) %collective-permute-start.5) | collective-permute-done | bytes 32800 | tf_op jit(solution)/shard_map/ppermute | solution.py:513
  17.7 2.9 %first.1 = (f32[64,128]{1,0:T(8,128)S(1)}, f32[32,24,256]{2,1,0:T(8,128)S(1)}, f32[32,24,256]{2,1,0:T(8,128)S(1)}, f32[32,24,256]{2,1,0:T(8,128)S(1)}, f32[32,24...) custom-call(f32[2,16,16,128]{3,2,1,0:T(8,128)S(1)} %pad_maximum_fusion., ...), custom_call_target="tpu_custom_call" | custom-call | tf_op jit(solution)/shard_map/first/pallas_call | solution.py:777
  20.6 3.6 %collective-permute-start.10 = (f32[64,128]{1,0:T(8,128)S(1)}, f32[64,128]{1,0:T(8,128)S(1)}, u32[]{:S(2)}, u32[]{:S(2)}) collective-permute-start(f32[64,128]{1,0:T(8,128)S(1)} %get-tuple-element.22), channel_id=1, source_target_pairs={{0,3},{1,2},{2,1},{3,0},{4,7},{5,6},{6,5},{7,4},{8,11},{9,10},{10,... | collective-permute-start | bytes 98312 | tf_op jit(solution)/shard_map/ppermute | solution.py:513
  24.2 2.1 %collective-permute-start.9 = (f32[64,128]{1,0:T(8,128)S(1)}, f32[64,128]{1,0:T(8,128)S(1)}, u32[]{:S(2)}, u32[]{:S(2)}) collective-permute-start(f32[64,128]{1,0:T(8,128)S(1)} %get-tuple-element.22), channel_id=1, source_target_pairs={{0,2},{1,3},{2,0},{3,1},{4,6},{5,7},{6,4},{7,5},{8,10},{9,11},{10,... | collective-permute-start | bytes 98312 | tf_op jit(solution)/shard_map/ppermute | solution.py:513
  26.4 0.5 %collective-permute-start.8 = (f32[64,128]{1,0:T(8,128)S(1)}, f32[64,128]{1,0:T(8,128)S(1)}, u32[]{:S(2)}, u32[]{:S(2)}) collective-permute-start(f32[64,128]{1,0:T(8,128)S(1)} %get-tuple-element.22), channel_id=1, source_target_pairs={{0,1},{1,0},{2,3},{3,2},{4,5},{5,4},{6,7},{7,6},{8,9},{9,8},{10,11... | collective-permute-start | bytes 98312 | tf_op jit(solution)/shard_map/ppermute | solution.py:513
  26.9 2.1 %collective-permute-done.9 = f32[64,128]{1,0:T(8,128)S(1)} collective-permute-done((f32[64,128]{1,0:T(8,128)S(1)}, f32[64,128]{1,0:T(8,128)S(1)}, u32[]{:S(2)}, u32[]{:S(2)}) %collective-permute-start.9) | collective-permute-done | bytes 32800 | tf_op jit(solution)/shard_map/ppermute | solution.py:513
  29.1 1.2 %collective-permute-done.8 = f32[64,128]{1,0:T(8,128)S(1)} collective-permute-done((f32[64,128]{1,0:T(8,128)S(1)}, f32[64,128]{1,0:T(8,128)S(1)}, u32[]{:S(2)}, u32[]{:S(2)}) %collective-permute-start.8) | collective-permute-done | bytes 32800 | tf_op jit(solution)/shard_map/ppermute | solution.py:513
  30.3 1.5 %collective-permute-start.13 = (f32[4,64,128]{2,1,0:T(8,128)S(1)}, f32[4,64,128]{2,1,0:T(8,128)S(1)}, u32[]{:S(2)}, u32[]{:S(2)}) collective-permute-start(f32[4,64,128]{2,1,0:T(8,128)S(1)} %pad_maximum_fusion.1.refs_0_), channel_id=1, source_target_pairs={{0,24},{8,16},{16,8},{24,0},{1,25},{9,17},{17,9},{25,1},{2,26},{10... | collective-permute-start | bytes 393224 | tf_op jit(solution)/shard_map/ppermute | solution.py:513
  31.8 2.0 %collective-permute-start.12 = (f32[4,64,128]{2,1,0:T(8,128)S(1)}, f32[4,64,128]{2,1,0:T(8,128)S(1)}, u32[]{:S(2)}, u32[]{:S(2)}) collective-permute-start(f32[4,64,128]{2,1,0:T(8,128)S(1)} %pad_maximum_fusion.1.refs_0_), channel_id=1, source_target_pairs={{0,16},{8,24},{16,0},{24,8},{1,17},{9,25},{17,1},{25,9},{2,18},{10... | collective-permute-start | bytes 393224 | tf_op jit(solution)/shard_map/ppermute | solution.py:513
  33.8 0.1 collective-permute-start.11
  33.9 3.4 %collective-permute-done.13.refs_3_ = f32[4,64,128]{2,1,0:T(8,128)S(1)} collective-permute-done((f32[4,64,128]{2,1,0:T(8,128)S(1)}, f32[4,64,128]{2,1,0:T(8,128)S(1)}, u32[]{:S(2)}, u32[]{:S(2)}) %collective-permute-start.13) | collective-permute-done | bytes 131104 | tf_op jit(solution)/shard_map/ppermute | solution.py:513
  37.3 1.1 %collective-permute-done.12.refs_2_ = f32[4,64,128]{2,1,0:T(8,128)S(1)} collective-permute-done((f32[4,64,128]{2,1,0:T(8,128)S(1)}, f32[4,64,128]{2,1,0:T(8,128)S(1)}, u32[]{:S(2)}, u32[]{:S(2)}) %collective-permute-start.12) | collective-permute-done | bytes 131104 | tf_op jit(solution)/shard_map/ppermute | solution.py:513
  38.4 0.5 %collective-permute-done.11.refs_1_ = f32[4,64,128]{2,1,0:T(8,128)S(1)} collective-permute-done((f32[4,64,128]{2,1,0:T(8,128)S(1)}, f32[4,64,128]{2,1,0:T(8,128)S(1)}, u32[]{:S(2)}, u32[]{:S(2)}) %collective-permute-start.11) | collective-permute-done | bytes 131104 | tf_op jit(solution)/shard_map/ppermute | solution.py:513
  39.0 0.8 %collective-permute-done.16.refs_6_ = f32[4,64,128]{2,1,0:T(8,128)S(1)} collective-permute-done((f32[4,64,128]{2,1,0:T(8,128)S(1)}, f32[4,64,128]{2,1,0:T(8,128)S(1)}, u32[]{:S(2)}, u32[]{:S(2)}) %collective-permute-start.16) | collective-permute-done | bytes 131104 | tf_op jit(solution)/shard_map/ppermute | solution.py:513
  39.8 0.5 %collective-permute-done.15.refs_5_ = f32[4,64,128]{2,1,0:T(8,128)S(1)} collective-permute-done((f32[4,64,128]{2,1,0:T(8,128)S(1)}, f32[4,64,128]{2,1,0:T(8,128)S(1)}, u32[]{:S(2)}, u32[]{:S(2)}) %collective-permute-start.15) | collective-permute-done | bytes 131104 | tf_op jit(solution)/shard_map/ppermute | solution.py:513
  40.4 9.6 %second.1 = (f32[16,16,128]{2,1,0:T(8,128)}, f32[16,16,128]{2,1,0:T(8,128)}) custom-call(f32[4,64,128]{2,1,0:T(8,128)S(1)} %pad_maximum_fusion.1.refs_0_, f32[4,64,128]{2,1,0:T(8,128)S(1)} %collective-permute-done.11.refs_1_, f32[4,64,128]{2,1,0:T(8,128)S(1)} %collective-permute-done.12.refs_2_, f32[4,64,128]{2,1,0:T(8,128)S(1)} %collective-permute-done.13.refs_3_, ...), custom_call_target="tpu_custom_call" | custom-call | tf_op jit(solution)/shard_map/second/pallas_call | solution.py:777
  (40 shorter events, 0.3 us)
Async XLA Ops:
  2.5 6.5 %collective-permute-start = (f32[2,16,128]{2,1,0:T(8,128)}, f32[2,16,128]{2,1,0:T(8,128)S(1)}, u32[]{:S(2)}, u32[]{:S(2)}) collective-permute-start(f32[2,16,128]{2,1,0:T(8,128)} %get-tuple-element.17), channel_id=1, source_target_pairs={{0,0},{8,16},{16,8},{24,24},{1,1},{9,17},{17,9},{25,25},{2,2},{10,... | collective-permute-start | bytes 49160 | tf_op jit(solution)/shard_map/ppermute | solution.py:513
  3.9 7.0 %collective-permute-start.1 = (f32[2,16,128]{2,1,0:T(8,128)}, f32[2,16,128]{2,1,0:T(8,128)S(1)}, u32[]{:S(2)}, u32[]{:S(2)}) collective-permute-start(f32[2,16,128]{2,1,0:T(8,128)} %get-tuple-element.18), channel_id=1, source_target_pairs={{0,8},{8,0},{16,24},{24,16},{1,9},{9,1},{17,25},{25,17},{2,10},{10... | collective-permute-start | bytes 49160 | tf_op jit(solution)/shard_map/ppermute | solution.py:513
  9.0 8.7 %collective-permute-start.4 = (f32[2,16,16,128]{3,2,1,0:T(8,128)S(1)}, f32[2,16,16,128]{3,2,1,0:T(8,128)S(1)}, u32[]{:S(2)}, u32[]{:S(2)}) collective-permute-start(f32[2,16,16,128]{3,2,1,0:T(8,128)S(1)} %pad_maximum_fusion.own.refs_0_), channel_id=1, source_target_pairs={{0,4},{4,0},{1,5},{5,1},{2,6},{6,2},{3,7},{7,3},{8,12},{12,8},{9,1... | collective-permute-start | bytes 786440 | tf_op jit(solution)/shard_map/ppermute | solution.py:513
  11.0 4.9 %collective-permute-start.2 = (f32[15,16,128]{2,1,0:T(8,128)S(1)}, f32[15,16,128]{2,1,0:T(8,128)S(1)}, u32[]{:S(2)}, u32[]{:S(2)}) collective-permute-start(f32[15,16,128]{2,1,0:T(8,128)S(1)} %get-tuple-element.20), channel_id=1, source_target_pairs={{0,1},{1,0},{2,3},{3,2},{4,5},{5,4},{6,7},{7,6},{8,9},{9,8},{10,11... | collective-permute-start | bytes 368648 | tf_op jit(solution)/shard_map/ppermute | solution.py:513
  12.6 3.3 %collective-permute-start.3 = (f32[15,16,128]{2,1,0:T(8,128)S(1)}, f32[15,16,128]{2,1,0:T(8,128)S(1)}, u32[]{:S(2)}, u32[]{:S(2)}) collective-permute-start(f32[15,16,128]{2,1,0:T(8,128)S(1)} %get-tuple-element.21), channel_id=1, source_target_pairs={{0,0},{1,2},{2,1},{3,3},{4,4},{5,6},{6,5},{7,7},{8,8},{9,10},{10,9... | collective-permute-start | bytes 368648 | tf_op jit(solution)/shard_map/ppermute | solution.py:513
  15.9 1.7 %collective-permute-start.6 = (f32[15,16,128]{2,1,0:T(8,128)S(1)}, f32[15,16,128]{2,1,0:T(8,128)S(1)}, u32[]{:S(2)}, u32[]{:S(2)}) collective-permute-start(f32[15,16,128]{2,1,0:T(8,128)S(1)} %collective-permute-done.2.refs_2_), channel_id=1, source_target_pairs={{0,4},{4,0},{1,5},{5,1},{2,6},{6,2},{3,7},{7,3},{8,12},{12,8},{9,1... | collective-permute-start | bytes 368648 | tf_op jit(solution)/shard_map/ppermute | solution.py:513
  15.9 1.7 %collective-permute-start.7 = (f32[15,16,128]{2,1,0:T(8,128)S(1)}, f32[15,16,128]{2,1,0:T(8,128)S(1)}, u32[]{:S(2)}, u32[]{:S(2)}) collective-permute-start(f32[15,16,128]{2,1,0:T(8,128)S(1)} %collective-permute-done.3.refs_3_), channel_id=1, source_target_pairs={{0,4},{4,0},{1,5},{5,1},{2,6},{6,2},{3,7},{7,3},{8,12},{12,8},{9,1... | collective-permute-start | bytes 368648 | tf_op jit(solution)/shard_map/ppermute | solution.py:513
  16.4 23.9 %copy-start = (bf16[4,256,256]{2,1,0:T(8,128)(2,1)S(1)}, bf16[4,256,256]{2,1,0:T(8,128)(2,1)}, u32[]{:S(2)}) copy-start(bf16[4,256,256]{2,1,0:T(8,128)(2,1)} %constant.22.clone.refs_16_) | copy-start | bytes 1572868
  16.4 1.2 %collective-permute-start.5 = (f32[2,2,16,128]{3,2,1,0:T(8,128)S(1)}, f32[2,2,16,128]{3,2,1,0:T(8,128)S(1)}, u32[]{:S(2)}, u32[]{:S(2)}) collective-permute-start(f32[2,2,16,128]{3,2,1,0:T(8,128)S(1)} %get-tuple-element.19.refs_1_), channel_id=1, source_target_pairs={{0,4},{4,0},{1,5},{5,1},{2,6},{6,2},{3,7},{7,3},{8,12},{12,8},{9,1... | collective-permute-start | bytes 98312 | tf_op jit(solution)/shard_map/ppermute | solution.py:513
  17.7 22.6 %copy-start.1 = (bf16[2,336,224]{2,1,0:T(8,128)(2,1)S(1)}, bf16[2,336,224]{2,1,0:T(8,128)(2,1)}, u32[]{:S(2)}) copy-start(bf16[2,336,224]{2,1,0:T(8,128)(2,1)} %constant.21.clone.refs_15_) | copy-start | bytes 903172
  20.6 6.3 %collective-permute-start.10 = (f32[64,128]{1,0:T(8,128)S(1)}, f32[64,128]{1,0:T(8,128)S(1)}, u32[]{:S(2)}, u32[]{:S(2)}) collective-permute-start(f32[64,128]{1,0:T(8,128)S(1)} %get-tuple-element.22), channel_id=1, source_target_pairs={{0,3},{1,2},{2,1},{3,0},{4,7},{5,6},{6,5},{7,4},{8,11},{9,10},{10,... | collective-permute-start | bytes 98312 | tf_op jit(solution)/shard_map/ppermute | solution.py:513
  24.2 4.8 %collective-permute-start.9 = (f32[64,128]{1,0:T(8,128)S(1)}, f32[64,128]{1,0:T(8,128)S(1)}, u32[]{:S(2)}, u32[]{:S(2)}) collective-permute-start(f32[64,128]{1,0:T(8,128)S(1)} %get-tuple-element.22), channel_id=1, source_target_pairs={{0,2},{1,3},{2,0},{3,1},{4,6},{5,7},{6,4},{7,5},{8,10},{9,11},{10,... | collective-permute-start | bytes 98312 | tf_op jit(solution)/shard_map/ppermute | solution.py:513
  26.4 3.9 %collective-permute-start.8 = (f32[64,128]{1,0:T(8,128)S(1)}, f32[64,128]{1,0:T(8,128)S(1)}, u32[]{:S(2)}, u32[]{:S(2)}) collective-permute-start(f32[64,128]{1,0:T(8,128)S(1)} %get-tuple-element.22), channel_id=1, source_target_pairs={{0,1},{1,0},{2,3},{3,2},{4,5},{5,4},{6,7},{7,6},{8,9},{9,8},{10,11... | collective-permute-start | bytes 98312 | tf_op jit(solution)/shard_map/ppermute | solution.py:513
  30.3 10.0 %copy-start.2 = (bf16[128,256]{1,0:T(8,128)(2,1)S(1)}, bf16[128,256]{1,0:T(8,128)(2,1)}, u32[]{:S(2)}) copy-start(bf16[128,256]{1,0:T(8,128)(2,1)} %constant.26.clone.refs_20_) | copy-start | bytes 196612
  30.3 10.0 %copy-start.3 = (bf16[256,128]{1,0:T(8,128)(2,1)S(1)}, bf16[256,128]{1,0:T(8,128)(2,1)}, u32[]{:S(2)}) copy-start(bf16[256,128]{1,0:T(8,128)(2,1)} %constant.25.clone.refs_19_) | copy-start | bytes 196612
  30.3 10.0 %copy-start.4 = (bf16[256,128]{1,0:T(8,128)(2,1)S(1)}, bf16[256,128]{1,0:T(8,128)(2,1)}, u32[]{:S(2)}) copy-start(bf16[256,128]{1,0:T(8,128)(2,1)} %constant.24.clone.refs_18_) | copy-start | bytes 196612
  30.3 10.0 %copy-start.5 = (bf16[128,256]{1,0:T(8,128)(2,1)S(1)}, bf16[128,256]{1,0:T(8,128)(2,1)}, u32[]{:S(2)}) copy-start(bf16[128,256]{1,0:T(8,128)(2,1)} %constant.23.clone.refs_17_) | copy-start | bytes 196612
  30.3 7.0 %collective-permute-start.13 = (f32[4,64,128]{2,1,0:T(8,128)S(1)}, f32[4,64,128]{2,1,0:T(8,128)S(1)}, u32[]{:S(2)}, u32[]{:S(2)}) collective-permute-start(f32[4,64,128]{2,1,0:T(8,128)S(1)} %pad_maximum_fusion.1.refs_0_), channel_id=1, source_target_pairs={{0,24},{8,16},{16,8},{24,0},{1,25},{9,17},{17,9},{25,1},{2,26},{10... | collective-permute-start | bytes 393224 | tf_op jit(solution)/shard_map/ppermute | solution.py:513
  31.8 6.6 %collective-permute-start.12 = (f32[4,64,128]{2,1,0:T(8,128)S(1)}, f32[4,64,128]{2,1,0:T(8,128)S(1)}, u32[]{:S(2)}, u32[]{:S(2)}) collective-permute-start(f32[4,64,128]{2,1,0:T(8,128)S(1)} %pad_maximum_fusion.1.refs_0_), channel_id=1, source_target_pairs={{0,16},{8,24},{16,0},{24,8},{1,17},{9,25},{17,1},{25,9},{2,18},{10... | collective-permute-start | bytes 393224 | tf_op jit(solution)/shard_map/ppermute | solution.py:513
  33.8 5.2 %collective-permute-start.11 = (f32[4,64,128]{2,1,0:T(8,128)S(1)}, f32[4,64,128]{2,1,0:T(8,128)S(1)}, u32[]{:S(2)}, u32[]{:S(2)}) collective-permute-start(f32[4,64,128]{2,1,0:T(8,128)S(1)} %pad_maximum_fusion.1.refs_0_), channel_id=1, source_target_pairs={{0,8},{8,0},{16,24},{24,16},{1,9},{9,1},{17,25},{25,17},{2,10},{10... | collective-permute-start | bytes 393224 | tf_op jit(solution)/shard_map/ppermute | solution.py:513
  33.9 5.1 %collective-permute-start.14 = (f32[4,64,128]{2,1,0:T(8,128)S(1)}, f32[4,64,128]{2,1,0:T(8,128)S(1)}, u32[]{:S(2)}, u32[]{:S(2)}) collective-permute-start(f32[4,64,128]{2,1,0:T(8,128)S(1)} %pad_maximum_fusion.1.refs_0_), channel_id=1, source_target_pairs={{0,4},{4,0},{1,5},{5,1},{2,6},{6,2},{3,7},{7,3},{8,12},{12,8},{9,1... | collective-permute-start | bytes 393224 | tf_op jit(solution)/shard_map/ppermute | solution.py:513
  37.3 1.7 %collective-permute-start.17 = (f32[4,64,128]{2,1,0:T(8,128)S(1)}, f32[4,64,128]{2,1,0:T(8,128)S(1)}, u32[]{:S(2)}, u32[]{:S(2)}) collective-permute-start(f32[4,64,128]{2,1,0:T(8,128)S(1)} %collective-permute-done.13.refs_3_), channel_id=1, source_target_pairs={{0,4},{4,0},{1,5},{5,1},{2,6},{6,2},{3,7},{7,3},{8,12},{12,8},{9,1... | collective-permute-start | bytes 393224 | tf_op jit(solution)/shard_map/ppermute | solution.py:513
  38.4 1.3 %collective-permute-start.16 = (f32[4,64,128]{2,1,0:T(8,128)S(1)}, f32[4,64,128]{2,1,0:T(8,128)S(1)}, u32[]{:S(2)}, u32[]{:S(2)}) collective-permute-start(f32[4,64,128]{2,1,0:T(8,128)S(1)} %collective-permute-done.12.refs_2_), channel_id=1, source_target_pairs={{0,4},{4,0},{1,5},{5,1},{2,6},{6,2},{3,7},{7,3},{8,12},{12,8},{9,1... | collective-permute-start | bytes 393224 | tf_op jit(solution)/shard_map/ppermute | solution.py:513
  39.0 1.3 %collective-permute-start.15 = (f32[4,64,128]{2,1,0:T(8,128)S(1)}, f32[4,64,128]{2,1,0:T(8,128)S(1)}, u32[]{:S(2)}, u32[]{:S(2)}) collective-permute-start(f32[4,64,128]{2,1,0:T(8,128)S(1)} %collective-permute-done.11.refs_1_), channel_id=1, source_target_pairs={{0,4},{4,0},{1,5},{5,1},{2,6},{6,2},{3,7},{7,3},{8,12},{12,8},{9,1... | collective-permute-start | bytes 393224 | tf_op jit(solution)/shard_map/ppermute | solution.py:513
  (5 other events, 40.8 us)

commit v18 on v16

--- a/solution.py
+++ b/solution.py
@@ -441,16 +441,24 @@
     return pairs.reshape((2 * value.shape[0],) + value.shape[1:])
 
 
-def sheet_cycle(source, coef, depth):
+def sheet_face_sets(coef):
+    face_sets = []
+    for level in range(2, LEVELS):
+        face_sets.append(sheet_faces(coef, 1 << (level - 2)))
+        if level < LEVELS - 1:
+            coef = 0.125 * sheet_down(coef, 1 << (level - 2))
+    return face_sets
+
+
+def sheet_cycle(source, face_sets, depth):
     stride = 1 << (depth - 2)
-    face_set = sheet_faces(coef, stride)
+    face_set = face_sets[depth - 2]
     estimate, residual, update = sheet_smooth(source, face_set)
     if depth == LEVELS - 1:
         return estimate
     residual = residual - sheet_apply(update, face_set)
     coarse_source = (4.0 / 8.0) * sheet_down(residual, stride)
-    correction = sheet_cycle(coarse_source, 0.125 * sheet_down(coef, stride), depth + 1)
-    estimate = estimate + sheet_up(correction, stride)
+    estimate = estimate + sheet_up(sheet_cycle(coarse_source, face_sets, depth + 1), stride)
     return sheet_smooth(source - sheet_apply(estimate, face_set), face_set, estimate)[0]
 
 
@@ -698,29 +706,31 @@
     link_x = jnp.where(lane == mid_x - 1, 0.0, 1.0)
     start, stop = PAD, PAD + mid_z
     plane_faces(mid_coef, mid_faces, start, stop, link_y, link_x, mid_source, mid_update, mid_z // 2)
-    ranges = [(start, stop)] * (DEGREE - 1)
-    plane_steps(mid_faces, ranges, mid_source, mid_residual, mid_update, mid_estimate, True, (mid_z, mid_z))
-
-    def finish_pairs(here, own):
-        before = mid_residual[here]
-
-        def store(value):
-            for target, whole in ((residual_pairs, before - value), (coef_pairs, mid_coef[here])):
-                whole = whole.reshape(mid_z // 2, 2, mid_y, mid_x)
-                target[...] = (whole[:, 0] + whole[:, 1]).reshape(target.shape)
-
-        return store
-
-    plane_sweep(mid_faces, start, stop, mid_update, finish_pairs, mid_z)
-
     for copy in copies:
         copy.wait()
     left_down, right_down, mid_left_up, mid_right_up = mid_refs
-    sheets = []
-    for ref, scale in ((residual_pairs, 4.0), (coef_pairs, 1.0)):
-        sheets.append(scale * times_right(times_left(left_down[...], ref[...]), right_down[...]))
     shape = (mid_z // 2, mid_y // 2, mid_x // 2)
-    correction = sheet_cycle(sheets[0].reshape(shape), sheets[1].reshape(shape), 2)
+
+    def pair_sums(whole, target):
+        whole = whole.reshape(mid_z // 2, 2, mid_y, mid_x)
+        target[...] = (whole[:, 0] + whole[:, 1]).reshape(target.shape)
+
+    def lowered(pairs):
+        return times_right(times_left(left_down[...], pairs[...]), right_down[...]).reshape(shape)
+
+    pair_sums(mid_coef[pl.ds(PAD, mid_z)], coef_pairs)
+    face_sets = sheet_face_sets(lowered(coef_pairs))
+
+    ranges = [(start, stop)] * (DEGREE - 1)
+    plane_steps(mid_faces, ranges, mid_source, mid_residual, mid_update, mid_estimate, True, (mid_z, mid_z))
+
+    def finish_pairs(here, own):
+        before = mid_residual[here]
+        return lambda value: pair_sums(before - value, residual_pairs)
+
+    plane_sweep(mid_faces, start, stop, mid_update, finish_pairs, mid_z)
+
+    correction = sheet_cycle(4.0 * lowered(residual_pairs), face_sets, 2)
     correction = correction.reshape(mid_z * mid_y // 4, mid_x // 2)
 
     raised = times_left(mid_left_up[...], times_right(correction, mid_right_up[...]))

time: 50.2 us -> 49.7 us (0.990)
    pallas_call x4, Pallas kernels: 14.5 us -> 14 us  [call(): pl.pallas_call(kernel, out_shape=tuple((jax.ShapeDtypeStruct(shape, F32)...]
where the time goes in v18:
time: 49.7 us; the launch traced here: 49.5 us
  starting transfers between devices  19.2 us (39%)
  waiting for transfers between devices  15.5 us (31%)
  Pallas kernels  14 us (28%)
  between operations  0.8 us (2%)
    ppermute x18, starting transfers between devices, swapped(): lax.ppermute(value, axes, [(int(source), int(target)) for source, target...  19.2 us
    ppermute x18, waiting for transfers between devices, swapped(): lax.ppermute(value, axes, [(int(source), int(target)) for source, target...  15.5 us
    pallas_call x4, Pallas kernels, call(): pl.pallas_call(kernel, out_shape=tuple((jax.ShapeDtypeStruct(shape, F32)...  14 us
  transfers between devices with their start and end apart: 18, of which 10 were waited for; matrix products, arithmetic and copies ran while one was open for 0% of the time, Pallas kernels for 0%

profile of v18, /device:TPU:0, one launch (start us, length us, event | category | flops | bytes accessed | tf_op | source)
XLA Modules:
  0.0 49.5 jit_solution(10236923363545252211)
XLA Ops:
  0.6 1.9 %start.1 = (f32[2,16,128]{2,1,0:T(8,128)}, f32[2,16,128]{2,1,0:T(8,128)}) custom-call(f32[16,16,128]{2,1,0:T(8,128)} %bitcast.10, f32[16,16,128]{2,1,0:T(8,128)} %coef.1), custom_call_target="tpu_custom_call" | custom-call | tf_op jit(solution)/shard_map/start/pallas_call | solution.py:785
  2.5 1.4 %collective-permute-start = (f32[2,16,128]{2,1,0:T(8,128)}, f32[2,16,128]{2,1,0:T(8,128)S(1)}, u32[]{:S(2)}, u32[]{:S(2)}) collective-permute-start(f32[2,16,128]{2,1,0:T(8,128)} %get-tuple-element.17), channel_id=1, source_target_pairs={{0,0},{8,16},{16,8},{24,24},{1,1},{9,17},{17,9},{25,25},{2,2},{10,... | collective-permute-start | bytes 49160 | tf_op jit(solution)/shard_map/ppermute | solution.py:517
  3.9 5.0 %collective-permute-start.1 = (f32[2,16,128]{2,1,0:T(8,128)}, f32[2,16,128]{2,1,0:T(8,128)S(1)}, u32[]{:S(2)}, u32[]{:S(2)}) collective-permute-start(f32[2,16,128]{2,1,0:T(8,128)} %get-tuple-element.18), channel_id=1, source_target_pairs={{0,8},{8,0},{16,24},{24,16},{1,9},{9,1},{17,25},{25,17},{2,10},{10... | collective-permute-start | bytes 49160 | tf_op jit(solution)/shard_map/ppermute | solution.py:517
  9.1 1.9 %collective-permute-done.1.x_a = f32[2,16,128]{2,1,0:T(8,128)S(1)} collective-permute-done((f32[2,16,128]{2,1,0:T(8,128)}, f32[2,16,128]{2,1,0:T(8,128)S(1)}, u32[]{:S(2)}, u32[]{:S(2)}) %collective-permute-start.1) | collective-permute-done | bytes 16416 | tf_op jit(solution)/shard_map/ppermute | solution.py:517
  11.0 1.6 %collective-permute-start.2 = (f32[15,16,128]{2,1,0:T(8,128)S(1)}, f32[15,16,128]{2,1,0:T(8,128)S(1)}, u32[]{:S(2)}, u32[]{:S(2)}) collective-permute-start(f32[15,16,128]{2,1,0:T(8,128)S(1)} %get-tuple-element.20), channel_id=1, source_target_pairs={{0,1},{1,0},{2,3},{3,2},{4,5},{5,4},{6,7},{7,6},{8,9},{9,8},{10,11... | collective-permute-start | bytes 368648 | tf_op jit(solution)/shard_map/ppermute | solution.py:517
  12.6 0.7 %collective-permute-start.3 = (f32[15,16,128]{2,1,0:T(8,128)S(1)}, f32[15,16,128]{2,1,0:T(8,128)S(1)}, u32[]{:S(2)}, u32[]{:S(2)}) collective-permute-start(f32[15,16,128]{2,1,0:T(8,128)S(1)} %get-tuple-element.21), channel_id=1, source_target_pairs={{0,0},{1,2},{2,1},{3,3},{4,4},{5,6},{6,5},{7,7},{8,8},{9,10},{10,9... | collective-permute-start | bytes 368648 | tf_op jit(solution)/shard_map/ppermute | solution.py:517
  13.3 2.6 %collective-permute-done.2.refs_2_ = f32[15,16,128]{2,1,0:T(8,128)S(1)} collective-permute-done((f32[15,16,128]{2,1,0:T(8,128)S(1)}, f32[15,16,128]{2,1,0:T(8,128)S(1)}, u32[]{:S(2)}, u32[]{:S(2)}) %collective-permute-start.2) | collective-permute-done | bytes 122912 | tf_op jit(solution)/shard_map/ppermute | solution.py:517
  15.9 0.5 %collective-permute-start.7 = (f32[15,16,128]{2,1,0:T(8,128)S(1)}, f32[15,16,128]{2,1,0:T(8,128)S(1)}, u32[]{:S(2)}, u32[]{:S(2)}) collective-permute-start(f32[15,16,128]{2,1,0:T(8,128)S(1)} %collective-permute-done.3.refs_3_), channel_id=1, source_target_pairs={{0,4},{4,0},{1,5},{5,1},{2,6},{6,2},{3,7},{7,3},{8,12},{12,8},{9,1... | collective-permute-start | bytes 368648 | tf_op jit(solution)/shard_map/ppermute | solution.py:517
  16.5 1.1 %collective-permute-done.5.refs_5_ = f32[2,2,16,128]{3,2,1,0:T(8,128)S(1)} collective-permute-done((f32[2,2,16,128]{3,2,1,0:T(8,128)S(1)}, f32[2,2,16,128]{3,2,1,0:T(8,128)S(1)}, u32[]{:S(2)}, u32[]{:S(2)}) %collective-permute-start.5) | collective-permute-done | bytes 32800 | tf_op jit(solution)/shard_map/ppermute | solution.py:517
  17.7 2.9 %first.1 = (f32[64,128]{1,0:T(8,128)S(1)}, f32[32,24,256]{2,1,0:T(8,128)S(1)}, f32[32,24,256]{2,1,0:T(8,128)S(1)}, f32[32,24,256]{2,1,0:T(8,128)S(1)}, f32[32,24...) custom-call(f32[2,16,16,128]{3,2,1,0:T(8,128)S(1)} %pad_maximum_fusion., ...), custom_call_target="tpu_custom_call" | custom-call | tf_op jit(solution)/shard_map/first/pallas_call | solution.py:785
  20.6 3.6 %collective-permute-start.10 = (f32[64,128]{1,0:T(8,128)S(1)}, f32[64,128]{1,0:T(8,128)S(1)}, u32[]{:S(2)}, u32[]{:S(2)}) collective-permute-start(f32[64,128]{1,0:T(8,128)S(1)} %get-tuple-element.22), channel_id=1, source_target_pairs={{0,3},{1,2},{2,1},{3,0},{4,7},{5,6},{6,5},{7,4},{8,11},{9,10},{10,... | collective-permute-start | bytes 98312 | tf_op jit(solution)/shard_map/ppermute | solution.py:517
  24.2 2.1 %collective-permute-start.9 = (f32[64,128]{1,0:T(8,128)S(1)}, f32[64,128]{1,0:T(8,128)S(1)}, u32[]{:S(2)}, u32[]{:S(2)}) collective-permute-start(f32[64,128]{1,0:T(8,128)S(1)} %get-tuple-element.22), channel_id=1, source_target_pairs={{0,2},{1,3},{2,0},{3,1},{4,6},{5,7},{6,4},{7,5},{8,10},{9,11},{10,... | collective-permute-start | bytes 98312 | tf_op jit(solution)/shard_map/ppermute | solution.py:517
  26.4 0.5 %collective-permute-start.8 = (f32[64,128]{1,0:T(8,128)S(1)}, f32[64,128]{1,0:T(8,128)S(1)}, u32[]{:S(2)}, u32[]{:S(2)}) collective-permute-start(f32[64,128]{1,0:T(8,128)S(1)} %get-tuple-element.22), channel_id=1, source_target_pairs={{0,1},{1,0},{2,3},{3,2},{4,5},{5,4},{6,7},{7,6},{8,9},{9,8},{10,11... | collective-permute-start | bytes 98312 | tf_op jit(solution)/shard_map/ppermute | solution.py:517
  26.9 2.1 %collective-permute-done.9 = f32[64,128]{1,0:T(8,128)S(1)} collective-permute-done((f32[64,128]{1,0:T(8,128)S(1)}, f32[64,128]{1,0:T(8,128)S(1)}, u32[]{:S(2)}, u32[]{:S(2)}) %collective-permute-start.9) | collective-permute-done | bytes 32800 | tf_op jit(solution)/shard_map/ppermute | solution.py:517
  29.1 1.2 %collective-permute-done.8 = f32[64,128]{1,0:T(8,128)S(1)} collective-permute-done((f32[64,128]{1,0:T(8,128)S(1)}, f32[64,128]{1,0:T(8,128)S(1)}, u32[]{:S(2)}, u32[]{:S(2)}) %collective-permute-start.8) | collective-permute-done | bytes 32800 | tf_op jit(solution)/shard_map/ppermute | solution.py:517
  30.3 1.5 %collective-permute-start.13 = (f32[4,64,128]{2,1,0:T(8,128)S(1)}, f32[4,64,128]{2,1,0:T(8,128)S(1)}, u32[]{:S(2)}, u32[]{:S(2)}) collective-permute-start(f32[4,64,128]{2,1,0:T(8,128)S(1)} %pad_maximum_fusion.1.refs_0_), channel_id=1, source_target_pairs={{0,24},{8,16},{16,8},{24,0},{1,25},{9,17},{17,9},{25,1},{2,26},{10... | collective-permute-start | bytes 393224 | tf_op jit(solution)/shard_map/ppermute | solution.py:517
  31.8 2.0 %collective-permute-start.12 = (f32[4,64,128]{2,1,0:T(8,128)S(1)}, f32[4,64,128]{2,1,0:T(8,128)S(1)}, u32[]{:S(2)}, u32[]{:S(2)}) collective-permute-start(f32[4,64,128]{2,1,0:T(8,128)S(1)} %pad_maximum_fusion.1.refs_0_), channel_id=1, source_target_pairs={{0,16},{8,24},{16,0},{24,8},{1,17},{9,25},{17,1},{25,9},{2,18},{10... | collective-permute-start | bytes 393224 | tf_op jit(solution)/shard_map/ppermute | solution.py:517
  33.8 0.1 collective-permute-start.11
  33.9 3.4 %collective-permute-done.13.refs_3_ = f32[4,64,128]{2,1,0:T(8,128)S(1)} collective-permute-done((f32[4,64,128]{2,1,0:T(8,128)S(1)}, f32[4,64,128]{2,1,0:T(8,128)S(1)}, u32[]{:S(2)}, u32[]{:S(2)}) %collective-permute-start.13) | collective-permute-done | bytes 131104 | tf_op jit(solution)/shard_map/ppermute | solution.py:517
  37.3 1.1 %collective-permute-done.12.refs_2_ = f32[4,64,128]{2,1,0:T(8,128)S(1)} collective-permute-done((f32[4,64,128]{2,1,0:T(8,128)S(1)}, f32[4,64,128]{2,1,0:T(8,128)S(1)}, u32[]{:S(2)}, u32[]{:S(2)}) %collective-permute-start.12) | collective-permute-done | bytes 131104 | tf_op jit(solution)/shard_map/ppermute | solution.py:517
  38.4 0.5 %collective-permute-done.11.refs_1_ = f32[4,64,128]{2,1,0:T(8,128)S(1)} collective-permute-done((f32[4,64,128]{2,1,0:T(8,128)S(1)}, f32[4,64,128]{2,1,0:T(8,128)S(1)}, u32[]{:S(2)}, u32[]{:S(2)}) %collective-permute-start.11) | collective-permute-done | bytes 131104 | tf_op jit(solution)/shard_map/ppermute | solution.py:517
  39.0 0.8 %collective-permute-done.16.refs_6_ = f32[4,64,128]{2,1,0:T(8,128)S(1)} collective-permute-done((f32[4,64,128]{2,1,0:T(8,128)S(1)}, f32[4,64,128]{2,1,0:T(8,128)S(1)}, u32[]{:S(2)}, u32[]{:S(2)}) %collective-permute-start.16) | collective-permute-done | bytes 131104 | tf_op jit(solution)/shard_map/ppermute | solution.py:517
  39.8 0.5 %collective-permute-done.15.refs_5_ = f32[4,64,128]{2,1,0:T(8,128)S(1)} collective-permute-done((f32[4,64,128]{2,1,0:T(8,128)S(1)}, f32[4,64,128]{2,1,0:T(8,128)S(1)}, u32[]{:S(2)}, u32[]{:S(2)}) %collective-permute-start.15) | collective-permute-done | bytes 131104 | tf_op jit(solution)/shard_map/ppermute | solution.py:517
  40.4 9.1 %second.1 = (f32[16,16,128]{2,1,0:T(8,128)}, f32[16,16,128]{2,1,0:T(8,128)}) custom-call(f32[4,64,128]{2,1,0:T(8,128)S(1)} %pad_maximum_fusion.1.refs_0_, f32[4,64,128]{2,1,0:T(8,128)S(1)} %collective-permute-done.11.refs_1_, f32[4,64,128]{2,1,0:T(8,128)S(1)} %collective-permute-done.12.refs_2_, f32[4,64,128]{2,1,0:T(8,128)S(1)} %collective-permute-done.13.refs_3_, ...), custom_call_target="tpu_custom_call" | custom-call | tf_op jit(solution)/shard_map/second/pallas_call | solution.py:785
  (40 shorter events, 0.3 us)
Async XLA Ops:
  2.5 6.5 %collective-permute-start = (f32[2,16,128]{2,1,0:T(8,128)}, f32[2,16,128]{2,1,0:T(8,128)S(1)}, u32[]{:S(2)}, u32[]{:S(2)}) collective-permute-start(f32[2,16,128]{2,1,0:T(8,128)} %get-tuple-element.17), channel_id=1, source_target_pairs={{0,0},{8,16},{16,8},{24,24},{1,1},{9,17},{17,9},{25,25},{2,2},{10,... | collective-permute-start | bytes 49160 | tf_op jit(solution)/shard_map/ppermute | solution.py:517
  3.9 7.0 %collective-permute-start.1 = (f32[2,16,128]{2,1,0:T(8,128)}, f32[2,16,128]{2,1,0:T(8,128)S(1)}, u32[]{:S(2)}, u32[]{:S(2)}) collective-permute-start(f32[2,16,128]{2,1,0:T(8,128)} %get-tuple-element.18), channel_id=1, source_target_pairs={{0,8},{8,0},{16,24},{24,16},{1,9},{9,1},{17,25},{25,17},{2,10},{10... | collective-permute-start | bytes 49160 | tf_op jit(solution)/shard_map/ppermute | solution.py:517
  9.0 8.7 %collective-permute-start.4 = (f32[2,16,16,128]{3,2,1,0:T(8,128)S(1)}, f32[2,16,16,128]{3,2,1,0:T(8,128)S(1)}, u32[]{:S(2)}, u32[]{:S(2)}) collective-permute-start(f32[2,16,16,128]{3,2,1,0:T(8,128)S(1)} %pad_maximum_fusion.own.refs_0_), channel_id=1, source_target_pairs={{0,4},{4,0},{1,5},{5,1},{2,6},{6,2},{3,7},{7,3},{8,12},{12,8},{9,1... | collective-permute-start | bytes 786440 | tf_op jit(solution)/shard_map/ppermute | solution.py:517
  11.0 4.9 %collective-permute-start.2 = (f32[15,16,128]{2,1,0:T(8,128)S(1)}, f32[15,16,128]{2,1,0:T(8,128)S(1)}, u32[]{:S(2)}, u32[]{:S(2)}) collective-permute-start(f32[15,16,128]{2,1,0:T(8,128)S(1)} %get-tuple-element.20), channel_id=1, source_target_pairs={{0,1},{1,0},{2,3},{3,2},{4,5},{5,4},{6,7},{7,6},{8,9},{9,8},{10,11... | collective-permute-start | bytes 368648 | tf_op jit(solution)/shard_map/ppermute | solution.py:517
  12.6 3.3 %collective-permute-start.3 = (f32[15,16,128]{2,1,0:T(8,128)S(1)}, f32[15,16,128]{2,1,0:T(8,128)S(1)}, u32[]{:S(2)}, u32[]{:S(2)}) collective-permute-start(f32[15,16,128]{2,1,0:T(8,128)S(1)} %get-tuple-element.21), channel_id=1, source_target_pairs={{0,0},{1,2},{2,1},{3,3},{4,4},{5,6},{6,5},{7,7},{8,8},{9,10},{10,9... | collective-permute-start | bytes 368648 | tf_op jit(solution)/shard_map/ppermute | solution.py:517
  15.9 1.7 %collective-permute-start.6 = (f32[15,16,128]{2,1,0:T(8,128)S(1)}, f32[15,16,128]{2,1,0:T(8,128)S(1)}, u32[]{:S(2)}, u32[]{:S(2)}) collective-permute-start(f32[15,16,128]{2,1,0:T(8,128)S(1)} %collective-permute-done.2.refs_2_), channel_id=1, source_target_pairs={{0,4},{4,0},{1,5},{5,1},{2,6},{6,2},{3,7},{7,3},{8,12},{12,8},{9,1... | collective-permute-start | bytes 368648 | tf_op jit(solution)/shard_map/ppermute | solution.py:517
  15.9 1.7 %collective-permute-start.7 = (f32[15,16,128]{2,1,0:T(8,128)S(1)}, f32[15,16,128]{2,1,0:T(8,128)S(1)}, u32[]{:S(2)}, u32[]{:S(2)}) collective-permute-start(f32[15,16,128]{2,1,0:T(8,128)S(1)} %collective-permute-done.3.refs_3_), channel_id=1, source_target_pairs={{0,4},{4,0},{1,5},{5,1},{2,6},{6,2},{3,7},{7,3},{8,12},{12,8},{9,1... | collective-permute-start | bytes 368648 | tf_op jit(solution)/shard_map/ppermute | solution.py:517
  16.4 23.9 %copy-start = (bf16[4,256,256]{2,1,0:T(8,128)(2,1)S(1)}, bf16[4,256,256]{2,1,0:T(8,128)(2,1)}, u32[]{:S(2)}) copy-start(bf16[4,256,256]{2,1,0:T(8,128)(2,1)} %constant.22.clone.refs_16_) | copy-start | bytes 1572868
  16.4 1.2 %collective-permute-start.5 = (f32[2,2,16,128]{3,2,1,0:T(8,128)S(1)}, f32[2,2,16,128]{3,2,1,0:T(8,128)S(1)}, u32[]{:S(2)}, u32[]{:S(2)}) collective-permute-start(f32[2,2,16,128]{3,2,1,0:T(8,128)S(1)} %get-tuple-element.19.refs_1_), channel_id=1, source_target_pairs={{0,4},{4,0},{1,5},{5,1},{2,6},{6,2},{3,7},{7,3},{8,12},{12,8},{9,1... | collective-permute-start | bytes 98312 | tf_op jit(solution)/shard_map/ppermute | solution.py:517
  17.7 22.6 %copy-start.1 = (bf16[2,336,224]{2,1,0:T(8,128)(2,1)S(1)}, bf16[2,336,224]{2,1,0:T(8,128)(2,1)}, u32[]{:S(2)}) copy-start(bf16[2,336,224]{2,1,0:T(8,128)(2,1)} %constant.21.clone.refs_15_) | copy-start | bytes 903172
  20.6 6.3 %collective-permute-start.10 = (f32[64,128]{1,0:T(8,128)S(1)}, f32[64,128]{1,0:T(8,128)S(1)}, u32[]{:S(2)}, u32[]{:S(2)}) collective-permute-start(f32[64,128]{1,0:T(8,128)S(1)} %get-tuple-element.22), channel_id=1, source_target_pairs={{0,3},{1,2},{2,1},{3,0},{4,7},{5,6},{6,5},{7,4},{8,11},{9,10},{10,... | collective-permute-start | bytes 98312 | tf_op jit(solution)/shard_map/ppermute | solution.py:517
  24.2 4.8 %collective-permute-start.9 = (f32[64,128]{1,0:T(8,128)S(1)}, f32[64,128]{1,0:T(8,128)S(1)}, u32[]{:S(2)}, u32[]{:S(2)}) collective-permute-start(f32[64,128]{1,0:T(8,128)S(1)} %get-tuple-element.22), channel_id=1, source_target_pairs={{0,2},{1,3},{2,0},{3,1},{4,6},{5,7},{6,4},{7,5},{8,10},{9,11},{10,... | collective-permute-start | bytes 98312 | tf_op jit(solution)/shard_map/ppermute | solution.py:517
  26.4 3.9 %collective-permute-start.8 = (f32[64,128]{1,0:T(8,128)S(1)}, f32[64,128]{1,0:T(8,128)S(1)}, u32[]{:S(2)}, u32[]{:S(2)}) collective-permute-start(f32[64,128]{1,0:T(8,128)S(1)} %get-tuple-element.22), channel_id=1, source_target_pairs={{0,1},{1,0},{2,3},{3,2},{4,5},{5,4},{6,7},{7,6},{8,9},{9,8},{10,11... | collective-permute-start | bytes 98312 | tf_op jit(solution)/shard_map/ppermute | solution.py:517
  30.3 10.0 %copy-start.2 = (bf16[128,256]{1,0:T(8,128)(2,1)S(1)}, bf16[128,256]{1,0:T(8,128)(2,1)}, u32[]{:S(2)}) copy-start(bf16[128,256]{1,0:T(8,128)(2,1)} %constant.26.clone.refs_20_) | copy-start | bytes 196612
  30.3 10.0 %copy-start.3 = (bf16[256,128]{1,0:T(8,128)(2,1)S(1)}, bf16[256,128]{1,0:T(8,128)(2,1)}, u32[]{:S(2)}) copy-start(bf16[256,128]{1,0:T(8,128)(2,1)} %constant.25.clone.refs_19_) | copy-start | bytes 196612
  30.3 10.0 %copy-start.4 = (bf16[256,128]{1,0:T(8,128)(2,1)S(1)}, bf16[256,128]{1,0:T(8,128)(2,1)}, u32[]{:S(2)}) copy-start(bf16[256,128]{1,0:T(8,128)(2,1)} %constant.24.clone.refs_18_) | copy-start | bytes 196612
  30.3 10.0 %copy-start.5 = (bf16[128,256]{1,0:T(8,128)(2,1)S(1)}, bf16[128,256]{1,0:T(8,128)(2,1)}, u32[]{:S(2)}) copy-start(bf16[128,256]{1,0:T(8,128)(2,1)} %constant.23.clone.refs_17_) | copy-start | bytes 196612
  30.3 7.0 %collective-permute-start.13 = (f32[4,64,128]{2,1,0:T(8,128)S(1)}, f32[4,64,128]{2,1,0:T(8,128)S(1)}, u32[]{:S(2)}, u32[]{:S(2)}) collective-permute-start(f32[4,64,128]{2,1,0:T(8,128)S(1)} %pad_maximum_fusion.1.refs_0_), channel_id=1, source_target_pairs={{0,24},{8,16},{16,8},{24,0},{1,25},{9,17},{17,9},{25,1},{2,26},{10... | collective-permute-start | bytes 393224 | tf_op jit(solution)/shard_map/ppermute | solution.py:517
  31.8 6.6 %collective-permute-start.12 = (f32[4,64,128]{2,1,0:T(8,128)S(1)}, f32[4,64,128]{2,1,0:T(8,128)S(1)}, u32[]{:S(2)}, u32[]{:S(2)}) collective-permute-start(f32[4,64,128]{2,1,0:T(8,128)S(1)} %pad_maximum_fusion.1.refs_0_), channel_id=1, source_target_pairs={{0,16},{8,24},{16,0},{24,8},{1,17},{9,25},{17,1},{25,9},{2,18},{10... | collective-permute-start | bytes 393224 | tf_op jit(solution)/shard_map/ppermute | solution.py:517
  33.8 5.2 %collective-permute-start.11 = (f32[4,64,128]{2,1,0:T(8,128)S(1)}, f32[4,64,128]{2,1,0:T(8,128)S(1)}, u32[]{:S(2)}, u32[]{:S(2)}) collective-permute-start(f32[4,64,128]{2,1,0:T(8,128)S(1)} %pad_maximum_fusion.1.refs_0_), channel_id=1, source_target_pairs={{0,8},{8,0},{16,24},{24,16},{1,9},{9,1},{17,25},{25,17},{2,10},{10... | collective-permute-start | bytes 393224 | tf_op jit(solution)/shard_map/ppermute | solution.py:517
  33.9 5.1 %collective-permute-start.14 = (f32[4,64,128]{2,1,0:T(8,128)S(1)}, f32[4,64,128]{2,1,0:T(8,128)S(1)}, u32[]{:S(2)}, u32[]{:S(2)}) collective-permute-start(f32[4,64,128]{2,1,0:T(8,128)S(1)} %pad_maximum_fusion.1.refs_0_), channel_id=1, source_target_pairs={{0,4},{4,0},{1,5},{5,1},{2,6},{6,2},{3,7},{7,3},{8,12},{12,8},{9,1... | collective-permute-start | bytes 393224 | tf_op jit(solution)/shard_map/ppermute | solution.py:517
  37.3 1.7 %collective-permute-start.17 = (f32[4,64,128]{2,1,0:T(8,128)S(1)}, f32[4,64,128]{2,1,0:T(8,128)S(1)}, u32[]{:S(2)}, u32[]{:S(2)}) collective-permute-start(f32[4,64,128]{2,1,0:T(8,128)S(1)} %collective-permute-done.13.refs_3_), channel_id=1, source_target_pairs={{0,4},{4,0},{1,5},{5,1},{2,6},{6,2},{3,7},{7,3},{8,12},{12,8},{9,1... | collective-permute-start | bytes 393224 | tf_op jit(solution)/shard_map/ppermute | solution.py:517
  38.4 1.3 %collective-permute-start.16 = (f32[4,64,128]{2,1,0:T(8,128)S(1)}, f32[4,64,128]{2,1,0:T(8,128)S(1)}, u32[]{:S(2)}, u32[]{:S(2)}) collective-permute-start(f32[4,64,128]{2,1,0:T(8,128)S(1)} %collective-permute-done.12.refs_2_), channel_id=1, source_target_pairs={{0,4},{4,0},{1,5},{5,1},{2,6},{6,2},{3,7},{7,3},{8,12},{12,8},{9,1... | collective-permute-start | bytes 393224 | tf_op jit(solution)/shard_map/ppermute | solution.py:517
  39.0 1.3 %collective-permute-start.15 = (f32[4,64,128]{2,1,0:T(8,128)S(1)}, f32[4,64,128]{2,1,0:T(8,128)S(1)}, u32[]{:S(2)}, u32[]{:S(2)}) collective-permute-start(f32[4,64,128]{2,1,0:T(8,128)S(1)} %collective-permute-done.11.refs_1_), channel_id=1, source_target_pairs={{0,4},{4,0},{1,5},{5,1},{2,6},{6,2},{3,7},{7,3},{8,12},{12,8},{9,1... | collective-permute-start | bytes 393224 | tf_op jit(solution)/shard_map/ppermute | solution.py:517
  (5 other events, 40.8 us)

commit v19 on v18

--- a/solution.py
+++ b/solution.py
@@ -641,18 +641,20 @@
     fill_window(own, got, far, source, coef, *counts)
     planes, rows, lanes = source.shape
     own_y = rows - HALO_Y
+
+    def gather_pairs(ref, target):
+        for pair in range((planes - 2 * HALO_Z) // 2):
+            low = HALO_Z + 2 * pair
+            target[pl.ds(pair * own_y, own_y)] = ref[low, :own_y, :128] + ref[low + 1, :own_y, :128]
+
+    gather_pairs(coef, pair_coef)
+    message[...] = times_right(times_left(left[...], pair_coef[...]), right_coef[...])
     plane_faces(coef, faces, 2, planes - 2, link_mask(rows, lanes), None, source, update, planes // 2 - 2)
     ranges = [(3, planes - 3), (4, planes - 4)]
     plane_steps(faces, ranges, source, residual, update, estimate, True, (planes - 6, planes - 8))
     plane_residual(faces, HALO_Z, planes - HALO_Z, residual, update, 16)
-    for pair in range((planes - 2 * HALO_Z) // 2):
-        low = HALO_Z + 2 * pair
-        target = pl.ds(pair * own_y, own_y)
-        pair_source[target] = residual[low, :own_y, :128] + residual[low + 1, :own_y, :128]
-        pair_coef[target] = coef[low, :own_y, :128] + coef[low + 1, :own_y, :128]
-    message[...] = times_right(times_left(left[...], pair_source[...]), right_source[...]) + times_right(
-        times_left(left[...], pair_coef[...]), right_coef[...]
-    )
+    gather_pairs(residual, pair_source)
+    message[...] = message[...] + times_right(times_left(left[...], pair_source[...]), right_source[...])
 
 
 def second_kernel(counts, matrix_count, *refs):

time: 49.7 us -> 49.7 us (level)
  no operation moved by 1% of the time
where the time goes in v19:
time: 49.7 us; the launch traced here: 49.5 us
  starting transfers between devices  19.2 us (39%)
  waiting for transfers between devices  15.5 us (31%)
  Pallas kernels  14 us (28%)
  between operations  0.8 us (2%)
    ppermute x18, starting transfers between devices, swapped(): lax.ppermute(value, axes, [(int(source), int(target)) for source, target...  19.2 us
    ppermute x18, waiting for transfers between devices, swapped(): lax.ppermute(value, axes, [(int(source), int(target)) for source, target...  15.5 us
    pallas_call x4, Pallas kernels, call(): pl.pallas_call(kernel, out_shape=tuple((jax.ShapeDtypeStruct(shape, F32)...  14 us
  transfers between devices with their start and end apart: 18, of which 10 were waited for; matrix products, arithmetic and copies ran while one was open for 0% of the time, Pallas kernels for 0%

profile of v19, /device:TPU:0, one launch (start us, length us, event | category | flops | bytes accessed | tf_op | source)
XLA Modules:
  0.0 49.5 jit_solution(16152541468786214718)
XLA Ops:
  0.6 1.9 %start.1 = (f32[2,16,128]{2,1,0:T(8,128)}, f32[2,16,128]{2,1,0:T(8,128)}) custom-call(f32[16,16,128]{2,1,0:T(8,128)} %bitcast.10, f32[16,16,128]{2,1,0:T(8,128)} %coef.1), custom_call_target="tpu_custom_call" | custom-call | tf_op jit(solution)/shard_map/start/pallas_call | solution.py:787
  2.5 1.4 %collective-permute-start = (f32[2,16,128]{2,1,0:T(8,128)}, f32[2,16,128]{2,1,0:T(8,128)S(1)}, u32[]{:S(2)}, u32[]{:S(2)}) collective-permute-start(f32[2,16,128]{2,1,0:T(8,128)} %get-tuple-element.17), channel_id=1, source_target_pairs={{0,0},{8,16},{16,8},{24,24},{1,1},{9,17},{17,9},{25,25},{2,2},{10,... | collective-permute-start | bytes 49160 | tf_op jit(solution)/shard_map/ppermute | solution.py:517
  3.9 5.0 %collective-permute-start.1 = (f32[2,16,128]{2,1,0:T(8,128)}, f32[2,16,128]{2,1,0:T(8,128)S(1)}, u32[]{:S(2)}, u32[]{:S(2)}) collective-permute-start(f32[2,16,128]{2,1,0:T(8,128)} %get-tuple-element.18), channel_id=1, source_target_pairs={{0,8},{8,0},{16,24},{24,16},{1,9},{9,1},{17,25},{25,17},{2,10},{10... | collective-permute-start | bytes 49160 | tf_op jit(solution)/shard_map/ppermute | solution.py:517
  9.1 1.9 %collective-permute-done.1.x_a = f32[2,16,128]{2,1,0:T(8,128)S(1)} collective-permute-done((f32[2,16,128]{2,1,0:T(8,128)}, f32[2,16,128]{2,1,0:T(8,128)S(1)}, u32[]{:S(2)}, u32[]{:S(2)}) %collective-permute-start.1) | collective-permute-done | bytes 16416 | tf_op jit(solution)/shard_map/ppermute | solution.py:517
  11.0 1.6 %collective-permute-start.2 = (f32[15,16,128]{2,1,0:T(8,128)S(1)}, f32[15,16,128]{2,1,0:T(8,128)S(1)}, u32[]{:S(2)}, u32[]{:S(2)}) collective-permute-start(f32[15,16,128]{2,1,0:T(8,128)S(1)} %get-tuple-element.20), channel_id=1, source_target_pairs={{0,1},{1,0},{2,3},{3,2},{4,5},{5,4},{6,7},{7,6},{8,9},{9,8},{10,11... | collective-permute-start | bytes 368648 | tf_op jit(solution)/shard_map/ppermute | solution.py:517
  12.6 0.7 %collective-permute-start.3 = (f32[15,16,128]{2,1,0:T(8,128)S(1)}, f32[15,16,128]{2,1,0:T(8,128)S(1)}, u32[]{:S(2)}, u32[]{:S(2)}) collective-permute-start(f32[15,16,128]{2,1,0:T(8,128)S(1)} %get-tuple-element.21), channel_id=1, source_target_pairs={{0,0},{1,2},{2,1},{3,3},{4,4},{5,6},{6,5},{7,7},{8,8},{9,10},{10,9... | collective-permute-start | bytes 368648 | tf_op jit(solution)/shard_map/ppermute | solution.py:517
  13.3 2.6 %collective-permute-done.2.refs_2_ = f32[15,16,128]{2,1,0:T(8,128)S(1)} collective-permute-done((f32[15,16,128]{2,1,0:T(8,128)S(1)}, f32[15,16,128]{2,1,0:T(8,128)S(1)}, u32[]{:S(2)}, u32[]{:S(2)}) %collective-permute-start.2) | collective-permute-done | bytes 122912 | tf_op jit(solution)/shard_map/ppermute | solution.py:517
  15.9 0.5 %collective-permute-start.7 = (f32[15,16,128]{2,1,0:T(8,128)S(1)}, f32[15,16,128]{2,1,0:T(8,128)S(1)}, u32[]{:S(2)}, u32[]{:S(2)}) collective-permute-start(f32[15,16,128]{2,1,0:T(8,128)S(1)} %collective-permute-done.3.refs_3_), channel_id=1, source_target_pairs={{0,4},{4,0},{1,5},{5,1},{2,6},{6,2},{3,7},{7,3},{8,12},{12,8},{9,1... | collective-permute-start | bytes 368648 | tf_op jit(solution)/shard_map/ppermute | solution.py:517
  16.5 1.1 %collective-permute-done.5.refs_5_ = f32[2,2,16,128]{3,2,1,0:T(8,128)S(1)} collective-permute-done((f32[2,2,16,128]{3,2,1,0:T(8,128)S(1)}, f32[2,2,16,128]{3,2,1,0:T(8,128)S(1)}, u32[]{:S(2)}, u32[]{:S(2)}) %collective-permute-start.5) | collective-permute-done | bytes 32800 | tf_op jit(solution)/shard_map/ppermute | solution.py:517
  17.7 2.9 %first.1 = (f32[64,128]{1,0:T(8,128)S(1)}, f32[32,24,256]{2,1,0:T(8,128)S(1)}, f32[32,24,256]{2,1,0:T(8,128)S(1)}, f32[32,24,256]{2,1,0:T(8,128)S(1)}, f32[32,24...) custom-call(f32[2,16,16,128]{3,2,1,0:T(8,128)S(1)} %pad_maximum_fusion., ...), custom_call_target="tpu_custom_call" | custom-call | tf_op jit(solution)/shard_map/first/pallas_call | solution.py:787
  20.6 3.6 %collective-permute-start.10 = (f32[64,128]{1,0:T(8,128)S(1)}, f32[64,128]{1,0:T(8,128)S(1)}, u32[]{:S(2)}, u32[]{:S(2)}) collective-permute-start(f32[64,128]{1,0:T(8,128)S(1)} %get-tuple-element.22), channel_id=1, source_target_pairs={{0,3},{1,2},{2,1},{3,0},{4,7},{5,6},{6,5},{7,4},{8,11},{9,10},{10,... | collective-permute-start | bytes 98312 | tf_op jit(solution)/shard_map/ppermute | solution.py:517
  24.3 2.1 %collective-permute-start.9 = (f32[64,128]{1,0:T(8,128)S(1)}, f32[64,128]{1,0:T(8,128)S(1)}, u32[]{:S(2)}, u32[]{:S(2)}) collective-permute-start(f32[64,128]{1,0:T(8,128)S(1)} %get-tuple-element.22), channel_id=1, source_target_pairs={{0,2},{1,3},{2,0},{3,1},{4,6},{5,7},{6,4},{7,5},{8,10},{9,11},{10,... | collective-permute-start | bytes 98312 | tf_op jit(solution)/shard_map/ppermute | solution.py:517
  26.4 0.5 %collective-permute-start.8 = (f32[64,128]{1,0:T(8,128)S(1)}, f32[64,128]{1,0:T(8,128)S(1)}, u32[]{:S(2)}, u32[]{:S(2)}) collective-permute-start(f32[64,128]{1,0:T(8,128)S(1)} %get-tuple-element.22), channel_id=1, source_target_pairs={{0,1},{1,0},{2,3},{3,2},{4,5},{5,4},{6,7},{7,6},{8,9},{9,8},{10,11... | collective-permute-start | bytes 98312 | tf_op jit(solution)/shard_map/ppermute | solution.py:517
  26.9 2.1 %collective-permute-done.9 = f32[64,128]{1,0:T(8,128)S(1)} collective-permute-done((f32[64,128]{1,0:T(8,128)S(1)}, f32[64,128]{1,0:T(8,128)S(1)}, u32[]{:S(2)}, u32[]{:S(2)}) %collective-permute-start.9) | collective-permute-done | bytes 32800 | tf_op jit(solution)/shard_map/ppermute | solution.py:517
  29.1 1.2 %collective-permute-done.8 = f32[64,128]{1,0:T(8,128)S(1)} collective-permute-done((f32[64,128]{1,0:T(8,128)S(1)}, f32[64,128]{1,0:T(8,128)S(1)}, u32[]{:S(2)}, u32[]{:S(2)}) %collective-permute-start.8) | collective-permute-done | bytes 32800 | tf_op jit(solution)/shard_map/ppermute | solution.py:517
  30.4 1.5 %collective-permute-start.13 = (f32[4,64,128]{2,1,0:T(8,128)S(1)}, f32[4,64,128]{2,1,0:T(8,128)S(1)}, u32[]{:S(2)}, u32[]{:S(2)}) collective-permute-start(f32[4,64,128]{2,1,0:T(8,128)S(1)} %pad_maximum_fusion.1.refs_0_), channel_id=1, source_target_pairs={{0,24},{8,16},{16,8},{24,0},{1,25},{9,17},{17,9},{25,1},{2,26},{10... | collective-permute-start | bytes 393224 | tf_op jit(solution)/shard_map/ppermute | solution.py:517
  31.9 2.0 %collective-permute-start.12 = (f32[4,64,128]{2,1,0:T(8,128)S(1)}, f32[4,64,128]{2,1,0:T(8,128)S(1)}, u32[]{:S(2)}, u32[]{:S(2)}) collective-permute-start(f32[4,64,128]{2,1,0:T(8,128)S(1)} %pad_maximum_fusion.1.refs_0_), channel_id=1, source_target_pairs={{0,16},{8,24},{16,0},{24,8},{1,17},{9,25},{17,1},{25,9},{2,18},{10... | collective-permute-start | bytes 393224 | tf_op jit(solution)/shard_map/ppermute | solution.py:517
  33.8 0.1 collective-permute-start.11
  33.9 3.4 %collective-permute-done.13.refs_3_ = f32[4,64,128]{2,1,0:T(8,128)S(1)} collective-permute-done((f32[4,64,128]{2,1,0:T(8,128)S(1)}, f32[4,64,128]{2,1,0:T(8,128)S(1)}, u32[]{:S(2)}, u32[]{:S(2)}) %collective-permute-start.13) | collective-permute-done | bytes 131104 | tf_op jit(solution)/shard_map/ppermute | solution.py:517
  37.3 1.1 %collective-permute-done.12.refs_2_ = f32[4,64,128]{2,1,0:T(8,128)S(1)} collective-permute-done((f32[4,64,128]{2,1,0:T(8,128)S(1)}, f32[4,64,128]{2,1,0:T(8,128)S(1)}, u32[]{:S(2)}, u32[]{:S(2)}) %collective-permute-start.12) | collective-permute-done | bytes 131104 | tf_op jit(solution)/shard_map/ppermute | solution.py:517
  38.5 0.5 %collective-permute-done.11.refs_1_ = f32[4,64,128]{2,1,0:T(8,128)S(1)} collective-permute-done((f32[4,64,128]{2,1,0:T(8,128)S(1)}, f32[4,64,128]{2,1,0:T(8,128)S(1)}, u32[]{:S(2)}, u32[]{:S(2)}) %collective-permute-start.11) | collective-permute-done | bytes 131104 | tf_op jit(solution)/shard_map/ppermute | solution.py:517
  39.0 0.8 %collective-permute-done.16.refs_6_ = f32[4,64,128]{2,1,0:T(8,128)S(1)} collective-permute-done((f32[4,64,128]{2,1,0:T(8,128)S(1)}, f32[4,64,128]{2,1,0:T(8,128)S(1)}, u32[]{:S(2)}, u32[]{:S(2)}) %collective-permute-start.16) | collective-permute-done | bytes 131104 | tf_op jit(solution)/shard_map/ppermute | solution.py:517
  39.8 0.5 %collective-permute-done.15.refs_5_ = f32[4,64,128]{2,1,0:T(8,128)S(1)} collective-permute-done((f32[4,64,128]{2,1,0:T(8,128)S(1)}, f32[4,64,128]{2,1,0:T(8,128)S(1)}, u32[]{:S(2)}, u32[]{:S(2)}) %collective-permute-start.15) | collective-permute-done | bytes 131104 | tf_op jit(solution)/shard_map/ppermute | solution.py:517
  40.4 9.1 %second.1 = (f32[16,16,128]{2,1,0:T(8,128)}, f32[16,16,128]{2,1,0:T(8,128)}) custom-call(f32[4,64,128]{2,1,0:T(8,128)S(1)} %pad_maximum_fusion.1.refs_0_, f32[4,64,128]{2,1,0:T(8,128)S(1)} %collective-permute-done.11.refs_1_, f32[4,64,128]{2,1,0:T(8,128)S(1)} %collective-permute-done.12.refs_2_, f32[4,64,128]{2,1,0:T(8,128)S(1)} %collective-permute-done.13.refs_3_, ...), custom_call_target="tpu_custom_call" | custom-call | tf_op jit(solution)/shard_map/second/pallas_call | solution.py:787
  (40 shorter events, 0.3 us)
Async XLA Ops:
  2.5 6.5 %collective-permute-start = (f32[2,16,128]{2,1,0:T(8,128)}, f32[2,16,128]{2,1,0:T(8,128)S(1)}, u32[]{:S(2)}, u32[]{:S(2)}) collective-permute-start(f32[2,16,128]{2,1,0:T(8,128)} %get-tuple-element.17), channel_id=1, source_target_pairs={{0,0},{8,16},{16,8},{24,24},{1,1},{9,17},{17,9},{25,25},{2,2},{10,... | collective-permute-start | bytes 49160 | tf_op jit(solution)/shard_map/ppermute | solution.py:517
  3.9 7.0 %collective-permute-start.1 = (f32[2,16,128]{2,1,0:T(8,128)}, f32[2,16,128]{2,1,0:T(8,128)S(1)}, u32[]{:S(2)}, u32[]{:S(2)}) collective-permute-start(f32[2,16,128]{2,1,0:T(8,128)} %get-tuple-element.18), channel_id=1, source_target_pairs={{0,8},{8,0},{16,24},{24,16},{1,9},{9,1},{17,25},{25,17},{2,10},{10... | collective-permute-start | bytes 49160 | tf_op jit(solution)/shard_map/ppermute | solution.py:517
  9.0 8.7 %collective-permute-start.4 = (f32[2,16,16,128]{3,2,1,0:T(8,128)S(1)}, f32[2,16,16,128]{3,2,1,0:T(8,128)S(1)}, u32[]{:S(2)}, u32[]{:S(2)}) collective-permute-start(f32[2,16,16,128]{3,2,1,0:T(8,128)S(1)} %pad_maximum_fusion.own.refs_0_), channel_id=1, source_target_pairs={{0,4},{4,0},{1,5},{5,1},{2,6},{6,2},{3,7},{7,3},{8,12},{12,8},{9,1... | collective-permute-start | bytes 786440 | tf_op jit(solution)/shard_map/ppermute | solution.py:517
  11.0 4.9 %collective-permute-start.2 = (f32[15,16,128]{2,1,0:T(8,128)S(1)}, f32[15,16,128]{2,1,0:T(8,128)S(1)}, u32[]{:S(2)}, u32[]{:S(2)}) collective-permute-start(f32[15,16,128]{2,1,0:T(8,128)S(1)} %get-tuple-element.20), channel_id=1, source_target_pairs={{0,1},{1,0},{2,3},{3,2},{4,5},{5,4},{6,7},{7,6},{8,9},{9,8},{10,11... | collective-permute-start | bytes 368648 | tf_op jit(solution)/shard_map/ppermute | solution.py:517
  12.6 3.3 %collective-permute-start.3 = (f32[15,16,128]{2,1,0:T(8,128)S(1)}, f32[15,16,128]{2,1,0:T(8,128)S(1)}, u32[]{:S(2)}, u32[]{:S(2)}) collective-permute-start(f32[15,16,128]{2,1,0:T(8,128)S(1)} %get-tuple-element.21), channel_id=1, source_target_pairs={{0,0},{1,2},{2,1},{3,3},{4,4},{5,6},{6,5},{7,7},{8,8},{9,10},{10,9... | collective-permute-start | bytes 368648 | tf_op jit(solution)/shard_map/ppermute | solution.py:517
  15.9 1.7 %collective-permute-start.6 = (f32[15,16,128]{2,1,0:T(8,128)S(1)}, f32[15,16,128]{2,1,0:T(8,128)S(1)}, u32[]{:S(2)}, u32[]{:S(2)}) collective-permute-start(f32[15,16,128]{2,1,0:T(8,128)S(1)} %collective-permute-done.2.refs_2_), channel_id=1, source_target_pairs={{0,4},{4,0},{1,5},{5,1},{2,6},{6,2},{3,7},{7,3},{8,12},{12,8},{9,1... | collective-permute-start | bytes 368648 | tf_op jit(solution)/shard_map/ppermute | solution.py:517
  15.9 1.7 %collective-permute-start.7 = (f32[15,16,128]{2,1,0:T(8,128)S(1)}, f32[15,16,128]{2,1,0:T(8,128)S(1)}, u32[]{:S(2)}, u32[]{:S(2)}) collective-permute-start(f32[15,16,128]{2,1,0:T(8,128)S(1)} %collective-permute-done.3.refs_3_), channel_id=1, source_target_pairs={{0,4},{4,0},{1,5},{5,1},{2,6},{6,2},{3,7},{7,3},{8,12},{12,8},{9,1... | collective-permute-start | bytes 368648 | tf_op jit(solution)/shard_map/ppermute | solution.py:517
  16.4 23.9 %copy-start = (bf16[4,256,256]{2,1,0:T(8,128)(2,1)S(1)}, bf16[4,256,256]{2,1,0:T(8,128)(2,1)}, u32[]{:S(2)}) copy-start(bf16[4,256,256]{2,1,0:T(8,128)(2,1)} %constant.22.clone.refs_16_) | copy-start | bytes 1572868
  16.4 1.2 %collective-permute-start.5 = (f32[2,2,16,128]{3,2,1,0:T(8,128)S(1)}, f32[2,2,16,128]{3,2,1,0:T(8,128)S(1)}, u32[]{:S(2)}, u32[]{:S(2)}) collective-permute-start(f32[2,2,16,128]{3,2,1,0:T(8,128)S(1)} %get-tuple-element.19.refs_1_), channel_id=1, source_target_pairs={{0,4},{4,0},{1,5},{5,1},{2,6},{6,2},{3,7},{7,3},{8,12},{12,8},{9,1... | collective-permute-start | bytes 98312 | tf_op jit(solution)/shard_map/ppermute | solution.py:517
  17.7 22.6 %copy-start.1 = (bf16[2,336,224]{2,1,0:T(8,128)(2,1)S(1)}, bf16[2,336,224]{2,1,0:T(8,128)(2,1)}, u32[]{:S(2)}) copy-start(bf16[2,336,224]{2,1,0:T(8,128)(2,1)} %constant.21.clone.refs_15_) | copy-start | bytes 903172
  20.6 6.3 %collective-permute-start.10 = (f32[64,128]{1,0:T(8,128)S(1)}, f32[64,128]{1,0:T(8,128)S(1)}, u32[]{:S(2)}, u32[]{:S(2)}) collective-permute-start(f32[64,128]{1,0:T(8,128)S(1)} %get-tuple-element.22), channel_id=1, source_target_pairs={{0,3},{1,2},{2,1},{3,0},{4,7},{5,6},{6,5},{7,4},{8,11},{9,10},{10,... | collective-permute-start | bytes 98312 | tf_op jit(solution)/shard_map/ppermute | solution.py:517
  24.3 4.8 %collective-permute-start.9 = (f32[64,128]{1,0:T(8,128)S(1)}, f32[64,128]{1,0:T(8,128)S(1)}, u32[]{:S(2)}, u32[]{:S(2)}) collective-permute-start(f32[64,128]{1,0:T(8,128)S(1)} %get-tuple-element.22), channel_id=1, source_target_pairs={{0,2},{1,3},{2,0},{3,1},{4,6},{5,7},{6,4},{7,5},{8,10},{9,11},{10,... | collective-permute-start | bytes 98312 | tf_op jit(solution)/shard_map/ppermute | solution.py:517
  26.4 3.9 %collective-permute-start.8 = (f32[64,128]{1,0:T(8,128)S(1)}, f32[64,128]{1,0:T(8,128)S(1)}, u32[]{:S(2)}, u32[]{:S(2)}) collective-permute-start(f32[64,128]{1,0:T(8,128)S(1)} %get-tuple-element.22), channel_id=1, source_target_pairs={{0,1},{1,0},{2,3},{3,2},{4,5},{5,4},{6,7},{7,6},{8,9},{9,8},{10,11... | collective-permute-start | bytes 98312 | tf_op jit(solution)/shard_map/ppermute | solution.py:517
  30.3 10.0 %copy-start.2 = (bf16[128,256]{1,0:T(8,128)(2,1)S(1)}, bf16[128,256]{1,0:T(8,128)(2,1)}, u32[]{:S(2)}) copy-start(bf16[128,256]{1,0:T(8,128)(2,1)} %constant.26.clone.refs_20_) | copy-start | bytes 196612
  30.3 10.0 %copy-start.3 = (bf16[256,128]{1,0:T(8,128)(2,1)S(1)}, bf16[256,128]{1,0:T(8,128)(2,1)}, u32[]{:S(2)}) copy-start(bf16[256,128]{1,0:T(8,128)(2,1)} %constant.25.clone.refs_19_) | copy-start | bytes 196612
  30.3 10.0 %copy-start.4 = (bf16[256,128]{1,0:T(8,128)(2,1)S(1)}, bf16[256,128]{1,0:T(8,128)(2,1)}, u32[]{:S(2)}) copy-start(bf16[256,128]{1,0:T(8,128)(2,1)} %constant.24.clone.refs_18_) | copy-start | bytes 196612
  30.3 10.0 %copy-start.5 = (bf16[128,256]{1,0:T(8,128)(2,1)S(1)}, bf16[128,256]{1,0:T(8,128)(2,1)}, u32[]{:S(2)}) copy-start(bf16[128,256]{1,0:T(8,128)(2,1)} %constant.23.clone.refs_17_) | copy-start | bytes 196612
  30.4 7.0 %collective-permute-start.13 = (f32[4,64,128]{2,1,0:T(8,128)S(1)}, f32[4,64,128]{2,1,0:T(8,128)S(1)}, u32[]{:S(2)}, u32[]{:S(2)}) collective-permute-start(f32[4,64,128]{2,1,0:T(8,128)S(1)} %pad_maximum_fusion.1.refs_0_), channel_id=1, source_target_pairs={{0,24},{8,16},{16,8},{24,0},{1,25},{9,17},{17,9},{25,1},{2,26},{10... | collective-permute-start | bytes 393224 | tf_op jit(solution)/shard_map/ppermute | solution.py:517
  31.9 6.6 %collective-permute-start.12 = (f32[4,64,128]{2,1,0:T(8,128)S(1)}, f32[4,64,128]{2,1,0:T(8,128)S(1)}, u32[]{:S(2)}, u32[]{:S(2)}) collective-permute-start(f32[4,64,128]{2,1,0:T(8,128)S(1)} %pad_maximum_fusion.1.refs_0_), channel_id=1, source_target_pairs={{0,16},{8,24},{16,0},{24,8},{1,17},{9,25},{17,1},{25,9},{2,18},{10... | collective-permute-start | bytes 393224 | tf_op jit(solution)/shard_map/ppermute | solution.py:517
  33.8 5.2 %collective-permute-start.11 = (f32[4,64,128]{2,1,0:T(8,128)S(1)}, f32[4,64,128]{2,1,0:T(8,128)S(1)}, u32[]{:S(2)}, u32[]{:S(2)}) collective-permute-start(f32[4,64,128]{2,1,0:T(8,128)S(1)} %pad_maximum_fusion.1.refs_0_), channel_id=1, source_target_pairs={{0,8},{8,0},{16,24},{24,16},{1,9},{9,1},{17,25},{25,17},{2,10},{10... | collective-permute-start | bytes 393224 | tf_op jit(solution)/shard_map/ppermute | solution.py:517
  33.9 5.1 %collective-permute-start.14 = (f32[4,64,128]{2,1,0:T(8,128)S(1)}, f32[4,64,128]{2,1,0:T(8,128)S(1)}, u32[]{:S(2)}, u32[]{:S(2)}) collective-permute-start(f32[4,64,128]{2,1,0:T(8,128)S(1)} %pad_maximum_fusion.1.refs_0_), channel_id=1, source_target_pairs={{0,4},{4,0},{1,5},{5,1},{2,6},{6,2},{3,7},{7,3},{8,12},{12,8},{9,1... | collective-permute-start | bytes 393224 | tf_op jit(solution)/shard_map/ppermute | solution.py:517
  37.3 1.7 %collective-permute-start.17 = (f32[4,64,128]{2,1,0:T(8,128)S(1)}, f32[4,64,128]{2,1,0:T(8,128)S(1)}, u32[]{:S(2)}, u32[]{:S(2)}) collective-permute-start(f32[4,64,128]{2,1,0:T(8,128)S(1)} %collective-permute-done.13.refs_3_), channel_id=1, source_target_pairs={{0,4},{4,0},{1,5},{5,1},{2,6},{6,2},{3,7},{7,3},{8,12},{12,8},{9,1... | collective-permute-start | bytes 393224 | tf_op jit(solution)/shard_map/ppermute | solution.py:517
  38.5 1.3 %collective-permute-start.16 = (f32[4,64,128]{2,1,0:T(8,128)S(1)}, f32[4,64,128]{2,1,0:T(8,128)S(1)}, u32[]{:S(2)}, u32[]{:S(2)}) collective-permute-start(f32[4,64,128]{2,1,0:T(8,128)S(1)} %collective-permute-done.12.refs_2_), channel_id=1, source_target_pairs={{0,4},{4,0},{1,5},{5,1},{2,6},{6,2},{3,7},{7,3},{8,12},{12,8},{9,1... | collective-permute-start | bytes 393224 | tf_op jit(solution)/shard_map/ppermute | solution.py:517
  39.0 1.3 %collective-permute-start.15 = (f32[4,64,128]{2,1,0:T(8,128)S(1)}, f32[4,64,128]{2,1,0:T(8,128)S(1)}, u32[]{:S(2)}, u32[]{:S(2)}) collective-permute-start(f32[4,64,128]{2,1,0:T(8,128)S(1)} %collective-permute-done.11.refs_1_), channel_id=1, source_target_pairs={{0,4},{4,0},{1,5},{5,1},{2,6},{6,2},{3,7},{7,3},{8,12},{12,8},{9,1... | collective-permute-start | bytes 393224 | tf_op jit(solution)/shard_map/ppermute | solution.py:517
  (5 other events, 40.8 us)
